TPU v7x, 32 devices: a whole 2x2x4 slice. The times are simulated.
32 devices in a mesh: groups: 2 (over x), dp: 16 (over z, y, core).
Axes of the slice: x: 2, y: 2, z: 4, core: 2. Of those that a mesh axis runs over, the one named last changes fastest.
Arguments:
- activations: bfloat16 [2, 32, 8192], P(None, ('groups', 'dp')), parts along dimension 1, may hold values from -6 to 6
- sample_ids: int32 [32], P(('groups', 'dp')), parts along dimension 0, may hold values from 0 to 31, as said below
- forward_exponent: int32 [2, 32, 64], P(None, ('groups', 'dp')), parts along dimension 1, may hold values from -8 to -2
- sender_base: float32 [2, 64, 8192], P(None, ('groups', 'dp')), parts along dimension 1, may hold values from -6 to 6
- receiver_base: float32 [2, 64, 8192], P(None, 'groups', 'dp'), parts along dimension 1, may hold values from -6 to 6
- norm_gain: float32 [8192], replicated, may hold values from 0.25 to 1.75
- up_weight: bfloat16 [8192, 14336], P(None, 'dp'), may hold values from -0.09375 to 0.09375
- down_weight: bfloat16 [14336, 8192], P('dp'), may hold values from -0.0625 to 0.0625
- cotangent: bfloat16 [2, 32, 8192], P(None, 'groups', 'dp'), parts along dimension 1, may hold values from -6 to 6
- backward_exponent: int32 [2, 32, 64], P(None, ('groups', 'dp')), parts along dimension 1, may hold values from -8 to -2
Outputs:
- new_sender_base: float32 [2, 64, 8192], P(None, ('groups', 'dp')), parts along dimension 1
- new_receiver_base: float32 [2, 64, 8192], P(None, 'groups', 'dp'), parts along dimension 1
- layer_out: bfloat16 [2, 32, 8192], P(None, 'groups', 'dp'), parts along dimension 1
- returned_grad: float32 [2, 32, 8192], P(None, ('groups', 'dp')), parts along dimension 1
There are 2 independent parts, one for each index of `groups`. A program takes and returns all parts, laid end to end along the dimension named above; an argument that names none is the same for every part. Nothing has to cross between parts.
Inputs may be any that keep to these rules, and one draw needn't show every extreme that they name: sample_ids[s] lies in s * 2 to s * 2 + 1.
All inputs are finite; a program needn't handle non-finite values.
Results may differ from a plain program's by a relative error of at most 0.0057.
Values may be sent and summed in bfloat16 or wider, within the bound.
No kernel may reach another device: no remote copies, remote signals or barrier semaphores. Data moves between devices by JAX's collectives and lax.ppermute only.
A program may use at most 128 MiB of HBM per device.

v0:
```python
import jax
import jax.numpy as jnp
import numpy as np
from jax import lax
from jax.sharding import PartitionSpec as P

clip_top = 448.0
eps = 1e-05


def powers(exponent, sign):
    levels = jnp.arange(-10, 1, dtype=jnp.int32)
    table = jnp.asarray(2.0 ** (sign * np.arange(-10, 1)), jnp.float32)
    matches = exponent[..., None] == levels
    return jnp.sum(jnp.where(matches, table, jnp.float32(0.0)), axis=-1)


def quantize(values, exponent):
    dims_all = values.shape
    blocks = values.reshape(
        dims_all[:-1] + (exponent.shape[-1], dims_all[-1] // exponent.shape[-1])
    )
    scaled = jnp.clip(blocks * powers(exponent, -1)[..., None], -clip_top, clip_top).astype(
        jnp.bfloat16
    )
    return (scaled.astype(jnp.float32) * powers(exponent, 1)[..., None]).reshape(dims_all)


def on_device(
    activations,
    sample_ids,
    forward_exponent,
    sender_base,
    receiver_base,
    norm_gain,
    up_weight,
    down_weight,
    cotangent,
    backward_exponent,
):
    my_index = lax.axis_index("dp")
    slot_count = sender_base.shape[1]
    local_ids = sample_ids - my_index * slot_count
    chosen_send = jnp.take(sender_base, local_ids, axis=1)
    delta = activations.astype(jnp.float32) - chosen_send
    sent = quantize(delta, forward_exponent).astype(jnp.bfloat16)
    new_sender_base = sender_base.at[:, local_ids, :].set(chosen_send + sent.astype(jnp.float32))
    arrived = lax.all_to_all(sent, "dp", split_axis=2, concat_axis=1, tiled=True)
    all_ids = lax.all_gather(sample_ids, "dp", axis=0, tiled=True)
    rebuilt = jnp.take(receiver_base, all_ids, axis=1) + arrived.astype(jnp.float32)
    new_receiver_base = receiver_base.at[:, all_ids, :].set(rebuilt)
    restored = rebuilt.astype(jnp.bfloat16)
    seq_len, seq_count, width_dev = restored.shape
    row_count = seq_len * seq_count
    width_all = up_weight.shape[0]
    start_col = my_index * width_dev
    gain_local = lax.dynamic_slice_in_dim(norm_gain, start_col, width_dev, 0)
    restored_wide = restored.astype(jnp.float32)
    piece = lax.all_gather(restored, "dp", axis=2, tiled=True)
    count = piece.shape[2]
    rows_in = piece.reshape(row_count, count).astype(jnp.float32)
    product = jnp.dot(
        (rows_in * norm_gain).astype(jnp.bfloat16), up_weight, preferred_element_type=jnp.float32
    )
    squares = jnp.sum(rows_in * rows_in, axis=1)
    inv_rms = lax.rsqrt(squares / width_all + eps)
    hidden = inv_rms[:, None] * product
    active = jax.nn.silu(hidden).astype(jnp.bfloat16)
    down_terms = jnp.dot(active, down_weight, preferred_element_type=jnp.float32).reshape(
        seq_len, seq_count, width_all
    )
    summed_out = lax.psum_scatter(down_terms, "dp", scatter_dimension=2, tiled=True)
    layer_out = (restored_wide + summed_out).astype(jnp.bfloat16)
    piece = lax.all_gather(cotangent, "dp", axis=2, tiled=True)
    count = piece.shape[2]
    grad_active = lax.dot_general(
        piece.reshape(row_count, count),
        down_weight,
        (((1,), (1,)), ((), ())),
        preferred_element_type=jnp.float32,
    )
    sigma = jax.nn.sigmoid(hidden)
    grad_hidden = (grad_active * sigma * (1.0 + hidden * (1.0 - sigma))).astype(jnp.bfloat16)
    curvature = lax.psum(jnp.sum(grad_hidden.astype(jnp.float32) * hidden, axis=1), "dp")
    correction = curvature * inv_rms * inv_rms / width_all
    grad_terms = lax.dot_general(
        grad_hidden, up_weight, (((1,), (1,)), ((), ())), preferred_element_type=jnp.float32
    )
    grad_share = lax.psum_scatter(
        grad_terms.reshape(seq_len, seq_count, width_all), "dp", scatter_dimension=2, tiled=True
    )
    grad_local = (
        cotangent.astype(jnp.float32)
        + inv_rms.reshape(seq_len, seq_count, 1) * gain_local * grad_share
        - correction.reshape(seq_len, seq_count, 1) * restored_wide
    )
    grad_input = lax.all_to_all(
        grad_local.astype(jnp.bfloat16), "dp", split_axis=1, concat_axis=2, tiled=True
    ).astype(grad_local.dtype)
    returned_grad = quantize(grad_input, backward_exponent)
    return (new_sender_base, new_receiver_base, layer_out, returned_grad)


def solution(mesh):
    placed = (
        P(None, ("groups", "dp"), None),
        P(("groups", "dp")),
        P(None, ("groups", "dp"), None),
        P(None, ("groups", "dp"), None),
        P(None, "groups", "dp"),
        P(),
        P(None, "dp"),
        P("dp", None),
        P(None, "groups", "dp"),
        P(None, ("groups", "dp"), None),
    )
    return jax.shard_map(
        on_device,
        mesh=mesh,
        in_specs=placed,
        out_specs=(
            P(None, ("groups", "dp"), None),
            P(None, "groups", "dp"),
            P(None, "groups", "dp"),
            P(None, ("groups", "dp"), None),
        ),
        check_vma=False,
    )
```

profile of v0, /device:TPU:0, one launch (start us, length us, event | category | flops | bytes accessed | tf_op | source)
XLA Modules:
  0.0 312.8 jit_solution(6439391207995139700)
XLA Ops:
  7.2 0.9 copy.70
  9.7 1.4 and_reduce_fusion
  12.2 1.5 add_select_fusion
  13.7 6.8 %copy.48 = bf16[2,1,8192]{0,1,2:T(2,128)(2,1)} copy(bf16[2,1,8192]{2,0,1:T(2,128)(2,1)S(1)} %get-tuple-element.54) | data formatting | bytes 65536 | tf_op jit(solution)/shard_map/convert_element_type | solution.py:46
  21.0 45.2 %reduce.13 = bf16[8192,2]{1,0:T(8,128)(2,1)S(1)} reduce(bf16[8192,1,2]{2,1,0:T(2,128)(2,1)} %bitcast.42, bf16[]{:T(256)} %broadcast.332), dimensions={1}, to_apply=%bitcast.33.reduce_sub_computation | reduce | bytes 65538
  66.3 3.8 %reshape.304 = bf16[16,2,512]{2,1,0:T(2,128)(2,1)} reshape(bf16[8192,2]{1,0:T(8,128)(2,1)S(1)} %reduce.13) | data formatting | bytes 65536
  70.1 1.2 dynamic-slice.14
  72.1 7.4 %all-to-all-start = ((bf16[16,2,512]{2,1,0:T(2,128)(2,1)}), bf16[16,2,512]{2,1,0:T(2,128)(2,1)S(1)}, u32[]{:S(2)}, u32[]{:S(2)}) async-start(bf16[16,2,512]{2,1,0:T(2,128)(2,1)} %reshape.304), calls=%async_computation | async-start | bytes 65536 | tf_op jit(solution)/shard_map/all_to_all | solution.py:48
  79.5 12.4 %all-reduce = s32[16]{0:T(128)S(1)} all-reduce(s32[16]{0:T(128)S(1)} %dynamic-update-slice.4), channel_id=1, replica_groups=mesh['groups'=2,'dp'=16] {'dp'}, use_global_device_ids=true, to_apply=%add | all-reduce | flops 16 | bytes 128
  92.0 19.6 %all_gather.11 = bf16[2,16,8192]{2,1,0:T(8,128)(2,1)S(1)} all-gather(bf16[2,16,512]{2,1,0:T(8,128)(2,1)} %param.24), channel_id=1, replica_groups=mesh['groups'=2,'dp'=16] {'dp'}, dimensions={2}, use_global_device_ids=true | all-gather | bytes 557056 | tf_op jit(solution)/shard_map/all_gather | solution.py:74
  112.3 8.4 %reshape.305 = bf16[8192,1,2]{2,1,0:T(2,128)(2,1)} reshape(bf16[16,2,512]{2,1,0:T(2,128)(2,1)S(1)} %all-to-all-done) | data formatting | bytes 65536
  120.6 8.1 %copy.49 = bf16[2,1,8192]{2,0,1:T(2,128)(2,1)S(1)} copy(bf16[2,1,8192]{0,1,2:T(2,128)(2,1)} %bitcast.43) | data formatting | bytes 65536 | tf_op jit(solution)/shard_map/all_to_all | solution.py:48
  128.8 19.8 %all_gather.10 = bf16[2,16,8192]{2,1,0:T(8,128)(2,1)S(1)} all-gather(bf16[2,16,512]{2,1,0:T(8,128)(2,1)S(1)} %get-tuple-element.55), channel_id=1, replica_groups=mesh['groups'=2,'dp'=16] {'dp'}, dimensions={2}, use_global_device_ids=true | all-gather | bytes 557056 | tf_op jit(solution)/shard_map/all_gather | solution.py:59
  149.1 7.5 %convolution_multiply_fusion.1 = f32[32,896]{1,0:T(8,128)S(1)} fusion(bf16[32,8192]{1,0:T(8,128)(2,1)S(1)} %fusion.2, bf16[8192,896]{1,0:T(8,128)(2,1)} %param.22, f32[32]{0:T(128)S(1)} %rsqrt.15), kind=kOutput, calls=%fused_computation.4 | convolution fusion | flops 469790720 | bytes 15319168 | tf_op jit(solution)/shard_map/dot_general | solution.py:62
  156.6 9.7 %multiply_reduce_fusion.1 = (f32[32]{0:T(128)S(1)}, bf16[32,896]{1,0:T(8,128)(2,1)S(1)}) fusion(f32[32,896]{1,0:T(8,128)S(1)} %convolution_multiply_fusion.1, bf16[32,8192]{1,0:T(8,128)(2,1)S(1)} %bitcast.46, bf16[896,8192]{1,0:T(8,128)(2,1)} %param.23), kind=kOutput, calls=%fused_computation.9 | convolution fusion | flops 470106080 | bytes 15376512 | tf_op jit(solution)/shard_map/dot_general | solution.py:76
  166.3 10.6 %fusion.18 = f32[32,8192]{1,0:T(8,128)} fusion(bf16[32,896]{1,0:T(8,128)(2,1)S(1)} %get-tuple-element.60, bf16[8192,896]{1,0:T(8,128)(2,1)} %param.22), kind=kOutput, calls=%fused_computation.48 | convolution fusion | flops 469762048 | bytes 15785984 | tf_op jit(solution)/shard_map/dot_general | solution.py:86
  177.0 8.9 %fusion.8 = f32[32,8192]{1,0:T(8,128)} fusion(bf16[896,8192]{1,0:T(8,128)(2,1)} %param.23, f32[32,896]{1,0:T(8,128)S(1)} %convolution_multiply_fusion.1), kind=kOutput, calls=%fused_computation.26 | convolution fusion | flops 469905408 | bytes 15843328 | tf_op jit(solution)/shard_map/dot_general | solution.py:69
  186.0 30.4 %psum.7 = f32[32]{0:T(128)S(1)} all-reduce(f32[32]{0:T(128)S(1)} %get-tuple-element.59), channel_id=1, replica_groups=mesh['groups'=2,'dp'=16] {'dp'}, use_global_device_ids=true, to_apply=%region_8.9 | all-reduce | flops 32 | bytes 256 | tf_op jit(solution)/shard_map/psum | solution.py:84
  216.5 15.7 %reduce-scatter.5.cloned.1.call-done = f32[2,16,512]{2,1,0:T(8,128)} async-done(((f32[2,16,8192]{2,1,0:T(8,128)}), f32[2,16,512]{2,1,0:T(8,128)}) %reduce-scatter.5.cloned.1.call-update) | async-done | bytes 65552 | tf_op jit(solution)/shard_map/reduce_scatter | solution.py:89
  232.2 60.5 %reduce-scatter.3.cloned.1.call-done = f32[2,16,512]{2,1,0:T(8,128)} async-done(((f32[2,16,8192]{2,1,0:T(8,128)}), f32[2,16,512]{2,1,0:T(8,128)}) %reduce-scatter.3.cloned.1.call-update) | async-done | bytes 65552 | tf_op jit(solution)/shard_map/reduce_scatter | solution.py:72
  292.7 1.5 fusion.5
  294.9 3.7 %all-to-all-start.1 = ((bf16[2,16,512]{2,0,1:T(2,128)(2,1)}), bf16[2,16,512]{2,0,1:T(2,128)(2,1)S(1)}, u32[]{:S(2)}, u32[]{:S(2)}) async-start(bf16[2,16,512]{2,0,1:T(2,128)(2,1)} %copy.50), calls=%async_computation.3 | async-start | bytes 65536 | tf_op jit(solution)/shard_map/all_to_all | solution.py:97
  299.7 1.4 scatter_fusion
  301.1 4.1 %all-to-all-done.1 = bf16[2,16,512]{2,0,1:T(2,128)(2,1)S(1)} async-done(((bf16[2,16,512]{2,0,1:T(2,128)(2,1)}), bf16[2,16,512]{2,0,1:T(2,128)(2,1)S(1)}, u32[]{:S(2)}, u32[]{:S(2)}) %all-to-all-start.1) | async-done | bytes 32800 | tf_op jit(solution)/shard_map/all_to_all | solution.py:97
  (46 shorter events, 7.2 us)
Async XLA Ops:
  7.2 141.8 %copy-start.3 = (f32[8192]{0:T(1024)S(1)}, f32[8192]{0:T(1024)}, u32[]{:S(2)}) copy-start(f32[8192]{0:T(1024)} %param.21) | copy-start | bytes 98308
  72.1 40.2 %all-to-all-start = ((bf16[16,2,512]{2,1,0:T(2,128)(2,1)}), bf16[16,2,512]{2,1,0:T(2,128)(2,1)S(1)}, u32[]{:S(2)}, u32[]{:S(2)}) async-start(bf16[16,2,512]{2,1,0:T(2,128)(2,1)} %reshape.304), calls=%async_computation | async-start | bytes 65536 | tf_op jit(solution)/shard_map/all_to_all | solution.py:48
  79.5 152.8 %reduce-scatter.5.cloned.1.call-start = ((), (), s32[]{:S(2)}) async-start(), calls=%async_computation.5 | async-start | bytes 1114112 | tf_op jit(solution)/shard_map/reduce_scatter | solution.py:89
  176.9 115.8 %copy-start.2 = (bf16[2,16,512]{2,1,0:T(8,128)(2,1)S(1)}, bf16[2,16,512]{2,1,0:T(8,128)(2,1)}, u32[]{:S(2)}) copy-start(bf16[2,16,512]{2,1,0:T(8,128)(2,1)} %param.24) | copy-start | bytes 98308
  176.9 115.8 %reduce-scatter.3.cloned.1.call-start = ((), (), s32[]{:S(2)}) async-start(), calls=%async_computation.4 | async-start | bytes 1114112 | tf_op jit(solution)/shard_map/reduce_scatter | solution.py:72
  294.9 10.4 %all-to-all-start.1 = ((bf16[2,16,512]{2,0,1:T(2,128)(2,1)}), bf16[2,16,512]{2,0,1:T(2,128)(2,1)S(1)}, u32[]{:S(2)}, u32[]{:S(2)}) async-start(bf16[2,16,512]{2,0,1:T(2,128)(2,1)} %copy.50), calls=%async_computation.3 | async-start | bytes 65536 | tf_op jit(solution)/shard_map/all_to_all | solution.py:97
  299.7 6.3 %copy-start.1 = (f32[2,2,8192]{2,1,0:T(2,128)}, f32[2,2,8192]{2,1,0:T(2,128)S(1)}, u32[]{:S(2)}) copy-start(f32[2,2,8192]{2,1,0:T(2,128)S(1)} %scatter.12) | copy-start | bytes 393220
  301.1 4.9 %copy-start = (f32[2,32,512]{2,1,0:T(8,128)}, f32[2,32,512]{2,1,0:T(8,128)S(1)}, u32[]{:S(2)}) copy-start(f32[2,32,512]{2,1,0:T(8,128)S(1)} %scatter_fusion) | copy-start | bytes 393220
Sparse Core Ops, SparseCore 0:
  177.1 55.1 reduce-scatter.4
  236.3 56.3 reduce-scatter.2
where the time goes:
time: 314 us; the launch traced here: 313 us
  blocking collectives  82.3 us (26%)
  waiting for transfers between devices  80.3 us (26%)
  other arithmetic  50.9 us (16%)
  matrix products  36.7 us (12%)
  local copies, waits for them, and re-layouts  36.4 us (12%)
  between operations  14.9 us (5%)
  starting transfers between devices  11.2 us (4%)
    reduce_scatter x1, waiting for transfers between devices, on_device(): lax.psum_scatter(down_terms, 'dp', scatter_dimension=2, tiled=True)  60.5 us
    unnamed x2, other arithmetic  45.2 us
    psum x1, blocking collectives, on_device(): lax.psum(jnp.sum(grad_hidden.astype(jnp.float32) * hidden, axis=1), 'dp')  30.4 us
    all_gather x1, blocking collectives, on_device(): piece = lax.all_gather(restored, 'dp', axis=2, tiled=True)  19.8 us
    all_gather x1, blocking collectives, on_device(): piece = lax.all_gather(cotangent, 'dp', axis=2, tiled=True)  19.6 us
    unnamed x17, local copies, waits for them, and re-layouts  17.3 us
    reduce_scatter x1, waiting for transfers between devices, on_device(): lax.psum_scatter(grad_terms.reshape(seq_len, seq_count, width_all), 'dp',...  15.7 us
    unnamed x1, blocking collectives  12.4 us
  transfers between devices with their start and end apart: 4, of which 3 were waited for; matrix products, arithmetic and copies ran while one was open for 4% of the time, Pallas kernels for 0%

commit v1 on v0

v1 whole, which is shorter than its diff:
```python
import functools

import jax
import jax.numpy as jnp
from jax import lax
from jax.experimental import pallas as pl
from jax.experimental.pallas import tpu as pltpu
from jax.sharding import PartitionSpec as P

clip_top = 448.0
eps = 1e-05
LANES = 128
f32 = jnp.float32
bf16 = jnp.bfloat16
VMEM = pl.BlockSpec(memory_space=pltpu.VMEM)
SMEM = pl.BlockSpec(memory_space=pltpu.SMEM)


def powers(exponent, sign):
    total = jnp.zeros(exponent.shape, f32)
    for level in range(-10, 1):
        total = jnp.where(exponent == level, f32(2.0 ** (sign * level)), total)
    return total


def params(megabytes):
    return pltpu.CompilerParams(vmem_limit_bytes=megabytes << 20)


def send_kernel(offset_ref, act_ref, expo_ref, base_ref, out_ref, new_ref, rows_ref):
    n, rows, _ = out_ref.shape
    width = act_ref.shape[1]
    per_dev = width // LANES // n
    first = offset_ref[0] == 0
    down, up = powers(expo_ref[...], -1), powers(expo_ref[...], 1)
    old = [base_ref[p] for p in range(2)]
    chosen = jnp.concatenate([jnp.where(first, o[0:1], o[1:2]) for o in old], axis=0)
    delta = act_ref[...].astype(f32) - chosen
    fill = jnp.full((rows - 2 * per_dev, LANES), offset_ref[0].astype(f32))
    pieces = []
    for b in range(width // LANES):
        scaled = delta[:, b * LANES : (b + 1) * LANES] * down[:, b : b + 1]
        kept = jnp.clip(scaled, -clip_top, clip_top).astype(bf16).astype(f32) * up[:, b : b + 1]
        d, c = divmod(b, per_dev)
        rows_ref[d, 2 * c : 2 * c + 2, :] = kept
        pieces.append(kept)
    for d in range(n):
        rows_ref[d, 2 * per_dev :, :] = fill
    out_ref[...] = rows_ref[...].astype(bf16)
    new = chosen + jnp.concatenate(pieces, axis=1)
    for p in range(2):
        row = new[p : p + 1]
        new_ref[p, 0:1, :] = jnp.where(first, row, old[p][0:1])
        new_ref[p, 1:2, :] = jnp.where(first, old[p][1:2], row)


def rebuild_kernel(arrived_ref, base_ref, new_ref, out_ref, share_ref, rows_ref, slots_ref):
    n, rows, _ = arrived_ref.shape
    copies, _, width = out_ref.shape
    rows_ref[...] = arrived_ref[...].astype(f32).reshape(n * rows, LANES)
    per_dev = width // LANES
    first = rows_ref[pl.ds(2 * per_dev, n, stride=rows), :] == 0.0
    for p in range(2):
        for c in range(per_dev):
            cols = slice(c * LANES, (c + 1) * LANES)
            sent = rows_ref[pl.ds(2 * c + p, n, stride=rows), :]
            at = p * per_dev + c
            slots_ref[at] = base_ref[p, :, cols]
            even = slots_ref[at, pl.ds(0, n, stride=2), :]
            odd = slots_ref[at, pl.ds(1, n, stride=2), :]
            rebuilt = jnp.where(first, even, odd) + sent
            slots_ref[at, pl.ds(0, n, stride=2), :] = jnp.where(first, rebuilt, even)
            slots_ref[at, pl.ds(1, n, stride=2), :] = jnp.where(first, odd, rebuilt)
            new_ref[p, :, cols] = slots_ref[at]
            restored = rebuilt.astype(bf16)
            share_ref[p * n : (p + 1) * n, cols] = restored
            for k in range(copies):
                out_ref[k, p * n : (p + 1) * n, cols] = restored


def dot_nt(a, b):
    return lax.dot_general(a, b, (((1,), (1,)), ((), ())), preferred_element_type=f32)


def own_rows(piece_ref, own_ref, me, owner):
    n = piece_ref.shape[0] // 2
    for p in range(2):
        own_ref[pl.ds(p * n + owner, 1), :] = piece_ref[pl.ds(p * n + me, 1), :]


def grad_active_kernel(owner_of, me_ref, a_ref, b_ref, weight_ref, out_ref, own_ref, piece_ref):
    i, half = pl.program_id(0), a_ref.shape[0]
    me = me_ref[0]

    @pl.when(i == 0)
    def _():
        out_ref[...] = jnp.zeros_like(out_ref)

    k = lax.rem(i, half)
    piece = jnp.where(i < half, a_ref[k], b_ref[k])
    out_ref[...] += dot_nt(piece, weight_ref[...])
    piece_ref[...] = piece.astype(f32)
    own_rows(piece_ref, own_ref, me, owner_of(i, me))


def up_kernel(
    owner_of, width_all, me_ref, a_ref, b_ref, gain_ref, weight_ref, ga_ref,
    active_ref, gh_ref, own_ref, piece_ref, acc_ref, square_ref,
):
    i, half = pl.program_id(0), a_ref.shape[0]
    me = me_ref[0]

    @pl.when(i == 0)
    def _():
        acc_ref[...] = jnp.zeros_like(acc_ref)
        square_ref[...] = jnp.zeros_like(square_ref)

    k = lax.rem(i, half)
    piece = jnp.where(i < half, a_ref[k], b_ref[k]).astype(f32)
    piece_ref[...] = piece
    own_rows(piece_ref, own_ref, me, owner_of(i, me))
    squares = piece * piece
    for c in range(piece.shape[1] // LANES):
        square_ref[...] += squares[:, c * LANES : (c + 1) * LANES]
    scaled = (piece * gain_ref[0]).astype(bf16)
    acc_ref[...] += jnp.dot(scaled, weight_ref[...], preferred_element_type=f32)

    @pl.when(i == pl.num_programs(0) - 1)
    def _():
        total = jnp.sum(square_ref[...], axis=1, keepdims=True)
        hidden = lax.rsqrt(total / width_all + eps) * acc_ref[...]
        sigma = jax.nn.sigmoid(hidden)
        active_ref[...] = (hidden * sigma).astype(bf16)
        gh_ref[...] = (ga_ref[...] * sigma * (1.0 + hidden * (1.0 - sigma))).astype(bf16)


def down_kernel(me_ref, active_ref, weight_ref, out_ref):
    out_ref[0] = jnp.dot(active_ref[...], weight_ref[...], preferred_element_type=f32).astype(bf16)


def grad_norm_kernel(me_ref, gh_ref, weight_ref, send_ref, keep_ref, rows_ref):
    i = pl.program_id(0)
    half, tokens, width = send_ref.shape
    n = 2 * half
    terms = dot_nt(gh_ref[...], weight_ref[...])
    per_step = terms.shape[1] // width
    chunks = width // LANES
    for j in range(per_step):
        share = i * per_step + j
        for p in range(2):
            for c in range(chunks):
                at = j * width + c * LANES
                rows_ref[c, pl.ds(p * n + share, n, stride=tokens), :] = terms[
                    p * n : (p + 1) * n, at : at + LANES
                ]

    @pl.when(i == pl.num_programs(0) - 1)
    def _():
        core = lax.rem(me_ref[0], 2)
        for k in range(half):
            keep_at = pl.multiple_of((2 * k + core) * tokens, tokens)
            send_at = pl.multiple_of((2 * k + 1 - core) * tokens, tokens)
            for c in range(chunks):
                cols = slice(c * LANES, (c + 1) * LANES)
                keep_ref[k, :, cols] = rows_ref[c, pl.ds(keep_at, tokens), :].astype(bf16)
                send_ref[k, :, cols] = rows_ref[c, pl.ds(send_at, tokens), :].astype(bf16)


def pair_kernel(grad_ref, grad_in_ref, out_ref, out_in_ref, sum_ref):
    sum_ref[:, 0] = (grad_ref[...].astype(f32) + grad_in_ref[...].astype(f32)).astype(bf16)
    sum_ref[:, 1] = (out_ref[...].astype(f32) + out_in_ref[...].astype(f32)).astype(bf16)


def final_kernel(
    width_all, terms_ref, restored_ref, own_ref, cot_ref, gain_ref, expo_ref, layer_ref, grad_ref
):
    half, _, tokens, width = terms_ref.shape
    n = 2 * half
    grad = terms_ref[0, 0].astype(f32)
    layer = terms_ref[0, 1].astype(f32)
    for k in range(1, half):
        grad = grad + terms_ref[k, 0].astype(f32)
        layer = layer + terms_ref[k, 1].astype(f32)
    layer_ref[...] = (restored_ref[...].astype(f32) + layer).astype(bf16)
    down, up = powers(expo_ref[...], -1), powers(expo_ref[...], 1)
    gain = gain_ref[...]
    per_dev = width // LANES
    blocks = n * per_dev
    at_row = lax.broadcasted_iota(jnp.int32, (n, blocks), 0)
    at_lane = lax.broadcasted_iota(jnp.int32, (n, blocks), 1)
    for p in range(2):
        rows = slice(p * n, (p + 1) * n)
        own, norm = own_ref[rows, :], grad[rows, :]
        inv_rms = lax.rsqrt(jnp.sum(own * own, keepdims=True) / width_all + eps)
        scaled_in = (own * gain).astype(bf16).astype(f32)
        curvature = inv_rms * jnp.sum(scaled_in * norm, keepdims=True)
        correction = curvature * inv_rms * inv_rms / width_all
        value = cot_ref[rows, :] + inv_rms * gain * norm - correction * own
        for c in range(per_dev):
            at = at_lane == at_row * per_dev + c
            shrink = jnp.sum(jnp.where(at, down[p : p + 1], 0.0), axis=1, keepdims=True)
            grow = jnp.sum(jnp.where(at, up[p : p + 1], 0.0), axis=1, keepdims=True)
            scaled = value[:, c * LANES : (c + 1) * LANES] * shrink
            kept = jnp.clip(scaled, -clip_top, clip_top).astype(bf16).astype(f32) * grow
            grad_ref[p, pl.ds(c, n, stride=per_dev), :] = kept


def on_device(
    activations,
    sample_ids,
    forward_exponent,
    sender_base,
    receiver_base,
    norm_gain,
    up_weight,
    down_weight,
    cotangent,
    backward_exponent,
    *,
    n,
):
    half, quarter = n // 2, n // 4
    tokens = 2 * n
    width_all, hidden_dev = up_weight.shape
    width = width_all // n
    me = lax.axis_index("dp").astype(jnp.int32)
    me_in = me.reshape(1)
    core_pair = [(d, d ^ 1) for d in range(n)]
    row_pair = [(d, d ^ 2) for d in range(n)]
    same_core = [[2 * k + c for k in range(half)] for c in range(2)]

    cot = cotangent.reshape(1, tokens, width)
    line = [cot]
    for r in range(1, quarter):
        line.append(lax.ppermute(cot, "dp", [(d, (d + 4 * r) % n) for d in range(n)]))
    line = jnp.concatenate(line, axis=0)
    cot_a = jnp.concatenate([line, lax.ppermute(line, "dp", row_pair)], axis=0)
    cot_b = lax.ppermute(cot_a, "dp", core_pair)

    def cot_owner(i, who):
        core, row, along = lax.rem(who, 2), lax.rem(who // 2, 2), who // 4
        other_core, other_row, back = i // half, lax.rem(i // quarter, 2), lax.rem(i, quarter)
        at = lax.rem(along - back + quarter, quarter)
        return 4 * at + 2 * lax.rem(row + other_row, 2) + lax.rem(core + other_core, 2)

    def token_owner(i, who):
        return 2 * lax.rem(i, half) + lax.rem(who + i // half, 2)

    slots = sender_base.shape[1]
    offset = sample_ids - slots * me
    rows = -(-(2 * width // LANES + 1) // 16) * 16
    blocks, new_sender_base = pl.pallas_call(
        send_kernel,
        out_shape=(
            jax.ShapeDtypeStruct((n, rows, LANES), bf16),
            jax.ShapeDtypeStruct(sender_base.shape, f32),
        ),
        in_specs=[SMEM, VMEM, VMEM, VMEM],
        out_specs=(VMEM, VMEM),
        scratch_shapes=[pltpu.VMEM((n, rows, LANES), f32)],
        compiler_params=params(16),
    )(offset, activations.reshape(2, width_all), forward_exponent.reshape(2, -1), sender_base)
    arrived = lax.all_to_all(blocks, "dp", split_axis=0, concat_axis=0, tiled=True)

    new_receiver_base, restored, share = pl.pallas_call(
        rebuild_kernel,
        out_shape=(
            jax.ShapeDtypeStruct(receiver_base.shape, f32),
            jax.ShapeDtypeStruct((half, tokens, width), bf16),
            jax.ShapeDtypeStruct((tokens, width), bf16),
        ),
        in_specs=[VMEM, VMEM],
        out_specs=(VMEM, VMEM, VMEM),
        scratch_shapes=[
            pltpu.VMEM((n * rows, LANES), f32),
            pltpu.VMEM((2 * width // LANES, 2 * n, LANES), f32),
        ],
        compiler_params=params(16),
    )(arrived, receiver_base)
    rest_a = lax.all_to_all(
        restored, "dp", split_axis=0, concat_axis=0, axis_index_groups=same_core, tiled=True
    )
    rest_b = lax.ppermute(rest_a, "dp", core_pair)

    whole = lambda *shape: pl.BlockSpec(shape, lambda i, who: (0,) * len(shape))
    pieces = whole(half, tokens, width)

    grad_active, own_cot = pl.pallas_call(
        functools.partial(grad_active_kernel, cot_owner),
        out_shape=(
            jax.ShapeDtypeStruct((tokens, hidden_dev), f32),
            jax.ShapeDtypeStruct((tokens, width), f32),
        ),
        grid_spec=pltpu.PrefetchScalarGridSpec(
            num_scalar_prefetch=1,
            grid=(n,),
            in_specs=[
                pieces,
                pieces,
                pl.BlockSpec((hidden_dev, width), lambda i, who: (0, cot_owner(i, who[0]))),
            ],
            out_specs=(whole(tokens, hidden_dev), whole(tokens, width)),
            scratch_shapes=[pltpu.VMEM((tokens, width), f32)],
        ),
        compiler_params=params(24),
        cost_estimate=pl.CostEstimate(
            flops=2 * tokens * width_all * hidden_dev,
            bytes_accessed=2 * width_all * hidden_dev,
            transcendentals=0,
        ),
    )(me_in, cot_a, cot_b, down_weight)

    active, grad_hidden, own_restored = pl.pallas_call(
        functools.partial(up_kernel, token_owner, width_all),
        out_shape=(
            jax.ShapeDtypeStruct((tokens, hidden_dev), bf16),
            jax.ShapeDtypeStruct((tokens, hidden_dev), bf16),
            jax.ShapeDtypeStruct((tokens, width), f32),
        ),
        grid_spec=pltpu.PrefetchScalarGridSpec(
            num_scalar_prefetch=1,
            grid=(n,),
            in_specs=[
                pieces,
                pieces,
                pl.BlockSpec((1, 1, width), lambda i, who: (token_owner(i, who[0]), 0, 0)),
                pl.BlockSpec((width, hidden_dev), lambda i, who: (token_owner(i, who[0]), 0)),
                whole(tokens, hidden_dev),
            ],
            out_specs=(whole(tokens, hidden_dev), whole(tokens, hidden_dev), whole(tokens, width)),
            scratch_shapes=[
                pltpu.VMEM((tokens, width), f32),
                pltpu.VMEM((tokens, hidden_dev), f32),
                pltpu.VMEM((tokens, LANES), f32),
            ],
        ),
        compiler_params=params(24),
        cost_estimate=pl.CostEstimate(
            flops=2 * tokens * width_all * hidden_dev,
            bytes_accessed=2 * width_all * hidden_dev,
            transcendentals=0,
        ),
    )(me_in, rest_a, rest_b, norm_gain.reshape(n, 1, width), up_weight, grad_active)

    step = max(width, 1024)
    grad_send, grad_keep = pl.pallas_call(
        grad_norm_kernel,
        out_shape=(jax.ShapeDtypeStruct((half, tokens, width), bf16),) * 2,
        grid_spec=pltpu.PrefetchScalarGridSpec(
            num_scalar_prefetch=1,
            grid=(width_all // step,),
            in_specs=[
                whole(tokens, hidden_dev),
                pl.BlockSpec((step, hidden_dev), lambda i, who: (i, 0)),
            ],
            out_specs=(pieces, pieces),
            scratch_shapes=[pltpu.VMEM((width // LANES, n * tokens, LANES), f32)],
        ),
        compiler_params=params(24),
        cost_estimate=pl.CostEstimate(
            flops=2 * tokens * width_all * hidden_dev,
            bytes_accessed=2 * width_all * hidden_dev,
            transcendentals=0,
        ),
    )(me_in, grad_hidden, up_weight)
    grad_in = lax.ppermute(grad_send, "dp", core_pair)

    def down_terms(other):
        return pl.pallas_call(
            down_kernel,
            out_shape=jax.ShapeDtypeStruct((half, tokens, width), bf16),
            grid_spec=pltpu.PrefetchScalarGridSpec(
                num_scalar_prefetch=1,
                grid=(half,),
                in_specs=[
                    whole(tokens, hidden_dev),
                    pl.BlockSpec(
                        (hidden_dev, width),
                        lambda i, who: (0, 2 * i + lax.rem(who[0] + other, 2)),
                    ),
                ],
                out_specs=pl.BlockSpec((1, tokens, width), lambda i, who: (i, 0, 0)),
            ),
            compiler_params=params(24),
            cost_estimate=pl.CostEstimate(
                flops=tokens * width_all * hidden_dev,
                bytes_accessed=width_all * hidden_dev,
                transcendentals=0,
            ),
        )(me_in, active, down_weight)

    out_in = lax.ppermute(down_terms(1), "dp", core_pair)
    out_keep = down_terms(0)

    sums = pl.pallas_call(
        pair_kernel,
        out_shape=jax.ShapeDtypeStruct((half, 2, tokens, width), bf16),
        in_specs=[VMEM] * 4,
        out_specs=VMEM,
        compiler_params=params(16),
    )(grad_keep, grad_in, out_keep, out_in)
    terms = lax.all_to_all(
        sums, "dp", split_axis=0, concat_axis=0, axis_index_groups=same_core, tiled=True
    )
    layer_out, returned = pl.pallas_call(
        functools.partial(final_kernel, width_all),
        out_shape=(
            jax.ShapeDtypeStruct((tokens, width), bf16),
            jax.ShapeDtypeStruct((2, width_all // LANES, LANES), f32),
        ),
        in_specs=[VMEM] * 6,
        out_specs=(VMEM, VMEM),
        compiler_params=params(16),
    )(
        terms,
        share,
        own_restored,
        own_cot,
        norm_gain.reshape(n, width),
        backward_exponent.reshape(2, -1),
    )
    return (
        new_sender_base,
        new_receiver_base,
        layer_out.reshape(2, n, width),
        returned.reshape(2, 1, width_all),
    )


def solution(mesh):
    placed = (
        P(None, ("groups", "dp"), None),
        P(("groups", "dp")),
        P(None, ("groups", "dp"), None),
        P(None, ("groups", "dp"), None),
        P(None, "groups", "dp"),
        P(),
        P(None, "dp"),
        P("dp", None),
        P(None, "groups", "dp"),
        P(None, ("groups", "dp"), None),
    )
    return jax.shard_map(
        functools.partial(on_device, n=mesh.shape["dp"]),
        mesh=mesh,
        in_specs=placed,
        out_specs=(
            P(None, ("groups", "dp"), None),
            P(None, "groups", "dp"),
            P(None, "groups", "dp"),
            P(None, ("groups", "dp"), None),
        ),
        check_vma=False,
    )
```

time: 314 us -> 97.7 us (0.31)
  blocking collectives: 82.3 us -> 0 us
  waiting for transfers between devices: 80.3 us -> 27.4 us
  other arithmetic: 50.9 us -> 0.78 us
  matrix products: 36.7 us -> 0 us
  Pallas kernels: 0 us -> 27.6 us
  local copies, waits for them, and re-layouts: 36.4 us -> 19.6 us
  between operations: 14.9 us -> 1.51 us
  starting transfers between devices: 11.2 us -> 20.1 us
    reduce_scatter x2 -> x0, waiting for transfers between devices: 76.2 us -> none  [the longest x1 60.5 us: on_device(): lax.psum_scatter(down_terms, 'dp', scatter_dimension=2, tiled=True)]
    unnamed x2 -> x1, other arithmetic: 45.2 us -> 0.01 us
    all_gather x2 -> x0, blocking collectives: 39.5 us -> none  [the longest x1 19.8 us: on_device(): piece = lax.all_gather(restored, 'dp', axis=2, tiled=True)]
    dot_general x4 -> x0, matrix products: 36.7 us -> none  [the longest x1 10.6 us: on_device(): lax.dot_general(grad_hidden, up_weight, (((1,), (1,)), ((), ())), preferr...]
    psum x1 -> x0, blocking collectives: 30.4 us -> none  [on_device(): lax.psum(jnp.sum(grad_hidden.astype(jnp.float32) * hidden, axis=1), 'dp')]
    pallas_call x0 -> x9, Pallas kernels: none -> 27.6 us  [the longest x1 7.86 us: on_device(): pl.pallas_call(functools.partial(grad_active_kernel, cot_owner), out_shap...]
    all_to_all x2 -> x3, waiting for transfers between devices: 4.12 us -> 27.4 us  [the longest x1 15.3 us: on_device(): lax.all_to_all(sums, 'dp', split_axis=0, concat_axis=0, axis_index_groups...]
    unnamed x1 -> x0, blocking collectives: 12.4 us -> none
  transfers between devices with their start and end apart: 4 -> 11, of which waited for: 3 -> 3; matrix products, arithmetic and copies ran while one was open for 4% -> 2% of each run, Pallas kernels for 0% -> 16%
where the time goes in v1:
time: 97.7 us; the launch traced here: 96.9 us
  Pallas kernels  27.6 us (28%)
  waiting for transfers between devices  27.4 us (28%)
  starting transfers between devices  20.1 us (21%)
  local copies, waits for them, and re-layouts  19.6 us (20%)
  between operations  1.51 us (2%)
    unnamed x30, local copies, waits for them, and re-layouts  19.5 us
    all_to_all x1, waiting for transfers between devices, on_device(): lax.all_to_all(sums, 'dp', split_axis=0, concat_axis=0, axis_index_groups...  15.3 us
    all_to_all x1, waiting for transfers between devices, on_device(): lax.all_to_all(restored, 'dp', split_axis=0, concat_axis=0, axis_index_gr...  8.71 us
    pallas_call x1, Pallas kernels, on_device(): pl.pallas_call(functools.partial(grad_active_kernel, cot_owner), out_shap...  7.86 us
    ppermute x3, starting transfers between devices, on_device(): lax.ppermute(cot, 'dp', [(d, (d + 4 * r) % n) for d in range(n)])  7.01 us
    pallas_call x1, Pallas kernels, on_device(): pl.pallas_call(grad_norm_kernel, out_shape=(jax.ShapeDtypeStruct((half, t...  6.01 us
    pallas_call x2, Pallas kernels, down_terms(): pl.pallas_call(down_kernel, out_shape=jax.ShapeDtypeStruct((half, tokens,...  5.55 us
    pallas_call x1, Pallas kernels, on_device(): pl.pallas_call(functools.partial(up_kernel, token_owner, width_all), out_...  4.61 us
  transfers between devices with their start and end apart: 11, of which 3 were waited for; matrix products, arithmetic and copies ran while one was open for 2% of the time, Pallas kernels for 16%

profile of v1, /device:TPU:0, one launch (start us, length us, event | category | flops | bytes accessed | tf_op | source)
XLA Modules:
  0.0 96.9 jit_solution(1313791681248794334)
XLA Ops:
  0.6 3.1 %collective-permute-start.1 = (bf16[1,32,512]{2,1,0:T(8,128)(2,1)}, bf16[1,32,512]{2,1,0:T(8,128)(2,1)S(1)}, u32[]{:S(2)}, u32[]{:S(2)}) collective-permute-start(bf16[1,32,512]{2,1,0:T(8,128)(2,1)} %bitcast.17), channel_id=1, source_target_pairs={{0,4},{1,5},{2,6},{3,7},{4,8},{5,9},{6,10},{7,11},{8,12},{9,13},{1... | collective-permute-start | bytes 98312 | tf_op jit(solution)/shard_map/ppermute | solution.py:235
  3.7 2.6 %collective-permute-start.2 = (bf16[1,32,512]{2,1,0:T(8,128)(2,1)}, bf16[1,32,512]{2,1,0:T(8,128)(2,1)S(1)}, u32[]{:S(2)}, u32[]{:S(2)}) collective-permute-start(bf16[1,32,512]{2,1,0:T(8,128)(2,1)} %bitcast.18), channel_id=1, source_target_pairs={{0,8},{1,9},{2,10},{3,11},{4,12},{5,13},{6,14},{7,15},{8,0},{9,1},... | collective-permute-start | bytes 98312 | tf_op jit(solution)/shard_map/ppermute | solution.py:235
  6.3 1.3 %collective-permute-start.3 = (bf16[1,32,512]{2,1,0:T(8,128)(2,1)}, bf16[1,32,512]{2,1,0:T(8,128)(2,1)S(1)}, u32[]{:S(2)}, u32[]{:S(2)}) collective-permute-start(bf16[1,32,512]{2,1,0:T(8,128)(2,1)} %bitcast.19), channel_id=1, source_target_pairs={{0,12},{1,13},{2,14},{3,15},{4,0},{5,1},{6,2},{7,3},{8,4},{9,5},{1... | collective-permute-start | bytes 98312 | tf_op jit(solution)/shard_map/ppermute | solution.py:235
  8.3 0.9 copy-done.4
  10.7 1.0 shard_map.129
  11.6 3.5 %all-to-all-start = ((bf16[16,16,128]{2,1,0:T(8,128)(2,1)}), bf16[16,16,128]{2,1,0:T(8,128)(2,1)S(1)}, u32[]{:S(2)}, u32[]{:S(2)}) async-start(bf16[16,16,128]{2,1,0:T(8,128)(2,1)} %get-tuple-element.19), calls=%async_computation | async-start | bytes 131072 | tf_op jit(solution)/shard_map/all_to_all | solution.py:263
  16.7 1.9 %collective-permute-start.4 = (bf16[4,32,512]{2,1,0:T(8,128)(2,1)S(1)}, bf16[4,32,512]{2,1,0:T(8,128)(2,1)S(1)}, u32[]{:S(2)}, u32[]{:S(2)}) collective-permute-start(bf16[4,32,512]{2,1,0:T(8,128)(2,1)S(1)} %pad_maximum_fusion), channel_id=1, source_target_pairs={{0,2},{1,3},{2,0},{3,1},{4,6},{5,7},{6,4},{7,5},{8,10},{9,11},{10,... | collective-permute-start | bytes 393224 | tf_op jit(solution)/shard_map/ppermute | solution.py:237
  18.6 3.4 %all-to-all-done.arrived_ref = bf16[16,16,128]{2,1,0:T(8,128)(2,1)S(1)} async-done(((bf16[16,16,128]{2,1,0:T(8,128)(2,1)}), bf16[16,16,128]{2,1,0:T(8,128)(2,1)S(1)}, u32[]{:S(2)}, u32[]{:S(2)}) %all-to-all-start) | async-done | bytes 65568 | tf_op jit(solution)/shard_map/all_to_all | solution.py:263
  22.0 0.9 copy-done.5
  22.9 0.9 shard_map.130
  23.7 3.4 %all-to-all-start.1 = ((bf16[8,32,512]{2,1,0:T(8,128)(2,1)}), bf16[8,32,512]{2,1,0:T(8,128)(2,1)S(1)}, u32[]{:S(2)}, u32[]{:S(2)}) async-start(bf16[8,32,512]{2,1,0:T(8,128)(2,1)} %get-tuple-element.21), calls=%async_computation.1 | async-start | bytes 524288 | tf_op jit(solution)/shard_map/all_to_all | solution.py:280
  27.3 8.7 %all-to-all-done.1.a_ref = bf16[8,32,512]{2,1,0:T(8,128)(2,1)S(1)} async-done(((bf16[8,32,512]{2,1,0:T(8,128)(2,1)}), bf16[8,32,512]{2,1,0:T(8,128)(2,1)S(1)}, u32[]{:S(2)}, u32[]{:S(2)}) %all-to-all-start.1) | async-done | bytes 262176 | tf_op jit(solution)/shard_map/all_to_all | solution.py:280
  36.0 5.2 %copy-done = bf16[896,8192]{1,0:T(8,128)(2,1)S(1)} copy-done((bf16[896,8192]{1,0:T(8,128)(2,1)S(1)}, bf16[896,8192]{1,0:T(8,128)(2,1)}, u32[]{:S(2)}) %copy-start) | copy-done | bytes 14680088
  41.2 7.9 %shard_map.131 = (f32[32,896]{1,0:T(8,128)S(1)}, f32[32,512]{1,0:T(8,128)S(1)}) custom-call(s32[1]{0:T(128)} %bitcast.3.me_ref, bf16[8,32,512]{2,1,0:T(8,128)(2,1)S(1)} %constant_dynamic-update-slice_fusion.a_ref, bf16[8,32,512]{2,1,0:T(8,128)(2,1)S(1)} %collective-permute-done.5.b_ref, bf16[896,8192]{1,0:T(8,128)(2,1)S(1)} %copy-done), custom_call_target="tpu_custom_call" | custom-call | flops 469762048 | bytes 14680064 | tf_op jit(solution)/shard_map/pallas_call | solution.py:288
  49.1 5.2 %copy-done.1 = bf16[8192,896]{1,0:T(8,128)(2,1)S(1)} copy-done((bf16[8192,896]{1,0:T(8,128)(2,1)S(1)}, bf16[8192,896]{1,0:T(8,128)(2,1)}, u32[]{:S(2)}) %copy-start.1) | copy-done | bytes 14680088
  54.3 4.6 %shard_map.132 = (bf16[32,896]{1,0:T(8,128)(2,1)S(1)}, bf16[32,896]{1,0:T(8,128)(2,1)S(1)}, f32[32,512]{1,0:T(8,128)S(1)}) custom-call(s32[1]{0:T(128)} %bitcast.3.me_ref, bf16[8,32,512]{2,1,0:T(8,128)(2,1)S(1)} %all-to-all-done.1.a_ref, bf16[8,32,512]{2,1,0:T(8,128)(2,1)S(1)} %collective-permute-done.b_ref, f32[16,1,512]{2,1,0:T(1,128)S(1)} %bitcast.13, ...), custom_call_target="tpu_custom_call" | custom-call | flops 469762048 | bytes 14680064 | tf_op jit(solution)/shard_map/pallas_call | solution.py:313
  58.9 5.2 %copy-done.2 = bf16[8192,896]{1,0:T(8,128)(2,1)S(1)} copy-done((bf16[8192,896]{1,0:T(8,128)(2,1)S(1)}, bf16[8192,896]{1,0:T(8,128)(2,1)}, u32[]{:S(2)}) %copy-start.2) | copy-done | bytes 14680088
  64.1 6.0 %shard_map.133 = (bf16[8,32,512]{2,1,0:T(8,128)(2,1)S(1)}, bf16[8,32,512]{2,1,0:T(8,128)(2,1)S(1)}) custom-call(s32[1]{0:T(128)} %bitcast.3.me_ref, bf16[32,896]{1,0:T(8,128)(2,1)S(1)} %get-tuple-element.23.gh_ref, bf16[8192,896]{1,0:T(8,128)(2,1)S(1)} %copy-done.2), custom_call_target="tpu_custom_call" | custom-call | flops 469762048 | bytes 14680064 | tf_op jit(solution)/shard_map/pallas_call | solution.py:346
  70.7 2.8 %shard_map.135 = bf16[8,32,512]{2,1,0:T(8,128)(2,1)S(1)} custom-call(s32[1]{0:T(128)} %bitcast.3.me_ref, bf16[32,896]{1,0:T(8,128)(2,1)S(1)} %get-tuple-element.26.active_ref, bf16[896,8192]{1,0:T(8,128)(2,1)S(1)} %bitcast.12), custom_call_target="tpu_custom_call" | custom-call | flops 234881024 | bytes 7340032 | tf_op jit(solution)/shard_map/pallas_call | solution.py:369
  73.5 2.8 %shard_map.134.out_ref = bf16[8,32,512]{2,1,0:T(8,128)(2,1)S(1)} custom-call(s32[1]{0:T(128)} %bitcast.3.me_ref, bf16[32,896]{1,0:T(8,128)(2,1)S(1)} %get-tuple-element.26.active_ref, bf16[896,8192]{1,0:T(8,128)(2,1)S(1)} %bitcast.12), custom_call_target="tpu_custom_call" | custom-call | flops 234881024 | bytes 7340032 | tf_op jit(solution)/shard_map/pallas_call | solution.py:369
  76.3 0.9 shard_map.136
  77.3 3.5 %all-to-all-start.2 = ((bf16[8,2,32,512]{3,2,1,0:T(8,128)(2,1)}), bf16[8,2,32,512]{3,2,1,0:T(8,128)(2,1)S(1)}, u32[]{:S(2)}, u32[]{:S(2)}) async-start(bf16[8,2,32,512]{3,2,1,0:T(8,128)(2,1)} %shard_map.136), calls=%async_computation.2 | async-start | bytes 1048576 | tf_op jit(solution)/shard_map/all_to_all | solution.py:402
  80.8 15.3 %all-to-all-done.2.terms_ref = bf16[8,2,32,512]{3,2,1,0:T(8,128)(2,1)S(1)} async-done(((bf16[8,2,32,512]{3,2,1,0:T(8,128)(2,1)}), bf16[8,2,32,512]{3,2,1,0:T(8,128)(2,1)S(1)}, u32[]{:S(2)}, u32[]{:S(2)}) %all-to-all-start.2) | async-done | bytes 524320 | tf_op jit(solution)/shard_map/all_to_all | solution.py:402
  96.1 0.8 shard_map.137
  (41 shorter events, 3.8 us)
Async XLA Ops:
  0.6 48.4 %copy-start.3 = (f32[8192]{0:T(1024)S(1)}, f32[8192]{0:T(1024)}, u32[]{:S(2)}) copy-start(f32[8192]{0:T(1024)} %param.15) | copy-start | bytes 98308
  0.6 15.2 %collective-permute-start.1 = (bf16[1,32,512]{2,1,0:T(8,128)(2,1)}, bf16[1,32,512]{2,1,0:T(8,128)(2,1)S(1)}, u32[]{:S(2)}, u32[]{:S(2)}) collective-permute-start(bf16[1,32,512]{2,1,0:T(8,128)(2,1)} %bitcast.17), channel_id=1, source_target_pairs={{0,4},{1,5},{2,6},{3,7},{4,8},{5,9},{6,10},{7,11},{8,12},{9,13},{1... | collective-permute-start | bytes 98312 | tf_op jit(solution)/shard_map/ppermute | solution.py:235
  3.7 12.2 %collective-permute-start.2 = (bf16[1,32,512]{2,1,0:T(8,128)(2,1)}, bf16[1,32,512]{2,1,0:T(8,128)(2,1)S(1)}, u32[]{:S(2)}, u32[]{:S(2)}) collective-permute-start(bf16[1,32,512]{2,1,0:T(8,128)(2,1)} %bitcast.18), channel_id=1, source_target_pairs={{0,8},{1,9},{2,10},{3,11},{4,12},{5,13},{6,14},{7,15},{8,0},{9,1},... | collective-permute-start | bytes 98312 | tf_op jit(solution)/shard_map/ppermute | solution.py:235
  6.3 9.6 %collective-permute-start.3 = (bf16[1,32,512]{2,1,0:T(8,128)(2,1)}, bf16[1,32,512]{2,1,0:T(8,128)(2,1)S(1)}, u32[]{:S(2)}, u32[]{:S(2)}) collective-permute-start(bf16[1,32,512]{2,1,0:T(8,128)(2,1)} %bitcast.19), channel_id=1, source_target_pairs={{0,12},{1,13},{2,14},{3,15},{4,0},{5,1},{6,2},{7,3},{8,4},{9,5},{1... | collective-permute-start | bytes 98312 | tf_op jit(solution)/shard_map/ppermute | solution.py:235
  8.3 0.9 copy-start.4
  9.2 0.8 copy-start.6
  10.0 0.7 copy-start.7
  11.6 10.4 %all-to-all-start = ((bf16[16,16,128]{2,1,0:T(8,128)(2,1)}), bf16[16,16,128]{2,1,0:T(8,128)(2,1)S(1)}, u32[]{:S(2)}, u32[]{:S(2)}) async-start(bf16[16,16,128]{2,1,0:T(8,128)(2,1)} %get-tuple-element.19), calls=%async_computation | async-start | bytes 131072 | tf_op jit(solution)/shard_map/all_to_all | solution.py:263
  16.7 10.5 %collective-permute-start.4 = (bf16[4,32,512]{2,1,0:T(8,128)(2,1)S(1)}, bf16[4,32,512]{2,1,0:T(8,128)(2,1)S(1)}, u32[]{:S(2)}, u32[]{:S(2)}) collective-permute-start(bf16[4,32,512]{2,1,0:T(8,128)(2,1)S(1)} %pad_maximum_fusion), channel_id=1, source_target_pairs={{0,2},{1,3},{2,0},{3,1},{4,6},{5,7},{6,4},{7,5},{8,10},{9,11},{10,... | collective-permute-start | bytes 393224 | tf_op jit(solution)/shard_map/ppermute | solution.py:237
  22.0 0.9 copy-start.5
  23.7 12.3 %all-to-all-start.1 = ((bf16[8,32,512]{2,1,0:T(8,128)(2,1)}), bf16[8,32,512]{2,1,0:T(8,128)(2,1)S(1)}, u32[]{:S(2)}, u32[]{:S(2)}) async-start(bf16[8,32,512]{2,1,0:T(8,128)(2,1)} %get-tuple-element.21), calls=%async_computation.1 | async-start | bytes 524288 | tf_op jit(solution)/shard_map/all_to_all | solution.py:280
  27.2 8.8 %collective-permute-start.5 = (bf16[8,32,512]{2,1,0:T(8,128)(2,1)S(1)}, bf16[8,32,512]{2,1,0:T(8,128)(2,1)S(1)}, u32[]{:S(2)}, u32[]{:S(2)}) collective-permute-start(bf16[8,32,512]{2,1,0:T(8,128)(2,1)S(1)} %constant_dynamic-update-slice_fusion.a_ref), channel_id=1, source_target_pairs={{0,1},{1,0},{2,3},{3,2},{4,5},{5,4},{6,7},{7,6},{8,9},{9,8},{10,11... | collective-permute-start | bytes 786440 | tf_op jit(solution)/shard_map/ppermute | solution.py:238
  36.0 13.0 %collective-permute-start = (bf16[8,32,512]{2,1,0:T(8,128)(2,1)S(1)}, bf16[8,32,512]{2,1,0:T(8,128)(2,1)S(1)}, u32[]{:S(2)}, u32[]{:S(2)}) collective-permute-start(bf16[8,32,512]{2,1,0:T(8,128)(2,1)S(1)} %all-to-all-done.1.a_ref), channel_id=1, source_target_pairs={{0,1},{1,0},{2,3},{3,2},{4,5},{5,4},{6,7},{7,6},{8,9},{9,8},{10,11... | collective-permute-start | bytes 786440 | tf_op jit(solution)/shard_map/ppermute | solution.py:283
  36.0 5.2 %copy-start = (bf16[896,8192]{1,0:T(8,128)(2,1)S(1)}, bf16[896,8192]{1,0:T(8,128)(2,1)}, u32[]{:S(2)}) copy-start(bf16[896,8192]{1,0:T(8,128)(2,1)} %weight_ref.9) | copy-start | bytes 44040196
  49.1 5.2 %copy-start.1 = (bf16[8192,896]{1,0:T(8,128)(2,1)S(1)}, bf16[8192,896]{1,0:T(8,128)(2,1)}, u32[]{:S(2)}) copy-start(bf16[8192,896]{1,0:T(8,128)(2,1)} %weight_ref.7) | copy-start | bytes 44040196
  54.3 16.4 %slice-start = ((s8[14680064]{0:T(1024)(128)(4,1)}), s8[2097152]{0:T(1024)(128)(4,1)S(1)}, s32[]{:S(2)}) async-start(s8[14680064]{0:T(1024)(128)(4,1)} %bitcast.11), calls=%async_computation.3 | async-start | bytes 4194304
  54.3 16.4 %slice-start.1 = ((s8[14680064]{0:T(1024)(128)(4,1)}), s8[4194304]{0:T(1024)(128)(4,1)S(1)}, s32[]{:S(2)}) async-start(s8[14680064]{0:T(1024)(128)(4,1)} %bitcast.11), calls=%async_computation.4 | async-start | bytes 8388608
  54.3 16.4 %slice-start.2 = ((s8[14680064]{0:T(1024)(128)(4,1)}), s8[4194304]{0:T(1024)(128)(4,1)S(1)}, s32[]{:S(2)}) async-start(s8[14680064]{0:T(1024)(128)(4,1)} %bitcast.11), calls=%async_computation.5 | async-start | bytes 8388608
  58.9 5.2 %copy-start.2 = (bf16[8192,896]{1,0:T(8,128)(2,1)S(1)}, bf16[8192,896]{1,0:T(8,128)(2,1)}, u32[]{:S(2)}) copy-start(bf16[8192,896]{1,0:T(8,128)(2,1)} %weight_ref.7) | copy-start | bytes 44040196
  64.1 6.6 %slice-start.3 = ((s8[14680064]{0:T(1024)(128)(4,1)}), s8[4194304]{0:T(1024)(128)(4,1)S(1)}, s32[]{:S(2)}) async-start(s8[14680064]{0:T(1024)(128)(4,1)} %bitcast.11), calls=%async_computation.6 | async-start | bytes 8388608
  70.1 6.2 %collective-permute-start.6 = (bf16[8,32,512]{2,1,0:T(8,128)(2,1)S(1)}, bf16[8,32,512]{2,1,0:T(8,128)(2,1)S(1)}, u32[]{:S(2)}, u32[]{:S(2)}) collective-permute-start(bf16[8,32,512]{2,1,0:T(8,128)(2,1)S(1)} %get-tuple-element.25), channel_id=1, source_target_pairs={{0,1},{1,0},{2,3},{3,2},{4,5},{5,4},{6,7},{7,6},{8,9},{9,8},{10,11... | collective-permute-start | bytes 786440 | tf_op jit(solution)/shard_map/ppermute | solution.py:366
  70.7 25.4 %copy-start.8 = (s32[2,1,64]{2,1,0:T(1,128)S(1)}, s32[2,1,64]{2,1,0:T(1,128)}, u32[]{:S(2)}) copy-start(s32[2,1,64]{2,1,0:T(1,128)} %param.19) | copy-start | bytes 1540
  73.5 2.9 %collective-permute-start.7 = (bf16[8,32,512]{2,1,0:T(8,128)(2,1)S(1)}, bf16[8,32,512]{2,1,0:T(8,128)(2,1)S(1)}, u32[]{:S(2)}, u32[]{:S(2)}) collective-permute-start(bf16[8,32,512]{2,1,0:T(8,128)(2,1)S(1)} %shard_map.135), channel_id=1, source_target_pairs={{0,1},{1,0},{2,3},{3,2},{4,5},{5,4},{6,7},{7,6},{8,9},{9,8},{10,11... | collective-permute-start | bytes 786440 | tf_op jit(solution)/shard_map/ppermute | solution.py:392
  77.3 18.8 %all-to-all-start.2 = ((bf16[8,2,32,512]{3,2,1,0:T(8,128)(2,1)}), bf16[8,2,32,512]{3,2,1,0:T(8,128)(2,1)S(1)}, u32[]{:S(2)}, u32[]{:S(2)}) async-start(bf16[8,2,32,512]{3,2,1,0:T(8,128)(2,1)} %shard_map.136), calls=%async_computation.2 | async-start | bytes 1048576 | tf_op jit(solution)/shard_map/all_to_all | solution.py:402

commit v2 on v1

--- a/solution.py
+++ b/solution.py
@@ -16,6 +16,10 @@
 SMEM = pl.BlockSpec(memory_space=pltpu.SMEM)
 
 
+def hbm(x):
+    return pltpu.with_memory_space_constraint(x, pltpu.HBM)
+
+
 def powers(exponent, sign):
     total = jnp.zeros(exponent.shape, f32)
     for level in range(-10, 1):
@@ -27,9 +31,14 @@
     return pltpu.CompilerParams(vmem_limit_bytes=megabytes << 20)
 
 
-def send_kernel(offset_ref, act_ref, expo_ref, base_ref, out_ref, new_ref, rows_ref):
+def send_kernel(
+    offset_ref, act_ref, expo_ref, base_ref, received_ref, cot_ref,
+    out_ref, new_ref, received_out_ref, cot_out_ref, rows_ref,
+):
     n, rows, _ = out_ref.shape
     width = act_ref.shape[1]
+    received_out_ref[...] = received_ref[...]
+    cot_out_ref[...] = cot_ref[...]
     per_dev = width // LANES // n
     first = offset_ref[0] == 0
     down, up = powers(expo_ref[...], -1), powers(expo_ref[...], 1)
@@ -88,16 +97,19 @@
         own_ref[pl.ds(p * n + owner, 1), :] = piece_ref[pl.ds(p * n + me, 1), :]
 
 
-def grad_active_kernel(owner_of, me_ref, a_ref, b_ref, weight_ref, out_ref, own_ref, piece_ref):
-    i, half = pl.program_id(0), a_ref.shape[0]
+def grad_active_kernel(
+    owner_of, me_ref, a_ref, b_ref, c_ref, d_ref, weight_ref, out_ref, own_ref, piece_ref
+):
+    i, quarter = pl.program_id(0), a_ref.shape[0]
     me = me_ref[0]
 
     @pl.when(i == 0)
     def _():
         out_ref[...] = jnp.zeros_like(out_ref)
 
-    k = lax.rem(i, half)
-    piece = jnp.where(i < half, a_ref[k], b_ref[k])
+    k, part = lax.rem(i, quarter), i // quarter
+    low = jnp.where(part == 0, a_ref[k], b_ref[k])
+    piece = jnp.where(part < 2, low, jnp.where(part == 2, c_ref[k], d_ref[k]))
     out_ref[...] += dot_nt(piece, weight_ref[...])
     piece_ref[...] = piece.astype(f32)
     own_rows(piece_ref, own_ref, me, owner_of(i, me))
@@ -166,22 +178,34 @@
                 send_ref[k, :, cols] = rows_ref[c, pl.ds(send_at, tokens), :].astype(bf16)
 
 
-def pair_kernel(grad_ref, grad_in_ref, out_ref, out_in_ref, sum_ref):
-    sum_ref[:, 0] = (grad_ref[...].astype(f32) + grad_in_ref[...].astype(f32)).astype(bf16)
-    sum_ref[:, 1] = (out_ref[...].astype(f32) + out_in_ref[...].astype(f32)).astype(bf16)
-
-
-def final_kernel(
-    width_all, terms_ref, restored_ref, own_ref, cot_ref, gain_ref, expo_ref, layer_ref, grad_ref
-):
-    half, _, tokens, width = terms_ref.shape
-    n = 2 * half
-    grad = terms_ref[0, 0].astype(f32)
-    layer = terms_ref[0, 1].astype(f32)
-    for k in range(1, half):
-        grad = grad + terms_ref[k, 0].astype(f32)
-        layer = layer + terms_ref[k, 1].astype(f32)
-    layer_ref[...] = (restored_ref[...].astype(f32) + layer).astype(bf16)
+def pair_kernel(me_ref, kept_ref, arrived_ref, send_ref, keep_ref):
+    quarter = send_ref.shape[0]
+    row = lax.rem(me_ref[0] // 2, 2)
+    for k in range(quarter):
+        for out_ref, at in ((send_ref, 2 * k + 1 - row), (keep_ref, 2 * k + row)):
+            out_ref[k] = (kept_ref[at].astype(f32) + arrived_ref[at].astype(f32)).astype(bf16)
+
+
+def line_kernel(me_ref, kept_ref, arrived_ref, *out_refs):
+    quarter = len(out_refs)
+    for r, out_ref in enumerate(out_refs):
+        at = lax.rem(me_ref[0] // 4 + r, quarter)
+        out_ref[...] = (kept_ref[at].astype(f32) + arrived_ref[at].astype(f32)).astype(bf16)
+
+
+def layer_kernel(restored_ref, *refs):
+    total = restored_ref[...].astype(f32)
+    for ref in refs[:-1]:
+        total = total + ref[...].astype(f32)
+    refs[-1][...] = total.astype(bf16)
+
+
+def final_kernel(width_all, own_ref, cot_ref, gain_ref, expo_ref, *refs):
+    grad_ref = refs[-1]
+    grad = refs[0][...].astype(f32)
+    for ref in refs[1:-1]:
+        grad = grad + ref[...].astype(f32)
+    n, width = gain_ref.shape
     down, up = powers(expo_ref[...], -1), powers(expo_ref[...], 1)
     gain = gain_ref[...]
     per_dev = width // LANES
@@ -229,14 +253,6 @@
     row_pair = [(d, d ^ 2) for d in range(n)]
     same_core = [[2 * k + c for k in range(half)] for c in range(2)]
 
-    cot = cotangent.reshape(1, tokens, width)
-    line = [cot]
-    for r in range(1, quarter):
-        line.append(lax.ppermute(cot, "dp", [(d, (d + 4 * r) % n) for d in range(n)]))
-    line = jnp.concatenate(line, axis=0)
-    cot_a = jnp.concatenate([line, lax.ppermute(line, "dp", row_pair)], axis=0)
-    cot_b = lax.ppermute(cot_a, "dp", core_pair)
-
     def cot_owner(i, who):
         core, row, along = lax.rem(who, 2), lax.rem(who // 2, 2), who // 4
         other_core, other_row, back = i // half, lax.rem(i // quarter, 2), lax.rem(i, quarter)
@@ -249,18 +265,51 @@
     slots = sender_base.shape[1]
     offset = sample_ids - slots * me
     rows = -(-(2 * width // LANES + 1) // 16) * 16
-    blocks, new_sender_base = pl.pallas_call(
+    once = lambda *shape: pl.BlockSpec(shape, lambda i: (0,) * len(shape))
+    share_shape = (tokens, width)
+    act_shape, expo_shape = (2, width_all), (2, width_all // LANES)
+    blocks, new_sender_base, received, cot = pl.pallas_call(
         send_kernel,
         out_shape=(
             jax.ShapeDtypeStruct((n, rows, LANES), bf16),
             jax.ShapeDtypeStruct(sender_base.shape, f32),
-        ),
-        in_specs=[SMEM, VMEM, VMEM, VMEM],
-        out_specs=(VMEM, VMEM),
+            jax.ShapeDtypeStruct(receiver_base.shape, f32),
+            jax.ShapeDtypeStruct(share_shape, bf16),
+        ),
+        grid=(1,),
+        in_specs=[
+            SMEM,
+            once(*act_shape),
+            once(*expo_shape),
+            once(*sender_base.shape),
+            once(*receiver_base.shape),
+            once(*share_shape),
+        ],
+        out_specs=(
+            once(n, rows, LANES),
+            once(*sender_base.shape),
+            once(*receiver_base.shape),
+            once(*share_shape),
+        ),
         scratch_shapes=[pltpu.VMEM((n, rows, LANES), f32)],
         compiler_params=params(16),
-    )(offset, activations.reshape(2, width_all), forward_exponent.reshape(2, -1), sender_base)
+    )(
+        offset,
+        hbm(activations.reshape(act_shape)),
+        hbm(forward_exponent.reshape(expo_shape)),
+        hbm(sender_base),
+        hbm(receiver_base),
+        hbm(cotangent.reshape(share_shape)),
+    )
     arrived = lax.all_to_all(blocks, "dp", split_axis=0, concat_axis=0, tiled=True)
+
+    cot = cot.reshape(1, tokens, width)
+    line = [cot]
+    for r in range(1, quarter):
+        line.append(lax.ppermute(cot, "dp", [(d, (d + 4 * r) % n) for d in range(n)]))
+    line = jnp.concatenate(line, axis=0)
+    rows_both = [line, lax.ppermute(line, "dp", row_pair)]
+    cots = rows_both + [lax.ppermute(x, "dp", core_pair) for x in rows_both]
 
     new_receiver_base, restored, share = pl.pallas_call(
         rebuild_kernel,
@@ -276,11 +325,10 @@
             pltpu.VMEM((2 * width // LANES, 2 * n, LANES), f32),
         ],
         compiler_params=params(16),
-    )(arrived, receiver_base)
+    )(arrived, received)
     rest_a = lax.all_to_all(
         restored, "dp", split_axis=0, concat_axis=0, axis_index_groups=same_core, tiled=True
     )
-    rest_b = lax.ppermute(rest_a, "dp", core_pair)
 
     whole = lambda *shape: pl.BlockSpec(shape, lambda i, who: (0,) * len(shape))
     pieces = whole(half, tokens, width)
@@ -295,8 +343,7 @@
             num_scalar_prefetch=1,
             grid=(n,),
             in_specs=[
-                pieces,
-                pieces,
+                *([whole(quarter, tokens, width)] * 4),
                 pl.BlockSpec((hidden_dev, width), lambda i, who: (0, cot_owner(i, who[0]))),
             ],
             out_specs=(whole(tokens, hidden_dev), whole(tokens, width)),
@@ -308,7 +355,9 @@
             bytes_accessed=2 * width_all * hidden_dev,
             transcendentals=0,
         ),
-    )(me_in, cot_a, cot_b, down_weight)
+    )(me_in, *cots, hbm(down_weight))
+    rest_a, grad_active = lax.optimization_barrier((rest_a, grad_active))
+    rest_b = lax.ppermute(rest_a, "dp", core_pair)
 
     active, grad_hidden, own_restored = pl.pallas_call(
         functools.partial(up_kernel, token_owner, width_all),
@@ -340,7 +389,7 @@
             bytes_accessed=2 * width_all * hidden_dev,
             transcendentals=0,
         ),
-    )(me_in, rest_a, rest_b, norm_gain.reshape(n, 1, width), up_weight, grad_active)
+    )(me_in, rest_a, rest_b, norm_gain.reshape(n, 1, width), hbm(up_weight), grad_active)
 
     step = max(width, 1024)
     grad_send, grad_keep = pl.pallas_call(
@@ -362,8 +411,7 @@
             bytes_accessed=2 * width_all * hidden_dev,
             transcendentals=0,
         ),
-    )(me_in, grad_hidden, up_weight)
-    grad_in = lax.ppermute(grad_send, "dp", core_pair)
+    )(me_in, grad_hidden, hbm(up_weight))
 
     def down_terms(other):
         return pl.pallas_call(
@@ -387,38 +435,58 @@
                 bytes_accessed=width_all * hidden_dev,
                 transcendentals=0,
             ),
-        )(me_in, active, down_weight)
-
+        )(me_in, active, hbm(down_weight))
+
+    def pair_sum(kept, arrived):
+        send, keep = pl.pallas_call(
+            pair_kernel,
+            out_shape=(jax.ShapeDtypeStruct((quarter, tokens, width), bf16),) * 2,
+            in_specs=[SMEM, VMEM, VMEM],
+            out_specs=(VMEM, VMEM),
+            compiler_params=params(16),
+        )(me_in, kept, arrived)
+        return keep, lax.ppermute(send, "dp", row_pair)
+
+    def line_sum(kept, arrived):
+        shares = pl.pallas_call(
+            line_kernel,
+            out_shape=(jax.ShapeDtypeStruct((tokens, width), bf16),) * quarter,
+            in_specs=[SMEM, VMEM, VMEM],
+            out_specs=(VMEM,) * quarter,
+            compiler_params=params(16),
+        )(me_in, kept, arrived)
+        moved = [
+            lax.ppermute(shares[r], "dp", [(d, (d + 4 * r) % n) for d in range(n)])
+            for r in range(1, quarter)
+        ]
+        return [shares[0], *moved]
+
+    grad_in = lax.ppermute(grad_send, "dp", core_pair)
     out_in = lax.ppermute(down_terms(1), "dp", core_pair)
-    out_keep = down_terms(0)
-
-    sums = pl.pallas_call(
-        pair_kernel,
-        out_shape=jax.ShapeDtypeStruct((half, 2, tokens, width), bf16),
-        in_specs=[VMEM] * 4,
+    grad_pair = pair_sum(grad_keep, grad_in)
+    out_pair = pair_sum(down_terms(0), out_in)
+    grad_line = line_sum(*grad_pair)
+    out_line = line_sum(*out_pair)
+    returned = pl.pallas_call(
+        functools.partial(final_kernel, width_all),
+        out_shape=jax.ShapeDtypeStruct((2, width_all // LANES, LANES), f32),
+        in_specs=[VMEM] * (4 + quarter),
         out_specs=VMEM,
         compiler_params=params(16),
-    )(grad_keep, grad_in, out_keep, out_in)
-    terms = lax.all_to_all(
-        sums, "dp", split_axis=0, concat_axis=0, axis_index_groups=same_core, tiled=True
-    )
-    layer_out, returned = pl.pallas_call(
-        functools.partial(final_kernel, width_all),
-        out_shape=(
-            jax.ShapeDtypeStruct((tokens, width), bf16),
-            jax.ShapeDtypeStruct((2, width_all // LANES, LANES), f32),
-        ),
-        in_specs=[VMEM] * 6,
-        out_specs=(VMEM, VMEM),
-        compiler_params=params(16),
     )(
-        terms,
-        share,
         own_restored,
         own_cot,
         norm_gain.reshape(n, width),
         backward_exponent.reshape(2, -1),
+        *grad_line,
     )
+    layer_out = pl.pallas_call(
+        layer_kernel,
+        out_shape=jax.ShapeDtypeStruct((tokens, width), bf16),
+        in_specs=[VMEM] * (1 + quarter),
+        out_specs=VMEM,
+        compiler_params=params(16),
+    )(share, *out_line)
     return (
         new_sender_base,
         new_receiver_base,

time: 97.7 us -> 110 us (1.13)
  Pallas kernels: 27.6 us -> 53.4 us
  local copies, waits for them, and re-layouts: 19.6 us -> 0.01 us
  blocking collectives: 0 us -> 14.1 us
  waiting for transfers between devices: 27.4 us -> 18.2 us
  starting transfers between devices: 20.1 us -> 21.7 us
    unnamed x30 -> x4, local copies, waits for them, and re-layouts: 19.5 us -> 0.01 us
    all_to_all x2 -> x0, waiting for transfers between devices: 18.7 us -> none  [the longest x1 15.3 us: on_device(): lax.all_to_all(sums, 'dp', split_axis=0, concat_axis=0, axis_index_groups...]
    all_to_all x0 -> x1, blocking collectives: none -> 14.1 us  [on_device(): lax.all_to_all(blocks, 'dp', split_axis=0, concat_axis=0, tiled=True)]
    ppermute x2 -> x11, starting transfers between devices: 1.95 us -> 12.6 us  [the longest x6 8.88 us: line_sum(): lax.ppermute(shares[r], 'dp', [(d, (d + 4 * r) % n) for d in range(n)])]
    ppermute x2 -> x11, waiting for transfers between devices: 0.01 us -> 9.96 us  [the longest x2 4.19 us: pair_sum(): return (keep, lax.ppermute(send, 'dp', row_pair))]
    all_to_all x1, waiting for transfers between devices: 8.71 us -> 0.01 us  [on_device(): lax.all_to_all(restored, 'dp', split_axis=0, concat_axis=0, axis_index_gr...]
    pallas_call x1, Pallas kernels: 4.61 us -> 12.6 us  [on_device(): pl.pallas_call(functools.partial(up_kernel, token_owner, width_all), out_...]
    all_to_all x2 -> x0, starting transfers between devices: 7.04 us -> none  [the longest x1 3.54 us: on_device(): lax.all_to_all(sums, 'dp', split_axis=0, concat_axis=0, axis_index_groups...]
  transfers between devices with their start and end apart: 11 -> 18, of which waited for: 3 -> 8; matrix products, arithmetic and copies ran while one was open for 2% -> 0% of each run, Pallas kernels for 16% -> 28%
where the time goes in v2:
time: 110 us; the launch traced here: 109 us
  Pallas kernels  53.4 us (49%)
  starting transfers between devices  21.7 us (20%)
  waiting for transfers between devices  18.2 us (17%)
  blocking collectives  14.1 us (13%)
  between operations  1.4 us (1%)
    all_to_all x1, blocking collectives, on_device(): lax.all_to_all(blocks, 'dp', split_axis=0, concat_axis=0, tiled=True)  14.1 us
    pallas_call x1, Pallas kernels, on_device(): pl.pallas_call(functools.partial(grad_active_kernel, cot_owner), out_shap...  13.6 us
    pallas_call x1, Pallas kernels, on_device(): pl.pallas_call(functools.partial(up_kernel, token_owner, width_all), out_...  12.6 us
    pallas_call x2, Pallas kernels, down_terms(): pl.pallas_call(down_kernel, out_shape=jax.ShapeDtypeStruct((half, tokens,...  12.6 us
    pallas_call x1, Pallas kernels, on_device(): pl.pallas_call(grad_norm_kernel, out_shape=(jax.ShapeDtypeStruct((half, t...  10.2 us
    ppermute x6, starting transfers between devices, line_sum(): lax.ppermute(shares[r], 'dp', [(d, (d + 4 * r) % n) for d in range(n)])  8.88 us
    ppermute x3, waiting for transfers between devices, on_device(): lax.ppermute(cot, 'dp', [(d, (d + 4 * r) % n) for d in range(n)])  6.78 us
    ppermute x3, starting transfers between devices, on_device(): lax.ppermute(cot, 'dp', [(d, (d + 4 * r) % n) for d in range(n)])  4.87 us
  transfers between devices with their start and end apart: 18, of which 8 were waited for; matrix products, arithmetic and copies ran while one was open for 0% of the time, Pallas kernels for 28%

profile of v2, /device:TPU:0, one launch (start us, length us, event | category | flops | bytes accessed | tf_op | source)
XLA Modules:
  0.0 108.7 jit_solution(17427270618271171638)
XLA Ops:
  1.3 1.9 %shard_map.129 = (bf16[16,16,128]{2,1,0:T(8,128)(2,1)S(1)}, f32[2,2,8192]{2,1,0:T(2,128)}, f32[2,32,512]{2,1,0:T(8,128)S(1)}, bf16[32,512]{1,0:T(8,128)(2,1)S(1)}) custom-call(s32[1]{0:T(128)S(6)} %sub.7.offset_ref, bf16[2,8192]{1,0:T(2,128)(2,1)} %bitcast.17, s32[2,64]{1,0:T(2,128)} %bitcast.20, f32[2,2,8192]{2,1,0:T(2,128)} %base_ref.1, ...), custom_call_target="tpu_custom_call" | custom-call | tf_op jit(solution)/shard_map/pallas_call | solution.py:271
  3.2 14.1 %all_to_all.10.arrived_ref = bf16[16,16,128]{2,1,0:T(8,128)(2,1)S(1)} all-to-all(bf16[16,16,128]{2,1,0:T(8,128)(2,1)S(1)} %get-tuple-element.33), channel_id=1, replica_groups=mesh['groups'=2,'dp'=16] {'dp'}, dimensions={0} | all-to-all | bytes 131072 | tf_op jit(solution)/shard_map/all_to_all | solution.py:304
  17.3 0.9 shard_map.130
  18.2 3.4 %all-to-all-start.1 = ((bf16[8,32,512]{2,1,0:T(8,128)(2,1)}), bf16[8,32,512]{2,1,0:T(8,128)(2,1)S(1)}, u32[]{:S(2)}, u32[]{:S(2)}) async-start(bf16[8,32,512]{2,1,0:T(8,128)(2,1)} %get-tuple-element.37), calls=%async_computation.1 | async-start | bytes 524288 | tf_op jit(solution)/shard_map/all_to_all | solution.py:329
  21.6 3.8 %collective-permute-start.2 = (bf16[1,32,512]{2,1,0:T(8,128)(2,1)S(1)}, bf16[1,32,512]{2,1,0:T(8,128)(2,1)S(1)}, u32[]{:S(2)}, u32[]{:S(2)}) collective-permute-start(bf16[1,32,512]{2,1,0:T(8,128)(2,1)S(1)} %bitcast.11), channel_id=1, source_target_pairs={{0,12},{1,13},{2,14},{3,15},{4,0},{5,1},{6,2},{7,3},{8,4},{9,5},{1... | collective-permute-start | bytes 98312 | tf_op jit(solution)/shard_map/ppermute | solution.py:309
  25.3 1.1 %collective-permute-start = (bf16[1,32,512]{2,1,0:T(8,128)(2,1)S(1)}, bf16[1,32,512]{2,1,0:T(8,128)(2,1)S(1)}, u32[]{:S(2)}, u32[]{:S(2)}) collective-permute-start(bf16[1,32,512]{2,1,0:T(8,128)(2,1)S(1)} %bitcast.13), channel_id=1, source_target_pairs={{0,4},{1,5},{2,6},{3,7},{4,8},{5,9},{6,10},{7,11},{8,12},{9,13},{1... | collective-permute-start | bytes 98312 | tf_op jit(solution)/shard_map/ppermute | solution.py:309
  26.5 1.3 %collective-permute-done.2 = bf16[1,32,512]{2,1,0:T(8,128)(2,1)S(1)} collective-permute-done((bf16[1,32,512]{2,1,0:T(8,128)(2,1)S(1)}, bf16[1,32,512]{2,1,0:T(8,128)(2,1)S(1)}, u32[]{:S(2)}, u32[]{:S(2)}) %collective-permute-start.2) | collective-permute-done | bytes 32800 | tf_op jit(solution)/shard_map/ppermute | solution.py:309
  27.7 5.5 %collective-permute-done.1 = bf16[1,32,512]{2,1,0:T(8,128)(2,1)S(1)} collective-permute-done((bf16[1,32,512]{2,1,0:T(8,128)(2,1)S(1)}, bf16[1,32,512]{2,1,0:T(8,128)(2,1)S(1)}, u32[]{:S(2)}, u32[]{:S(2)}) %collective-permute-start.1) | collective-permute-done | bytes 32800 | tf_op jit(solution)/shard_map/ppermute | solution.py:309
  33.3 1.5 %collective-permute-start.3 = (bf16[4,32,512]{2,1,0:T(8,128)(2,1)S(1)}, bf16[4,32,512]{2,1,0:T(8,128)(2,1)S(1)}, u32[]{:S(2)}, u32[]{:S(2)}) collective-permute-start(bf16[4,32,512]{2,1,0:T(8,128)(2,1)S(1)} %pad_maximum_fusion.a_ref), channel_id=1, source_target_pairs={{0,2},{1,3},{2,0},{3,1},{4,6},{5,7},{6,4},{7,5},{8,10},{9,11},{10,... | collective-permute-start | bytes 393224 | tf_op jit(solution)/shard_map/ppermute | solution.py:311
  34.8 3.5 %collective-permute-done.3.b_ref = bf16[4,32,512]{2,1,0:T(8,128)(2,1)S(1)} collective-permute-done((bf16[4,32,512]{2,1,0:T(8,128)(2,1)S(1)}, bf16[4,32,512]{2,1,0:T(8,128)(2,1)S(1)}, u32[]{:S(2)}, u32[]{:S(2)}) %collective-permute-start.3) | collective-permute-done | bytes 131104 | tf_op jit(solution)/shard_map/ppermute | solution.py:311
  38.3 1.3 %collective-permute-done.5.d_ref = bf16[4,32,512]{2,1,0:T(8,128)(2,1)S(1)} collective-permute-done((bf16[4,32,512]{2,1,0:T(8,128)(2,1)S(1)}, bf16[4,32,512]{2,1,0:T(8,128)(2,1)S(1)}, u32[]{:S(2)}, u32[]{:S(2)}) %collective-permute-start.5) | collective-permute-done | bytes 131104 | tf_op jit(solution)/shard_map/ppermute | solution.py:312
  39.6 13.6 %shard_map.131 = (f32[32,896]{1,0:T(8,128)S(1)}, f32[32,512]{1,0:T(8,128)S(1)}) custom-call(s32[1]{0:T(128)} %bitcast.4.me_ref, bf16[4,32,512]{2,1,0:T(8,128)(2,1)S(1)} %pad_maximum_fusion.a_ref, bf16[4,32,512]{2,1,0:T(8,128)(2,1)S(1)} %collective-permute-done.3.b_ref, bf16[4,32,512]{2,1,0:T(8,128)(2,1)S(1)} %collective-permute-done.4.c_ref, ...), custom_call_target="tpu_custom_call" | custom-call | flops 469762048 | bytes 14680064 | tf_op jit(solution)/shard_map/pallas_call | solution.py:336
  53.5 1.4 %collective-permute-done.6.b_ref = bf16[8,32,512]{2,1,0:T(8,128)(2,1)S(1)} collective-permute-done((bf16[8,32,512]{2,1,0:T(8,128)(2,1)S(1)}, bf16[8,32,512]{2,1,0:T(8,128)(2,1)S(1)}, u32[]{:S(2)}, u32[]{:S(2)}) %collective-permute-start.6) | collective-permute-done | bytes 262176 | tf_op jit(solution)/shard_map/ppermute | solution.py:360
  54.9 12.6 %shard_map.132 = (bf16[32,896]{1,0:T(8,128)(2,1)S(1)}, bf16[32,896]{1,0:T(8,128)(2,1)S(1)}, f32[32,512]{1,0:T(8,128)S(1)}) custom-call(s32[1]{0:T(128)} %bitcast.4.me_ref, bf16[8,32,512]{2,1,0:T(8,128)(2,1)S(1)} %all-to-all-done.1.a_ref, bf16[8,32,512]{2,1,0:T(8,128)(2,1)S(1)} %collective-permute-done.6.b_ref, f32[16,1,512]{2,1,0:T(1,128)S(1)} %bitcast.10, ...), custom_call_target="tpu_custom_call" | custom-call | flops 469762048 | bytes 14680064 | tf_op jit(solution)/shard_map/pallas_call | solution.py:362
  67.5 6.3 %shard_map.134 = bf16[8,32,512]{2,1,0:T(8,128)(2,1)S(1)} custom-call(s32[1]{0:T(128)} %bitcast.4.me_ref, bf16[32,896]{1,0:T(8,128)(2,1)S(1)} %get-tuple-element.42.active_ref, bf16[896,8192]{1,0:T(8,128)(2,1)} %weight_ref.8), custom_call_target="tpu_custom_call" | custom-call | flops 234881024 | bytes 7340032 | tf_op jit(solution)/shard_map/pallas_call | solution.py:417
  73.9 10.2 %shard_map.138 = (bf16[8,32,512]{2,1,0:T(8,128)(2,1)S(1)}, bf16[8,32,512]{2,1,0:T(8,128)(2,1)S(1)}) custom-call(s32[1]{0:T(128)} %bitcast.4.me_ref, bf16[32,896]{1,0:T(8,128)(2,1)S(1)} %get-tuple-element.51.gh_ref, bf16[8192,896]{1,0:T(8,128)(2,1)} %weight_ref.9), custom_call_target="tpu_custom_call" | custom-call | flops 469762048 | bytes 14680064 | tf_op jit(solution)/shard_map/pallas_call | solution.py:395
  84.6 6.3 %shard_map.133.kept_ref = bf16[8,32,512]{2,1,0:T(8,128)(2,1)S(1)} custom-call(s32[1]{0:T(128)} %bitcast.4.me_ref, bf16[32,896]{1,0:T(8,128)(2,1)S(1)} %get-tuple-element.42.active_ref, bf16[896,8192]{1,0:T(8,128)(2,1)} %weight_ref.8), custom_call_target="tpu_custom_call" | custom-call | flops 234881024 | bytes 7340032 | tf_op jit(solution)/shard_map/pallas_call | solution.py:417
  91.0 1.5 %collective-permute-start.8 = (bf16[4,32,512]{2,1,0:T(8,128)(2,1)S(1)}, bf16[4,32,512]{2,1,0:T(8,128)(2,1)S(1)}, u32[]{:S(2)}, u32[]{:S(2)}) collective-permute-start(bf16[4,32,512]{2,1,0:T(8,128)(2,1)S(1)} %get-tuple-element.44), channel_id=1, source_target_pairs={{0,2},{1,3},{2,0},{3,1},{4,6},{5,7},{6,4},{7,5},{8,10},{9,11},{10,... | collective-permute-start | bytes 393224 | tf_op jit(solution)/shard_map/ppermute | solution.py:448
  93.2 4.2 %collective-permute-done.8.arrived_ref = bf16[4,32,512]{2,1,0:T(8,128)(2,1)S(1)} collective-permute-done((bf16[4,32,512]{2,1,0:T(8,128)(2,1)S(1)}, bf16[4,32,512]{2,1,0:T(8,128)(2,1)S(1)}, u32[]{:S(2)}, u32[]{:S(2)}) %collective-permute-start.8) | collective-permute-done | bytes 131104 | tf_op jit(solution)/shard_map/ppermute | solution.py:448
  97.7 1.1 %collective-permute-start.10 = (bf16[32,512]{1,0:T(8,128)(2,1)S(1)}, bf16[32,512]{1,0:T(8,128)(2,1)S(1)}, u32[]{:S(2)}, u32[]{:S(2)}) collective-permute-start(bf16[32,512]{1,0:T(8,128)(2,1)S(1)} %get-tuple-element.47), channel_id=1, source_target_pairs={{0,8},{1,9},{2,10},{3,11},{4,12},{5,13},{6,14},{7,15},{8,0},{9,1},... | collective-permute-start | bytes 98312 | tf_op jit(solution)/shard_map/ppermute | solution.py:459
  98.8 2.5 %collective-permute-start.11 = (bf16[32,512]{1,0:T(8,128)(2,1)S(1)}, bf16[32,512]{1,0:T(8,128)(2,1)S(1)}, u32[]{:S(2)}, u32[]{:S(2)}) collective-permute-start(bf16[32,512]{1,0:T(8,128)(2,1)S(1)} %get-tuple-element.48), channel_id=1, source_target_pairs={{0,12},{1,13},{2,14},{3,15},{4,0},{5,1},{6,2},{7,3},{8,4},{9,5},{1... | collective-permute-start | bytes 98312 | tf_op jit(solution)/shard_map/ppermute | solution.py:459
  101.9 1.5 %collective-permute-start.15 = (bf16[32,512]{1,0:T(8,128)(2,1)S(1)}, bf16[32,512]{1,0:T(8,128)(2,1)S(1)}, u32[]{:S(2)}, u32[]{:S(2)}) collective-permute-start(bf16[32,512]{1,0:T(8,128)(2,1)S(1)} %get-tuple-element.58), channel_id=1, source_target_pairs={{0,8},{1,9},{2,10},{3,11},{4,12},{5,13},{6,14},{7,15},{8,0},{9,1},... | collective-permute-start | bytes 98312 | tf_op jit(solution)/shard_map/ppermute | solution.py:459
  103.5 2.8 %collective-permute-start.16 = (bf16[32,512]{1,0:T(8,128)(2,1)S(1)}, bf16[32,512]{1,0:T(8,128)(2,1)S(1)}, u32[]{:S(2)}, u32[]{:S(2)}) collective-permute-start(bf16[32,512]{1,0:T(8,128)(2,1)S(1)} %get-tuple-element.59), channel_id=1, source_target_pairs={{0,12},{1,13},{2,14},{3,15},{4,0},{5,1},{6,2},{7,3},{8,4},{9,5},{1... | collective-permute-start | bytes 98312 | tf_op jit(solution)/shard_map/ppermute | solution.py:459
  107.1 0.8 collective-permute-done.16.refs_3_
  (32 shorter events, 4.2 us)
Async XLA Ops:
  0.6 54.2 %copy-start = (f32[8192]{0:T(1024)S(1)}, f32[8192]{0:T(1024)}, u32[]{:S(2)}) copy-start(f32[8192]{0:T(1024)} %param.15) | copy-start | bytes 98308
  18.2 35.1 %all-to-all-start.1 = ((bf16[8,32,512]{2,1,0:T(8,128)(2,1)}), bf16[8,32,512]{2,1,0:T(8,128)(2,1)S(1)}, u32[]{:S(2)}, u32[]{:S(2)}) async-start(bf16[8,32,512]{2,1,0:T(8,128)(2,1)} %get-tuple-element.37), calls=%async_computation.1 | async-start | bytes 524288 | tf_op jit(solution)/shard_map/all_to_all | solution.py:329
  21.6 6.1 %collective-permute-start.2 = (bf16[1,32,512]{2,1,0:T(8,128)(2,1)S(1)}, bf16[1,32,512]{2,1,0:T(8,128)(2,1)S(1)}, u32[]{:S(2)}, u32[]{:S(2)}) collective-permute-start(bf16[1,32,512]{2,1,0:T(8,128)(2,1)S(1)} %bitcast.11), channel_id=1, source_target_pairs={{0,12},{1,13},{2,14},{3,15},{4,0},{5,1},{6,2},{7,3},{8,4},{9,5},{1... | collective-permute-start | bytes 98312 | tf_op jit(solution)/shard_map/ppermute | solution.py:309
  25.3 7.9 %collective-permute-start.1 = (bf16[1,32,512]{2,1,0:T(8,128)(2,1)S(1)}, bf16[1,32,512]{2,1,0:T(8,128)(2,1)S(1)}, u32[]{:S(2)}, u32[]{:S(2)}) collective-permute-start(bf16[1,32,512]{2,1,0:T(8,128)(2,1)S(1)} %bitcast.12), channel_id=1, source_target_pairs={{0,8},{1,9},{2,10},{3,11},{4,12},{5,13},{6,14},{7,15},{8,0},{9,1},... | collective-permute-start | bytes 98312 | tf_op jit(solution)/shard_map/ppermute | solution.py:309
  25.3 7.9 %collective-permute-start = (bf16[1,32,512]{2,1,0:T(8,128)(2,1)S(1)}, bf16[1,32,512]{2,1,0:T(8,128)(2,1)S(1)}, u32[]{:S(2)}, u32[]{:S(2)}) collective-permute-start(bf16[1,32,512]{2,1,0:T(8,128)(2,1)S(1)} %bitcast.13), channel_id=1, source_target_pairs={{0,4},{1,5},{2,6},{3,7},{4,8},{5,9},{6,10},{7,11},{8,12},{9,13},{1... | collective-permute-start | bytes 98312 | tf_op jit(solution)/shard_map/ppermute | solution.py:309
  33.3 5.0 %collective-permute-start.3 = (bf16[4,32,512]{2,1,0:T(8,128)(2,1)S(1)}, bf16[4,32,512]{2,1,0:T(8,128)(2,1)S(1)}, u32[]{:S(2)}, u32[]{:S(2)}) collective-permute-start(bf16[4,32,512]{2,1,0:T(8,128)(2,1)S(1)} %pad_maximum_fusion.a_ref), channel_id=1, source_target_pairs={{0,2},{1,3},{2,0},{3,1},{4,6},{5,7},{6,4},{7,5},{8,10},{9,11},{10,... | collective-permute-start | bytes 393224 | tf_op jit(solution)/shard_map/ppermute | solution.py:311
  34.8 3.5 %collective-permute-start.4 = (bf16[4,32,512]{2,1,0:T(8,128)(2,1)S(1)}, bf16[4,32,512]{2,1,0:T(8,128)(2,1)S(1)}, u32[]{:S(2)}, u32[]{:S(2)}) collective-permute-start(bf16[4,32,512]{2,1,0:T(8,128)(2,1)S(1)} %pad_maximum_fusion.a_ref), channel_id=1, source_target_pairs={{0,1},{1,0},{2,3},{3,2},{4,5},{5,4},{6,7},{7,6},{8,9},{9,8},{10,11... | collective-permute-start | bytes 393224 | tf_op jit(solution)/shard_map/ppermute | solution.py:312
  38.3 1.3 %collective-permute-start.5 = (bf16[4,32,512]{2,1,0:T(8,128)(2,1)S(1)}, bf16[4,32,512]{2,1,0:T(8,128)(2,1)S(1)}, u32[]{:S(2)}, u32[]{:S(2)}) collective-permute-start(bf16[4,32,512]{2,1,0:T(8,128)(2,1)S(1)} %collective-permute-done.3.b_ref), channel_id=1, source_target_pairs={{0,1},{1,0},{2,3},{3,2},{4,5},{5,4},{6,7},{7,6},{8,9},{9,8},{10,11... | collective-permute-start | bytes 393224 | tf_op jit(solution)/shard_map/ppermute | solution.py:312
  53.3 1.6 %collective-permute-start.6 = (bf16[8,32,512]{2,1,0:T(8,128)(2,1)S(1)}, bf16[8,32,512]{2,1,0:T(8,128)(2,1)S(1)}, u32[]{:S(2)}, u32[]{:S(2)}) collective-permute-start(bf16[8,32,512]{2,1,0:T(8,128)(2,1)S(1)} %all-to-all-done.1.a_ref), channel_id=1, source_target_pairs={{0,1},{1,0},{2,3},{3,2},{4,5},{5,4},{6,7},{7,6},{8,9},{9,8},{10,11... | collective-permute-start | bytes 786440 | tf_op jit(solution)/shard_map/ppermute | solution.py:360
  73.7 17.1 %collective-permute-start.7 = (bf16[8,32,512]{2,1,0:T(8,128)(2,1)S(1)}, bf16[8,32,512]{2,1,0:T(8,128)(2,1)S(1)}, u32[]{:S(2)}, u32[]{:S(2)}) collective-permute-start(bf16[8,32,512]{2,1,0:T(8,128)(2,1)S(1)} %shard_map.134), channel_id=1, source_target_pairs={{0,1},{1,0},{2,3},{3,2},{4,5},{5,4},{6,7},{7,6},{8,9},{9,8},{10,11... | collective-permute-start | bytes 786440 | tf_op jit(solution)/shard_map/ppermute | solution.py:465
  73.9 34.0 %copy-start.1 = (s32[2,1,64]{2,1,0:T(1,128)S(1)}, s32[2,1,64]{2,1,0:T(1,128)}, u32[]{:S(2)}) copy-start(s32[2,1,64]{2,1,0:T(1,128)} %param.19) | copy-start | bytes 1540
  84.1 8.3 %collective-permute-start.12 = (bf16[8,32,512]{2,1,0:T(8,128)(2,1)S(1)}, bf16[8,32,512]{2,1,0:T(8,128)(2,1)S(1)}, u32[]{:S(2)}, u32[]{:S(2)}) collective-permute-start(bf16[8,32,512]{2,1,0:T(8,128)(2,1)S(1)} %get-tuple-element.53), channel_id=1, source_target_pairs={{0,1},{1,0},{2,3},{3,2},{4,5},{5,4},{6,7},{7,6},{8,9},{9,8},{10,11... | collective-permute-start | bytes 786440 | tf_op jit(solution)/shard_map/ppermute | solution.py:464
  91.0 6.4 %collective-permute-start.8 = (bf16[4,32,512]{2,1,0:T(8,128)(2,1)S(1)}, bf16[4,32,512]{2,1,0:T(8,128)(2,1)S(1)}, u32[]{:S(2)}, u32[]{:S(2)}) collective-permute-start(bf16[4,32,512]{2,1,0:T(8,128)(2,1)S(1)} %get-tuple-element.44), channel_id=1, source_target_pairs={{0,2},{1,3},{2,0},{3,1},{4,6},{5,7},{6,4},{7,5},{8,10},{9,11},{10,... | collective-permute-start | bytes 393224 | tf_op jit(solution)/shard_map/ppermute | solution.py:448
  92.6 8.7 %collective-permute-start.13 = (bf16[4,32,512]{2,1,0:T(8,128)(2,1)S(1)}, bf16[4,32,512]{2,1,0:T(8,128)(2,1)S(1)}, u32[]{:S(2)}, u32[]{:S(2)}) collective-permute-start(bf16[4,32,512]{2,1,0:T(8,128)(2,1)S(1)} %get-tuple-element.55), channel_id=1, source_target_pairs={{0,2},{1,3},{2,0},{3,1},{4,6},{5,7},{6,4},{7,5},{8,10},{9,11},{10,... | collective-permute-start | bytes 393224 | tf_op jit(solution)/shard_map/ppermute | solution.py:448
  97.4 6.1 %collective-permute-start.9 = (bf16[32,512]{1,0:T(8,128)(2,1)S(1)}, bf16[32,512]{1,0:T(8,128)(2,1)S(1)}, u32[]{:S(2)}, u32[]{:S(2)}) collective-permute-start(bf16[32,512]{1,0:T(8,128)(2,1)S(1)} %get-tuple-element.46), channel_id=1, source_target_pairs={{0,4},{1,5},{2,6},{3,7},{4,8},{5,9},{6,10},{7,11},{8,12},{9,13},{1... | collective-permute-start | bytes 98312 | tf_op jit(solution)/shard_map/ppermute | solution.py:459
  97.7 8.7 %collective-permute-start.10 = (bf16[32,512]{1,0:T(8,128)(2,1)S(1)}, bf16[32,512]{1,0:T(8,128)(2,1)S(1)}, u32[]{:S(2)}, u32[]{:S(2)}) collective-permute-start(bf16[32,512]{1,0:T(8,128)(2,1)S(1)} %get-tuple-element.47), channel_id=1, source_target_pairs={{0,8},{1,9},{2,10},{3,11},{4,12},{5,13},{6,14},{7,15},{8,0},{9,1},... | collective-permute-start | bytes 98312 | tf_op jit(solution)/shard_map/ppermute | solution.py:459
  98.8 7.5 %collective-permute-start.11 = (bf16[32,512]{1,0:T(8,128)(2,1)S(1)}, bf16[32,512]{1,0:T(8,128)(2,1)S(1)}, u32[]{:S(2)}, u32[]{:S(2)}) collective-permute-start(bf16[32,512]{1,0:T(8,128)(2,1)S(1)} %get-tuple-element.48), channel_id=1, source_target_pairs={{0,12},{1,13},{2,14},{3,15},{4,0},{5,1},{6,2},{7,3},{8,4},{9,5},{1... | collective-permute-start | bytes 98312 | tf_op jit(solution)/shard_map/ppermute | solution.py:459
  101.3 5.8 %collective-permute-start.14 = (bf16[32,512]{1,0:T(8,128)(2,1)S(1)}, bf16[32,512]{1,0:T(8,128)(2,1)S(1)}, u32[]{:S(2)}, u32[]{:S(2)}) collective-permute-start(bf16[32,512]{1,0:T(8,128)(2,1)S(1)} %get-tuple-element.57), channel_id=1, source_target_pairs={{0,4},{1,5},{2,6},{3,7},{4,8},{5,9},{6,10},{7,11},{8,12},{9,13},{1... | collective-permute-start | bytes 98312 | tf_op jit(solution)/shard_map/ppermute | solution.py:459
  101.9 5.2 %collective-permute-start.15 = (bf16[32,512]{1,0:T(8,128)(2,1)S(1)}, bf16[32,512]{1,0:T(8,128)(2,1)S(1)}, u32[]{:S(2)}, u32[]{:S(2)}) collective-permute-start(bf16[32,512]{1,0:T(8,128)(2,1)S(1)} %get-tuple-element.58), channel_id=1, source_target_pairs={{0,8},{1,9},{2,10},{3,11},{4,12},{5,13},{6,14},{7,15},{8,0},{9,1},... | collective-permute-start | bytes 98312 | tf_op jit(solution)/shard_map/ppermute | solution.py:459
  103.5 4.4 %collective-permute-start.16 = (bf16[32,512]{1,0:T(8,128)(2,1)S(1)}, bf16[32,512]{1,0:T(8,128)(2,1)S(1)}, u32[]{:S(2)}, u32[]{:S(2)}) collective-permute-start(bf16[32,512]{1,0:T(8,128)(2,1)S(1)} %get-tuple-element.59), channel_id=1, source_target_pairs={{0,12},{1,13},{2,14},{3,15},{4,0},{5,1},{6,2},{7,3},{8,4},{9,5},{1... | collective-permute-start | bytes 98312 | tf_op jit(solution)/shard_map/ppermute | solution.py:459

commit v3 on v0

v3 whole, which is shorter than its diff:
```python
import functools

import jax
import jax.numpy as jnp
from jax import lax
from jax.experimental import pallas as pl
from jax.experimental.pallas import tpu as pltpu
from jax.sharding import PartitionSpec as P

clip_top = 448.0
eps = 1e-05
LANES = 128
f32 = jnp.float32
bf16 = jnp.bfloat16
VMEM = pl.BlockSpec(memory_space=pltpu.VMEM)
SMEM = pl.BlockSpec(memory_space=pltpu.SMEM)


def hbm(x):
    return pltpu.with_memory_space_constraint(x, pltpu.HBM)


def powers(exponent, sign):
    total = jnp.zeros(exponent.shape, f32)
    for level in range(-10, 1):
        total = jnp.where(exponent == level, f32(2.0 ** (sign * level)), total)
    return total


def params(megabytes):
    return pltpu.CompilerParams(vmem_limit_bytes=megabytes << 20)


def flip(bit, by):
    return lax.rem(bit + by, 2)


def place(me):
    return me // 4, lax.rem(me // 2, 2), lax.rem(me, 2)


def owner_of(me, n, part, back):
    along, row, core = place(me)
    at = lax.rem(along - back + n // 4, n // 4)
    return 4 * at + 2 * flip(row, part % 2) + flip(core, part // 2)


def block_spot(q, tokens, rows, width):
    per_column = tokens // rows
    r, c = rows * (q % per_column), width + LANES * (q // per_column)
    return slice(r, r + rows), slice(c, c + LANES)


def send_kernel(
    me_ref, offset_ref, act_ref, expo_ref, base_ref, received_ref, cot_ref, gain_ref,
    new_ref, received_out_ref, gain_out_ref, *refs,
):
    *packed_refs, rows_ref = refs
    n, rows, _ = rows_ref.shape
    tokens, share = cot_ref.shape
    width = act_ref.shape[1]
    per_dev = width // LANES // n
    received_out_ref[...] = received_ref[...]
    for j in range(n):
        gain_out_ref[j : j + 1, :] = gain_ref[:, j * share : (j + 1) * share]
    first = offset_ref[0] == 0
    down, up = powers(expo_ref[...], -1), powers(expo_ref[...], 1)
    old = [base_ref[p] for p in range(2)]
    chosen = jnp.concatenate([jnp.where(first, o[0:1], o[1:2]) for o in old], axis=0)
    delta = act_ref[...].astype(f32) - chosen
    fill = jnp.full((rows - 2 * per_dev, LANES), offset_ref[0].astype(f32))
    pieces = []
    for b in range(width // LANES):
        scaled = delta[:, b * LANES : (b + 1) * LANES] * down[:, b : b + 1]
        kept = jnp.clip(scaled, -clip_top, clip_top).astype(bf16).astype(f32) * up[:, b : b + 1]
        d, c = divmod(b, per_dev)
        rows_ref[d, 2 * c : 2 * c + 2, :] = kept
        pieces.append(kept)
    for d in range(n):
        rows_ref[d, 2 * per_dev :, :] = fill
    along, _, _ = place(me_ref[0])
    cot = cot_ref[...]
    for r, packed_ref in enumerate(packed_refs):
        to = lax.rem(along + r, n // 4)
        packed_ref[:, :share] = cot
        for q in range(4):
            packed_ref[block_spot(q, tokens, rows, share)] = rows_ref[4 * to + q].astype(bf16)
    new = chosen + jnp.concatenate(pieces, axis=1)
    for p in range(2):
        row = new[p : p + 1]
        new_ref[p, 0:1, :] = jnp.where(first, row, old[p][0:1])
        new_ref[p, 1:2, :] = jnp.where(first, old[p][1:2], row)


def sort_kernel(me_ref, *refs):
    *packed_refs, line_ref, b0, b1, b2, b3 = refs
    quarter, tokens, share = line_ref.shape
    rows = b0.shape[1]
    _, row, core = place(me_ref[0])
    for r, packed_ref in enumerate(packed_refs):
        line_ref[r] = packed_ref[:, :share]
        block = [packed_ref[block_spot(q, tokens, rows, share)] for q in range(4)]
        for e, out_ref in enumerate((b0, b1, b2, b3)):
            to_row, to_core = flip(row, e // 2), flip(core, e % 2)
            low = jnp.where(to_core == 0, block[0], block[1])
            high = jnp.where(to_core == 0, block[2], block[3])
            out_ref[r] = jnp.where(to_row == 0, low, high)


def rebuild_kernel(me_ref, b0, b1, b2, b3, base_ref, new_ref, share_ref, rows_ref, slots_ref):
    quarter, rows, _ = b0.shape
    n, width = 4 * quarter, share_ref.shape[1]
    for e, block_ref in enumerate((b0, b1, b2, b3)):
        for r in range(quarter):
            sender = owner_of(me_ref[0], n, 2 * (e % 2) + e // 2, r)
            rows_ref[pl.ds(pl.multiple_of(sender * rows, rows), rows), :] = block_ref[r].astype(f32)
    per_dev = width // LANES
    first = rows_ref[pl.ds(2 * per_dev, n, stride=rows), :] == 0.0
    for p in range(2):
        for c in range(per_dev):
            cols = slice(c * LANES, (c + 1) * LANES)
            sent = rows_ref[pl.ds(2 * c + p, n, stride=rows), :]
            at = p * per_dev + c
            slots_ref[at] = base_ref[p, :, cols]
            even = slots_ref[at, pl.ds(0, n, stride=2), :]
            odd = slots_ref[at, pl.ds(1, n, stride=2), :]
            rebuilt = jnp.where(first, even, odd) + sent
            slots_ref[at, pl.ds(0, n, stride=2), :] = jnp.where(first, rebuilt, even)
            slots_ref[at, pl.ds(1, n, stride=2), :] = jnp.where(first, odd, rebuilt)
            new_ref[p, :, cols] = slots_ref[at]
            restored = rebuilt.astype(bf16)
            share_ref[p * n : (p + 1) * n, cols] = restored


def dot_nt(a, b):
    return lax.dot_general(a, b, (((1,), (1,)), ((), ())), preferred_element_type=f32)


def own_rows(piece_ref, own_ref, me, owner):
    n = piece_ref.shape[0] // 2
    for p in range(2):
        own_ref[pl.ds(p * n + owner, 1), :] = piece_ref[pl.ds(p * n + me, 1), :]


def grad_active_kernel(first, me_ref, a_ref, b_ref, weight_ref, acc_in_ref, own_in_ref, acc_ref, own_ref, piece_ref):
    quarter, _, width = a_ref.shape
    me = me_ref[0]
    acc_ref[...] = acc_in_ref[...]
    own_ref[...] = own_in_ref[...]
    for part, cot_ref in enumerate((a_ref, b_ref)):

        @pl.loop(0, quarter)
        def _(k):
            owner = owner_of(me, 4 * quarter, first + part, k)
            piece = cot_ref[k]
            columns = pl.ds(pl.multiple_of(owner * width, width), width)
            acc_ref[...] += dot_nt(weight_ref[:, columns], piece)
            piece_ref[...] = piece.astype(f32)
            own_rows(piece_ref, own_ref, me, owner)


def up_kernel(
    first, me_ref, a_ref, b_ref, gain_ref, weight_ref, acc_in_ref, square_in_ref, own_in_ref, *refs
):
    if first == 0:
        acc_ref, square_ref, own_ref, piece_ref = refs
    else:
        ga_ref, active_ref, gh_ref, own_ref, piece_ref, acc_ref, square_ref = refs
    quarter, _, width = a_ref.shape
    width_all = weight_ref.shape[0]
    me = me_ref[0]
    acc_ref[...] = acc_in_ref[...]
    square_ref[...] = square_in_ref[...]
    own_ref[...] = own_in_ref[...]
    for part, rest_ref in enumerate((a_ref, b_ref)):

        @pl.loop(0, quarter)
        def _(k):
            owner = owner_of(me, 4 * quarter, first + part, k)
            piece = rest_ref[k].astype(f32)
            piece_ref[...] = piece
            own_rows(piece_ref, own_ref, me, owner)
            squares = piece * piece
            total = square_ref[...]
            for c in range(width // LANES):
                total = total + squares[:, c * LANES : (c + 1) * LANES]
            square_ref[...] = total
            scaled = (piece * gain_ref[pl.ds(owner, 1), :]).astype(bf16)
            rows = pl.ds(pl.multiple_of(owner * width, width), width)
            acc_ref[...] += jnp.dot(scaled, weight_ref[rows, :], preferred_element_type=f32)

    if first == 0:
        return
    total = jnp.sum(square_ref[...], axis=1, keepdims=True)
    hidden = lax.rsqrt(total / width_all + eps) * acc_ref[...]
    sigma = jax.nn.sigmoid(hidden)
    active_ref[...] = (hidden * sigma).astype(bf16)
    grad_active = ga_ref[...].T
    gh_ref[...] = (grad_active * sigma * (1.0 + hidden * (1.0 - sigma))).astype(bf16)


def down_kernel(other, me_ref, active_ref, weight_ref, after_ref, out_ref):
    half, _, width = out_ref.shape
    core = lax.rem(me_ref[0] + other, 2)

    @pl.loop(0, half)
    def _(k):
        columns = pl.ds(pl.multiple_of((2 * k + core) * width, width), width)
        terms = jnp.dot(active_ref[...], weight_ref[:, columns], preferred_element_type=f32)
        out_ref[k] = terms.astype(bf16)


def grad_norm_kernel(me_ref, gh_ref, weight_ref, send_ref, keep_ref, rows_ref):
    half, tokens, width = send_ref.shape
    n, chunks = 2 * half, width // LANES

    @pl.loop(0, n)
    def _(share):
        block = weight_ref[pl.ds(pl.multiple_of(share * width, width), width), :]
        terms = dot_nt(gh_ref[...], block)
        for p in range(2):
            for c in range(chunks):
                rows_ref[c, pl.ds(p * n + share, n, stride=tokens), :] = terms[
                    p * n : (p + 1) * n, c * LANES : (c + 1) * LANES
                ]

    core = lax.rem(me_ref[0], 2)
    for k in range(half):
        keep_at = pl.multiple_of((2 * k + core) * tokens, tokens)
        send_at = pl.multiple_of((2 * k + 1 - core) * tokens, tokens)
        for c in range(chunks):
            cols = slice(c * LANES, (c + 1) * LANES)
            keep_ref[k, :, cols] = rows_ref[c, pl.ds(keep_at, tokens), :].astype(bf16)
            send_ref[k, :, cols] = rows_ref[c, pl.ds(send_at, tokens), :].astype(bf16)


def pair_kernel(me_ref, kept_ref, arrived_ref, send_ref, keep_ref):
    quarter = send_ref.shape[0]
    row = lax.rem(me_ref[0] // 2, 2)
    for k in range(quarter):
        for out_ref, at in ((send_ref, 2 * k + 1 - row), (keep_ref, 2 * k + row)):
            out_ref[k] = (kept_ref[at].astype(f32) + arrived_ref[at].astype(f32)).astype(bf16)


def line_kernel(me_ref, grad_ref, grad_in_ref, out_ref, out_in_ref, *refs):
    quarter = len(refs)
    for r, ref in enumerate(refs):
        at = lax.rem(me_ref[0] // 4 + r, quarter)
        ref[0] = (grad_ref[at].astype(f32) + grad_in_ref[at].astype(f32)).astype(bf16)
        ref[1] = (out_ref[at].astype(f32) + out_in_ref[at].astype(f32)).astype(bf16)


def final_kernel(width_all, share_ref, own_ref, cot_ref, gain_ref, expo_ref, *refs):
    *refs, layer_ref, grad_ref = refs
    grad = refs[0][0].astype(f32)
    layer = refs[0][1].astype(f32)
    for ref in refs[1:]:
        grad = grad + ref[0].astype(f32)
        layer = layer + ref[1].astype(f32)
    layer_ref[...] = (share_ref[...].astype(f32) + layer).astype(bf16)
    n, width = gain_ref.shape
    down, up = powers(expo_ref[...], -1), powers(expo_ref[...], 1)
    gain = gain_ref[...]
    per_dev = width // LANES
    blocks = n * per_dev
    at_row = lax.broadcasted_iota(jnp.int32, (n, blocks), 0)
    at_lane = lax.broadcasted_iota(jnp.int32, (n, blocks), 1)
    for p in range(2):
        rows = slice(p * n, (p + 1) * n)
        own, norm = own_ref[rows, :], grad[rows, :]
        inv_rms = lax.rsqrt(jnp.sum(own * own, keepdims=True) / width_all + eps)
        scaled_in = (own * gain).astype(bf16).astype(f32)
        curvature = inv_rms * jnp.sum(scaled_in * norm, keepdims=True)
        correction = curvature * inv_rms * inv_rms / width_all
        value = cot_ref[rows, :].astype(f32) + inv_rms * gain * norm - correction * own
        for c in range(per_dev):
            at = at_lane == at_row * per_dev + c
            shrink = jnp.sum(jnp.where(at, down[p : p + 1], 0.0), axis=1, keepdims=True)
            grow = jnp.sum(jnp.where(at, up[p : p + 1], 0.0), axis=1, keepdims=True)
            scaled = value[:, c * LANES : (c + 1) * LANES] * shrink
            kept = jnp.clip(scaled, -clip_top, clip_top).astype(bf16).astype(f32) * grow
            grad_ref[p, pl.ds(c, n, stride=per_dev), :] = kept


def on_device(
    activations,
    sample_ids,
    forward_exponent,
    sender_base,
    receiver_base,
    norm_gain,
    up_weight,
    down_weight,
    cotangent,
    backward_exponent,
    *,
    n,
):
    half, quarter = n // 2, n // 4
    tokens = 2 * n
    width_all, hidden_dev = up_weight.shape
    width = width_all // n
    me = lax.axis_index("dp").astype(jnp.int32)
    me_in = me.reshape(1)

    def shift(x, r):
        return lax.ppermute(x, "dp", [(d, (d + 4 * r) % n) for d in range(n)]) if r else x

    def swap(x, bits):
        return lax.ppermute(x, "dp", [(d, d ^ bits) for d in range(n)])

    struct = jax.ShapeDtypeStruct
    share_shape, hidden_shape = (tokens, width), (tokens, hidden_dev)
    line_shape = (quarter, tokens, width)

    def call(kernel, outs, ins, args, scratch=(), cost=0):
        return pl.pallas_call(
            kernel,
            out_shape=outs,
            in_specs=ins,
            out_specs=jax.tree.map(lambda _: VMEM, outs),
            scratch_shapes=list(scratch),
            compiler_params=params(8),
            cost_estimate=pl.CostEstimate(
                flops=cost * tokens * width_all * hidden_dev,
                bytes_accessed=cost * width_all * hidden_dev,
                transcendentals=0,
            ),
        )(*args)

    offset = sample_ids - sender_base.shape[1] * me
    rows = -(-(2 * width // LANES + 1) // 16) * 16
    packed_shape = (tokens, width + LANES * -(-4 * rows // tokens))
    act_shape, expo_shape = (2, width_all), (2, width_all // LANES)
    once = lambda shape: pl.BlockSpec(shape, lambda i: (0,) * len(shape))
    in_shapes = [act_shape, expo_shape, sender_base.shape, receiver_base.shape, share_shape, (1, width_all)]
    outs = (
        struct(sender_base.shape, f32),
        struct(receiver_base.shape, f32),
        struct((n, width), f32),
    ) + (struct(packed_shape, bf16),) * quarter
    new_sender_base, received, gain, *packed = pl.pallas_call(
        send_kernel,
        out_shape=outs,
        grid=(1,),
        in_specs=[SMEM, SMEM] + [once(x) for x in in_shapes],
        out_specs=tuple(once(x.shape) for x in outs),
        scratch_shapes=[pltpu.VMEM((n, rows, LANES), f32)],
        compiler_params=params(8),
    )(
        me_in,
        offset,
        hbm(activations.reshape(act_shape)),
        hbm(forward_exponent.reshape(expo_shape)),
        hbm(sender_base),
        hbm(receiver_base),
        hbm(cotangent.reshape(share_shape)),
        hbm(norm_gain.reshape(1, width_all)),
    )
    packed = [shift(x, r) for r, x in enumerate(packed)]
    cot_line, *blocks = call(
        sort_kernel,
        (struct(line_shape, bf16),) + (struct((quarter, rows, LANES), bf16),) * 4,
        [SMEM] + [VMEM] * quarter,
        [me_in, *packed],
    )
    blocks = [blocks[0]] + [swap(blocks[e], e) for e in range(1, 4)]
    cot_row = swap(cot_line, 2)
    cots = [cot_line, cot_row, swap(cot_line, 1), swap(cot_row, 1)]

    new_receiver_base, share = call(
        rebuild_kernel,
        (struct(receiver_base.shape, f32), struct(share_shape, bf16)),
        [SMEM] + [VMEM] * 5,
        [me_in, *blocks, received],
        [pltpu.VMEM((n * rows, LANES), f32), pltpu.VMEM((2 * width // LANES, 2 * n, LANES), f32)],
    )
    rest_line = jnp.stack([shift(share, r) for r in range(quarter)])
    rest_row = swap(rest_line, 2)
    rests = [rest_line, rest_row, swap(rest_line, 1), swap(rest_row, 1)]

    ga, own_cot = jnp.zeros((hidden_dev, tokens), f32), jnp.zeros(share_shape, f32)
    acc, square, own = jnp.zeros(hidden_shape, f32), jnp.zeros((tokens, LANES), f32), own_cot
    for first in (0, 2):
        ga, own_cot = call(
            functools.partial(grad_active_kernel, first),
            (struct((hidden_dev, tokens), f32), struct(share_shape, f32)),
            [SMEM] + [VMEM] * 5,
            [me_in, cots[first], cots[first + 1], down_weight, ga, own_cot],
            [pltpu.VMEM(share_shape, f32)],
            cost=1,
        )
    sums = (struct(hidden_shape, f32), struct((tokens, LANES), f32))
    acc, square, own = call(
        functools.partial(up_kernel, 0),
        sums + (struct(share_shape, f32),),
        [SMEM] + [VMEM] * 7,
        [me_in, rests[0], rests[1], gain, up_weight, acc, square, own],
        [pltpu.VMEM(share_shape, f32)],
        cost=1,
    )
    active, grad_hidden, own = call(
        functools.partial(up_kernel, 2),
        (struct(hidden_shape, bf16), struct(hidden_shape, bf16), struct(share_shape, f32)),
        [SMEM] + [VMEM] * 8,
        [me_in, rests[2], rests[3], gain, up_weight, acc, square, own, ga],
        [pltpu.VMEM(share_shape, f32)] + [pltpu.VMEM(x.shape, x.dtype) for x in sums],
        cost=1,
    )

    half_out = struct((half, tokens, width), bf16)
    grad_send, grad_keep = call(
        grad_norm_kernel,
        (half_out, half_out),
        [SMEM] + [VMEM] * 2,
        [me_in, grad_hidden, up_weight],
        [pltpu.VMEM((width // LANES, n * tokens, LANES), f32)],
        cost=2,
    )

    def down_terms(other, after):
        return call(
            functools.partial(down_kernel, other),
            half_out,
            [SMEM] + [VMEM] * 2 + [pl.BlockSpec(memory_space=pl.ANY)],
            [me_in, active, down_weight, after],
            cost=1,
        )

    def pair_sum(kept, arrived):
        pair_out = struct(line_shape, bf16)
        return call(
            pair_kernel, (pair_out, pair_out), [SMEM] + [VMEM] * 2, [me_in, kept, arrived]
        )

    grad_in = swap(grad_send, 1)
    out_in = swap(down_terms(1, grad_send), 1)
    grad_send, grad_row = pair_sum(grad_keep, grad_in)
    grad_row_in = swap(grad_send, 2)
    out_send, out_row = pair_sum(down_terms(0, grad_send), out_in)
    out_row_in = swap(out_send, 2)
    shares = call(
        line_kernel,
        (struct((2, tokens, width), bf16),) * quarter,
        [SMEM] + [VMEM] * 4,
        [me_in, grad_row, grad_row_in, out_row, out_row_in],
    )
    moved = [shift(x, r) for r, x in enumerate(shares)]
    layer_out, returned = call(
        functools.partial(final_kernel, width_all),
        (struct(share_shape, bf16), struct((2, width_all // LANES, LANES), f32)),
        [VMEM] * (5 + quarter),
        [share, own, own_cot, gain, backward_exponent.reshape(expo_shape), *moved],
    )
    return (
        new_sender_base,
        new_receiver_base,
        layer_out.reshape(2, n, width),
        returned.reshape(2, 1, width_all),
    )


def solution(mesh):
    placed = (
        P(None, ("groups", "dp"), None),
        P(("groups", "dp")),
        P(None, ("groups", "dp"), None),
        P(None, ("groups", "dp"), None),
        P(None, "groups", "dp"),
        P(),
        P(None, "dp"),
        P("dp", None),
        P(None, "groups", "dp"),
        P(None, ("groups", "dp"), None),
    )
    return jax.shard_map(
        functools.partial(on_device, n=mesh.shape["dp"]),
        mesh=mesh,
        in_specs=placed,
        out_specs=(
            P(None, ("groups", "dp"), None),
            P(None, "groups", "dp"),
            P(None, "groups", "dp"),
            P(None, ("groups", "dp"), None),
        ),
        check_vma=False,
    )
```

time: 314 us -> 84.4 us (0.27)
  blocking collectives: 82.3 us -> 0 us
  waiting for transfers between devices: 80.3 us -> 23.6 us
  other arithmetic: 50.9 us -> 0.02 us
  matrix products: 36.7 us -> 0 us
  Pallas kernels: 0 us -> 26.1 us
  local copies, waits for them, and re-layouts: 36.4 us -> 11.4 us
  between operations: 14.9 us -> 1.53 us
  starting transfers between devices: 11.2 us -> 21.5 us
    reduce_scatter x2 -> x0, waiting for transfers between devices: 76.2 us -> none  [the longest x1 60.5 us: on_device(): lax.psum_scatter(down_terms, 'dp', scatter_dimension=2, tiled=True)]
    unnamed x2, other arithmetic: 45.2 us -> 0.01 us
    all_gather x2 -> x0, blocking collectives: 39.5 us -> none  [the longest x1 19.8 us: on_device(): piece = lax.all_gather(restored, 'dp', axis=2, tiled=True)]
    dot_general x4 -> x0, matrix products: 36.7 us -> none  [the longest x1 10.6 us: on_device(): lax.dot_general(grad_hidden, up_weight, (((1,), (1,)), ((), ())), preferr...]
    psum x1 -> x0, blocking collectives: 30.4 us -> none  [on_device(): lax.psum(jnp.sum(grad_hidden.astype(jnp.float32) * hidden, axis=1), 'dp')]
    pallas_call x0 -> x14, Pallas kernels: none -> 26.1 us  [the longest x13 24.2 us: call(): pl.pallas_call(kernel, out_shape=outs, in_specs=ins, out_specs=jax.tree.m...]
    ppermute x0 -> x22, waiting for transfers between devices: none -> 23.6 us  [the longest x13 13.5 us: swap(): return lax.ppermute(x, 'dp', [(d, d ^ bits) for d in range(n)])]
    ppermute x0 -> x22, starting transfers between devices: none -> 21.5 us  [the longest x9 14.9 us: shift(): lax.ppermute(x, 'dp', [(d, (d + 4 * r) % n) for d in range(n)])]
  transfers between devices with their start and end apart: 4 -> 22, of which waited for: 3 -> 14; matrix products, arithmetic and copies ran while one was open for 4% -> 0% of each run, Pallas kernels for 0% -> 15%
where the time goes in v3:
time: 84.4 us; the launch traced here: 84.2 us
  Pallas kernels  26.1 us (31%)
  waiting for transfers between devices  23.6 us (28%)
  starting transfers between devices  21.5 us (25%)
  local copies, waits for them, and re-layouts  11.4 us (14%)
  between operations  1.53 us (2%)
    pallas_call x13, Pallas kernels, call(): pl.pallas_call(kernel, out_shape=outs, in_specs=ins, out_specs=jax.tree.m...  24.2 us
    ppermute x9, starting transfers between devices, shift(): lax.ppermute(x, 'dp', [(d, (d + 4 * r) % n) for d in range(n)])  14.9 us
    ppermute x13, waiting for transfers between devices, swap(): return lax.ppermute(x, 'dp', [(d, d ^ bits) for d in range(n)])  13.5 us
    unnamed x22, local copies, waits for them, and re-layouts  11.4 us
    ppermute x9, waiting for transfers between devices, shift(): lax.ppermute(x, 'dp', [(d, (d + 4 * r) % n) for d in range(n)])  10.2 us
    ppermute x13, starting transfers between devices, swap(): return lax.ppermute(x, 'dp', [(d, d ^ bits) for d in range(n)])  6.59 us
    pallas_call x1, Pallas kernels, on_device(): pl.pallas_call(send_kernel, out_shape=outs, grid=(1,), in_specs=[SMEM, SM...  1.94 us
  transfers between devices with their start and end apart: 22, of which 14 were waited for; matrix products, arithmetic and copies ran while one was open for 0% of the time, Pallas kernels for 15%

profile of v3, /device:TPU:0, one launch (start us, length us, event | category | flops | bytes accessed | tf_op | source)
XLA Modules:
  0.0 84.2 jit_solution(11194845131055772781)
XLA Ops:
  1.3 1.9 %shard_map.129 = (f32[2,2,8192]{2,1,0:T(2,128)}, f32[2,32,512]{2,1,0:T(8,128)S(1)}, f32[16,512]{1,0:T(8,128)S(1)}, bf16[32,768]{1,0:T(8,128)(2,1)S(1)}, bf16[32,...) custom-call(s32[1]{0:T(128)} %bitcast.me_ref, s32[1]{0:T(128)S(6)} %sub.7.offset_ref, ...), custom_call_target="tpu_custom_call" | custom-call | tf_op jit(solution)/shard_map/pallas_call | solution.py:342
  3.2 3.0 %collective-permute-start = (bf16[32,768]{1,0:T(8,128)(2,1)S(1)}, bf16[32,768]{1,0:T(8,128)(2,1)S(1)}, u32[]{:S(2)}, u32[]{:S(2)}) collective-permute-start(bf16[32,768]{1,0:T(8,128)(2,1)S(1)} %get-tuple-element.42), channel_id=1, source_target_pairs={{0,4},{1,5},{2,6},{3,7},{4,8},{5,9},{6,10},{7,11},{8,12},{9,13},{1... | collective-permute-start | bytes 147464 | tf_op jit(solution)/shard_map/ppermute | solution.py:307
  6.2 2.6 %collective-permute-start.1 = (bf16[32,768]{1,0:T(8,128)(2,1)S(1)}, bf16[32,768]{1,0:T(8,128)(2,1)S(1)}, u32[]{:S(2)}, u32[]{:S(2)}) collective-permute-start(bf16[32,768]{1,0:T(8,128)(2,1)S(1)} %get-tuple-element.43), channel_id=1, source_target_pairs={{0,8},{1,9},{2,10},{3,11},{4,12},{5,13},{6,14},{7,15},{8,0},{9,1},... | collective-permute-start | bytes 147464 | tf_op jit(solution)/shard_map/ppermute | solution.py:307
  8.8 1.3 %collective-permute-start.2 = (bf16[32,768]{1,0:T(8,128)(2,1)S(1)}, bf16[32,768]{1,0:T(8,128)(2,1)S(1)}, u32[]{:S(2)}, u32[]{:S(2)}) collective-permute-start(bf16[32,768]{1,0:T(8,128)(2,1)S(1)} %get-tuple-element.44), channel_id=1, source_target_pairs={{0,12},{1,13},{2,14},{3,15},{4,0},{5,1},{6,2},{7,3},{8,4},{9,5},{1... | collective-permute-start | bytes 147464 | tf_op jit(solution)/shard_map/ppermute | solution.py:307
  10.4 2.0 %collective-permute-done.1.refs_2_ = bf16[32,768]{1,0:T(8,128)(2,1)S(1)} collective-permute-done((bf16[32,768]{1,0:T(8,128)(2,1)S(1)}, bf16[32,768]{1,0:T(8,128)(2,1)S(1)}, u32[]{:S(2)}, u32[]{:S(2)}) %collective-permute-start.1) | collective-permute-done | bytes 49184 | tf_op jit(solution)/shard_map/ppermute | solution.py:307
  13.1 1.7 %collective-permute-start.4 = (bf16[4,16,128]{2,1,0:T(8,128)(2,1)S(1)}, bf16[4,16,128]{2,1,0:T(8,128)(2,1)S(1)}, u32[]{:S(2)}, u32[]{:S(2)}) collective-permute-start(bf16[4,16,128]{2,1,0:T(8,128)(2,1)S(1)} %get-tuple-element.47), channel_id=1, source_target_pairs={{0,2},{1,3},{2,0},{3,1},{4,6},{5,7},{6,4},{7,5},{8,10},{9,11},{10,... | collective-permute-start | bytes 49160 | tf_op jit(solution)/shard_map/ppermute | solution.py:310
  14.9 1.9 %collective-permute-done.4.b2 = bf16[4,16,128]{2,1,0:T(8,128)(2,1)S(1)} collective-permute-done((bf16[4,16,128]{2,1,0:T(8,128)(2,1)S(1)}, bf16[4,16,128]{2,1,0:T(8,128)(2,1)S(1)}, u32[]{:S(2)}, u32[]{:S(2)}) %collective-permute-start.4) | collective-permute-done | bytes 16416 | tf_op jit(solution)/shard_map/ppermute | solution.py:310
  19.4 2.9 %collective-permute-start.7 = (bf16[32,512]{1,0:T(8,128)(2,1)S(1)}, bf16[32,512]{1,0:T(8,128)(2,1)S(1)}, u32[]{:S(2)}, u32[]{:S(2)}) collective-permute-start(bf16[32,512]{1,0:T(8,128)(2,1)S(1)} %get-tuple-element.51.share_ref), channel_id=1, source_target_pairs={{0,8},{1,9},{2,10},{3,11},{4,12},{5,13},{6,14},{7,15},{8,0},{9,1},... | collective-permute-start | bytes 98312 | tf_op jit(solution)/shard_map/ppermute | solution.py:307
  23.2 1.4 %collective-permute-done.6 = bf16[32,512]{1,0:T(8,128)(2,1)S(1)} collective-permute-done((bf16[32,512]{1,0:T(8,128)(2,1)S(1)}, bf16[32,512]{1,0:T(8,128)(2,1)S(1)}, u32[]{:S(2)}, u32[]{:S(2)}) %collective-permute-start.6) | collective-permute-done | bytes 32800 | tf_op jit(solution)/shard_map/ppermute | solution.py:307
  28.0 3.2 %collective-permute-done.10.b_ref = bf16[4,32,512]{2,1,0:T(8,128)(2,1)S(1)} collective-permute-done((bf16[4,32,512]{2,1,0:T(8,128)(2,1)S(1)}, bf16[4,32,512]{2,1,0:T(8,128)(2,1)S(1)}, u32[]{:S(2)}, u32[]{:S(2)}) %collective-permute-start.10) | collective-permute-done | bytes 131104 | tf_op jit(solution)/shard_map/ppermute | solution.py:310
  31.3 5.2 %copy-done = bf16[896,8192]{1,0:T(8,128)(2,1)S(1)} copy-done((bf16[896,8192]{1,0:T(8,128)(2,1)S(1)}, bf16[896,8192]{1,0:T(8,128)(2,1)}, u32[]{:S(2)}) %copy-start) | copy-done | bytes 14680088
  36.4 3.1 %shard_map.133 = (f32[896,32]{1,0:T(8,128)S(1)}, f32[32,512]{1,0:T(8,128)S(1)}) custom-call(s32[1]{0:T(128)} %bitcast.me_ref, bf16[4,32,512]{2,1,0:T(8,128)(2,1)S(1)} %get-tuple-element.56.a_ref, bf16[4,32,512]{2,1,0:T(8,128)(2,1)S(1)} %collective-permute-done.13.b_ref, bf16[896,8192]{1,0:T(8,128)(2,1)S(1)} %copy-done, ...), custom_call_target="tpu_custom_call" | custom-call | flops 234881024 | bytes 7340032 | tf_op jit(solution)/shard_map/pallas_call | solution.py:317
  39.6 5.7 %copy-done.1 = bf16[8192,896]{1,0:T(8,128)(2,1)S(1)} copy-done((bf16[8192,896]{1,0:T(8,128)(2,1)S(1)}, bf16[8192,896]{1,0:T(8,128)(2,1)}, u32[]{:S(2)}) %copy-start.1) | copy-done | bytes 14680088
  45.3 2.3 %shard_map.132 = (f32[32,896]{1,0:T(8,128)S(1)}, f32[32,128]{1,0:T(8,128)S(1)}, f32[32,512]{1,0:T(8,128)S(1)}) custom-call(s32[1]{0:T(128)} %bitcast.me_ref, bf16[4,32,512]{2,1,0:T(8,128)(2,1)S(1)} %pad_maximum_fusion.a_ref, bf16[4,32,512]{2,1,0:T(8,128)(2,1)S(1)} %collective-permute-done.10.b_ref, f32[16,512]{1,0:T(8,128)S(1)} %get-tuple-element.52.gain_ref, ...), custom_call_target="tpu_custom_call" | custom-call | flops 234881024 | bytes 7340032 | tf_op jit(solution)/shard_map/pallas_call | solution.py:317
  47.7 3.1 %shard_map.134 = (f32[896,32]{1,0:T(8,128)S(1)}, f32[32,512]{1,0:T(8,128)S(1)}) custom-call(s32[1]{0:T(128)} %bitcast.me_ref, bf16[4,32,512]{2,1,0:T(8,128)(2,1)S(1)} %collective-permute-done.12.a_ref, bf16[4,32,512]{2,1,0:T(8,128)(2,1)S(1)} %collective-permute-done.14.b_ref, bf16[896,8192]{1,0:T(8,128)(2,1)S(1)} %bitcast.14, ...), custom_call_target="tpu_custom_call" | custom-call | flops 234881024 | bytes 7340032 | tf_op jit(solution)/shard_map/pallas_call | solution.py:317
  51.3 2.5 %shard_map.135 = (bf16[32,896]{1,0:T(8,128)(2,1)S(1)}, bf16[32,896]{1,0:T(8,128)(2,1)S(1)}, f32[32,512]{1,0:T(8,128)S(1)}) custom-call(s32[1]{0:T(128)} %bitcast.me_ref, bf16[4,32,512]{2,1,0:T(8,128)(2,1)S(1)} %collective-permute-done.9.a_ref, bf16[4,32,512]{2,1,0:T(8,128)(2,1)S(1)} %collective-permute-done.11.b_ref, ...), custom_call_target="tpu_custom_call" | custom-call | flops 234881024 | bytes 7340032 | tf_op jit(solution)/shard_map/pallas_call | solution.py:317
  53.8 7.1 %shard_map.136 = (bf16[8,32,512]{2,1,0:T(8,128)(2,1)S(1)}, bf16[8,32,512]{2,1,0:T(8,128)(2,1)S(1)}) custom-call(s32[1]{0:T(128)} %bitcast.me_ref, bf16[32,896]{1,0:T(8,128)(2,1)S(1)} %get-tuple-element.62.gh_ref, bf16[8192,896]{1,0:T(8,128)(2,1)S(1)} %bitcast.16), custom_call_target="tpu_custom_call" | custom-call | flops 469762048 | bytes 14680064 | tf_op jit(solution)/shard_map/pallas_call | solution.py:317
  61.5 2.2 %shard_map.139 = bf16[8,32,512]{2,1,0:T(8,128)(2,1)S(1)} custom-call(s32[1]{0:T(128)} %bitcast.me_ref, bf16[32,896]{1,0:T(8,128)(2,1)S(1)} %get-tuple-element.67.active_ref, bf16[896,8192]{1,0:T(8,128)(2,1)S(1)} %bitcast.14, bf16[8,32,512]{2,1,0:T(8,128)(2,1)S(1)} %get-tuple-element.64.after_ref), custom_call_target="tpu_custom_call" | custom-call | flops 234881024 | bytes 7340032 | tf_op jit(solution)/shard_map/pallas_call | solution.py:317
  63.8 2.2 %shard_map.138.kept_ref = bf16[8,32,512]{2,1,0:T(8,128)(2,1)S(1)} custom-call(s32[1]{0:T(128)} %bitcast.me_ref, bf16[32,896]{1,0:T(8,128)(2,1)S(1)} %get-tuple-element.67.active_ref, bf16[896,8192]{1,0:T(8,128)(2,1)S(1)} %bitcast.14, bf16[4,32,512]{2,1,0:T(8,128)(2,1)S(1)} %get-tuple-element.66.after_ref), custom_call_target="tpu_custom_call" | custom-call | flops 234881024 | bytes 7340032 | tf_op jit(solution)/shard_map/pallas_call | solution.py:317
  68.1 4.3 %collective-permute-done.18.out_in_ref = bf16[4,32,512]{2,1,0:T(8,128)(2,1)S(1)} collective-permute-done((bf16[4,32,512]{2,1,0:T(8,128)(2,1)S(1)}, bf16[4,32,512]{2,1,0:T(8,128)(2,1)S(1)}, u32[]{:S(2)}, u32[]{:S(2)}) %collective-permute-start.18) | collective-permute-done | bytes 131104 | tf_op jit(solution)/shard_map/ppermute | solution.py:310
  72.4 2.4 %collective-permute-done.16.grad_in_ref = bf16[4,32,512]{2,1,0:T(8,128)(2,1)S(1)} collective-permute-done((bf16[4,32,512]{2,1,0:T(8,128)(2,1)S(1)}, bf16[4,32,512]{2,1,0:T(8,128)(2,1)S(1)}, u32[]{:S(2)}, u32[]{:S(2)}) %collective-permute-start.16) | collective-permute-done | bytes 131104 | tf_op jit(solution)/shard_map/ppermute | solution.py:310
  75.8 1.9 %collective-permute-start.20 = (bf16[2,32,512]{2,1,0:T(8,128)(2,1)S(1)}, bf16[2,32,512]{2,1,0:T(8,128)(2,1)S(1)}, u32[]{:S(2)}, u32[]{:S(2)}) collective-permute-start(bf16[2,32,512]{2,1,0:T(8,128)(2,1)S(1)} %get-tuple-element.72), channel_id=1, source_target_pairs={{0,8},{1,9},{2,10},{3,11},{4,12},{5,13},{6,14},{7,15},{8,0},{9,1},... | collective-permute-start | bytes 196616 | tf_op jit(solution)/shard_map/ppermute | solution.py:307
  79.0 2.8 %collective-permute-done.19.refs_1_ = bf16[2,32,512]{2,1,0:T(8,128)(2,1)S(1)} collective-permute-done((bf16[2,32,512]{2,1,0:T(8,128)(2,1)S(1)}, bf16[2,32,512]{2,1,0:T(8,128)(2,1)S(1)}, u32[]{:S(2)}, u32[]{:S(2)}) %collective-permute-start.19) | collective-permute-done | bytes 65568 | tf_op jit(solution)/shard_map/ppermute | solution.py:307
  81.8 1.6 %collective-permute-done.20.refs_2_ = bf16[2,32,512]{2,1,0:T(8,128)(2,1)S(1)} collective-permute-done((bf16[2,32,512]{2,1,0:T(8,128)(2,1)S(1)}, bf16[2,32,512]{2,1,0:T(8,128)(2,1)S(1)}, u32[]{:S(2)}, u32[]{:S(2)}) %collective-permute-start.20) | collective-permute-done | bytes 65568 | tf_op jit(solution)/shard_map/ppermute | solution.py:307
  (63 shorter events, 14.4 us)
Async XLA Ops:
  3.2 7.2 %collective-permute-start = (bf16[32,768]{1,0:T(8,128)(2,1)S(1)}, bf16[32,768]{1,0:T(8,128)(2,1)S(1)}, u32[]{:S(2)}, u32[]{:S(2)}) collective-permute-start(bf16[32,768]{1,0:T(8,128)(2,1)S(1)} %get-tuple-element.42), channel_id=1, source_target_pairs={{0,4},{1,5},{2,6},{3,7},{4,8},{5,9},{6,10},{7,11},{8,12},{9,13},{1... | collective-permute-start | bytes 147464 | tf_op jit(solution)/shard_map/ppermute | solution.py:307
  6.2 6.2 %collective-permute-start.1 = (bf16[32,768]{1,0:T(8,128)(2,1)S(1)}, bf16[32,768]{1,0:T(8,128)(2,1)S(1)}, u32[]{:S(2)}, u32[]{:S(2)}) collective-permute-start(bf16[32,768]{1,0:T(8,128)(2,1)S(1)} %get-tuple-element.43), channel_id=1, source_target_pairs={{0,8},{1,9},{2,10},{3,11},{4,12},{5,13},{6,14},{7,15},{8,0},{9,1},... | collective-permute-start | bytes 147464 | tf_op jit(solution)/shard_map/ppermute | solution.py:307
  8.8 4.1 %collective-permute-start.2 = (bf16[32,768]{1,0:T(8,128)(2,1)S(1)}, bf16[32,768]{1,0:T(8,128)(2,1)S(1)}, u32[]{:S(2)}, u32[]{:S(2)}) collective-permute-start(bf16[32,768]{1,0:T(8,128)(2,1)S(1)} %get-tuple-element.44), channel_id=1, source_target_pairs={{0,12},{1,13},{2,14},{3,15},{4,0},{5,1},{6,2},{7,3},{8,4},{9,5},{1... | collective-permute-start | bytes 147464 | tf_op jit(solution)/shard_map/ppermute | solution.py:307
  13.0 1.9 %collective-permute-start.3 = (bf16[4,16,128]{2,1,0:T(8,128)(2,1)S(1)}, bf16[4,16,128]{2,1,0:T(8,128)(2,1)S(1)}, u32[]{:S(2)}, u32[]{:S(2)}) collective-permute-start(bf16[4,16,128]{2,1,0:T(8,128)(2,1)S(1)} %get-tuple-element.46), channel_id=1, source_target_pairs={{0,1},{1,0},{2,3},{3,2},{4,5},{5,4},{6,7},{7,6},{8,9},{9,8},{10,11... | collective-permute-start | bytes 49160 | tf_op jit(solution)/shard_map/ppermute | solution.py:310
  13.1 3.8 %collective-permute-start.4 = (bf16[4,16,128]{2,1,0:T(8,128)(2,1)S(1)}, bf16[4,16,128]{2,1,0:T(8,128)(2,1)S(1)}, u32[]{:S(2)}, u32[]{:S(2)}) collective-permute-start(bf16[4,16,128]{2,1,0:T(8,128)(2,1)S(1)} %get-tuple-element.47), channel_id=1, source_target_pairs={{0,2},{1,3},{2,0},{3,1},{4,6},{5,7},{6,4},{7,5},{8,10},{9,11},{10,... | collective-permute-start | bytes 49160 | tf_op jit(solution)/shard_map/ppermute | solution.py:310
  14.8 3.2 %collective-permute-start.5 = (bf16[4,16,128]{2,1,0:T(8,128)(2,1)S(1)}, bf16[4,16,128]{2,1,0:T(8,128)(2,1)S(1)}, u32[]{:S(2)}, u32[]{:S(2)}) collective-permute-start(bf16[4,16,128]{2,1,0:T(8,128)(2,1)S(1)} %get-tuple-element.48), channel_id=1, source_target_pairs={{0,3},{1,2},{2,1},{3,0},{4,7},{5,6},{6,5},{7,4},{8,11},{9,10},{10,... | collective-permute-start | bytes 49160 | tf_op jit(solution)/shard_map/ppermute | solution.py:310
  18.7 6.0 %collective-permute-start.6 = (bf16[32,512]{1,0:T(8,128)(2,1)S(1)}, bf16[32,512]{1,0:T(8,128)(2,1)S(1)}, u32[]{:S(2)}, u32[]{:S(2)}) collective-permute-start(bf16[32,512]{1,0:T(8,128)(2,1)S(1)} %get-tuple-element.51.share_ref), channel_id=1, source_target_pairs={{0,4},{1,5},{2,6},{3,7},{4,8},{5,9},{6,10},{7,11},{8,12},{9,13},{1... | collective-permute-start | bytes 98312 | tf_op jit(solution)/shard_map/ppermute | solution.py:307
  19.4 5.8 %collective-permute-start.7 = (bf16[32,512]{1,0:T(8,128)(2,1)S(1)}, bf16[32,512]{1,0:T(8,128)(2,1)S(1)}, u32[]{:S(2)}, u32[]{:S(2)}) collective-permute-start(bf16[32,512]{1,0:T(8,128)(2,1)S(1)} %get-tuple-element.51.share_ref), channel_id=1, source_target_pairs={{0,8},{1,9},{2,10},{3,11},{4,12},{5,13},{6,14},{7,15},{8,0},{9,1},... | collective-permute-start | bytes 98312 | tf_op jit(solution)/shard_map/ppermute | solution.py:307
  22.2 3.9 %collective-permute-start.8 = (bf16[32,512]{1,0:T(8,128)(2,1)S(1)}, bf16[32,512]{1,0:T(8,128)(2,1)S(1)}, u32[]{:S(2)}, u32[]{:S(2)}) collective-permute-start(bf16[32,512]{1,0:T(8,128)(2,1)S(1)} %get-tuple-element.51.share_ref), channel_id=1, source_target_pairs={{0,12},{1,13},{2,14},{3,15},{4,0},{5,1},{6,2},{7,3},{8,4},{9,5},{1... | collective-permute-start | bytes 98312 | tf_op jit(solution)/shard_map/ppermute | solution.py:307
  22.5 5.0 %collective-permute-start.13 = (bf16[4,32,512]{2,1,0:T(8,128)(2,1)S(1)}, bf16[4,32,512]{2,1,0:T(8,128)(2,1)S(1)}, u32[]{:S(2)}, u32[]{:S(2)}) collective-permute-start(bf16[4,32,512]{2,1,0:T(8,128)(2,1)S(1)} %get-tuple-element.56.a_ref), channel_id=1, source_target_pairs={{0,2},{1,3},{2,0},{3,1},{4,6},{5,7},{6,4},{7,5},{8,10},{9,11},{10,... | collective-permute-start | bytes 393224 | tf_op jit(solution)/shard_map/ppermute | solution.py:310
  26.2 5.0 %collective-permute-start.10 = (bf16[4,32,512]{2,1,0:T(8,128)(2,1)S(1)}, bf16[4,32,512]{2,1,0:T(8,128)(2,1)S(1)}, u32[]{:S(2)}, u32[]{:S(2)}) collective-permute-start(bf16[4,32,512]{2,1,0:T(8,128)(2,1)S(1)} %pad_maximum_fusion.a_ref), channel_id=1, source_target_pairs={{0,2},{1,3},{2,0},{3,1},{4,6},{5,7},{6,4},{7,5},{8,10},{9,11},{10,... | collective-permute-start | bytes 393224 | tf_op jit(solution)/shard_map/ppermute | solution.py:310
  26.9 20.6 %collective-permute-start.12 = (bf16[4,32,512]{2,1,0:T(8,128)(2,1)S(1)}, bf16[4,32,512]{2,1,0:T(8,128)(2,1)S(1)}, u32[]{:S(2)}, u32[]{:S(2)}) collective-permute-start(bf16[4,32,512]{2,1,0:T(8,128)(2,1)S(1)} %get-tuple-element.56.a_ref), channel_id=1, source_target_pairs={{0,1},{1,0},{2,3},{3,2},{4,5},{5,4},{6,7},{7,6},{8,9},{9,8},{10,11... | collective-permute-start | bytes 393224 | tf_op jit(solution)/shard_map/ppermute | solution.py:310
  27.5 20.1 %collective-permute-start.14 = (bf16[4,32,512]{2,1,0:T(8,128)(2,1)S(1)}, bf16[4,32,512]{2,1,0:T(8,128)(2,1)S(1)}, u32[]{:S(2)}, u32[]{:S(2)}) collective-permute-start(bf16[4,32,512]{2,1,0:T(8,128)(2,1)S(1)} %collective-permute-done.13.b_ref), channel_id=1, source_target_pairs={{0,1},{1,0},{2,3},{3,2},{4,5},{5,4},{6,7},{7,6},{8,9},{9,8},{10,11... | collective-permute-start | bytes 393224 | tf_op jit(solution)/shard_map/ppermute | solution.py:310
  27.5 23.3 %collective-permute-start.9 = (bf16[4,32,512]{2,1,0:T(8,128)(2,1)S(1)}, bf16[4,32,512]{2,1,0:T(8,128)(2,1)S(1)}, u32[]{:S(2)}, u32[]{:S(2)}) collective-permute-start(bf16[4,32,512]{2,1,0:T(8,128)(2,1)S(1)} %pad_maximum_fusion.a_ref), channel_id=1, source_target_pairs={{0,1},{1,0},{2,3},{3,2},{4,5},{5,4},{6,7},{7,6},{8,9},{9,8},{10,11... | collective-permute-start | bytes 393224 | tf_op jit(solution)/shard_map/ppermute | solution.py:310
  31.2 19.6 %collective-permute-start.11 = (bf16[4,32,512]{2,1,0:T(8,128)(2,1)S(1)}, bf16[4,32,512]{2,1,0:T(8,128)(2,1)S(1)}, u32[]{:S(2)}, u32[]{:S(2)}) collective-permute-start(bf16[4,32,512]{2,1,0:T(8,128)(2,1)S(1)} %collective-permute-done.10.b_ref), channel_id=1, source_target_pairs={{0,1},{1,0},{2,3},{3,2},{4,5},{5,4},{6,7},{7,6},{8,9},{9,8},{10,11... | collective-permute-start | bytes 393224 | tf_op jit(solution)/shard_map/ppermute | solution.py:310
  36.4 11.2 %slice-start.2 = ((s8[14680064]{0:T(1024)(128)(4,1)}), s8[4194304]{0:T(1024)(128)(4,1)S(1)}, s32[]{:S(2)}) async-start(s8[14680064]{0:T(1024)(128)(4,1)} %bitcast.13), calls=%async_computation.2 | async-start | bytes 8388608
  60.9 2.8 %collective-permute-start.15 = (bf16[8,32,512]{2,1,0:T(8,128)(2,1)S(1)}, bf16[8,32,512]{2,1,0:T(8,128)(2,1)S(1)}, u32[]{:S(2)}, u32[]{:S(2)}) collective-permute-start(bf16[8,32,512]{2,1,0:T(8,128)(2,1)S(1)} %get-tuple-element.64.after_ref), channel_id=1, source_target_pairs={{0,1},{1,0},{2,3},{3,2},{4,5},{5,4},{6,7},{7,6},{8,9},{9,8},{10,11... | collective-permute-start | bytes 786440 | tf_op jit(solution)/shard_map/ppermute | solution.py:310
  61.5 21.9 %copy-start.2 = (s32[2,1,64]{2,1,0:T(1,128)S(1)}, s32[2,1,64]{2,1,0:T(1,128)}, u32[]{:S(2)}) copy-start(s32[2,1,64]{2,1,0:T(1,128)} %param.19) | copy-start | bytes 1540
  63.6 2.3 %collective-permute-start.17 = (bf16[8,32,512]{2,1,0:T(8,128)(2,1)S(1)}, bf16[8,32,512]{2,1,0:T(8,128)(2,1)S(1)}, u32[]{:S(2)}, u32[]{:S(2)}) collective-permute-start(bf16[8,32,512]{2,1,0:T(8,128)(2,1)S(1)} %shard_map.139), channel_id=1, source_target_pairs={{0,1},{1,0},{2,3},{3,2},{4,5},{5,4},{6,7},{7,6},{8,9},{9,8},{10,11... | collective-permute-start | bytes 786440 | tf_op jit(solution)/shard_map/ppermute | solution.py:310
  66.1 6.4 %collective-permute-start.18 = (bf16[4,32,512]{2,1,0:T(8,128)(2,1)S(1)}, bf16[4,32,512]{2,1,0:T(8,128)(2,1)S(1)}, u32[]{:S(2)}, u32[]{:S(2)}) collective-permute-start(bf16[4,32,512]{2,1,0:T(8,128)(2,1)S(1)} %get-tuple-element.69), channel_id=1, source_target_pairs={{0,2},{1,3},{2,0},{3,1},{4,6},{5,7},{6,4},{7,5},{8,10},{9,11},{10,... | collective-permute-start | bytes 393224 | tf_op jit(solution)/shard_map/ppermute | solution.py:310
  66.8 8.0 %collective-permute-start.16 = (bf16[4,32,512]{2,1,0:T(8,128)(2,1)S(1)}, bf16[4,32,512]{2,1,0:T(8,128)(2,1)S(1)}, u32[]{:S(2)}, u32[]{:S(2)}) collective-permute-start(bf16[4,32,512]{2,1,0:T(8,128)(2,1)S(1)} %get-tuple-element.66.after_ref), channel_id=1, source_target_pairs={{0,2},{1,3},{2,0},{3,1},{4,6},{5,7},{6,4},{7,5},{8,10},{9,11},{10,... | collective-permute-start | bytes 393224 | tf_op jit(solution)/shard_map/ppermute | solution.py:310
  74.9 6.9 %collective-permute-start.19 = (bf16[2,32,512]{2,1,0:T(8,128)(2,1)S(1)}, bf16[2,32,512]{2,1,0:T(8,128)(2,1)S(1)}, u32[]{:S(2)}, u32[]{:S(2)}) collective-permute-start(bf16[2,32,512]{2,1,0:T(8,128)(2,1)S(1)} %get-tuple-element.71), channel_id=1, source_target_pairs={{0,4},{1,5},{2,6},{3,7},{4,8},{5,9},{6,10},{7,11},{8,12},{9,13},{1... | collective-permute-start | bytes 196616 | tf_op jit(solution)/shard_map/ppermute | solution.py:307
  75.8 7.6 %collective-permute-start.20 = (bf16[2,32,512]{2,1,0:T(8,128)(2,1)S(1)}, bf16[2,32,512]{2,1,0:T(8,128)(2,1)S(1)}, u32[]{:S(2)}, u32[]{:S(2)}) collective-permute-start(bf16[2,32,512]{2,1,0:T(8,128)(2,1)S(1)} %get-tuple-element.72), channel_id=1, source_target_pairs={{0,8},{1,9},{2,10},{3,11},{4,12},{5,13},{6,14},{7,15},{8,0},{9,1},... | collective-permute-start | bytes 196616 | tf_op jit(solution)/shard_map/ppermute | solution.py:307
  77.7 5.8 %collective-permute-start.21 = (bf16[2,32,512]{2,1,0:T(8,128)(2,1)S(1)}, bf16[2,32,512]{2,1,0:T(8,128)(2,1)S(1)}, u32[]{:S(2)}, u32[]{:S(2)}) collective-permute-start(bf16[2,32,512]{2,1,0:T(8,128)(2,1)S(1)} %get-tuple-element.73), channel_id=1, source_target_pairs={{0,12},{1,13},{2,14},{3,15},{4,0},{5,1},{6,2},{7,3},{8,4},{9,5},{1... | collective-permute-start | bytes 196616 | tf_op jit(solution)/shard_map/ppermute | solution.py:307
  (9 other events, 53.5 us)

commit v4 on v3

--- a/solution.py
+++ b/solution.py
@@ -41,7 +41,7 @@
 
 def owner_of(me, n, part, back):
     along, row, core = place(me)
-    at = lax.rem(along - back + n // 4, n // 4)
+    at = jnp.bitwise_xor(along, back)
     return 4 * at + 2 * flip(row, part % 2) + flip(core, part // 2)
 
 
@@ -81,7 +81,7 @@
     along, _, _ = place(me_ref[0])
     cot = cot_ref[...]
     for r, packed_ref in enumerate(packed_refs):
-        to = lax.rem(along + r, n // 4)
+        to = jnp.bitwise_xor(along, r)
         packed_ref[:, :share] = cot
         for q in range(4):
             packed_ref[block_spot(q, tokens, rows, share)] = rows_ref[4 * to + q].astype(bf16)
@@ -142,89 +142,107 @@
         own_ref[pl.ds(p * n + owner, 1), :] = piece_ref[pl.ds(p * n + me, 1), :]
 
 
-def grad_active_kernel(first, me_ref, a_ref, b_ref, weight_ref, acc_in_ref, own_in_ref, acc_ref, own_ref, piece_ref):
-    quarter, _, width = a_ref.shape
+def dot_by_halves(rows, tokens):
+    middle = tokens.shape[1] // 2 // LANES * LANES
+    if middle == 0:
+        return dot_nt(rows, tokens)
+    return dot_nt(rows[:, :middle], tokens[:, :middle]) + dot_nt(rows[:, middle:], tokens[:, middle:])
+
+
+def grad_active_kernel(part, me_ref, cot_ref, weight_ref, acc_ref, own_ref, held_ref, piece_ref, sems):
+    quarter, _, width = cot_ref.shape
     me = me_ref[0]
-    acc_ref[...] = acc_in_ref[...]
-    own_ref[...] = own_in_ref[...]
-    for part, cot_ref in enumerate((a_ref, b_ref)):
-
-        @pl.loop(0, quarter)
-        def _(k):
-            owner = owner_of(me, 4 * quarter, first + part, k)
-            piece = cot_ref[k]
-            columns = pl.ds(pl.multiple_of(owner * width, width), width)
-            acc_ref[...] += dot_nt(weight_ref[:, columns], piece)
-            piece_ref[...] = piece.astype(f32)
-            own_rows(piece_ref, own_ref, me, owner)
+    owners = [owner_of(me, 4 * quarter, part, k) for k in range(quarter)]
+    copies = []
+    for k, owner in enumerate(owners):
+        columns = pl.ds(pl.multiple_of(owner * width, width), width)
+        copies.append(pltpu.make_async_copy(weight_ref.at[:, columns], held_ref.at[k], sems.at[k]))
+        copies[-1].start()
+    own_ref[...] = jnp.zeros_like(own_ref)
+    for k, owner in enumerate(owners):
+        piece_ref[...] = cot_ref[k].astype(f32)
+        own_rows(piece_ref, own_ref, me, owner)
+    for k, copy in enumerate(copies):
+        copy.wait()
+        terms = dot_by_halves(held_ref[k], cot_ref[k])
+        acc_ref[...] = terms if k == 0 else acc_ref[...] + terms
+
+
+def up_part(part, me, rest_ref, gain_ref, held_ref, waits, acc_ref, square_ref, own_ref, piece_ref):
+    quarter, _, width = rest_ref.shape
+    own_ref[...] = jnp.zeros_like(own_ref)
+    scaled = []
+    for k in range(quarter):
+        owner = owner_of(me, 4 * quarter, part, k)
+        piece = rest_ref[k].astype(f32)
+        piece_ref[...] = piece
+        own_rows(piece_ref, own_ref, me, owner)
+        squares = piece * piece
+        total = sum(squares[:, c * LANES : (c + 1) * LANES] for c in range(width // LANES))
+        square_ref[...] = total if k == 0 else square_ref[...] + total
+        scaled.append((piece * gain_ref[pl.ds(owner, 1), :]).astype(bf16))
+    for k in range(quarter):
+        waits[k].wait()
+        terms = jnp.dot(scaled[k], held_ref[k], preferred_element_type=f32)
+        acc_ref[...] = terms if k == 0 else acc_ref[...] + terms
+
+
+def share_copies(part, me, weight_ref, held_ref, sems, base=0):
+    quarter, width, _ = held_ref.shape
+    quarter = min(quarter, weight_ref.shape[0] // width // 4)
+    n = 4 * quarter
+    copies = []
+    for k in range(quarter):
+        rows = pl.ds(pl.multiple_of(owner_of(me, n, part, k) * width, width), width)
+        copies.append(
+            pltpu.make_async_copy(weight_ref.at[rows], held_ref.at[base + k], sems.at[base + k])
+        )
+        copies[-1].start()
+    return copies
 
 
 def up_kernel(
-    first, me_ref, a_ref, b_ref, gain_ref, weight_ref, acc_in_ref, square_in_ref, own_in_ref, *refs
+    part, me_ref, rest_ref, gain_ref, weight_ref,
+    acc_ref, square_ref, own_ref, held_ref, piece_ref, sems,
 ):
-    if first == 0:
-        acc_ref, square_ref, own_ref, piece_ref = refs
-    else:
-        ga_ref, active_ref, gh_ref, own_ref, piece_ref, acc_ref, square_ref = refs
-    quarter, _, width = a_ref.shape
+    me = me_ref[0]
+    copies = share_copies(part, me, weight_ref, held_ref, sems)
+    up_part(part, me, rest_ref, gain_ref, held_ref, copies, acc_ref, square_ref, own_ref, piece_ref)
+
+
+def middle_kernel(me_ref, rest_ref, gain_ref, weight_ref, *refs):
+    ins, refs = refs[:10], refs[10:]
+    active_ref, own_ref, send_ref, keep_ref, acc_ref, square_ref, piece_ref, held_ref, rows_ref, sems = refs
+    quarter, tokens, width = rest_ref.shape
+    half, n, chunks = 2 * quarter, 4 * quarter, width // LANES
     width_all = weight_ref.shape[0]
     me = me_ref[0]
-    acc_ref[...] = acc_in_ref[...]
-    square_ref[...] = square_in_ref[...]
-    own_ref[...] = own_in_ref[...]
-    for part, rest_ref in enumerate((a_ref, b_ref)):
-
-        @pl.loop(0, quarter)
-        def _(k):
-            owner = owner_of(me, 4 * quarter, first + part, k)
-            piece = rest_ref[k].astype(f32)
-            piece_ref[...] = piece
-            own_rows(piece_ref, own_ref, me, owner)
-            squares = piece * piece
-            total = square_ref[...]
-            for c in range(width // LANES):
-                total = total + squares[:, c * LANES : (c + 1) * LANES]
-            square_ref[...] = total
-            scaled = (piece * gain_ref[pl.ds(owner, 1), :]).astype(bf16)
-            rows = pl.ds(pl.multiple_of(owner * width, width), width)
-            acc_ref[...] += jnp.dot(scaled, weight_ref[rows, :], preferred_element_type=f32)
-
-    if first == 0:
-        return
-    total = jnp.sum(square_ref[...], axis=1, keepdims=True)
-    hidden = lax.rsqrt(total / width_all + eps) * acc_ref[...]
+    parts = (3, 0, 1, 2)
+    copies = []
+    for i, part in enumerate(parts):
+        copies += share_copies(part, me, weight_ref, held_ref, sems, i * quarter)
+    up_part(3, me, rest_ref, gain_ref, held_ref, copies, acc_ref, square_ref, own_ref, piece_ref)
+    product = acc_ref[...] + (ins[0][...] + ins[1][...] + ins[2][...])
+    squares = square_ref[...] + (ins[3][...] + ins[4][...] + ins[5][...])
+    total = jnp.sum(squares, axis=1, keepdims=True)
+    hidden = lax.rsqrt(total / width_all + eps) * product
     sigma = jax.nn.sigmoid(hidden)
     active_ref[...] = (hidden * sigma).astype(bf16)
-    grad_active = ga_ref[...].T
-    gh_ref[...] = (grad_active * sigma * (1.0 + hidden * (1.0 - sigma))).astype(bf16)
-
-
-def down_kernel(other, me_ref, active_ref, weight_ref, after_ref, out_ref):
-    half, _, width = out_ref.shape
-    core = lax.rem(me_ref[0] + other, 2)
-
-    @pl.loop(0, half)
-    def _(k):
-        columns = pl.ds(pl.multiple_of((2 * k + core) * width, width), width)
-        terms = jnp.dot(active_ref[...], weight_ref[:, columns], preferred_element_type=f32)
-        out_ref[k] = terms.astype(bf16)
-
-
-def grad_norm_kernel(me_ref, gh_ref, weight_ref, send_ref, keep_ref, rows_ref):
-    half, tokens, width = send_ref.shape
-    n, chunks = 2 * half, width // LANES
-
-    @pl.loop(0, n)
-    def _(share):
-        block = weight_ref[pl.ds(pl.multiple_of(share * width, width), width), :]
-        terms = dot_nt(gh_ref[...], block)
-        for p in range(2):
-            for c in range(chunks):
-                rows_ref[c, pl.ds(p * n + share, n, stride=tokens), :] = terms[
-                    p * n : (p + 1) * n, c * LANES : (c + 1) * LANES
-                ]
-
-    core = lax.rem(me_ref[0], 2)
+    grad_active = (ins[6][...] + ins[7][...] + (ins[8][...] + ins[9][...])).T
+    gh = (grad_active * sigma * (1.0 + hidden * (1.0 - sigma))).astype(bf16)
+    for i, part in enumerate(parts):
+        for k in range(quarter):
+            at = i * quarter + k
+            if i > 0:
+                copies[at].wait()
+            share = owner_of(me, n, part, k)
+            terms = dot_by_halves(held_ref[at], gh).T
+            for p in range(2):
+                for c in range(chunks):
+                    rows_ref[c, pl.ds(p * n + share, n, stride=tokens), :] = terms[
+                        p * n : (p + 1) * n, c * LANES : (c + 1) * LANES
+                    ]
+    core = lax.rem(me, 2)
     for k in range(half):
         keep_at = pl.multiple_of((2 * k + core) * tokens, tokens)
         send_at = pl.multiple_of((2 * k + 1 - core) * tokens, tokens)
@@ -234,29 +252,45 @@
             send_ref[k, :, cols] = rows_ref[c, pl.ds(send_at, tokens), :].astype(bf16)
 
 
-def pair_kernel(me_ref, kept_ref, arrived_ref, send_ref, keep_ref):
+def down_kernel(other, me_ref, active_ref, weight_ref, after_ref, out_ref):
+    half, _, width = out_ref.shape
+    core = lax.rem(me_ref[0] + other, 2)
+
+    def share(k):
+        columns = pl.ds(pl.multiple_of((2 * k + core) * width, width), width)
+        terms = jnp.dot(active_ref[...], weight_ref[:, columns], preferred_element_type=f32)
+        out_ref[k] = terms.astype(bf16)
+
+    pl.loop(0, half, unroll=4)(share)
+
+
+def pair_kernel(me_ref, kept_ref, arrived_ref, *refs):
+    ins, (send_ref, keep_ref), shares = (refs[:2], refs[2:4], refs[4:]) if len(refs) > 2 else ((), refs, ())
     quarter = send_ref.shape[0]
-    row = lax.rem(me_ref[0] // 2, 2)
+    _, row, _ = place(me_ref[0])
     for k in range(quarter):
         for out_ref, at in ((send_ref, 2 * k + 1 - row), (keep_ref, 2 * k + row)):
             out_ref[k] = (kept_ref[at].astype(f32) + arrived_ref[at].astype(f32)).astype(bf16)
-
-
-def line_kernel(me_ref, grad_ref, grad_in_ref, out_ref, out_in_ref, *refs):
-    quarter = len(refs)
+    if shares:
+        line_kernel(me_ref, *ins, *shares)
+
+
+def line_kernel(me_ref, kept_ref, arrived_ref, *refs):
+    along, _, _ = place(me_ref[0])
     for r, ref in enumerate(refs):
-        at = lax.rem(me_ref[0] // 4 + r, quarter)
-        ref[0] = (grad_ref[at].astype(f32) + grad_in_ref[at].astype(f32)).astype(bf16)
-        ref[1] = (out_ref[at].astype(f32) + out_in_ref[at].astype(f32)).astype(bf16)
-
-
-def final_kernel(width_all, share_ref, own_ref, cot_ref, gain_ref, expo_ref, *refs):
+        at = jnp.bitwise_xor(along, r)
+        ref[...] = (kept_ref[at].astype(f32) + arrived_ref[at].astype(f32)).astype(bf16)
+
+
+def added(refs):
+    return functools.reduce(lambda a, b: a + b, [ref[...].astype(f32) for ref in refs])
+
+
+def final_kernel(width_all, share_ref, gain_ref, expo_ref, *refs):
     *refs, layer_ref, grad_ref = refs
-    grad = refs[0][0].astype(f32)
-    layer = refs[0][1].astype(f32)
-    for ref in refs[1:]:
-        grad = grad + ref[0].astype(f32)
-        layer = layer + ref[1].astype(f32)
+    quarter = (len(refs) - 8) // 2
+    own_all, cot_all = added(refs[:4]), added(refs[4:8])
+    grad, layer = added(refs[8 : 8 + quarter]), added(refs[8 + quarter :])
     layer_ref[...] = (share_ref[...].astype(f32) + layer).astype(bf16)
     n, width = gain_ref.shape
     down, up = powers(expo_ref[...], -1), powers(expo_ref[...], 1)
@@ -267,12 +301,12 @@
     at_lane = lax.broadcasted_iota(jnp.int32, (n, blocks), 1)
     for p in range(2):
         rows = slice(p * n, (p + 1) * n)
-        own, norm = own_ref[rows, :], grad[rows, :]
+        own, norm = own_all[rows, :], grad[rows, :]
         inv_rms = lax.rsqrt(jnp.sum(own * own, keepdims=True) / width_all + eps)
         scaled_in = (own * gain).astype(bf16).astype(f32)
         curvature = inv_rms * jnp.sum(scaled_in * norm, keepdims=True)
         correction = curvature * inv_rms * inv_rms / width_all
-        value = cot_ref[rows, :].astype(f32) + inv_rms * gain * norm - correction * own
+        value = cot_all[rows, :] + inv_rms * gain * norm - correction * own
         for c in range(per_dev):
             at = at_lane == at_row * per_dev + c
             shrink = jnp.sum(jnp.where(at, down[p : p + 1], 0.0), axis=1, keepdims=True)
@@ -304,7 +338,7 @@
     me_in = me.reshape(1)
 
     def shift(x, r):
-        return lax.ppermute(x, "dp", [(d, (d + 4 * r) % n) for d in range(n)]) if r else x
+        return lax.ppermute(x, "dp", [(d, d ^ (4 * r)) for d in range(n)]) if r else x
 
     def swap(x, bits):
         return lax.ppermute(x, "dp", [(d, d ^ bits) for d in range(n)])
@@ -313,17 +347,17 @@
     share_shape, hidden_shape = (tokens, width), (tokens, hidden_dev)
     line_shape = (quarter, tokens, width)
 
-    def call(kernel, outs, ins, args, scratch=(), cost=0):
+    def call(kernel, outs, ins, args, scratch=(), cost=0, grant=8):
         return pl.pallas_call(
             kernel,
             out_shape=outs,
             in_specs=ins,
             out_specs=jax.tree.map(lambda _: VMEM, outs),
             scratch_shapes=list(scratch),
-            compiler_params=params(8),
+            compiler_params=params(grant),
             cost_estimate=pl.CostEstimate(
-                flops=cost * tokens * width_all * hidden_dev,
-                bytes_accessed=cost * width_all * hidden_dev,
+                flops=int(cost * tokens * width_all * hidden_dev),
+                bytes_accessed=int(cost * width_all * hidden_dev),
                 transcendentals=0,
             ),
         )(*args)
@@ -368,6 +402,45 @@
     cot_row = swap(cot_line, 2)
     cots = [cot_line, cot_row, swap(cot_line, 1), swap(cot_row, 1)]
 
+    ANY = pl.BlockSpec(memory_space=pl.ANY)
+    sems = lambda count: pltpu.SemaphoreType.DMA((count,))
+    share_f32 = struct(share_shape, f32)
+    sums = (struct(hidden_shape, f32), struct((tokens, LANES), f32))
+
+    def grad_active_part(part):
+        return call(
+            functools.partial(grad_active_kernel, part),
+            (struct((hidden_dev, tokens), f32), share_f32),
+            [SMEM, VMEM, ANY],
+            [me_in, cots[part], hbm(down_weight)],
+            [
+                pltpu.VMEM((quarter, hidden_dev, width), bf16),
+                pltpu.VMEM(share_shape, f32),
+                sems(quarter),
+            ],
+            cost=0.5,
+            grant=12,
+        )
+
+    def up_product_part(part):
+        return call(
+            functools.partial(up_kernel, part),
+            sums + (share_f32,),
+            [SMEM, VMEM, VMEM, ANY],
+            [me_in, rests[part], gain, hbm(up_weight)],
+            [
+                pltpu.VMEM((quarter, width, hidden_dev), bf16),
+                pltpu.VMEM(share_shape, f32),
+                sems(quarter),
+            ],
+            cost=0.5,
+            grant=12,
+        )
+
+    together = lax.optimization_barrier
+    grads = [grad_active_part(0)]
+    blocks, grads[0] = together((blocks, grads[0]))
+
     new_receiver_base, share = call(
         rebuild_kernel,
         (struct(receiver_base.shape, f32), struct(share_shape, bf16)),
@@ -375,82 +448,80 @@
         [me_in, *blocks, received],
         [pltpu.VMEM((n * rows, LANES), f32), pltpu.VMEM((2 * width // LANES, 2 * n, LANES), f32)],
     )
-    rest_line = jnp.stack([shift(share, r) for r in range(quarter)])
+    lines = [shift(share, r) for r in range(quarter)]
+    grads.append(grad_active_part(1))
+    lines, grads[1] = together((lines, grads[1]))
+    rest_line = jnp.stack(lines)
     rest_row = swap(rest_line, 2)
-    rests = [rest_line, rest_row, swap(rest_line, 1), swap(rest_row, 1)]
-
-    ga, own_cot = jnp.zeros((hidden_dev, tokens), f32), jnp.zeros(share_shape, f32)
-    acc, square, own = jnp.zeros(hidden_shape, f32), jnp.zeros((tokens, LANES), f32), own_cot
-    for first in (0, 2):
-        ga, own_cot = call(
-            functools.partial(grad_active_kernel, first),
-            (struct((hidden_dev, tokens), f32), struct(share_shape, f32)),
-            [SMEM] + [VMEM] * 5,
-            [me_in, cots[first], cots[first + 1], down_weight, ga, own_cot],
-            [pltpu.VMEM(share_shape, f32)],
-            cost=1,
-        )
-    sums = (struct(hidden_shape, f32), struct((tokens, LANES), f32))
-    acc, square, own = call(
-        functools.partial(up_kernel, 0),
-        sums + (struct(share_shape, f32),),
-        [SMEM] + [VMEM] * 7,
-        [me_in, rests[0], rests[1], gain, up_weight, acc, square, own],
-        [pltpu.VMEM(share_shape, f32)],
-        cost=1,
-    )
-    active, grad_hidden, own = call(
-        functools.partial(up_kernel, 2),
-        (struct(hidden_shape, bf16), struct(hidden_shape, bf16), struct(share_shape, f32)),
-        [SMEM] + [VMEM] * 8,
-        [me_in, rests[2], rests[3], gain, up_weight, acc, square, own, ga],
-        [pltpu.VMEM(share_shape, f32)] + [pltpu.VMEM(x.shape, x.dtype) for x in sums],
-        cost=1,
-    )
+    rests = [rest_line, rest_row, swap(rest_line, 1)]
+    grads.append(grad_active_part(2))
+    products = [up_product_part(0)]
+    rest_row, grads[2], products[0] = together((rest_row, grads[2], products[0]))
+    rests[1] = rest_row
+    rests.append(swap(rest_row, 1))
+    grads.append(grad_active_part(3))
+    products += [up_product_part(1), up_product_part(2)]
+    gas, own_cots = zip(*grads)
+    accs, squares, owns = map(list, zip(*products))
 
     half_out = struct((half, tokens, width), bf16)
-    grad_send, grad_keep = call(
-        grad_norm_kernel,
-        (half_out, half_out),
-        [SMEM] + [VMEM] * 2,
-        [me_in, grad_hidden, up_weight],
-        [pltpu.VMEM((width // LANES, n * tokens, LANES), f32)],
-        cost=2,
-    )
+    active, own, grad_send, grad_keep = call(
+        middle_kernel,
+        (struct(hidden_shape, bf16), share_f32, half_out, half_out),
+        [SMEM, VMEM, VMEM, ANY] + [VMEM] * 10,
+        [me_in, rests[3], gain, hbm(up_weight), *accs, *squares, *gas],
+        [pltpu.VMEM(x.shape, x.dtype) for x in sums]
+        + [
+            pltpu.VMEM(share_shape, f32),
+            pltpu.VMEM((n, width, hidden_dev), bf16),
+            pltpu.VMEM((width // LANES, n * tokens, LANES), f32),
+            sems(n),
+        ],
+        cost=2.5,
+        grant=24,
+    )
+    owns.append(own)
 
     def down_terms(other, after):
         return call(
             functools.partial(down_kernel, other),
             half_out,
-            [SMEM] + [VMEM] * 2 + [pl.BlockSpec(memory_space=pl.ANY)],
+            [SMEM] + [VMEM] * 2 + [ANY],
             [me_in, active, down_weight, after],
             cost=1,
         )
 
-    def pair_sum(kept, arrived):
-        pair_out = struct(line_shape, bf16)
-        return call(
-            pair_kernel, (pair_out, pair_out), [SMEM] + [VMEM] * 2, [me_in, kept, arrived]
-        )
-
+    pair_out = (struct(line_shape, bf16),) * 2
+    line_out = (struct(share_shape, bf16),) * quarter
     grad_in = swap(grad_send, 1)
     out_in = swap(down_terms(1, grad_send), 1)
-    grad_send, grad_row = pair_sum(grad_keep, grad_in)
+    grad_send, grad_row = call(
+        pair_kernel, pair_out, [SMEM] + [VMEM] * 2, [me_in, grad_keep, grad_in]
+    )
     grad_row_in = swap(grad_send, 2)
-    out_send, out_row = pair_sum(down_terms(0, grad_send), out_in)
+    out_send, out_row, *grad_line = call(
+        pair_kernel,
+        pair_out + line_out,
+        [SMEM] + [VMEM] * 4,
+        [me_in, down_terms(0, grad_send), out_in, grad_row, grad_row_in],
+    )
     out_row_in = swap(out_send, 2)
-    shares = call(
-        line_kernel,
-        (struct((2, tokens, width), bf16),) * quarter,
-        [SMEM] + [VMEM] * 4,
-        [me_in, grad_row, grad_row_in, out_row, out_row_in],
-    )
-    moved = [shift(x, r) for r, x in enumerate(shares)]
+    grad_line = [shift(x, r) for r, x in enumerate(grad_line)]
+    out_line = call(line_kernel, line_out, [SMEM] + [VMEM] * 2, [me_in, out_row, out_row_in])
+    out_line = [shift(x, r) for r, x in enumerate(out_line)]
     layer_out, returned = call(
         functools.partial(final_kernel, width_all),
         (struct(share_shape, bf16), struct((2, width_all // LANES, LANES), f32)),
-        [VMEM] * (5 + quarter),
-        [share, own, own_cot, gain, backward_exponent.reshape(expo_shape), *moved],
+        [VMEM] * (11 + 2 * quarter),
+        [
+            share,
+            gain,
+            backward_exponent.reshape(expo_shape),
+            *owns,
+            *own_cots,
+            *grad_line,
+            *out_line,
+        ],
     )
     return (
         new_sender_base,

time: 84.4 us -> 79.2 us (0.938)
  Pallas kernels: 26.1 us -> 38.6 us
  waiting for transfers between devices: 23.6 us -> 11.5 us
  local copies, waits for them, and re-layouts: 11.4 us -> 0.03 us
  starting transfers between devices: 21.5 us -> 27.4 us
    pallas_call x13 -> x16, Pallas kernels: 24.2 us -> 36.6 us  [call(): pl.pallas_call(kernel, out_shape=outs, in_specs=ins, out_specs=jax.tree.m...]
    unnamed x22 -> x10, local copies, waits for them, and re-layouts: 11.4 us -> 0.03 us
    ppermute x13, waiting for transfers between devices: 13.5 us -> 2.71 us  [swap(): return lax.ppermute(x, 'dp', [(d, d ^ bits) for d in range(n)])]
    ppermute x9 -> x12, starting transfers between devices: 14.9 us -> 18.8 us  [shift(): return lax.ppermute(x, 'dp', [(d, d ^ 4 * r) for d in range(n)]) if r else x]
    ppermute x13, starting transfers between devices: 6.59 us -> 8.58 us  [swap(): return lax.ppermute(x, 'dp', [(d, d ^ bits) for d in range(n)])]
    ppermute x9 -> x12, waiting for transfers between devices: 10.2 us -> 8.79 us  [shift(): return lax.ppermute(x, 'dp', [(d, d ^ 4 * r) for d in range(n)]) if r else x]
  transfers between devices with their start and end apart: 22 -> 25, of which waited for: 14 -> 5; matrix products, arithmetic and copies ran while one was open for 0% -> 0% of each run, Pallas kernels for 15% -> 30%
where the time goes in v4:
time: 79.2 us; the launch traced here: 79.1 us
  Pallas kernels  38.6 us (49%)
  starting transfers between devices  27.4 us (35%)
  waiting for transfers between devices  11.5 us (15%)
  between operations  1.55 us (2%)
    pallas_call x16, Pallas kernels, call(): pl.pallas_call(kernel, out_shape=outs, in_specs=ins, out_specs=jax.tree.m...  36.6 us
    ppermute x12, starting transfers between devices, shift(): return lax.ppermute(x, 'dp', [(d, d ^ 4 * r) for d in range(n)]) if r else x  18.8 us
    ppermute x12, waiting for transfers between devices, shift(): return lax.ppermute(x, 'dp', [(d, d ^ 4 * r) for d in range(n)]) if r else x  8.79 us
    ppermute x13, starting transfers between devices, swap(): return lax.ppermute(x, 'dp', [(d, d ^ bits) for d in range(n)])  8.58 us
    ppermute x13, waiting for transfers between devices, swap(): return lax.ppermute(x, 'dp', [(d, d ^ bits) for d in range(n)])  2.71 us
    pallas_call x1, Pallas kernels, on_device(): pl.pallas_call(send_kernel, out_shape=outs, grid=(1,), in_specs=[SMEM, SM...  1.93 us
  transfers between devices with their start and end apart: 25, of which 5 were waited for; matrix products, arithmetic and copies ran while one was open for 0% of the time, Pallas kernels for 30%

profile of v4, /device:TPU:0, one launch (start us, length us, event | category | flops | bytes accessed | tf_op | source)
XLA Modules:
  0.0 79.1 jit_solution(18038639554139463961)
XLA Ops:
  1.3 1.9 %shard_map.129 = (f32[2,2,8192]{2,1,0:T(2,128)}, f32[2,32,512]{2,1,0:T(8,128)S(1)}, f32[16,512]{1,0:T(8,128)S(1)}, bf16[32,768]{1,0:T(8,128)(2,1)S(1)}, bf16[32,...) custom-call(s32[1]{0:T(128)} %bitcast.me_ref, s32[1]{0:T(128)S(6)} %sub.7.offset_ref, ...), custom_call_target="tpu_custom_call" | custom-call | tf_op jit(solution)/shard_map/pallas_call | solution.py:376
  3.2 3.0 %collective-permute-start = (bf16[32,768]{1,0:T(8,128)(2,1)S(1)}, bf16[32,768]{1,0:T(8,128)(2,1)S(1)}, u32[]{:S(2)}, u32[]{:S(2)}) collective-permute-start(bf16[32,768]{1,0:T(8,128)(2,1)S(1)} %get-tuple-element.73), channel_id=1, source_target_pairs={{0,4},{1,5},{2,6},{3,7},{4,0},{5,1},{6,2},{7,3},{8,12},{9,13},{10,... | collective-permute-start | bytes 147464 | tf_op jit(solution)/shard_map/ppermute | solution.py:341
  6.2 2.6 %collective-permute-start.1 = (bf16[32,768]{1,0:T(8,128)(2,1)S(1)}, bf16[32,768]{1,0:T(8,128)(2,1)S(1)}, u32[]{:S(2)}, u32[]{:S(2)}) collective-permute-start(bf16[32,768]{1,0:T(8,128)(2,1)S(1)} %get-tuple-element.74), channel_id=1, source_target_pairs={{0,8},{1,9},{2,10},{3,11},{4,12},{5,13},{6,14},{7,15},{8,0},{9,1},... | collective-permute-start | bytes 147464 | tf_op jit(solution)/shard_map/ppermute | solution.py:341
  8.8 3.3 %collective-permute-done.1.refs_2_ = bf16[32,768]{1,0:T(8,128)(2,1)S(1)} collective-permute-done((bf16[32,768]{1,0:T(8,128)(2,1)S(1)}, bf16[32,768]{1,0:T(8,128)(2,1)S(1)}, u32[]{:S(2)}, u32[]{:S(2)}) %collective-permute-start.1) | collective-permute-done | bytes 49184 | tf_op jit(solution)/shard_map/ppermute | solution.py:341
  12.2 2.6 %collective-permute-done.2.refs_3_ = bf16[32,768]{1,0:T(8,128)(2,1)S(1)} collective-permute-done((bf16[32,768]{1,0:T(8,128)(2,1)S(1)}, bf16[32,768]{1,0:T(8,128)(2,1)S(1)}, u32[]{:S(2)}, u32[]{:S(2)}) %collective-permute-start.2) | collective-permute-done | bytes 49184 | tf_op jit(solution)/shard_map/ppermute | solution.py:341
  14.7 1.6 %collective-permute-start.9 = (bf16[4,32,512]{2,1,0:T(8,128)(2,1)S(1)}, bf16[4,32,512]{2,1,0:T(8,128)(2,1)S(1)}, u32[]{:S(2)}, u32[]{:S(2)}) collective-permute-start(bf16[4,32,512]{2,1,0:T(8,128)(2,1)S(1)} %get-tuple-element.80.cot_ref), channel_id=1, source_target_pairs={{0,2},{1,3},{2,0},{3,1},{4,6},{5,7},{6,4},{7,5},{8,10},{9,11},{10,... | collective-permute-start | bytes 393224 | tf_op jit(solution)/shard_map/ppermute | solution.py:344
  18.2 3.2 %shard_map.131 = (f32[896,32]{1,0:T(8,128)S(1)}, f32[32,512]{1,0:T(8,128)S(1)}) custom-call(s32[1]{0:T(128)} %bitcast.me_ref, bf16[4,32,512]{2,1,0:T(8,128)(2,1)S(1)} %get-tuple-element.80.cot_ref, bf16[896,8192]{1,0:T(8,128)(2,1)} %weight_ref.19), custom_call_target="tpu_custom_call" | custom-call | flops 117440512 | bytes 3670016 | tf_op jit(solution)/shard_map/pallas_call | solution.py:351
  22.9 3.7 %collective-permute-start.6 = (bf16[32,512]{1,0:T(8,128)(2,1)S(1)}, bf16[32,512]{1,0:T(8,128)(2,1)S(1)}, u32[]{:S(2)}, u32[]{:S(2)}) collective-permute-start(bf16[32,512]{1,0:T(8,128)(2,1)S(1)} %get-tuple-element.93.share_ref), channel_id=1, source_target_pairs={{0,4},{1,5},{2,6},{3,7},{4,0},{5,1},{6,2},{7,3},{8,12},{9,13},{10,... | collective-permute-start | bytes 98312 | tf_op jit(solution)/shard_map/ppermute | solution.py:341
  26.6 3.2 %shard_map.133 = (f32[896,32]{1,0:T(8,128)S(1)}, f32[32,512]{1,0:T(8,128)S(1)}) custom-call(s32[1]{0:T(128)} %bitcast.me_ref, bf16[4,32,512]{2,1,0:T(8,128)(2,1)S(1)} %collective-permute-done.9.cot_ref, bf16[896,8192]{1,0:T(8,128)(2,1)} %weight_ref.19), custom_call_target="tpu_custom_call" | custom-call | flops 117440512 | bytes 3670016 | tf_op jit(solution)/shard_map/pallas_call | solution.py:351
  30.9 2.3 %shard_map.135 = (f32[32,896]{1,0:T(8,128)S(1)}, f32[32,128]{1,0:T(8,128)S(1)}, f32[32,512]{1,0:T(8,128)S(1)}) custom-call(s32[1]{0:T(128)} %bitcast.me_ref, bf16[4,32,512]{2,1,0:T(8,128)(2,1)S(1)} %pad_maximum_fusion.rest_ref, f32[16,512]{1,0:T(8,128)S(1)} %get-tuple-element.90.gain_ref, bf16[8192,896]{1,0:T(8,128)(2,1)} %weight_ref.17), custom_call_target="tpu_custom_call" | custom-call | flops 117440512 | bytes 3670016 | tf_op jit(solution)/shard_map/pallas_call | solution.py:351
  33.3 3.2 %shard_map.134 = (f32[896,32]{1,0:T(8,128)S(1)}, f32[32,512]{1,0:T(8,128)S(1)}) custom-call(s32[1]{0:T(128)} %bitcast.me_ref, bf16[4,32,512]{2,1,0:T(8,128)(2,1)S(1)} %collective-permute-done.11.cot_ref, bf16[896,8192]{1,0:T(8,128)(2,1)} %weight_ref.19), custom_call_target="tpu_custom_call" | custom-call | flops 117440512 | bytes 3670016 | tf_op jit(solution)/shard_map/pallas_call | solution.py:351
  36.8 2.3 %shard_map.136 = (f32[32,896]{1,0:T(8,128)S(1)}, f32[32,128]{1,0:T(8,128)S(1)}, f32[32,512]{1,0:T(8,128)S(1)}) custom-call(s32[1]{0:T(128)} %bitcast.me_ref, bf16[4,32,512]{2,1,0:T(8,128)(2,1)S(1)} %collective-permute-done.10.rest_ref, f32[16,512]{1,0:T(8,128)S(1)} %get-tuple-element.90.gain_ref, bf16[8192,896]{1,0:T(8,128)(2,1)} %weight_ref.17), custom_call_target="tpu_custom_call" | custom-call | flops 117440512 | bytes 3670016 | tf_op jit(solution)/shard_map/pallas_call | solution.py:351
  39.1 3.2 %shard_map.138 = (f32[896,32]{1,0:T(8,128)S(1)}, f32[32,512]{1,0:T(8,128)S(1)}) custom-call(s32[1]{0:T(128)} %bitcast.me_ref, bf16[4,32,512]{2,1,0:T(8,128)(2,1)S(1)} %collective-permute-done.14.cot_ref, bf16[896,8192]{1,0:T(8,128)(2,1)} %weight_ref.19), custom_call_target="tpu_custom_call" | custom-call | flops 117440512 | bytes 3670016 | tf_op jit(solution)/shard_map/pallas_call | solution.py:351
  42.4 2.5 %shard_map.137 = (f32[32,896]{1,0:T(8,128)S(1)}, f32[32,128]{1,0:T(8,128)S(1)}, f32[32,512]{1,0:T(8,128)S(1)}) custom-call(s32[1]{0:T(128)} %bitcast.me_ref, bf16[4,32,512]{2,1,0:T(8,128)(2,1)S(1)} %collective-permute-done.12.rest_ref, f32[16,512]{1,0:T(8,128)S(1)} %get-tuple-element.90.gain_ref, bf16[8192,896]{1,0:T(8,128)(2,1)} %weight_ref.17), custom_call_target="tpu_custom_call" | custom-call | flops 117440512 | bytes 3670016 | tf_op jit(solution)/shard_map/pallas_call | solution.py:351
  44.9 11.9 %shard_map.139 = (bf16[32,896]{1,0:T(8,128)(2,1)S(1)}, f32[32,512]{1,0:T(8,128)S(1)}, bf16[8,32,512]{2,1,0:T(8,128)(2,1)S(1)}, bf16[8,32,512]{2,1,0:T(8,128)(2,1)S(1)}) custom-call(s32[1]{0:T(128)} %bitcast.me_ref, bf16[4,32,512]{2,1,0:T(8,128)(2,1)S(1)} %collective-permute-done.13.rest_ref, f32[16,512]{1,0:T(8,128)S(1)} %get-tuple-element.90.gain_ref, ...), custom_call_target="tpu_custom_call" | custom-call | flops 587202560 | bytes 18350080 | tf_op jit(solution)/shard_map/pallas_call | solution.py:351
  57.2 1.5 %shard_map.142 = bf16[8,32,512]{2,1,0:T(8,128)(2,1)S(1)} custom-call(s32[1]{0:T(128)} %bitcast.me_ref, bf16[32,896]{1,0:T(8,128)(2,1)S(1)} %get-tuple-element.121.active_ref, bf16[896,8192]{1,0:T(8,128)(2,1)S(1)} %bitcast.14, bf16[8,32,512]{2,1,0:T(8,128)(2,1)S(1)} %get-tuple-element.123.after_ref), custom_call_target="tpu_custom_call" | custom-call | flops 234881024 | bytes 7340032 | tf_op jit(solution)/shard_map/pallas_call | solution.py:351
  59.0 1.6 %collective-permute-start.17 = (bf16[4,32,512]{2,1,0:T(8,128)(2,1)S(1)}, bf16[4,32,512]{2,1,0:T(8,128)(2,1)S(1)}, u32[]{:S(2)}, u32[]{:S(2)}) collective-permute-start(bf16[4,32,512]{2,1,0:T(8,128)(2,1)S(1)} %get-tuple-element.124.after_ref), channel_id=1, source_target_pairs={{0,2},{1,3},{2,0},{3,1},{4,6},{5,7},{6,4},{7,5},{8,10},{9,11},{10,... | collective-permute-start | bytes 393224 | tf_op jit(solution)/shard_map/ppermute | solution.py:344
  60.6 1.5 %shard_map.141.kept_ref = bf16[8,32,512]{2,1,0:T(8,128)(2,1)S(1)} custom-call(s32[1]{0:T(128)} %bitcast.me_ref, bf16[32,896]{1,0:T(8,128)(2,1)S(1)} %get-tuple-element.121.active_ref, bf16[896,8192]{1,0:T(8,128)(2,1)S(1)} %bitcast.14, bf16[4,32,512]{2,1,0:T(8,128)(2,1)S(1)} %get-tuple-element.124.after_ref), custom_call_target="tpu_custom_call" | custom-call | flops 234881024 | bytes 7340032 | tf_op jit(solution)/shard_map/pallas_call | solution.py:351
  62.1 2.7 %collective-permute-done.17.refs_1_ = bf16[4,32,512]{2,1,0:T(8,128)(2,1)S(1)} collective-permute-done((bf16[4,32,512]{2,1,0:T(8,128)(2,1)S(1)}, bf16[4,32,512]{2,1,0:T(8,128)(2,1)S(1)}, u32[]{:S(2)}, u32[]{:S(2)}) %collective-permute-start.17) | collective-permute-done | bytes 131104 | tf_op jit(solution)/shard_map/ppermute | solution.py:344
  64.9 1.6 %collective-permute-start.21 = (bf16[4,32,512]{2,1,0:T(8,128)(2,1)S(1)}, bf16[4,32,512]{2,1,0:T(8,128)(2,1)S(1)}, u32[]{:S(2)}, u32[]{:S(2)}) collective-permute-start(bf16[4,32,512]{2,1,0:T(8,128)(2,1)S(1)} %get-tuple-element.131), channel_id=1, source_target_pairs={{0,2},{1,3},{2,0},{3,1},{4,6},{5,7},{6,4},{7,5},{8,10},{9,11},{10,... | collective-permute-start | bytes 393224 | tf_op jit(solution)/shard_map/ppermute | solution.py:344
  68.0 2.8 %collective-permute-start.20 = (bf16[32,512]{1,0:T(8,128)(2,1)S(1)}, bf16[32,512]{1,0:T(8,128)(2,1)S(1)}, u32[]{:S(2)}, u32[]{:S(2)}) collective-permute-start(bf16[32,512]{1,0:T(8,128)(2,1)S(1)} %get-tuple-element.129), channel_id=1, source_target_pairs={{0,12},{1,13},{2,14},{3,15},{4,8},{5,9},{6,10},{7,11},{8,4},{9,5},... | collective-permute-start | bytes 98312 | tf_op jit(solution)/shard_map/ppermute | solution.py:341
  71.0 1.6 %collective-permute-start.23 = (bf16[32,512]{1,0:T(8,128)(2,1)S(1)}, bf16[32,512]{1,0:T(8,128)(2,1)S(1)}, u32[]{:S(2)}, u32[]{:S(2)}) collective-permute-start(bf16[32,512]{1,0:T(8,128)(2,1)S(1)} %get-tuple-element.134), channel_id=1, source_target_pairs={{0,8},{1,9},{2,10},{3,11},{4,12},{5,13},{6,14},{7,15},{8,0},{9,1},... | collective-permute-start | bytes 98312 | tf_op jit(solution)/shard_map/ppermute | solution.py:341
  72.5 2.8 %collective-permute-start.24 = (bf16[32,512]{1,0:T(8,128)(2,1)S(1)}, bf16[32,512]{1,0:T(8,128)(2,1)S(1)}, u32[]{:S(2)}, u32[]{:S(2)}) collective-permute-start(bf16[32,512]{1,0:T(8,128)(2,1)S(1)} %get-tuple-element.135), channel_id=1, source_target_pairs={{0,12},{1,13},{2,14},{3,15},{4,8},{5,9},{6,10},{7,11},{8,4},{9,5},... | collective-permute-start | bytes 98312 | tf_op jit(solution)/shard_map/ppermute | solution.py:341
  75.9 2.4 %collective-permute-done.24.refs_15_ = bf16[32,512]{1,0:T(8,128)(2,1)S(1)} collective-permute-done((bf16[32,512]{1,0:T(8,128)(2,1)S(1)}, bf16[32,512]{1,0:T(8,128)(2,1)S(1)}, u32[]{:S(2)}, u32[]{:S(2)}) %collective-permute-start.24) | collective-permute-done | bytes 32800 | tf_op jit(solution)/shard_map/ppermute | solution.py:341
  (55 shorter events, 8.6 us)
Async XLA Ops:
  3.2 5.6 %collective-permute-start = (bf16[32,768]{1,0:T(8,128)(2,1)S(1)}, bf16[32,768]{1,0:T(8,128)(2,1)S(1)}, u32[]{:S(2)}, u32[]{:S(2)}) collective-permute-start(bf16[32,768]{1,0:T(8,128)(2,1)S(1)} %get-tuple-element.73), channel_id=1, source_target_pairs={{0,4},{1,5},{2,6},{3,7},{4,0},{5,1},{6,2},{7,3},{8,12},{9,13},{10,... | collective-permute-start | bytes 147464 | tf_op jit(solution)/shard_map/ppermute | solution.py:341
  6.2 5.9 %collective-permute-start.1 = (bf16[32,768]{1,0:T(8,128)(2,1)S(1)}, bf16[32,768]{1,0:T(8,128)(2,1)S(1)}, u32[]{:S(2)}, u32[]{:S(2)}) collective-permute-start(bf16[32,768]{1,0:T(8,128)(2,1)S(1)} %get-tuple-element.74), channel_id=1, source_target_pairs={{0,8},{1,9},{2,10},{3,11},{4,12},{5,13},{6,14},{7,15},{8,0},{9,1},... | collective-permute-start | bytes 147464 | tf_op jit(solution)/shard_map/ppermute | solution.py:341
  8.8 5.9 %collective-permute-start.2 = (bf16[32,768]{1,0:T(8,128)(2,1)S(1)}, bf16[32,768]{1,0:T(8,128)(2,1)S(1)}, u32[]{:S(2)}, u32[]{:S(2)}) collective-permute-start(bf16[32,768]{1,0:T(8,128)(2,1)S(1)} %get-tuple-element.75), channel_id=1, source_target_pairs={{0,12},{1,13},{2,14},{3,15},{4,8},{5,9},{6,10},{7,11},{8,4},{9,5},... | collective-permute-start | bytes 147464 | tf_op jit(solution)/shard_map/ppermute | solution.py:341
  14.7 11.8 %collective-permute-start.9 = (bf16[4,32,512]{2,1,0:T(8,128)(2,1)S(1)}, bf16[4,32,512]{2,1,0:T(8,128)(2,1)S(1)}, u32[]{:S(2)}, u32[]{:S(2)}) collective-permute-start(bf16[4,32,512]{2,1,0:T(8,128)(2,1)S(1)} %get-tuple-element.80.cot_ref), channel_id=1, source_target_pairs={{0,2},{1,3},{2,0},{3,1},{4,6},{5,7},{6,4},{7,5},{8,10},{9,11},{10,... | collective-permute-start | bytes 393224 | tf_op jit(solution)/shard_map/ppermute | solution.py:344
  16.3 5.1 %collective-permute-start.3 = (bf16[4,16,128]{2,1,0:T(8,128)(2,1)S(1)}, bf16[4,16,128]{2,1,0:T(8,128)(2,1)S(1)}, u32[]{:S(2)}, u32[]{:S(2)}) collective-permute-start(bf16[4,16,128]{2,1,0:T(8,128)(2,1)S(1)} %get-tuple-element.77), channel_id=1, source_target_pairs={{0,1},{1,0},{2,3},{3,2},{4,5},{5,4},{6,7},{7,6},{8,9},{9,8},{10,11... | collective-permute-start | bytes 49160 | tf_op jit(solution)/shard_map/ppermute | solution.py:344
  16.3 5.1 %collective-permute-start.4 = (bf16[4,16,128]{2,1,0:T(8,128)(2,1)S(1)}, bf16[4,16,128]{2,1,0:T(8,128)(2,1)S(1)}, u32[]{:S(2)}, u32[]{:S(2)}) collective-permute-start(bf16[4,16,128]{2,1,0:T(8,128)(2,1)S(1)} %get-tuple-element.78), channel_id=1, source_target_pairs={{0,2},{1,3},{2,0},{3,1},{4,6},{5,7},{6,4},{7,5},{8,10},{9,11},{10,... | collective-permute-start | bytes 49160 | tf_op jit(solution)/shard_map/ppermute | solution.py:344
  16.8 4.6 %collective-permute-start.5 = (bf16[4,16,128]{2,1,0:T(8,128)(2,1)S(1)}, bf16[4,16,128]{2,1,0:T(8,128)(2,1)S(1)}, u32[]{:S(2)}, u32[]{:S(2)}) collective-permute-start(bf16[4,16,128]{2,1,0:T(8,128)(2,1)S(1)} %get-tuple-element.79), channel_id=1, source_target_pairs={{0,3},{1,2},{2,1},{3,0},{4,7},{5,6},{6,5},{7,4},{8,11},{9,10},{10,... | collective-permute-start | bytes 49160 | tf_op jit(solution)/shard_map/ppermute | solution.py:344
  22.2 7.6 %collective-permute-start.8 = (bf16[32,512]{1,0:T(8,128)(2,1)S(1)}, bf16[32,512]{1,0:T(8,128)(2,1)S(1)}, u32[]{:S(2)}, u32[]{:S(2)}) collective-permute-start(bf16[32,512]{1,0:T(8,128)(2,1)S(1)} %get-tuple-element.93.share_ref), channel_id=1, source_target_pairs={{0,12},{1,13},{2,14},{3,15},{4,8},{5,9},{6,10},{7,11},{8,4},{9,5},... | collective-permute-start | bytes 98312 | tf_op jit(solution)/shard_map/ppermute | solution.py:341
  22.9 6.9 %collective-permute-start.7 = (bf16[32,512]{1,0:T(8,128)(2,1)S(1)}, bf16[32,512]{1,0:T(8,128)(2,1)S(1)}, u32[]{:S(2)}, u32[]{:S(2)}) collective-permute-start(bf16[32,512]{1,0:T(8,128)(2,1)S(1)} %get-tuple-element.93.share_ref), channel_id=1, source_target_pairs={{0,8},{1,9},{2,10},{3,11},{4,12},{5,13},{6,14},{7,15},{8,0},{9,1},... | collective-permute-start | bytes 98312 | tf_op jit(solution)/shard_map/ppermute | solution.py:341
  22.9 6.9 %collective-permute-start.6 = (bf16[32,512]{1,0:T(8,128)(2,1)S(1)}, bf16[32,512]{1,0:T(8,128)(2,1)S(1)}, u32[]{:S(2)}, u32[]{:S(2)}) collective-permute-start(bf16[32,512]{1,0:T(8,128)(2,1)S(1)} %get-tuple-element.93.share_ref), channel_id=1, source_target_pairs={{0,4},{1,5},{2,6},{3,7},{4,0},{5,1},{6,2},{7,3},{8,12},{9,13},{10,... | collective-permute-start | bytes 98312 | tf_op jit(solution)/shard_map/ppermute | solution.py:341
  26.6 6.7 %collective-permute-start.11 = (bf16[4,32,512]{2,1,0:T(8,128)(2,1)S(1)}, bf16[4,32,512]{2,1,0:T(8,128)(2,1)S(1)}, u32[]{:S(2)}, u32[]{:S(2)}) collective-permute-start(bf16[4,32,512]{2,1,0:T(8,128)(2,1)S(1)} %get-tuple-element.80.cot_ref), channel_id=1, source_target_pairs={{0,1},{1,0},{2,3},{3,2},{4,5},{5,4},{6,7},{7,6},{8,9},{9,8},{10,11... | collective-permute-start | bytes 393224 | tf_op jit(solution)/shard_map/ppermute | solution.py:344
  29.8 6.7 %collective-permute-start.10 = (bf16[4,32,512]{2,1,0:T(8,128)(2,1)S(1)}, bf16[4,32,512]{2,1,0:T(8,128)(2,1)S(1)}, u32[]{:S(2)}, u32[]{:S(2)}) collective-permute-start(bf16[4,32,512]{2,1,0:T(8,128)(2,1)S(1)} %pad_maximum_fusion.rest_ref), channel_id=1, source_target_pairs={{0,2},{1,3},{2,0},{3,1},{4,6},{5,7},{6,4},{7,5},{8,10},{9,11},{10,... | collective-permute-start | bytes 393224 | tf_op jit(solution)/shard_map/ppermute | solution.py:344
  30.4 12.0 %collective-permute-start.12 = (bf16[4,32,512]{2,1,0:T(8,128)(2,1)S(1)}, bf16[4,32,512]{2,1,0:T(8,128)(2,1)S(1)}, u32[]{:S(2)}, u32[]{:S(2)}) collective-permute-start(bf16[4,32,512]{2,1,0:T(8,128)(2,1)S(1)} %pad_maximum_fusion.rest_ref), channel_id=1, source_target_pairs={{0,1},{1,0},{2,3},{3,2},{4,5},{5,4},{6,7},{7,6},{8,9},{9,8},{10,11... | collective-permute-start | bytes 393224 | tf_op jit(solution)/shard_map/ppermute | solution.py:344
  30.6 8.5 %collective-permute-start.14 = (bf16[4,32,512]{2,1,0:T(8,128)(2,1)S(1)}, bf16[4,32,512]{2,1,0:T(8,128)(2,1)S(1)}, u32[]{:S(2)}, u32[]{:S(2)}) collective-permute-start(bf16[4,32,512]{2,1,0:T(8,128)(2,1)S(1)} %collective-permute-done.9.cot_ref), channel_id=1, source_target_pairs={{0,1},{1,0},{2,3},{3,2},{4,5},{5,4},{6,7},{7,6},{8,9},{9,8},{10,11... | collective-permute-start | bytes 393224 | tf_op jit(solution)/shard_map/ppermute | solution.py:344
  36.5 8.4 %collective-permute-start.13 = (bf16[4,32,512]{2,1,0:T(8,128)(2,1)S(1)}, bf16[4,32,512]{2,1,0:T(8,128)(2,1)S(1)}, u32[]{:S(2)}, u32[]{:S(2)}) collective-permute-start(bf16[4,32,512]{2,1,0:T(8,128)(2,1)S(1)} %collective-permute-done.10.rest_ref), channel_id=1, source_target_pairs={{0,1},{1,0},{2,3},{3,2},{4,5},{5,4},{6,7},{7,6},{8,9},{9,8},{10,11... | collective-permute-start | bytes 393224 | tf_op jit(solution)/shard_map/ppermute | solution.py:344
  58.7 3.4 %collective-permute-start.16 = (bf16[8,32,512]{2,1,0:T(8,128)(2,1)S(1)}, bf16[8,32,512]{2,1,0:T(8,128)(2,1)S(1)}, u32[]{:S(2)}, u32[]{:S(2)}) collective-permute-start(bf16[8,32,512]{2,1,0:T(8,128)(2,1)S(1)} %shard_map.142), channel_id=1, source_target_pairs={{0,1},{1,0},{2,3},{3,2},{4,5},{5,4},{6,7},{7,6},{8,9},{9,8},{10,11... | collective-permute-start | bytes 786440 | tf_op jit(solution)/shard_map/ppermute | solution.py:344
  59.0 5.8 %collective-permute-start.17 = (bf16[4,32,512]{2,1,0:T(8,128)(2,1)S(1)}, bf16[4,32,512]{2,1,0:T(8,128)(2,1)S(1)}, u32[]{:S(2)}, u32[]{:S(2)}) collective-permute-start(bf16[4,32,512]{2,1,0:T(8,128)(2,1)S(1)} %get-tuple-element.124.after_ref), channel_id=1, source_target_pairs={{0,2},{1,3},{2,0},{3,1},{4,6},{5,7},{6,4},{7,5},{8,10},{9,11},{10,... | collective-permute-start | bytes 393224 | tf_op jit(solution)/shard_map/ppermute | solution.py:344
  64.9 6.0 %collective-permute-start.21 = (bf16[4,32,512]{2,1,0:T(8,128)(2,1)S(1)}, bf16[4,32,512]{2,1,0:T(8,128)(2,1)S(1)}, u32[]{:S(2)}, u32[]{:S(2)}) collective-permute-start(bf16[4,32,512]{2,1,0:T(8,128)(2,1)S(1)} %get-tuple-element.131), channel_id=1, source_target_pairs={{0,2},{1,3},{2,0},{3,1},{4,6},{5,7},{6,4},{7,5},{8,10},{9,11},{10,... | collective-permute-start | bytes 393224 | tf_op jit(solution)/shard_map/ppermute | solution.py:344
  66.5 6.1 %collective-permute-start.18 = (bf16[32,512]{1,0:T(8,128)(2,1)S(1)}, bf16[32,512]{1,0:T(8,128)(2,1)S(1)}, u32[]{:S(2)}, u32[]{:S(2)}) collective-permute-start(bf16[32,512]{1,0:T(8,128)(2,1)S(1)} %get-tuple-element.127), channel_id=1, source_target_pairs={{0,4},{1,5},{2,6},{3,7},{4,0},{5,1},{6,2},{7,3},{8,12},{9,13},{10,... | collective-permute-start | bytes 98312 | tf_op jit(solution)/shard_map/ppermute | solution.py:341
  67.2 8.2 %collective-permute-start.19 = (bf16[32,512]{1,0:T(8,128)(2,1)S(1)}, bf16[32,512]{1,0:T(8,128)(2,1)S(1)}, u32[]{:S(2)}, u32[]{:S(2)}) collective-permute-start(bf16[32,512]{1,0:T(8,128)(2,1)S(1)} %get-tuple-element.128), channel_id=1, source_target_pairs={{0,8},{1,9},{2,10},{3,11},{4,12},{5,13},{6,14},{7,15},{8,0},{9,1},... | collective-permute-start | bytes 98312 | tf_op jit(solution)/shard_map/ppermute | solution.py:341
  68.0 7.3 %collective-permute-start.20 = (bf16[32,512]{1,0:T(8,128)(2,1)S(1)}, bf16[32,512]{1,0:T(8,128)(2,1)S(1)}, u32[]{:S(2)}, u32[]{:S(2)}) collective-permute-start(bf16[32,512]{1,0:T(8,128)(2,1)S(1)} %get-tuple-element.129), channel_id=1, source_target_pairs={{0,12},{1,13},{2,14},{3,15},{4,8},{5,9},{6,10},{7,11},{8,4},{9,5},... | collective-permute-start | bytes 98312 | tf_op jit(solution)/shard_map/ppermute | solution.py:341
  70.9 4.5 %collective-permute-start.22 = (bf16[32,512]{1,0:T(8,128)(2,1)S(1)}, bf16[32,512]{1,0:T(8,128)(2,1)S(1)}, u32[]{:S(2)}, u32[]{:S(2)}) collective-permute-start(bf16[32,512]{1,0:T(8,128)(2,1)S(1)} %get-tuple-element.133), channel_id=1, source_target_pairs={{0,4},{1,5},{2,6},{3,7},{4,0},{5,1},{6,2},{7,3},{8,12},{9,13},{10,... | collective-permute-start | bytes 98312 | tf_op jit(solution)/shard_map/ppermute | solution.py:341
  71.0 4.9 %collective-permute-start.23 = (bf16[32,512]{1,0:T(8,128)(2,1)S(1)}, bf16[32,512]{1,0:T(8,128)(2,1)S(1)}, u32[]{:S(2)}, u32[]{:S(2)}) collective-permute-start(bf16[32,512]{1,0:T(8,128)(2,1)S(1)} %get-tuple-element.134), channel_id=1, source_target_pairs={{0,8},{1,9},{2,10},{3,11},{4,12},{5,13},{6,14},{7,15},{8,0},{9,1},... | collective-permute-start | bytes 98312 | tf_op jit(solution)/shard_map/ppermute | solution.py:341
  72.5 5.7 %collective-permute-start.24 = (bf16[32,512]{1,0:T(8,128)(2,1)S(1)}, bf16[32,512]{1,0:T(8,128)(2,1)S(1)}, u32[]{:S(2)}, u32[]{:S(2)}) collective-permute-start(bf16[32,512]{1,0:T(8,128)(2,1)S(1)} %get-tuple-element.135), channel_id=1, source_target_pairs={{0,12},{1,13},{2,14},{3,15},{4,8},{5,9},{6,10},{7,11},{8,4},{9,5},... | collective-permute-start | bytes 98312 | tf_op jit(solution)/shard_map/ppermute | solution.py:341
  (6 other events, 77.5 us)

commit v5 on v4

v5 whole, which is shorter than its diff:
```python
import functools

import jax
import jax.numpy as jnp
from jax import lax
from jax.experimental import pallas as pl
from jax.experimental.pallas import tpu as pltpu
from jax.sharding import PartitionSpec as P

clip_top = 448.0
eps = 1e-05
LANES = 128
f32 = jnp.float32
bf16 = jnp.bfloat16
VMEM = pl.BlockSpec(memory_space=pltpu.VMEM)
SMEM = pl.BlockSpec(memory_space=pltpu.SMEM)


def hbm(x):
    return pltpu.with_memory_space_constraint(x, pltpu.HBM)


def powers(exponent, sign):
    total = jnp.zeros(exponent.shape, f32)
    for level in range(-10, 1):
        total = jnp.where(exponent == level, f32(2.0 ** (sign * level)), total)
    return total


def params(megabytes):
    return pltpu.CompilerParams(vmem_limit_bytes=megabytes << 20)


def flip(bit, by):
    return lax.rem(bit + by, 2)


def place(me):
    return me // 4, lax.rem(me // 2, 2), lax.rem(me, 2)


def owner_of(me, part, k):
    return 2 * k + flip(lax.rem(me, 2), part)


def send_kernel(
    offset_ref, act_ref, expo_ref, base_ref, received_ref, cot_ref, gain_ref,
    out_ref, new_ref, received_out_ref, gain_out_ref, cots_ref, rows_ref,
):
    n, rows, _ = rows_ref.shape
    share = cot_ref.shape[1]
    width = act_ref.shape[1]
    per_dev = width // LANES // n
    received_out_ref[...] = received_ref[...]
    for j in range(n):
        gain_out_ref[j : j + 1, :] = gain_ref[:, j * share : (j + 1) * share]
    first = offset_ref[0] == 0
    down, up = powers(expo_ref[...], -1), powers(expo_ref[...], 1)
    old = [base_ref[p] for p in range(2)]
    chosen = jnp.concatenate([jnp.where(first, o[0:1], o[1:2]) for o in old], axis=0)
    delta = act_ref[...].astype(f32) - chosen
    fill = jnp.full((rows - 2 * per_dev, LANES), offset_ref[0].astype(f32))
    pieces = []
    for b in range(width // LANES):
        scaled = delta[:, b * LANES : (b + 1) * LANES] * down[:, b : b + 1]
        kept = jnp.clip(scaled, -clip_top, clip_top).astype(bf16).astype(f32) * up[:, b : b + 1]
        d, c = divmod(b, per_dev)
        rows_ref[d, 2 * c : 2 * c + 2, :] = kept
        pieces.append(kept)
    for d in range(n):
        rows_ref[d, 2 * per_dev :, :] = fill
    out_ref[...] = rows_ref[...].astype(bf16)
    for k in range(n // 2):
        cots_ref[k] = cot_ref[...]
    new = chosen + jnp.concatenate(pieces, axis=1)
    for p in range(2):
        row = new[p : p + 1]
        new_ref[p, 0:1, :] = jnp.where(first, row, old[p][0:1])
        new_ref[p, 1:2, :] = jnp.where(first, old[p][1:2], row)


def rebuild_kernel(arrived_ref, base_ref, new_ref, share_ref, copies_ref, rows_ref, slots_ref):
    n, rows, _ = arrived_ref.shape
    width = share_ref.shape[1]
    rows_ref[...] = arrived_ref[...].astype(f32).reshape(n * rows, LANES)
    per_dev = width // LANES
    first = rows_ref[pl.ds(2 * per_dev, n, stride=rows), :] == 0.0
    for p in range(2):
        for c in range(per_dev):
            cols = slice(c * LANES, (c + 1) * LANES)
            sent = rows_ref[pl.ds(2 * c + p, n, stride=rows), :]
            at = p * per_dev + c
            slots_ref[at] = base_ref[p, :, cols]
            even = slots_ref[at, pl.ds(0, n, stride=2), :]
            odd = slots_ref[at, pl.ds(1, n, stride=2), :]
            rebuilt = jnp.where(first, even, odd) + sent
            slots_ref[at, pl.ds(0, n, stride=2), :] = jnp.where(first, rebuilt, even)
            slots_ref[at, pl.ds(1, n, stride=2), :] = jnp.where(first, odd, rebuilt)
            new_ref[p, :, cols] = slots_ref[at]
            restored = rebuilt.astype(bf16)
            share_ref[p * n : (p + 1) * n, cols] = restored
            for k in range(copies_ref.shape[0]):
                copies_ref[k, p * n : (p + 1) * n, cols] = restored


def dot_nt(a, b):
    return lax.dot_general(a, b, (((1,), (1,)), ((), ())), preferred_element_type=f32)


def own_rows(piece_ref, own_ref, me, owner):
    n = piece_ref.shape[0] // 2
    for p in range(2):
        own_ref[pl.ds(p * n + owner, 1), :] = piece_ref[pl.ds(p * n + me, 1), :]


def dot_by_halves(rows, tokens):
    middle = tokens.shape[1] // 2 // LANES * LANES
    if middle == 0:
        return dot_nt(rows, tokens)
    return dot_nt(rows[:, :middle], tokens[:, :middle]) + dot_nt(rows[:, middle:], tokens[:, middle:])


class Stream:
    flying = 4

    def __init__(self, sources, held_ref, sems):
        self.copies = [
            pltpu.make_async_copy(source, held_ref.at[i], sems.at[i])
            for i, source in enumerate(sources)
        ]
        self.held_ref = held_ref
        for copy in self.copies[: self.flying]:
            copy.start()

    def block(self, i):
        self.copies[i].wait()
        if i + self.flying < len(self.copies):
            self.copies[i + self.flying].start()
        return self.held_ref[i]


def row_blocks(weight_ref, owners, width):
    return [weight_ref.at[pl.ds(pl.multiple_of(o * width, width), width)] for o in owners]


def grad_active_kernel(part, me_ref, cot_ref, weight_ref, acc_ref, own_ref, held_ref, piece_ref, sems):
    half, _, width = cot_ref.shape
    me = me_ref[0]
    owners = [owner_of(me, part, k) for k in range(half)]
    columns = [weight_ref.at[:, pl.ds(pl.multiple_of(o * width, width), width)] for o in owners]
    stream = Stream(columns, held_ref, sems)
    own_ref[...] = jnp.zeros_like(own_ref)
    for k, owner in enumerate(owners):
        piece_ref[...] = cot_ref[k].astype(f32)
        own_rows(piece_ref, own_ref, me, owner)
    for k in range(half):
        terms = dot_by_halves(stream.block(k), cot_ref[k])
        acc_ref[...] = terms if k == 0 else acc_ref[...] + terms


def up_part(part, me, rest_ref, gain_ref, stream, acc_ref, square_ref, own_ref, piece_ref):
    half, _, width = rest_ref.shape
    own_ref[...] = jnp.zeros_like(own_ref)
    scaled = []
    for k in range(half):
        owner = owner_of(me, part, k)
        piece = rest_ref[k].astype(f32)
        piece_ref[...] = piece
        own_rows(piece_ref, own_ref, me, owner)
        squares = piece * piece
        total = sum(squares[:, c * LANES : (c + 1) * LANES] for c in range(width // LANES))
        square_ref[...] = total if k == 0 else square_ref[...] + total
        scaled.append((piece * gain_ref[pl.ds(owner, 1), :]).astype(bf16))
    for k in range(half):
        terms = jnp.dot(scaled[k], stream.block(k), preferred_element_type=f32)
        acc_ref[...] = terms if k == 0 else acc_ref[...] + terms


def up_kernel(
    me_ref, rest_ref, gain_ref, weight_ref,
    acc_ref, square_ref, own_ref, held_ref, piece_ref, sems,
):
    half, _, width = rest_ref.shape
    me = me_ref[0]
    owners = [owner_of(me, 0, k) for k in range(half)]
    stream = Stream(row_blocks(weight_ref, owners, width), held_ref, sems)
    up_part(0, me, rest_ref, gain_ref, stream, acc_ref, square_ref, own_ref, piece_ref)


def middle_kernel(
    me_ref, rest_ref, gain_ref, weight_ref, acc_in_ref, square_in_ref, ga_ref, ga_too_ref,
    active_ref, own_ref, send_ref, keep_ref, acc_ref, square_ref, piece_ref, held_ref, rows_ref, sems,
):
    half, tokens, width = rest_ref.shape
    n, chunks = 2 * half, width // LANES
    width_all = weight_ref.shape[0]
    me = me_ref[0]
    owners = [owner_of(me, part, k) for part in (1, 0) for k in range(half)]
    stream = Stream(row_blocks(weight_ref, owners, width), held_ref, sems)
    up_part(1, me, rest_ref, gain_ref, stream, acc_ref, square_ref, own_ref, piece_ref)
    product = acc_ref[...] + acc_in_ref[...]
    total = jnp.sum(square_ref[...] + square_in_ref[...], axis=1, keepdims=True)
    hidden = lax.rsqrt(total / width_all + eps) * product
    sigma = jax.nn.sigmoid(hidden)
    active_ref[...] = (hidden * sigma).astype(bf16)
    grad_active = (ga_ref[...] + ga_too_ref[...]).T
    gh = (grad_active * sigma * (1.0 + hidden * (1.0 - sigma))).astype(bf16)
    for i, share in enumerate(owners):
        block = held_ref[i] if i < half else stream.block(i)
        terms = dot_by_halves(block, gh).T
        for p in range(2):
            for c in range(chunks):
                rows_ref[c, pl.ds(p * n + share, n, stride=tokens), :] = terms[
                    p * n : (p + 1) * n, c * LANES : (c + 1) * LANES
                ]
    core = lax.rem(me, 2)
    for k in range(half):
        keep_at = pl.multiple_of((2 * k + core) * tokens, tokens)
        send_at = pl.multiple_of((2 * k + 1 - core) * tokens, tokens)
        for c in range(chunks):
            cols = slice(c * LANES, (c + 1) * LANES)
            keep_ref[k, :, cols] = rows_ref[c, pl.ds(keep_at, tokens), :].astype(bf16)
            send_ref[k, :, cols] = rows_ref[c, pl.ds(send_at, tokens), :].astype(bf16)


def down_kernel(other, me_ref, active_ref, weight_ref, after_ref, out_ref):
    half, _, width = out_ref.shape
    core = lax.rem(me_ref[0] + other, 2)

    def share(k):
        columns = pl.ds(pl.multiple_of((2 * k + core) * width, width), width)
        terms = jnp.dot(active_ref[...], weight_ref[:, columns], preferred_element_type=f32)
        out_ref[k] = terms.astype(bf16)

    pl.loop(0, half, unroll=4)(share)


def pair_kernel(me_ref, kept_ref, arrived_ref, *refs):
    ins, (send_ref, keep_ref), shares = (refs[:2], refs[2:4], refs[4:]) if len(refs) > 2 else ((), refs, ())
    quarter = send_ref.shape[0]
    _, row, _ = place(me_ref[0])
    for k in range(quarter):
        for out_ref, at in ((send_ref, 2 * k + 1 - row), (keep_ref, 2 * k + row)):
            out_ref[k] = (kept_ref[at].astype(f32) + arrived_ref[at].astype(f32)).astype(bf16)
    if shares:
        line_kernel(me_ref, *ins, *shares)


def line_kernel(me_ref, kept_ref, arrived_ref, *refs):
    along, _, _ = place(me_ref[0])
    for r, ref in enumerate(refs):
        at = jnp.bitwise_xor(along, r)
        ref[...] = (kept_ref[at].astype(f32) + arrived_ref[at].astype(f32)).astype(bf16)


def added(refs):
    return functools.reduce(lambda a, b: a + b, [ref[...].astype(f32) for ref in refs])


def final_kernel(width_all, share_ref, gain_ref, expo_ref, *refs):
    *refs, layer_ref, grad_ref = refs
    quarter = (len(refs) - 4) // 2
    own_all, cot_all = added(refs[:2]), added(refs[2:4])
    grad, layer = added(refs[4 : 4 + quarter]), added(refs[4 + quarter :])
    layer_ref[...] = (share_ref[...].astype(f32) + layer).astype(bf16)
    n, width = gain_ref.shape
    down, up = powers(expo_ref[...], -1), powers(expo_ref[...], 1)
    gain = gain_ref[...]
    per_dev = width // LANES
    blocks = n * per_dev
    at_row = lax.broadcasted_iota(jnp.int32, (n, blocks), 0)
    at_lane = lax.broadcasted_iota(jnp.int32, (n, blocks), 1)
    for p in range(2):
        rows = slice(p * n, (p + 1) * n)
        own, norm = own_all[rows, :], grad[rows, :]
        inv_rms = lax.rsqrt(jnp.sum(own * own, keepdims=True) / width_all + eps)
        scaled_in = (own * gain).astype(bf16).astype(f32)
        curvature = inv_rms * jnp.sum(scaled_in * norm, keepdims=True)
        correction = curvature * inv_rms * inv_rms / width_all
        value = cot_all[rows, :] + inv_rms * gain * norm - correction * own
        for c in range(per_dev):
            at = at_lane == at_row * per_dev + c
            shrink = jnp.sum(jnp.where(at, down[p : p + 1], 0.0), axis=1, keepdims=True)
            grow = jnp.sum(jnp.where(at, up[p : p + 1], 0.0), axis=1, keepdims=True)
            scaled = value[:, c * LANES : (c + 1) * LANES] * shrink
            kept = jnp.clip(scaled, -clip_top, clip_top).astype(bf16).astype(f32) * grow
            grad_ref[p, pl.ds(c, n, stride=per_dev), :] = kept


def on_device(
    activations,
    sample_ids,
    forward_exponent,
    sender_base,
    receiver_base,
    norm_gain,
    up_weight,
    down_weight,
    cotangent,
    backward_exponent,
    *,
    n,
):
    half, quarter = n // 2, n // 4
    tokens = 2 * n
    width_all, hidden_dev = up_weight.shape
    width = width_all // n
    me = lax.axis_index("dp").astype(jnp.int32)
    me_in = me.reshape(1)

    def shift(x, r):
        return lax.ppermute(x, "dp", [(d, d ^ (4 * r)) for d in range(n)]) if r else x

    def swap(x, bits):
        return lax.ppermute(x, "dp", [(d, d ^ bits) for d in range(n)])

    def exchange(x, among=None):
        return lax.all_to_all(
            x, "dp", split_axis=0, concat_axis=0, axis_index_groups=among, tiled=True
        )

    same_core = [[2 * k + c for k in range(half)] for c in range(2)]
    struct = jax.ShapeDtypeStruct
    share_shape, hidden_shape = (tokens, width), (tokens, hidden_dev)
    line_shape = (quarter, tokens, width)

    def call(kernel, outs, ins, args, scratch=(), cost=0, grant=8):
        return pl.pallas_call(
            kernel,
            out_shape=outs,
            in_specs=ins,
            out_specs=jax.tree.map(lambda _: VMEM, outs),
            scratch_shapes=list(scratch),
            compiler_params=params(grant),
            cost_estimate=pl.CostEstimate(
                flops=int(cost * tokens * width_all * hidden_dev),
                bytes_accessed=int(cost * width_all * hidden_dev),
                transcendentals=0,
            ),
        )(*args)

    offset = sample_ids - sender_base.shape[1] * me
    rows = -(-(2 * width // LANES + 1) // 16) * 16
    act_shape, expo_shape = (2, width_all), (2, width_all // LANES)
    once = lambda shape: pl.BlockSpec(shape, lambda i: (0,) * len(shape))
    in_shapes = [act_shape, expo_shape, sender_base.shape, receiver_base.shape, share_shape, (1, width_all)]
    outs = (
        struct((n, rows, LANES), bf16),
        struct(sender_base.shape, f32),
        struct(receiver_base.shape, f32),
        struct((n, width), f32),
        struct((half, tokens, width), bf16),
    )
    blocks, new_sender_base, received, gain, cots = pl.pallas_call(
        send_kernel,
        out_shape=outs,
        grid=(1,),
        in_specs=[SMEM] + [once(x) for x in in_shapes],
        out_specs=tuple(once(x.shape) for x in outs),
        scratch_shapes=[pltpu.VMEM((n, rows, LANES), f32)],
        compiler_params=params(8),
    )(
        offset,
        hbm(activations.reshape(act_shape)),
        hbm(forward_exponent.reshape(expo_shape)),
        hbm(sender_base),
        hbm(receiver_base),
        hbm(cotangent.reshape(share_shape)),
        hbm(norm_gain.reshape(1, width_all)),
    )
    arrived = exchange(blocks)
    cots = exchange(cots, same_core)
    cots = [cots, swap(cots, 1)]

    ANY = pl.BlockSpec(memory_space=pl.ANY)
    sems = lambda count: pltpu.SemaphoreType.DMA((count,))
    share_f32 = struct(share_shape, f32)
    sums = (struct(hidden_shape, f32), struct((tokens, LANES), f32))

    def weight_call(kernel, outs, args, weight, blocks, cost, more=(), scratch=(), grant=16):
        return call(
            kernel,
            outs,
            [SMEM] + [VMEM] * (len(args) - 1) + [ANY] + [VMEM] * len(more),
            [*args, hbm(weight), *more],
            [*scratch, pltpu.VMEM(blocks, bf16), pltpu.VMEM(share_shape, f32), sems(blocks[0])],
            cost=cost,
            grant=grant,
        )

    new_receiver_base, share, copies = call(
        rebuild_kernel,
        (
            struct(receiver_base.shape, f32),
            struct(share_shape, bf16),
            struct((half, tokens, width), bf16),
        ),
        [VMEM] * 2,
        [arrived, received],
        [pltpu.VMEM((n * rows, LANES), f32), pltpu.VMEM((2 * width // LANES, 2 * n, LANES), f32)],
    )
    rest = exchange(copies, same_core)
    gas, own_cots = zip(*[
        weight_call(
            functools.partial(grad_active_kernel, part),
            (struct((hidden_dev, tokens), f32), share_f32),
            [me_in, cots[part]],
            down_weight,
            (half, hidden_dev, width),
            1,
        )
        for part in range(2)
    ])
    rest, gas = lax.optimization_barrier((rest, gas))
    rest_other = swap(rest, 1)
    acc, square, own = weight_call(
        up_kernel,
        sums + (share_f32,),
        [me_in, rest, gain],
        up_weight,
        (half, width, hidden_dev),
        1,
    )
    half_out = struct((half, tokens, width), bf16)
    active, own_too, grad_send, grad_keep = call(
        middle_kernel,
        (struct(hidden_shape, bf16), share_f32, half_out, half_out),
        [SMEM, VMEM, VMEM, ANY] + [VMEM] * 4,
        [me_in, rest_other, gain, hbm(up_weight), acc, square, *gas],
        [pltpu.VMEM(x.shape, x.dtype) for x in sums]
        + [
            pltpu.VMEM(share_shape, f32),
            pltpu.VMEM((n, width, hidden_dev), bf16),
            pltpu.VMEM((width // LANES, n * tokens, LANES), f32),
            sems(n),
        ],
        cost=3,
        grant=24,
    )

    def down_terms(other, after):
        return call(
            functools.partial(down_kernel, other),
            half_out,
            [SMEM] + [VMEM] * 2 + [ANY],
            [me_in, active, down_weight, after],
            cost=1,
        )

    pair_out = (struct(line_shape, bf16),) * 2
    line_out = (struct(share_shape, bf16),) * quarter
    grad_in = swap(grad_send, 1)
    out_in = swap(down_terms(1, grad_send), 1)
    grad_send, grad_row = call(
        pair_kernel, pair_out, [SMEM] + [VMEM] * 2, [me_in, grad_keep, grad_in]
    )
    grad_row_in = swap(grad_send, 2)
    out_send, out_row, *grad_line = call(
        pair_kernel,
        pair_out + line_out,
        [SMEM] + [VMEM] * 4,
        [me_in, down_terms(0, grad_send), out_in, grad_row, grad_row_in],
    )
    out_row_in = swap(out_send, 2)
    grad_line = [shift(x, r) for r, x in enumerate(grad_line)]
    out_line = call(line_kernel, line_out, [SMEM] + [VMEM] * 2, [me_in, out_row, out_row_in])
    out_line = [shift(x, r) for r, x in enumerate(out_line)]
    layer_out, returned = call(
        functools.partial(final_kernel, width_all),
        (struct(share_shape, bf16), struct((2, width_all // LANES, LANES), f32)),
        [VMEM] * (7 + 2 * quarter),
        [
            share,
            gain,
            backward_exponent.reshape(expo_shape),
            own,
            own_too,
            *own_cots,
            *grad_line,
            *out_line,
        ],
    )
    return (
        new_sender_base,
        new_receiver_base,
        layer_out.reshape(2, n, width),
        returned.reshape(2, 1, width_all),
    )


def solution(mesh):
    placed = (
        P(None, ("groups", "dp"), None),
        P(("groups", "dp")),
        P(None, ("groups", "dp"), None),
        P(None, ("groups", "dp"), None),
        P(None, "groups", "dp"),
        P(),
        P(None, "dp"),
        P("dp", None),
        P(None, "groups", "dp"),
        P(None, ("groups", "dp"), None),
    )
    return jax.shard_map(
        functools.partial(on_device, n=mesh.shape["dp"]),
        mesh=mesh,
        in_specs=placed,
        out_specs=(
            P(None, ("groups", "dp"), None),
            P(None, "groups", "dp"),
            P(None, "groups", "dp"),
            P(None, ("groups", "dp"), None),
        ),
        check_vma=False,
    )
```

time: 79.2 us -> 84.8 us (1.071)
  blocking collectives: 0 us -> 14.1 us
  starting transfers between devices: 27.4 us -> 20.9 us
  Pallas kernels: 38.6 us -> 32.7 us
  waiting for transfers between devices: 11.5 us -> 15.4 us
    all_to_all x0 -> x1, blocking collectives: none -> 14.1 us  [exchange(): lax.all_to_all(x, 'dp', split_axis=0, concat_axis=0, axis_index_groups=am...]
    ppermute x12 -> x6, starting transfers between devices: 18.8 us -> 8.84 us  [shift(): return lax.ppermute(x, 'dp', [(d, d ^ 4 * r) for d in range(n)]) if r else x]
    all_to_all x0 -> x2, waiting for transfers between devices: none -> 8 us  [exchange(): lax.all_to_all(x, 'dp', split_axis=0, concat_axis=0, axis_index_groups=am...]
    all_to_all x0 -> x2, starting transfers between devices: none -> 6.96 us  [exchange(): lax.all_to_all(x, 'dp', split_axis=0, concat_axis=0, axis_index_groups=am...]
    pallas_call x16 -> x11, Pallas kernels: 36.6 us -> 30.7 us  [call(): pl.pallas_call(kernel, out_shape=outs, in_specs=ins, out_specs=jax.tree.m...]
    ppermute x12 -> x6, waiting for transfers between devices: 8.79 us -> 5.17 us  [shift(): return lax.ppermute(x, 'dp', [(d, d ^ 4 * r) for d in range(n)]) if r else x]
    ppermute x13 -> x6, starting transfers between devices: 8.58 us -> 5.05 us  [swap(): return lax.ppermute(x, 'dp', [(d, d ^ bits) for d in range(n)])]
    ppermute x13 -> x6, waiting for transfers between devices: 2.71 us -> 2.22 us  [swap(): return lax.ppermute(x, 'dp', [(d, d ^ bits) for d in range(n)])]
  transfers between devices with their start and end apart: 25 -> 14, of which waited for: 5 -> 5; matrix products, arithmetic and copies ran while one was open for 0% -> 0% of each run, Pallas kernels for 30% -> 21%
where the time goes in v5:
time: 84.8 us; the launch traced here: 84.4 us
  Pallas kernels  32.7 us (39%)
  starting transfers between devices  20.9 us (25%)
  waiting for transfers between devices  15.4 us (18%)
  blocking collectives  14.1 us (17%)
  between operations  1.43 us (2%)
    pallas_call x11, Pallas kernels, call(): pl.pallas_call(kernel, out_shape=outs, in_specs=ins, out_specs=jax.tree.m...  30.7 us
    all_to_all x1, blocking collectives, exchange(): lax.all_to_all(x, 'dp', split_axis=0, concat_axis=0, axis_index_groups=am...  14.1 us
    ppermute x6, starting transfers between devices, shift(): return lax.ppermute(x, 'dp', [(d, d ^ 4 * r) for d in range(n)]) if r else x  8.84 us
    all_to_all x2, waiting for transfers between devices, exchange(): lax.all_to_all(x, 'dp', split_axis=0, concat_axis=0, axis_index_groups=am...  8 us
    all_to_all x2, starting transfers between devices, exchange(): lax.all_to_all(x, 'dp', split_axis=0, concat_axis=0, axis_index_groups=am...  6.96 us
    ppermute x6, waiting for transfers between devices, shift(): return lax.ppermute(x, 'dp', [(d, d ^ 4 * r) for d in range(n)]) if r else x  5.17 us
    ppermute x6, starting transfers between devices, swap(): return lax.ppermute(x, 'dp', [(d, d ^ bits) for d in range(n)])  5.05 us
    ppermute x6, waiting for transfers between devices, swap(): return lax.ppermute(x, 'dp', [(d, d ^ bits) for d in range(n)])  2.22 us
  transfers between devices with their start and end apart: 14, of which 5 were waited for; matrix products, arithmetic and copies ran while one was open for 0% of the time, Pallas kernels for 21%

profile of v5, /device:TPU:0, one launch (start us, length us, event | category | flops | bytes accessed | tf_op | source)
XLA Modules:
  0.0 84.4 jit_solution(10038683518074052558)
XLA Ops:
  1.3 2.0 %shard_map.129 = (bf16[16,16,128]{2,1,0:T(8,128)(2,1)S(1)}, f32[2,2,8192]{2,1,0:T(2,128)}, f32[2,32,512]{2,1,0:T(8,128)S(1)}, f32[16,512]{1,0:T(8,128)S(1)}, bf16[8,32,512]{2,1,0:T(8,128)(2,1)}) custom-call(s32[1]{0:T(128)S(6)} %sub.7.offset_ref, bf16[2,8192]{1,0:T(2,128)(2,1)} %bitcast.12, s32[2,64]{1,0:T(2,128)} %bitcast.15, f32[2,2,8192]{2,1,0:T(2,128)} %base_ref.1, ...), custom_call_target="tpu_custom_call" | custom-call | tf_op jit(solution)/shard_map/pallas_call | solution.py:354
  3.3 14.1 %all_to_all.15.arrived_ref = bf16[16,16,128]{2,1,0:T(8,128)(2,1)S(1)} all-to-all(bf16[16,16,128]{2,1,0:T(8,128)(2,1)S(1)} %get-tuple-element.41), channel_id=1, replica_groups=mesh['groups'=2,'dp'=16] {'dp'}, dimensions={0} | all-to-all | bytes 131072 | tf_op jit(solution)/shard_map/all_to_all | solution.py:318
  17.3 3.4 %all-to-all-start.2 = ((bf16[8,32,512]{2,1,0:T(8,128)(2,1)}), bf16[8,32,512]{2,1,0:T(8,128)(2,1)S(1)}, u32[]{:S(2)}, u32[]{:S(2)}) async-start(bf16[8,32,512]{2,1,0:T(8,128)(2,1)} %get-tuple-element.47), calls=%async_computation.2 | async-start | bytes 524288 | tf_op jit(solution)/shard_map/all_to_all | solution.py:318
  20.7 0.9 %shard_map.130 = (f32[2,32,512]{2,1,0:T(8,128)}, bf16[32,512]{1,0:T(8,128)(2,1)S(1)}, bf16[8,32,512]{2,1,0:T(8,128)(2,1)}) custom-call(bf16[16,16,128]{2,1,0:T(8,128)(2,1)S(1)} %all_to_all.15.arrived_ref, f32[2,32,512]{2,1,0:T(8,128)S(1)} %get-tuple-element.42.base_ref), custom_call_target="tpu_custom_call" | custom-call | tf_op jit(solution)/shard_map/pallas_call | solution.py:328
  21.6 8.0 %all-to-all-done.2.cot_ref = bf16[8,32,512]{2,1,0:T(8,128)(2,1)S(1)} async-done(((bf16[8,32,512]{2,1,0:T(8,128)(2,1)}), bf16[8,32,512]{2,1,0:T(8,128)(2,1)S(1)}, u32[]{:S(2)}, u32[]{:S(2)}) %all-to-all-start.2) | async-done | bytes 262176 | tf_op jit(solution)/shard_map/all_to_all | solution.py:318
  29.6 3.6 %all-to-all-start.1 = ((bf16[8,32,512]{2,1,0:T(8,128)(2,1)}), bf16[8,32,512]{2,1,0:T(8,128)(2,1)S(1)}, u32[]{:S(2)}, u32[]{:S(2)}) async-start(bf16[8,32,512]{2,1,0:T(8,128)(2,1)} %get-tuple-element.46), calls=%async_computation.1 | async-start | bytes 524288 | tf_op jit(solution)/shard_map/all_to_all | solution.py:318
  33.2 4.7 %shard_map.131 = (f32[896,32]{1,0:T(8,128)S(1)}, f32[32,512]{1,0:T(8,128)S(1)}) custom-call(s32[1]{0:T(128)} %bitcast.6.me_ref, bf16[8,32,512]{2,1,0:T(8,128)(2,1)S(1)} %all-to-all-done.2.cot_ref, bf16[896,8192]{1,0:T(8,128)(2,1)} %weight_ref.11), custom_call_target="tpu_custom_call" | custom-call | flops 234881024 | bytes 7340032 | tf_op jit(solution)/shard_map/pallas_call | solution.py:328
  37.9 4.7 %shard_map.132 = (f32[896,32]{1,0:T(8,128)S(1)}, f32[32,512]{1,0:T(8,128)S(1)}) custom-call(s32[1]{0:T(128)} %bitcast.6.me_ref, bf16[8,32,512]{2,1,0:T(8,128)(2,1)S(1)} %collective-permute-done.cot_ref, bf16[896,8192]{1,0:T(8,128)(2,1)} %weight_ref.11), custom_call_target="tpu_custom_call" | custom-call | flops 234881024 | bytes 7340032 | tf_op jit(solution)/shard_map/pallas_call | solution.py:328
  42.6 0.6 collective-permute-start.1
  43.2 4.6 %shard_map.133 = (f32[32,896]{1,0:T(8,128)S(1)}, f32[32,128]{1,0:T(8,128)S(1)}, f32[32,512]{1,0:T(8,128)S(1)}) custom-call(s32[1]{0:T(128)} %bitcast.6.me_ref, bf16[8,32,512]{2,1,0:T(8,128)(2,1)S(1)} %all-to-all-done.1.rest_ref, f32[16,512]{1,0:T(8,128)S(1)} %get-tuple-element.45.gain_ref, bf16[8192,896]{1,0:T(8,128)(2,1)} %weight_ref.9), custom_call_target="tpu_custom_call" | custom-call | flops 234881024 | bytes 7340032 | tf_op jit(solution)/shard_map/pallas_call | solution.py:328
  47.9 11.9 %shard_map.134 = (bf16[32,896]{1,0:T(8,128)(2,1)S(1)}, f32[32,512]{1,0:T(8,128)S(1)}, bf16[8,32,512]{2,1,0:T(8,128)(2,1)S(1)}, bf16[8,32,512]{2,1,0:T(8,128)(2,1)S(1)}) custom-call(s32[1]{0:T(128)} %bitcast.6.me_ref, bf16[8,32,512]{2,1,0:T(8,128)(2,1)S(1)} %collective-permute-done.1.rest_ref, f32[16,512]{1,0:T(8,128)S(1)} %get-tuple-element.45.gain_ref, ...), custom_call_target="tpu_custom_call" | custom-call | flops 704643072 | bytes 22020096 | tf_op jit(solution)/shard_map/pallas_call | solution.py:328
  59.9 1.5 %shard_map.137 = bf16[8,32,512]{2,1,0:T(8,128)(2,1)S(1)} custom-call(s32[1]{0:T(128)} %bitcast.6.me_ref, bf16[32,896]{1,0:T(8,128)(2,1)S(1)} %get-tuple-element.59.active_ref, bf16[896,8192]{1,0:T(8,128)(2,1)S(1)} %bitcast.10, bf16[8,32,512]{2,1,0:T(8,128)(2,1)S(1)} %get-tuple-element.61.after_ref), custom_call_target="tpu_custom_call" | custom-call | flops 234881024 | bytes 7340032 | tf_op jit(solution)/shard_map/pallas_call | solution.py:328
  61.9 2.1 %collective-permute-start.4 = (bf16[4,32,512]{2,1,0:T(8,128)(2,1)S(1)}, bf16[4,32,512]{2,1,0:T(8,128)(2,1)S(1)}, u32[]{:S(2)}, u32[]{:S(2)}) collective-permute-start(bf16[4,32,512]{2,1,0:T(8,128)(2,1)S(1)} %get-tuple-element.62.after_ref), channel_id=1, source_target_pairs={{0,2},{1,3},{2,0},{3,1},{4,6},{5,7},{6,4},{7,5},{8,10},{9,11},{10,... | collective-permute-start | bytes 393224 | tf_op jit(solution)/shard_map/ppermute | solution.py:315
  64.0 1.5 %shard_map.136.kept_ref = bf16[8,32,512]{2,1,0:T(8,128)(2,1)S(1)} custom-call(s32[1]{0:T(128)} %bitcast.6.me_ref, bf16[32,896]{1,0:T(8,128)(2,1)S(1)} %get-tuple-element.59.active_ref, bf16[896,8192]{1,0:T(8,128)(2,1)S(1)} %bitcast.10, bf16[4,32,512]{2,1,0:T(8,128)(2,1)S(1)} %get-tuple-element.62.after_ref), custom_call_target="tpu_custom_call" | custom-call | flops 234881024 | bytes 7340032 | tf_op jit(solution)/shard_map/pallas_call | solution.py:328
  65.5 2.2 %collective-permute-done.4.refs_1_ = bf16[4,32,512]{2,1,0:T(8,128)(2,1)S(1)} collective-permute-done((bf16[4,32,512]{2,1,0:T(8,128)(2,1)S(1)}, bf16[4,32,512]{2,1,0:T(8,128)(2,1)S(1)}, u32[]{:S(2)}, u32[]{:S(2)}) %collective-permute-start.4) | collective-permute-done | bytes 131104 | tf_op jit(solution)/shard_map/ppermute | solution.py:315
  67.8 1.8 %collective-permute-start.8 = (bf16[4,32,512]{2,1,0:T(8,128)(2,1)S(1)}, bf16[4,32,512]{2,1,0:T(8,128)(2,1)S(1)}, u32[]{:S(2)}, u32[]{:S(2)}) collective-permute-start(bf16[4,32,512]{2,1,0:T(8,128)(2,1)S(1)} %get-tuple-element.69), channel_id=1, source_target_pairs={{0,2},{1,3},{2,0},{3,1},{4,6},{5,7},{6,4},{7,5},{8,10},{9,11},{10,... | collective-permute-start | bytes 393224 | tf_op jit(solution)/shard_map/ppermute | solution.py:315
  69.6 1.5 %collective-permute-start.5 = (bf16[32,512]{1,0:T(8,128)(2,1)S(1)}, bf16[32,512]{1,0:T(8,128)(2,1)S(1)}, u32[]{:S(2)}, u32[]{:S(2)}) collective-permute-start(bf16[32,512]{1,0:T(8,128)(2,1)S(1)} %get-tuple-element.65), channel_id=1, source_target_pairs={{0,4},{1,5},{2,6},{3,7},{4,0},{5,1},{6,2},{7,3},{8,12},{9,13},{10,... | collective-permute-start | bytes 98312 | tf_op jit(solution)/shard_map/ppermute | solution.py:312
  71.1 2.4 %collective-permute-start.6 = (bf16[32,512]{1,0:T(8,128)(2,1)S(1)}, bf16[32,512]{1,0:T(8,128)(2,1)S(1)}, u32[]{:S(2)}, u32[]{:S(2)}) collective-permute-start(bf16[32,512]{1,0:T(8,128)(2,1)S(1)} %get-tuple-element.66), channel_id=1, source_target_pairs={{0,8},{1,9},{2,10},{3,11},{4,12},{5,13},{6,14},{7,15},{8,0},{9,1},... | collective-permute-start | bytes 98312 | tf_op jit(solution)/shard_map/ppermute | solution.py:312
  74.0 0.6 collective-permute-start.9
  74.7 3.3 %collective-permute-start.10 = (bf16[32,512]{1,0:T(8,128)(2,1)S(1)}, bf16[32,512]{1,0:T(8,128)(2,1)S(1)}, u32[]{:S(2)}, u32[]{:S(2)}) collective-permute-start(bf16[32,512]{1,0:T(8,128)(2,1)S(1)} %get-tuple-element.72), channel_id=1, source_target_pairs={{0,8},{1,9},{2,10},{3,11},{4,12},{5,13},{6,14},{7,15},{8,0},{9,1},... | collective-permute-start | bytes 98312 | tf_op jit(solution)/shard_map/ppermute | solution.py:312
  78.5 0.7 collective-permute-done.7.refs_7_
  79.1 0.7 collective-permute-done.10.refs_10_
  79.8 3.8 %collective-permute-done.11.refs_11_ = bf16[32,512]{1,0:T(8,128)(2,1)S(1)} collective-permute-done((bf16[32,512]{1,0:T(8,128)(2,1)S(1)}, bf16[32,512]{1,0:T(8,128)(2,1)S(1)}, u32[]{:S(2)}, u32[]{:S(2)}) %collective-permute-start.11) | collective-permute-done | bytes 32800 | tf_op jit(solution)/shard_map/ppermute | solution.py:312
  83.6 0.8 shard_map.140
  (28 shorter events, 1.9 us)
Async XLA Ops:
  17.3 12.3 %all-to-all-start.2 = ((bf16[8,32,512]{2,1,0:T(8,128)(2,1)}), bf16[8,32,512]{2,1,0:T(8,128)(2,1)S(1)}, u32[]{:S(2)}, u32[]{:S(2)}) async-start(bf16[8,32,512]{2,1,0:T(8,128)(2,1)} %get-tuple-element.47), calls=%async_computation.2 | async-start | bytes 524288 | tf_op jit(solution)/shard_map/all_to_all | solution.py:318
  29.6 13.0 %all-to-all-start.1 = ((bf16[8,32,512]{2,1,0:T(8,128)(2,1)}), bf16[8,32,512]{2,1,0:T(8,128)(2,1)S(1)}, u32[]{:S(2)}, u32[]{:S(2)}) async-start(bf16[8,32,512]{2,1,0:T(8,128)(2,1)} %get-tuple-element.46), calls=%async_computation.1 | async-start | bytes 524288 | tf_op jit(solution)/shard_map/all_to_all | solution.py:318
  33.2 4.7 %collective-permute-start = (bf16[8,32,512]{2,1,0:T(8,128)(2,1)S(1)}, bf16[8,32,512]{2,1,0:T(8,128)(2,1)S(1)}, u32[]{:S(2)}, u32[]{:S(2)}) collective-permute-start(bf16[8,32,512]{2,1,0:T(8,128)(2,1)S(1)} %all-to-all-done.2.cot_ref), channel_id=1, source_target_pairs={{0,1},{1,0},{2,3},{3,2},{4,5},{5,4},{6,7},{7,6},{8,9},{9,8},{10,11... | collective-permute-start | bytes 786440 | tf_op jit(solution)/shard_map/ppermute | solution.py:315
  42.6 5.2 %collective-permute-start.1 = (bf16[8,32,512]{2,1,0:T(8,128)(2,1)S(1)}, bf16[8,32,512]{2,1,0:T(8,128)(2,1)S(1)}, u32[]{:S(2)}, u32[]{:S(2)}) collective-permute-start(bf16[8,32,512]{2,1,0:T(8,128)(2,1)S(1)} %all-to-all-done.1.rest_ref), channel_id=1, source_target_pairs={{0,1},{1,0},{2,3},{3,2},{4,5},{5,4},{6,7},{7,6},{8,9},{9,8},{10,11... | collective-permute-start | bytes 786440 | tf_op jit(solution)/shard_map/ppermute | solution.py:315
  43.2 16.6 %slice-start = ((s8[14680064]{0:T(1024)(128)(4,1)}), s8[4194304]{0:T(1024)(128)(4,1)S(1)}, s32[]{:S(2)}) async-start(s8[14680064]{0:T(1024)(128)(4,1)} %bitcast.9), calls=%async_computation.3 | async-start | bytes 8388608
  43.2 16.6 %slice-start.1 = ((s8[14680064]{0:T(1024)(128)(4,1)}), s8[4194304]{0:T(1024)(128)(4,1)S(1)}, s32[]{:S(2)}) async-start(s8[14680064]{0:T(1024)(128)(4,1)} %bitcast.9), calls=%async_computation.4 | async-start | bytes 8388608
  47.8 12.0 %slice-start.2 = ((s8[14680064]{0:T(1024)(128)(4,1)}), s8[4194304]{0:T(1024)(128)(4,1)S(1)}, s32[]{:S(2)}) async-start(s8[14680064]{0:T(1024)(128)(4,1)} %bitcast.9), calls=%async_computation.5 | async-start | bytes 8388608
  47.8 12.0 %slice-start.3 = ((s8[14680064]{0:T(1024)(128)(4,1)}), s8[2097152]{0:T(1024)(128)(4,1)S(1)}, s32[]{:S(2)}) async-start(s8[14680064]{0:T(1024)(128)(4,1)} %bitcast.9), calls=%async_computation.6 | async-start | bytes 4194304
  59.7 2.1 %collective-permute-start.2 = (bf16[8,32,512]{2,1,0:T(8,128)(2,1)S(1)}, bf16[8,32,512]{2,1,0:T(8,128)(2,1)S(1)}, u32[]{:S(2)}, u32[]{:S(2)}) collective-permute-start(bf16[8,32,512]{2,1,0:T(8,128)(2,1)S(1)} %get-tuple-element.61.after_ref), channel_id=1, source_target_pairs={{0,1},{1,0},{2,3},{3,2},{4,5},{5,4},{6,7},{7,6},{8,9},{9,8},{10,11... | collective-permute-start | bytes 786440 | tf_op jit(solution)/shard_map/ppermute | solution.py:315
  59.8 23.8 %copy-start = (s32[2,1,64]{2,1,0:T(1,128)S(1)}, s32[2,1,64]{2,1,0:T(1,128)}, u32[]{:S(2)}) copy-start(s32[2,1,64]{2,1,0:T(1,128)} %param.19) | copy-start | bytes 1540
  61.3 4.1 %collective-permute-start.3 = (bf16[8,32,512]{2,1,0:T(8,128)(2,1)S(1)}, bf16[8,32,512]{2,1,0:T(8,128)(2,1)S(1)}, u32[]{:S(2)}, u32[]{:S(2)}) collective-permute-start(bf16[8,32,512]{2,1,0:T(8,128)(2,1)S(1)} %shard_map.137), channel_id=1, source_target_pairs={{0,1},{1,0},{2,3},{3,2},{4,5},{5,4},{6,7},{7,6},{8,9},{9,8},{10,11... | collective-permute-start | bytes 786440 | tf_op jit(solution)/shard_map/ppermute | solution.py:315
  61.9 5.8 %collective-permute-start.4 = (bf16[4,32,512]{2,1,0:T(8,128)(2,1)S(1)}, bf16[4,32,512]{2,1,0:T(8,128)(2,1)S(1)}, u32[]{:S(2)}, u32[]{:S(2)}) collective-permute-start(bf16[4,32,512]{2,1,0:T(8,128)(2,1)S(1)} %get-tuple-element.62.after_ref), channel_id=1, source_target_pairs={{0,2},{1,3},{2,0},{3,1},{4,6},{5,7},{6,4},{7,5},{8,10},{9,11},{10,... | collective-permute-start | bytes 393224 | tf_op jit(solution)/shard_map/ppermute | solution.py:315
  67.8 6.2 %collective-permute-start.8 = (bf16[4,32,512]{2,1,0:T(8,128)(2,1)S(1)}, bf16[4,32,512]{2,1,0:T(8,128)(2,1)S(1)}, u32[]{:S(2)}, u32[]{:S(2)}) collective-permute-start(bf16[4,32,512]{2,1,0:T(8,128)(2,1)S(1)} %get-tuple-element.69), channel_id=1, source_target_pairs={{0,2},{1,3},{2,0},{3,1},{4,6},{5,7},{6,4},{7,5},{8,10},{9,11},{10,... | collective-permute-start | bytes 393224 | tf_op jit(solution)/shard_map/ppermute | solution.py:315
  69.6 8.3 %collective-permute-start.5 = (bf16[32,512]{1,0:T(8,128)(2,1)S(1)}, bf16[32,512]{1,0:T(8,128)(2,1)S(1)}, u32[]{:S(2)}, u32[]{:S(2)}) collective-permute-start(bf16[32,512]{1,0:T(8,128)(2,1)S(1)} %get-tuple-element.65), channel_id=1, source_target_pairs={{0,4},{1,5},{2,6},{3,7},{4,0},{5,1},{6,2},{7,3},{8,12},{9,13},{10,... | collective-permute-start | bytes 98312 | tf_op jit(solution)/shard_map/ppermute | solution.py:312
  71.1 7.4 %collective-permute-start.6 = (bf16[32,512]{1,0:T(8,128)(2,1)S(1)}, bf16[32,512]{1,0:T(8,128)(2,1)S(1)}, u32[]{:S(2)}, u32[]{:S(2)}) collective-permute-start(bf16[32,512]{1,0:T(8,128)(2,1)S(1)} %get-tuple-element.66), channel_id=1, source_target_pairs={{0,8},{1,9},{2,10},{3,11},{4,12},{5,13},{6,14},{7,15},{8,0},{9,1},... | collective-permute-start | bytes 98312 | tf_op jit(solution)/shard_map/ppermute | solution.py:312
  73.4 5.7 %collective-permute-start.7 = (bf16[32,512]{1,0:T(8,128)(2,1)S(1)}, bf16[32,512]{1,0:T(8,128)(2,1)S(1)}, u32[]{:S(2)}, u32[]{:S(2)}) collective-permute-start(bf16[32,512]{1,0:T(8,128)(2,1)S(1)} %get-tuple-element.67), channel_id=1, source_target_pairs={{0,12},{1,13},{2,14},{3,15},{4,8},{5,9},{6,10},{7,11},{8,4},{9,5},... | collective-permute-start | bytes 98312 | tf_op jit(solution)/shard_map/ppermute | solution.py:312
  74.0 5.1 %collective-permute-start.9 = (bf16[32,512]{1,0:T(8,128)(2,1)S(1)}, bf16[32,512]{1,0:T(8,128)(2,1)S(1)}, u32[]{:S(2)}, u32[]{:S(2)}) collective-permute-start(bf16[32,512]{1,0:T(8,128)(2,1)S(1)} %get-tuple-element.71), channel_id=1, source_target_pairs={{0,4},{1,5},{2,6},{3,7},{4,0},{5,1},{6,2},{7,3},{8,12},{9,13},{10,... | collective-permute-start | bytes 98312 | tf_op jit(solution)/shard_map/ppermute | solution.py:312
  74.7 5.2 %collective-permute-start.10 = (bf16[32,512]{1,0:T(8,128)(2,1)S(1)}, bf16[32,512]{1,0:T(8,128)(2,1)S(1)}, u32[]{:S(2)}, u32[]{:S(2)}) collective-permute-start(bf16[32,512]{1,0:T(8,128)(2,1)S(1)} %get-tuple-element.72), channel_id=1, source_target_pairs={{0,8},{1,9},{2,10},{3,11},{4,12},{5,13},{6,14},{7,15},{8,0},{9,1},... | collective-permute-start | bytes 98312 | tf_op jit(solution)/shard_map/ppermute | solution.py:312
  77.9 5.7 %collective-permute-start.11 = (bf16[32,512]{1,0:T(8,128)(2,1)S(1)}, bf16[32,512]{1,0:T(8,128)(2,1)S(1)}, u32[]{:S(2)}, u32[]{:S(2)}) collective-permute-start(bf16[32,512]{1,0:T(8,128)(2,1)S(1)} %get-tuple-element.73), channel_id=1, source_target_pairs={{0,12},{1,13},{2,14},{3,15},{4,8},{5,9},{6,10},{7,11},{8,4},{9,5},... | collective-permute-start | bytes 98312 | tf_op jit(solution)/shard_map/ppermute | solution.py:312

commit v6 on v4

--- a/solution.py
+++ b/solution.py
@@ -10,6 +10,8 @@
 clip_top = 448.0
 eps = 1e-05
 LANES = 128
+STAGE = 7
+FLOPS_PER_MICRO = 1.15e9
 f32 = jnp.float32
 bf16 = jnp.bfloat16
 VMEM = pl.BlockSpec(memory_space=pltpu.VMEM)
@@ -149,29 +151,25 @@
     return dot_nt(rows[:, :middle], tokens[:, :middle]) + dot_nt(rows[:, middle:], tokens[:, middle:])
 
 
-def grad_active_kernel(part, me_ref, cot_ref, weight_ref, acc_ref, own_ref, held_ref, piece_ref, sems):
+def grad_active_kernel(part, me_ref, cot_ref, weight_ref, acc_ref, own_ref, piece_ref):
     quarter, _, width = cot_ref.shape
     me = me_ref[0]
-    owners = [owner_of(me, 4 * quarter, part, k) for k in range(quarter)]
-    copies = []
-    for k, owner in enumerate(owners):
-        columns = pl.ds(pl.multiple_of(owner * width, width), width)
-        copies.append(pltpu.make_async_copy(weight_ref.at[:, columns], held_ref.at[k], sems.at[k]))
-        copies[-1].start()
     own_ref[...] = jnp.zeros_like(own_ref)
-    for k, owner in enumerate(owners):
+    for k in range(quarter):
+        owner = owner_of(me, 4 * quarter, part, k)
         piece_ref[...] = cot_ref[k].astype(f32)
         own_rows(piece_ref, own_ref, me, owner)
-    for k, copy in enumerate(copies):
-        copy.wait()
-        terms = dot_by_halves(held_ref[k], cot_ref[k])
+        columns = pl.ds(pl.multiple_of(owner * width, width), width)
+        terms = dot_by_halves(weight_ref[:, columns], cot_ref[k])
         acc_ref[...] = terms if k == 0 else acc_ref[...] + terms
 
 
-def up_part(part, me, rest_ref, gain_ref, held_ref, waits, acc_ref, square_ref, own_ref, piece_ref):
+def up_kernel(
+    part, me_ref, rest_ref, gain_ref, weight_ref, acc_ref, square_ref, own_ref, piece_ref
+):
     quarter, _, width = rest_ref.shape
+    me = me_ref[0]
     own_ref[...] = jnp.zeros_like(own_ref)
-    scaled = []
     for k in range(quarter):
         owner = owner_of(me, 4 * quarter, part, k)
         piece = rest_ref[k].astype(f32)
@@ -180,48 +178,20 @@
         squares = piece * piece
         total = sum(squares[:, c * LANES : (c + 1) * LANES] for c in range(width // LANES))
         square_ref[...] = total if k == 0 else square_ref[...] + total
-        scaled.append((piece * gain_ref[pl.ds(owner, 1), :]).astype(bf16))
-    for k in range(quarter):
-        waits[k].wait()
-        terms = jnp.dot(scaled[k], held_ref[k], preferred_element_type=f32)
+        scaled = (piece * gain_ref[pl.ds(owner, 1), :]).astype(bf16)
+        rows = pl.ds(pl.multiple_of(owner * width, width), width)
+        terms = jnp.dot(scaled, weight_ref[rows, :], preferred_element_type=f32)
         acc_ref[...] = terms if k == 0 else acc_ref[...] + terms
-
-
-def share_copies(part, me, weight_ref, held_ref, sems, base=0):
-    quarter, width, _ = held_ref.shape
-    quarter = min(quarter, weight_ref.shape[0] // width // 4)
-    n = 4 * quarter
-    copies = []
-    for k in range(quarter):
-        rows = pl.ds(pl.multiple_of(owner_of(me, n, part, k) * width, width), width)
-        copies.append(
-            pltpu.make_async_copy(weight_ref.at[rows], held_ref.at[base + k], sems.at[base + k])
-        )
-        copies[-1].start()
-    return copies
-
-
-def up_kernel(
-    part, me_ref, rest_ref, gain_ref, weight_ref,
-    acc_ref, square_ref, own_ref, held_ref, piece_ref, sems,
-):
-    me = me_ref[0]
-    copies = share_copies(part, me, weight_ref, held_ref, sems)
-    up_part(part, me, rest_ref, gain_ref, held_ref, copies, acc_ref, square_ref, own_ref, piece_ref)
 
 
 def middle_kernel(me_ref, rest_ref, gain_ref, weight_ref, *refs):
     ins, refs = refs[:10], refs[10:]
-    active_ref, own_ref, send_ref, keep_ref, acc_ref, square_ref, piece_ref, held_ref, rows_ref, sems = refs
+    active_ref, own_ref, send_ref, keep_ref, acc_ref, square_ref, piece_ref, rows_ref = refs
     quarter, tokens, width = rest_ref.shape
     half, n, chunks = 2 * quarter, 4 * quarter, width // LANES
     width_all = weight_ref.shape[0]
     me = me_ref[0]
-    parts = (3, 0, 1, 2)
-    copies = []
-    for i, part in enumerate(parts):
-        copies += share_copies(part, me, weight_ref, held_ref, sems, i * quarter)
-    up_part(3, me, rest_ref, gain_ref, held_ref, copies, acc_ref, square_ref, own_ref, piece_ref)
+    up_kernel(3, me_ref, rest_ref, gain_ref, weight_ref, acc_ref, square_ref, own_ref, piece_ref)
     product = acc_ref[...] + (ins[0][...] + ins[1][...] + ins[2][...])
     squares = square_ref[...] + (ins[3][...] + ins[4][...] + ins[5][...])
     total = jnp.sum(squares, axis=1, keepdims=True)
@@ -230,18 +200,14 @@
     active_ref[...] = (hidden * sigma).astype(bf16)
     grad_active = (ins[6][...] + ins[7][...] + (ins[8][...] + ins[9][...])).T
     gh = (grad_active * sigma * (1.0 + hidden * (1.0 - sigma))).astype(bf16)
-    for i, part in enumerate(parts):
-        for k in range(quarter):
-            at = i * quarter + k
-            if i > 0:
-                copies[at].wait()
-            share = owner_of(me, n, part, k)
-            terms = dot_by_halves(held_ref[at], gh).T
-            for p in range(2):
-                for c in range(chunks):
-                    rows_ref[c, pl.ds(p * n + share, n, stride=tokens), :] = terms[
-                        p * n : (p + 1) * n, c * LANES : (c + 1) * LANES
-                    ]
+    for share in range(n):
+        block = weight_ref[share * width : (share + 1) * width, :]
+        terms = dot_by_halves(block, gh).T
+        for p in range(2):
+            for c in range(chunks):
+                rows_ref[c, pl.ds(p * n + share, n, stride=tokens), :] = terms[
+                    p * n : (p + 1) * n, c * LANES : (c + 1) * LANES
+                ]
     core = lax.rem(me, 2)
     for k in range(half):
         keep_at = pl.multiple_of((2 * k + core) * tokens, tokens)
@@ -347,18 +313,16 @@
     share_shape, hidden_shape = (tokens, width), (tokens, hidden_dev)
     line_shape = (quarter, tokens, width)
 
-    def call(kernel, outs, ins, args, scratch=(), cost=0, grant=8):
+    def call(kernel, outs, ins, args, scratch=(), micros=0.5):
         return pl.pallas_call(
             kernel,
             out_shape=outs,
             in_specs=ins,
             out_specs=jax.tree.map(lambda _: VMEM, outs),
             scratch_shapes=list(scratch),
-            compiler_params=params(grant),
+            compiler_params=params(8),
             cost_estimate=pl.CostEstimate(
-                flops=int(cost * tokens * width_all * hidden_dev),
-                bytes_accessed=int(cost * width_all * hidden_dev),
-                transcendentals=0,
+                flops=int(micros * FLOPS_PER_MICRO), bytes_accessed=0, transcendentals=0
             ),
         )(*args)
 
@@ -397,13 +361,13 @@
         (struct(line_shape, bf16),) + (struct((quarter, rows, LANES), bf16),) * 4,
         [SMEM] + [VMEM] * quarter,
         [me_in, *packed],
+        micros=STAGE,
     )
     blocks = [blocks[0]] + [swap(blocks[e], e) for e in range(1, 4)]
     cot_row = swap(cot_line, 2)
     cots = [cot_line, cot_row, swap(cot_line, 1), swap(cot_row, 1)]
 
     ANY = pl.BlockSpec(memory_space=pl.ANY)
-    sems = lambda count: pltpu.SemaphoreType.DMA((count,))
     share_f32 = struct(share_shape, f32)
     sums = (struct(hidden_shape, f32), struct((tokens, LANES), f32))
 
@@ -411,30 +375,20 @@
         return call(
             functools.partial(grad_active_kernel, part),
             (struct((hidden_dev, tokens), f32), share_f32),
-            [SMEM, VMEM, ANY],
-            [me_in, cots[part], hbm(down_weight)],
-            [
-                pltpu.VMEM((quarter, hidden_dev, width), bf16),
-                pltpu.VMEM(share_shape, f32),
-                sems(quarter),
-            ],
-            cost=0.5,
-            grant=12,
+            [SMEM, VMEM, VMEM],
+            [me_in, cots[part], down_weight],
+            [pltpu.VMEM(share_shape, f32)],
+            micros=1.6,
         )
 
     def up_product_part(part):
         return call(
             functools.partial(up_kernel, part),
             sums + (share_f32,),
-            [SMEM, VMEM, VMEM, ANY],
-            [me_in, rests[part], gain, hbm(up_weight)],
-            [
-                pltpu.VMEM((quarter, width, hidden_dev), bf16),
-                pltpu.VMEM(share_shape, f32),
-                sems(quarter),
-            ],
-            cost=0.5,
-            grant=12,
+            [SMEM] + [VMEM] * 3,
+            [me_in, rests[part], gain, up_weight],
+            [pltpu.VMEM(share_shape, f32)],
+            micros=1.2,
         )
 
     together = lax.optimization_barrier
@@ -447,6 +401,7 @@
         [SMEM] + [VMEM] * 5,
         [me_in, *blocks, received],
         [pltpu.VMEM((n * rows, LANES), f32), pltpu.VMEM((2 * width // LANES, 2 * n, LANES), f32)],
+        micros=STAGE,
     )
     lines = [shift(share, r) for r in range(quarter)]
     grads.append(grad_active_part(1))
@@ -468,17 +423,14 @@
     active, own, grad_send, grad_keep = call(
         middle_kernel,
         (struct(hidden_shape, bf16), share_f32, half_out, half_out),
-        [SMEM, VMEM, VMEM, ANY] + [VMEM] * 10,
-        [me_in, rests[3], gain, hbm(up_weight), *accs, *squares, *gas],
+        [SMEM] + [VMEM] * 13,
+        [me_in, rests[3], gain, up_weight, *accs, *squares, *gas],
         [pltpu.VMEM(x.shape, x.dtype) for x in sums]
         + [
             pltpu.VMEM(share_shape, f32),
-            pltpu.VMEM((n, width, hidden_dev), bf16),
             pltpu.VMEM((width // LANES, n * tokens, LANES), f32),
-            sems(n),
         ],
-        cost=2.5,
-        grant=24,
+        micros=6.5,
     )
     owns.append(own)
 
@@ -488,7 +440,7 @@
             half_out,
             [SMEM] + [VMEM] * 2 + [ANY],
             [me_in, active, down_weight, after],
-            cost=1,
+            micros=1.5,
         )
 
     pair_out = (struct(line_shape, bf16),) * 2

time: 79.2 us -> 66.5 us (0.84)
  Pallas kernels: 38.6 us -> 19.2 us
  waiting for transfers between devices: 11.5 us -> 17.2 us
    pallas_call x16, Pallas kernels: 36.6 us -> 17.1 us  [call(): pl.pallas_call(kernel, out_shape=outs, in_specs=ins, out_specs=jax.tree.m...]
    ppermute x13, waiting for transfers between devices: 2.71 us -> 6.34 us  [swap(): return lax.ppermute(x, 'dp', [(d, d ^ bits) for d in range(n)])]
    ppermute x12, waiting for transfers between devices: 8.79 us -> 10.8 us  [shift(): return lax.ppermute(x, 'dp', [(d, d ^ 4 * r) for d in range(n)]) if r else x]
  transfers between devices with their start and end apart: 25 -> 25, of which waited for: 5 -> 9; matrix products, arithmetic and copies ran while one was open for 0% -> 0% of each run, Pallas kernels for 30% -> 16%
where the time goes in v6:
time: 66.5 us; the launch traced here: 66.4 us
  starting transfers between devices  28 us (42%)
  Pallas kernels  19.2 us (29%)
  waiting for transfers between devices  17.2 us (26%)
  between operations  1.47 us (2%)
    ppermute x12, starting transfers between devices, shift(): return lax.ppermute(x, 'dp', [(d, d ^ 4 * r) for d in range(n)]) if r else x  18.8 us
    pallas_call x16, Pallas kernels, call(): pl.pallas_call(kernel, out_shape=outs, in_specs=ins, out_specs=jax.tree.m...  17.1 us
    ppermute x12, waiting for transfers between devices, shift(): return lax.ppermute(x, 'dp', [(d, d ^ 4 * r) for d in range(n)]) if r else x  10.8 us
    ppermute x13, starting transfers between devices, swap(): return lax.ppermute(x, 'dp', [(d, d ^ bits) for d in range(n)])  9.15 us
    ppermute x13, waiting for transfers between devices, swap(): return lax.ppermute(x, 'dp', [(d, d ^ bits) for d in range(n)])  6.34 us
    pallas_call x1, Pallas kernels, on_device(): pl.pallas_call(send_kernel, out_shape=outs, grid=(1,), in_specs=[SMEM, SM...  2.08 us
  transfers between devices with their start and end apart: 25, of which 9 were waited for; matrix products, arithmetic and copies ran while one was open for 0% of the time, Pallas kernels for 16%

profile of v6, /device:TPU:0, one launch (start us, length us, event | category | flops | bytes accessed | tf_op | source)
XLA Modules:
  0.0 66.4 jit_solution(10197916173557016085)
XLA Ops:
  1.3 2.1 %shard_map.129 = (f32[2,2,8192]{2,1,0:T(2,128)}, f32[2,32,512]{2,1,0:T(8,128)S(1)}, f32[16,512]{1,0:T(8,128)S(1)}, bf16[32,768]{1,0:T(8,128)(2,1)S(1)}, bf16[32,...) custom-call(s32[1]{0:T(128)} %bitcast.me_ref, s32[1]{0:T(128)S(6)} %sub.7.offset_ref, ...), custom_call_target="tpu_custom_call" | custom-call | tf_op jit(solution)/shard_map/pallas_call | solution.py:340
  3.4 3.0 %collective-permute-start = (bf16[32,768]{1,0:T(8,128)(2,1)S(1)}, bf16[32,768]{1,0:T(8,128)(2,1)S(1)}, u32[]{:S(2)}, u32[]{:S(2)}) collective-permute-start(bf16[32,768]{1,0:T(8,128)(2,1)S(1)} %get-tuple-element.73), channel_id=1, source_target_pairs={{0,4},{1,5},{2,6},{3,7},{4,0},{5,1},{6,2},{7,3},{8,12},{9,13},{10,... | collective-permute-start | bytes 147464 | tf_op jit(solution)/shard_map/ppermute | solution.py:307
  6.4 2.6 %collective-permute-start.1 = (bf16[32,768]{1,0:T(8,128)(2,1)S(1)}, bf16[32,768]{1,0:T(8,128)(2,1)S(1)}, u32[]{:S(2)}, u32[]{:S(2)}) collective-permute-start(bf16[32,768]{1,0:T(8,128)(2,1)S(1)} %get-tuple-element.74), channel_id=1, source_target_pairs={{0,8},{1,9},{2,10},{3,11},{4,12},{5,13},{6,14},{7,15},{8,0},{9,1},... | collective-permute-start | bytes 147464 | tf_op jit(solution)/shard_map/ppermute | solution.py:307
  9.0 3.3 %collective-permute-done.1.refs_2_ = bf16[32,768]{1,0:T(8,128)(2,1)S(1)} collective-permute-done((bf16[32,768]{1,0:T(8,128)(2,1)S(1)}, bf16[32,768]{1,0:T(8,128)(2,1)S(1)}, u32[]{:S(2)}, u32[]{:S(2)}) %collective-permute-start.1) | collective-permute-done | bytes 49184 | tf_op jit(solution)/shard_map/ppermute | solution.py:307
  12.3 2.6 %collective-permute-done.2.refs_3_ = bf16[32,768]{1,0:T(8,128)(2,1)S(1)} collective-permute-done((bf16[32,768]{1,0:T(8,128)(2,1)S(1)}, bf16[32,768]{1,0:T(8,128)(2,1)S(1)}, u32[]{:S(2)}, u32[]{:S(2)}) %collective-permute-start.2) | collective-permute-done | bytes 49184 | tf_op jit(solution)/shard_map/ppermute | solution.py:307
  15.0 1.6 %collective-permute-start.9 = (bf16[4,32,512]{2,1,0:T(8,128)(2,1)S(1)}, bf16[4,32,512]{2,1,0:T(8,128)(2,1)S(1)}, u32[]{:S(2)}, u32[]{:S(2)}) collective-permute-start(bf16[4,32,512]{2,1,0:T(8,128)(2,1)S(1)} %get-tuple-element.80.cot_ref), channel_id=1, source_target_pairs={{0,2},{1,3},{2,0},{3,1},{4,6},{5,7},{6,4},{7,5},{8,10},{9,11},{10,... | collective-permute-start | bytes 393224 | tf_op jit(solution)/shard_map/ppermute | solution.py:310
  20.2 1.3 %collective-permute-done.4.b2 = bf16[4,16,128]{2,1,0:T(8,128)(2,1)S(1)} collective-permute-done((bf16[4,16,128]{2,1,0:T(8,128)(2,1)S(1)}, bf16[4,16,128]{2,1,0:T(8,128)(2,1)S(1)}, u32[]{:S(2)}, u32[]{:S(2)}) %collective-permute-start.4) | collective-permute-done | bytes 16416 | tf_op jit(solution)/shard_map/ppermute | solution.py:310
  22.9 3.6 %collective-permute-start.6 = (bf16[32,512]{1,0:T(8,128)(2,1)S(1)}, bf16[32,512]{1,0:T(8,128)(2,1)S(1)}, u32[]{:S(2)}, u32[]{:S(2)}) collective-permute-start(bf16[32,512]{1,0:T(8,128)(2,1)S(1)} %get-tuple-element.93.share_ref), channel_id=1, source_target_pairs={{0,4},{1,5},{2,6},{3,7},{4,0},{5,1},{6,2},{7,3},{8,12},{9,13},{10,... | collective-permute-start | bytes 98312 | tf_op jit(solution)/shard_map/ppermute | solution.py:307
  26.6 1.2 %shard_map.133 = (f32[896,32]{1,0:T(8,128)S(1)}, f32[32,512]{1,0:T(8,128)S(1)}) custom-call(s32[1]{0:T(128)} %bitcast.me_ref, bf16[4,32,512]{2,1,0:T(8,128)(2,1)S(1)} %collective-permute-done.9.cot_ref, bf16[896,8192]{1,0:T(8,128)(2,1)S(1)} %bitcast.14), custom_call_target="tpu_custom_call" | custom-call | flops 1840000000 | tf_op jit(solution)/shard_map/pallas_call | solution.py:317
  28.6 1.6 %collective-permute-start.10 = (bf16[4,32,512]{2,1,0:T(8,128)(2,1)S(1)}, bf16[4,32,512]{2,1,0:T(8,128)(2,1)S(1)}, u32[]{:S(2)}, u32[]{:S(2)}) collective-permute-start(bf16[4,32,512]{2,1,0:T(8,128)(2,1)S(1)} %pad_maximum_fusion.rest_ref), channel_id=1, source_target_pairs={{0,2},{1,3},{2,0},{3,1},{4,6},{5,7},{6,4},{7,5},{8,10},{9,11},{10,... | collective-permute-start | bytes 393224 | tf_op jit(solution)/shard_map/ppermute | solution.py:310
  32.3 2.2 %collective-permute-done.10.rest_ref = bf16[4,32,512]{2,1,0:T(8,128)(2,1)S(1)} collective-permute-done((bf16[4,32,512]{2,1,0:T(8,128)(2,1)S(1)}, bf16[4,32,512]{2,1,0:T(8,128)(2,1)S(1)}, u32[]{:S(2)}, u32[]{:S(2)}) %collective-permute-start.10) | collective-permute-done | bytes 131104 | tf_op jit(solution)/shard_map/ppermute | solution.py:310
  37.2 5.4 %shard_map.139 = (bf16[32,896]{1,0:T(8,128)(2,1)S(1)}, f32[32,512]{1,0:T(8,128)S(1)}, bf16[8,32,512]{2,1,0:T(8,128)(2,1)S(1)}, bf16[8,32,512]{2,1,0:T(8,128)(2,1)S(1)}) custom-call(s32[1]{0:T(128)} %bitcast.me_ref, bf16[4,32,512]{2,1,0:T(8,128)(2,1)S(1)} %collective-permute-done.13.rest_ref, f32[16,512]{1,0:T(8,128)S(1)} %get-tuple-element.90.gain_ref, ...), custom_call_target="tpu_custom_call" | custom-call | flops 7474999808 | tf_op jit(solution)/shard_map/pallas_call | solution.py:317
  43.2 1.5 %shard_map.142 = bf16[8,32,512]{2,1,0:T(8,128)(2,1)S(1)} custom-call(s32[1]{0:T(128)} %bitcast.me_ref, bf16[32,896]{1,0:T(8,128)(2,1)S(1)} %get-tuple-element.121.active_ref, bf16[896,8192]{1,0:T(8,128)(2,1)S(1)} %bitcast.14, bf16[8,32,512]{2,1,0:T(8,128)(2,1)S(1)} %get-tuple-element.123.after_ref), custom_call_target="tpu_custom_call" | custom-call | flops 1724999936 | tf_op jit(solution)/shard_map/pallas_call | solution.py:317
  44.8 1.6 %collective-permute-start.17 = (bf16[4,32,512]{2,1,0:T(8,128)(2,1)S(1)}, bf16[4,32,512]{2,1,0:T(8,128)(2,1)S(1)}, u32[]{:S(2)}, u32[]{:S(2)}) collective-permute-start(bf16[4,32,512]{2,1,0:T(8,128)(2,1)S(1)} %get-tuple-element.124.after_ref), channel_id=1, source_target_pairs={{0,2},{1,3},{2,0},{3,1},{4,6},{5,7},{6,4},{7,5},{8,10},{9,11},{10,... | collective-permute-start | bytes 393224 | tf_op jit(solution)/shard_map/ppermute | solution.py:310
  46.4 1.5 %shard_map.141.kept_ref = bf16[8,32,512]{2,1,0:T(8,128)(2,1)S(1)} custom-call(s32[1]{0:T(128)} %bitcast.me_ref, bf16[32,896]{1,0:T(8,128)(2,1)S(1)} %get-tuple-element.121.active_ref, bf16[896,8192]{1,0:T(8,128)(2,1)S(1)} %bitcast.14, bf16[4,32,512]{2,1,0:T(8,128)(2,1)S(1)} %get-tuple-element.124.after_ref), custom_call_target="tpu_custom_call" | custom-call | flops 1724999936 | tf_op jit(solution)/shard_map/pallas_call | solution.py:317
  47.9 2.9 %collective-permute-done.17.refs_1_ = bf16[4,32,512]{2,1,0:T(8,128)(2,1)S(1)} collective-permute-done((bf16[4,32,512]{2,1,0:T(8,128)(2,1)S(1)}, bf16[4,32,512]{2,1,0:T(8,128)(2,1)S(1)}, u32[]{:S(2)}, u32[]{:S(2)}) %collective-permute-start.17) | collective-permute-done | bytes 131104 | tf_op jit(solution)/shard_map/ppermute | solution.py:310
  50.9 1.6 %collective-permute-start.21 = (bf16[4,32,512]{2,1,0:T(8,128)(2,1)S(1)}, bf16[4,32,512]{2,1,0:T(8,128)(2,1)S(1)}, u32[]{:S(2)}, u32[]{:S(2)}) collective-permute-start(bf16[4,32,512]{2,1,0:T(8,128)(2,1)S(1)} %get-tuple-element.131), channel_id=1, source_target_pairs={{0,2},{1,3},{2,0},{3,1},{4,6},{5,7},{6,4},{7,5},{8,10},{9,11},{10,... | collective-permute-start | bytes 393224 | tf_op jit(solution)/shard_map/ppermute | solution.py:310
  52.4 2.0 %collective-permute-start.18 = (bf16[32,512]{1,0:T(8,128)(2,1)S(1)}, bf16[32,512]{1,0:T(8,128)(2,1)S(1)}, u32[]{:S(2)}, u32[]{:S(2)}) collective-permute-start(bf16[32,512]{1,0:T(8,128)(2,1)S(1)} %get-tuple-element.127), channel_id=1, source_target_pairs={{0,4},{1,5},{2,6},{3,7},{4,0},{5,1},{6,2},{7,3},{8,12},{9,13},{10,... | collective-permute-start | bytes 98312 | tf_op jit(solution)/shard_map/ppermute | solution.py:307
  55.4 1.5 %collective-permute-start.20 = (bf16[32,512]{1,0:T(8,128)(2,1)S(1)}, bf16[32,512]{1,0:T(8,128)(2,1)S(1)}, u32[]{:S(2)}, u32[]{:S(2)}) collective-permute-start(bf16[32,512]{1,0:T(8,128)(2,1)S(1)} %get-tuple-element.129), channel_id=1, source_target_pairs={{0,12},{1,13},{2,14},{3,15},{4,8},{5,9},{6,10},{7,11},{8,4},{9,5},... | collective-permute-start | bytes 98312 | tf_op jit(solution)/shard_map/ppermute | solution.py:307
  56.9 1.2 %collective-permute-start.22 = (bf16[32,512]{1,0:T(8,128)(2,1)S(1)}, bf16[32,512]{1,0:T(8,128)(2,1)S(1)}, u32[]{:S(2)}, u32[]{:S(2)}) collective-permute-start(bf16[32,512]{1,0:T(8,128)(2,1)S(1)} %get-tuple-element.133), channel_id=1, source_target_pairs={{0,4},{1,5},{2,6},{3,7},{4,0},{5,1},{6,2},{7,3},{8,12},{9,13},{10,... | collective-permute-start | bytes 98312 | tf_op jit(solution)/shard_map/ppermute | solution.py:307
  58.1 1.7 %collective-permute-start.23 = (bf16[32,512]{1,0:T(8,128)(2,1)S(1)}, bf16[32,512]{1,0:T(8,128)(2,1)S(1)}, u32[]{:S(2)}, u32[]{:S(2)}) collective-permute-start(bf16[32,512]{1,0:T(8,128)(2,1)S(1)} %get-tuple-element.134), channel_id=1, source_target_pairs={{0,8},{1,9},{2,10},{3,11},{4,12},{5,13},{6,14},{7,15},{8,0},{9,1},... | collective-permute-start | bytes 98312 | tf_op jit(solution)/shard_map/ppermute | solution.py:307
  59.8 1.5 %collective-permute-start.24 = (bf16[32,512]{1,0:T(8,128)(2,1)S(1)}, bf16[32,512]{1,0:T(8,128)(2,1)S(1)}, u32[]{:S(2)}, u32[]{:S(2)}) collective-permute-start(bf16[32,512]{1,0:T(8,128)(2,1)S(1)} %get-tuple-element.135), channel_id=1, source_target_pairs={{0,12},{1,13},{2,14},{3,15},{4,8},{5,9},{6,10},{7,11},{8,4},{9,5},... | collective-permute-start | bytes 98312 | tf_op jit(solution)/shard_map/ppermute | solution.py:307
  61.3 2.0 %collective-permute-done.23.refs_14_ = bf16[32,512]{1,0:T(8,128)(2,1)S(1)} collective-permute-done((bf16[32,512]{1,0:T(8,128)(2,1)S(1)}, bf16[32,512]{1,0:T(8,128)(2,1)S(1)}, u32[]{:S(2)}, u32[]{:S(2)}) %collective-permute-start.23) | collective-permute-done | bytes 32800 | tf_op jit(solution)/shard_map/ppermute | solution.py:307
  63.3 2.3 %collective-permute-done.24.refs_15_ = bf16[32,512]{1,0:T(8,128)(2,1)S(1)} collective-permute-done((bf16[32,512]{1,0:T(8,128)(2,1)S(1)}, bf16[32,512]{1,0:T(8,128)(2,1)S(1)}, u32[]{:S(2)}, u32[]{:S(2)}) %collective-permute-start.24) | collective-permute-done | bytes 32800 | tf_op jit(solution)/shard_map/ppermute | solution.py:307
  (64 shorter events, 13.3 us)
Async XLA Ops:
  3.4 5.6 %collective-permute-start = (bf16[32,768]{1,0:T(8,128)(2,1)S(1)}, bf16[32,768]{1,0:T(8,128)(2,1)S(1)}, u32[]{:S(2)}, u32[]{:S(2)}) collective-permute-start(bf16[32,768]{1,0:T(8,128)(2,1)S(1)} %get-tuple-element.73), channel_id=1, source_target_pairs={{0,4},{1,5},{2,6},{3,7},{4,0},{5,1},{6,2},{7,3},{8,12},{9,13},{10,... | collective-permute-start | bytes 147464 | tf_op jit(solution)/shard_map/ppermute | solution.py:307
  6.4 5.9 %collective-permute-start.1 = (bf16[32,768]{1,0:T(8,128)(2,1)S(1)}, bf16[32,768]{1,0:T(8,128)(2,1)S(1)}, u32[]{:S(2)}, u32[]{:S(2)}) collective-permute-start(bf16[32,768]{1,0:T(8,128)(2,1)S(1)} %get-tuple-element.74), channel_id=1, source_target_pairs={{0,8},{1,9},{2,10},{3,11},{4,12},{5,13},{6,14},{7,15},{8,0},{9,1},... | collective-permute-start | bytes 147464 | tf_op jit(solution)/shard_map/ppermute | solution.py:307
  9.0 5.9 %collective-permute-start.2 = (bf16[32,768]{1,0:T(8,128)(2,1)S(1)}, bf16[32,768]{1,0:T(8,128)(2,1)S(1)}, u32[]{:S(2)}, u32[]{:S(2)}) collective-permute-start(bf16[32,768]{1,0:T(8,128)(2,1)S(1)} %get-tuple-element.75), channel_id=1, source_target_pairs={{0,12},{1,13},{2,14},{3,15},{4,8},{5,9},{6,10},{7,11},{8,4},{9,5},... | collective-permute-start | bytes 147464 | tf_op jit(solution)/shard_map/ppermute | solution.py:307
  14.9 15.4 %collective-permute-start.11 = (bf16[4,32,512]{2,1,0:T(8,128)(2,1)S(1)}, bf16[4,32,512]{2,1,0:T(8,128)(2,1)S(1)}, u32[]{:S(2)}, u32[]{:S(2)}) collective-permute-start(bf16[4,32,512]{2,1,0:T(8,128)(2,1)S(1)} %get-tuple-element.80.cot_ref), channel_id=1, source_target_pairs={{0,1},{1,0},{2,3},{3,2},{4,5},{5,4},{6,7},{7,6},{8,9},{9,8},{10,11... | collective-permute-start | bytes 393224 | tf_op jit(solution)/shard_map/ppermute | solution.py:310
  15.0 11.6 %collective-permute-start.9 = (bf16[4,32,512]{2,1,0:T(8,128)(2,1)S(1)}, bf16[4,32,512]{2,1,0:T(8,128)(2,1)S(1)}, u32[]{:S(2)}, u32[]{:S(2)}) collective-permute-start(bf16[4,32,512]{2,1,0:T(8,128)(2,1)S(1)} %get-tuple-element.80.cot_ref), channel_id=1, source_target_pairs={{0,2},{1,3},{2,0},{3,1},{4,6},{5,7},{6,4},{7,5},{8,10},{9,11},{10,... | collective-permute-start | bytes 393224 | tf_op jit(solution)/shard_map/ppermute | solution.py:310
  16.6 3.6 %collective-permute-start.3 = (bf16[4,16,128]{2,1,0:T(8,128)(2,1)S(1)}, bf16[4,16,128]{2,1,0:T(8,128)(2,1)S(1)}, u32[]{:S(2)}, u32[]{:S(2)}) collective-permute-start(bf16[4,16,128]{2,1,0:T(8,128)(2,1)S(1)} %get-tuple-element.77), channel_id=1, source_target_pairs={{0,1},{1,0},{2,3},{3,2},{4,5},{5,4},{6,7},{7,6},{8,9},{9,8},{10,11... | collective-permute-start | bytes 49160 | tf_op jit(solution)/shard_map/ppermute | solution.py:310
  16.7 4.7 %collective-permute-start.4 = (bf16[4,16,128]{2,1,0:T(8,128)(2,1)S(1)}, bf16[4,16,128]{2,1,0:T(8,128)(2,1)S(1)}, u32[]{:S(2)}, u32[]{:S(2)}) collective-permute-start(bf16[4,16,128]{2,1,0:T(8,128)(2,1)S(1)} %get-tuple-element.78), channel_id=1, source_target_pairs={{0,2},{1,3},{2,0},{3,1},{4,6},{5,7},{6,4},{7,5},{8,10},{9,11},{10,... | collective-permute-start | bytes 49160 | tf_op jit(solution)/shard_map/ppermute | solution.py:310
  17.2 4.2 %collective-permute-start.5 = (bf16[4,16,128]{2,1,0:T(8,128)(2,1)S(1)}, bf16[4,16,128]{2,1,0:T(8,128)(2,1)S(1)}, u32[]{:S(2)}, u32[]{:S(2)}) collective-permute-start(bf16[4,16,128]{2,1,0:T(8,128)(2,1)S(1)} %get-tuple-element.79), channel_id=1, source_target_pairs={{0,3},{1,2},{2,1},{3,0},{4,7},{5,6},{6,5},{7,4},{8,11},{9,10},{10,... | collective-permute-start | bytes 49160 | tf_op jit(solution)/shard_map/ppermute | solution.py:310
  22.2 6.0 %collective-permute-start.8 = (bf16[32,512]{1,0:T(8,128)(2,1)S(1)}, bf16[32,512]{1,0:T(8,128)(2,1)S(1)}, u32[]{:S(2)}, u32[]{:S(2)}) collective-permute-start(bf16[32,512]{1,0:T(8,128)(2,1)S(1)} %get-tuple-element.93.share_ref), channel_id=1, source_target_pairs={{0,12},{1,13},{2,14},{3,15},{4,8},{5,9},{6,10},{7,11},{8,4},{9,5},... | collective-permute-start | bytes 98312 | tf_op jit(solution)/shard_map/ppermute | solution.py:307
  22.9 5.2 %collective-permute-start.7 = (bf16[32,512]{1,0:T(8,128)(2,1)S(1)}, bf16[32,512]{1,0:T(8,128)(2,1)S(1)}, u32[]{:S(2)}, u32[]{:S(2)}) collective-permute-start(bf16[32,512]{1,0:T(8,128)(2,1)S(1)} %get-tuple-element.93.share_ref), channel_id=1, source_target_pairs={{0,8},{1,9},{2,10},{3,11},{4,12},{5,13},{6,14},{7,15},{8,0},{9,1},... | collective-permute-start | bytes 98312 | tf_op jit(solution)/shard_map/ppermute | solution.py:307
  22.9 5.6 %collective-permute-start.6 = (bf16[32,512]{1,0:T(8,128)(2,1)S(1)}, bf16[32,512]{1,0:T(8,128)(2,1)S(1)}, u32[]{:S(2)}, u32[]{:S(2)}) collective-permute-start(bf16[32,512]{1,0:T(8,128)(2,1)S(1)} %get-tuple-element.93.share_ref), channel_id=1, source_target_pairs={{0,4},{1,5},{2,6},{3,7},{4,0},{5,1},{6,2},{7,3},{8,12},{9,13},{10,... | collective-permute-start | bytes 98312 | tf_op jit(solution)/shard_map/ppermute | solution.py:307
  28.5 7.9 %collective-permute-start.12 = (bf16[4,32,512]{2,1,0:T(8,128)(2,1)S(1)}, bf16[4,32,512]{2,1,0:T(8,128)(2,1)S(1)}, u32[]{:S(2)}, u32[]{:S(2)}) collective-permute-start(bf16[4,32,512]{2,1,0:T(8,128)(2,1)S(1)} %pad_maximum_fusion.rest_ref), channel_id=1, source_target_pairs={{0,1},{1,0},{2,3},{3,2},{4,5},{5,4},{6,7},{7,6},{8,9},{9,8},{10,11... | collective-permute-start | bytes 393224 | tf_op jit(solution)/shard_map/ppermute | solution.py:310
  28.6 5.9 %collective-permute-start.10 = (bf16[4,32,512]{2,1,0:T(8,128)(2,1)S(1)}, bf16[4,32,512]{2,1,0:T(8,128)(2,1)S(1)}, u32[]{:S(2)}, u32[]{:S(2)}) collective-permute-start(bf16[4,32,512]{2,1,0:T(8,128)(2,1)S(1)} %pad_maximum_fusion.rest_ref), channel_id=1, source_target_pairs={{0,2},{1,3},{2,0},{3,1},{4,6},{5,7},{6,4},{7,5},{8,10},{9,11},{10,... | collective-permute-start | bytes 393224 | tf_op jit(solution)/shard_map/ppermute | solution.py:310
  30.2 4.3 %collective-permute-start.14 = (bf16[4,32,512]{2,1,0:T(8,128)(2,1)S(1)}, bf16[4,32,512]{2,1,0:T(8,128)(2,1)S(1)}, u32[]{:S(2)}, u32[]{:S(2)}) collective-permute-start(bf16[4,32,512]{2,1,0:T(8,128)(2,1)S(1)} %collective-permute-done.9.cot_ref), channel_id=1, source_target_pairs={{0,1},{1,0},{2,3},{3,2},{4,5},{5,4},{6,7},{7,6},{8,9},{9,8},{10,11... | collective-permute-start | bytes 393224 | tf_op jit(solution)/shard_map/ppermute | solution.py:310
  34.5 2.7 %collective-permute-start.13 = (bf16[4,32,512]{2,1,0:T(8,128)(2,1)S(1)}, bf16[4,32,512]{2,1,0:T(8,128)(2,1)S(1)}, u32[]{:S(2)}, u32[]{:S(2)}) collective-permute-start(bf16[4,32,512]{2,1,0:T(8,128)(2,1)S(1)} %collective-permute-done.10.rest_ref), channel_id=1, source_target_pairs={{0,1},{1,0},{2,3},{3,2},{4,5},{5,4},{6,7},{7,6},{8,9},{9,8},{10,11... | collective-permute-start | bytes 393224 | tf_op jit(solution)/shard_map/ppermute | solution.py:310
  44.7 3.2 %collective-permute-start.16 = (bf16[8,32,512]{2,1,0:T(8,128)(2,1)S(1)}, bf16[8,32,512]{2,1,0:T(8,128)(2,1)S(1)}, u32[]{:S(2)}, u32[]{:S(2)}) collective-permute-start(bf16[8,32,512]{2,1,0:T(8,128)(2,1)S(1)} %shard_map.142), channel_id=1, source_target_pairs={{0,1},{1,0},{2,3},{3,2},{4,5},{5,4},{6,7},{7,6},{8,9},{9,8},{10,11... | collective-permute-start | bytes 786440 | tf_op jit(solution)/shard_map/ppermute | solution.py:310
  44.8 5.9 %collective-permute-start.17 = (bf16[4,32,512]{2,1,0:T(8,128)(2,1)S(1)}, bf16[4,32,512]{2,1,0:T(8,128)(2,1)S(1)}, u32[]{:S(2)}, u32[]{:S(2)}) collective-permute-start(bf16[4,32,512]{2,1,0:T(8,128)(2,1)S(1)} %get-tuple-element.124.after_ref), channel_id=1, source_target_pairs={{0,2},{1,3},{2,0},{3,1},{4,6},{5,7},{6,4},{7,5},{8,10},{9,11},{10,... | collective-permute-start | bytes 393224 | tf_op jit(solution)/shard_map/ppermute | solution.py:310
  50.9 6.0 %collective-permute-start.21 = (bf16[4,32,512]{2,1,0:T(8,128)(2,1)S(1)}, bf16[4,32,512]{2,1,0:T(8,128)(2,1)S(1)}, u32[]{:S(2)}, u32[]{:S(2)}) collective-permute-start(bf16[4,32,512]{2,1,0:T(8,128)(2,1)S(1)} %get-tuple-element.131), channel_id=1, source_target_pairs={{0,2},{1,3},{2,0},{3,1},{4,6},{5,7},{6,4},{7,5},{8,10},{9,11},{10,... | collective-permute-start | bytes 393224 | tf_op jit(solution)/shard_map/ppermute | solution.py:310
  52.4 7.4 %collective-permute-start.18 = (bf16[32,512]{1,0:T(8,128)(2,1)S(1)}, bf16[32,512]{1,0:T(8,128)(2,1)S(1)}, u32[]{:S(2)}, u32[]{:S(2)}) collective-permute-start(bf16[32,512]{1,0:T(8,128)(2,1)S(1)} %get-tuple-element.127), channel_id=1, source_target_pairs={{0,4},{1,5},{2,6},{3,7},{4,0},{5,1},{6,2},{7,3},{8,12},{9,13},{10,... | collective-permute-start | bytes 98312 | tf_op jit(solution)/shard_map/ppermute | solution.py:307
  54.4 6.9 %collective-permute-start.19 = (bf16[32,512]{1,0:T(8,128)(2,1)S(1)}, bf16[32,512]{1,0:T(8,128)(2,1)S(1)}, u32[]{:S(2)}, u32[]{:S(2)}) collective-permute-start(bf16[32,512]{1,0:T(8,128)(2,1)S(1)} %get-tuple-element.128), channel_id=1, source_target_pairs={{0,8},{1,9},{2,10},{3,11},{4,12},{5,13},{6,14},{7,15},{8,0},{9,1},... | collective-permute-start | bytes 98312 | tf_op jit(solution)/shard_map/ppermute | solution.py:307
  55.4 6.0 %collective-permute-start.20 = (bf16[32,512]{1,0:T(8,128)(2,1)S(1)}, bf16[32,512]{1,0:T(8,128)(2,1)S(1)}, u32[]{:S(2)}, u32[]{:S(2)}) collective-permute-start(bf16[32,512]{1,0:T(8,128)(2,1)S(1)} %get-tuple-element.129), channel_id=1, source_target_pairs={{0,12},{1,13},{2,14},{3,15},{4,8},{5,9},{6,10},{7,11},{8,4},{9,5},... | collective-permute-start | bytes 98312 | tf_op jit(solution)/shard_map/ppermute | solution.py:307
  56.9 4.5 %collective-permute-start.22 = (bf16[32,512]{1,0:T(8,128)(2,1)S(1)}, bf16[32,512]{1,0:T(8,128)(2,1)S(1)}, u32[]{:S(2)}, u32[]{:S(2)}) collective-permute-start(bf16[32,512]{1,0:T(8,128)(2,1)S(1)} %get-tuple-element.133), channel_id=1, source_target_pairs={{0,4},{1,5},{2,6},{3,7},{4,0},{5,1},{6,2},{7,3},{8,12},{9,13},{10,... | collective-permute-start | bytes 98312 | tf_op jit(solution)/shard_map/ppermute | solution.py:307
  58.1 5.2 %collective-permute-start.23 = (bf16[32,512]{1,0:T(8,128)(2,1)S(1)}, bf16[32,512]{1,0:T(8,128)(2,1)S(1)}, u32[]{:S(2)}, u32[]{:S(2)}) collective-permute-start(bf16[32,512]{1,0:T(8,128)(2,1)S(1)} %get-tuple-element.134), channel_id=1, source_target_pairs={{0,8},{1,9},{2,10},{3,11},{4,12},{5,13},{6,14},{7,15},{8,0},{9,1},... | collective-permute-start | bytes 98312 | tf_op jit(solution)/shard_map/ppermute | solution.py:307
  59.8 5.7 %collective-permute-start.24 = (bf16[32,512]{1,0:T(8,128)(2,1)S(1)}, bf16[32,512]{1,0:T(8,128)(2,1)S(1)}, u32[]{:S(2)}, u32[]{:S(2)}) collective-permute-start(bf16[32,512]{1,0:T(8,128)(2,1)S(1)} %get-tuple-element.135), channel_id=1, source_target_pairs={{0,12},{1,13},{2,14},{3,15},{4,8},{5,9},{6,10},{7,11},{8,4},{9,5},... | collective-permute-start | bytes 98312 | tf_op jit(solution)/shard_map/ppermute | solution.py:307
  (10 other events, 85.5 us)

commit v7 on v6

--- a/solution.py
+++ b/solution.py
@@ -55,7 +55,7 @@
 
 def send_kernel(
     me_ref, offset_ref, act_ref, expo_ref, base_ref, received_ref, cot_ref, gain_ref,
-    new_ref, received_out_ref, gain_out_ref, *refs,
+    new_rows_ref, received_out_ref, gain_out_ref, *refs,
 ):
     *packed_refs, rows_ref = refs
     n, rows, _ = rows_ref.shape
@@ -87,11 +87,15 @@
         packed_ref[:, :share] = cot
         for q in range(4):
             packed_ref[block_spot(q, tokens, rows, share)] = rows_ref[4 * to + q].astype(bf16)
-    new = chosen + jnp.concatenate(pieces, axis=1)
+    new_rows_ref[...] = chosen + jnp.concatenate(pieces, axis=1)
+
+
+def sender_base_kernel(offset_ref, rows_ref, base_ref, new_ref):
+    first = offset_ref[0] == 0
     for p in range(2):
-        row = new[p : p + 1]
-        new_ref[p, 0:1, :] = jnp.where(first, row, old[p][0:1])
-        new_ref[p, 1:2, :] = jnp.where(first, old[p][1:2], row)
+        row, old = rows_ref[p : p + 1, :], base_ref[p]
+        new_ref[p, 0:1, :] = jnp.where(first, row, old[0:1])
+        new_ref[p, 1:2, :] = jnp.where(first, old[1:2], row)
 
 
 def sort_kernel(me_ref, *refs):
@@ -109,9 +113,10 @@
             out_ref[r] = jnp.where(to_row == 0, low, high)
 
 
-def rebuild_kernel(me_ref, b0, b1, b2, b3, base_ref, new_ref, share_ref, rows_ref, slots_ref):
+def rebuild_kernel(me_ref, b0, b1, b2, b3, base_ref, out_ref, rows_ref, slots_ref):
     quarter, rows, _ = b0.shape
-    n, width = 4 * quarter, share_ref.shape[1]
+    n, width = 4 * quarter, base_ref.shape[2]
+    whole = out_ref.shape == base_ref.shape
     for e, block_ref in enumerate((b0, b1, b2, b3)):
         for r in range(quarter):
             sender = owner_of(me_ref[0], n, 2 * (e % 2) + e // 2, r)
@@ -127,11 +132,12 @@
             even = slots_ref[at, pl.ds(0, n, stride=2), :]
             odd = slots_ref[at, pl.ds(1, n, stride=2), :]
             rebuilt = jnp.where(first, even, odd) + sent
+            if not whole:
+                out_ref[p * n : (p + 1) * n, cols] = rebuilt.astype(bf16)
+                continue
             slots_ref[at, pl.ds(0, n, stride=2), :] = jnp.where(first, rebuilt, even)
             slots_ref[at, pl.ds(1, n, stride=2), :] = jnp.where(first, odd, rebuilt)
-            new_ref[p, :, cols] = slots_ref[at]
-            restored = rebuilt.astype(bf16)
-            share_ref[p * n : (p + 1) * n, cols] = restored
+            out_ref[p, :, cols] = slots_ref[at]
 
 
 def dot_nt(a, b):
@@ -333,16 +339,16 @@
     once = lambda shape: pl.BlockSpec(shape, lambda i: (0,) * len(shape))
     in_shapes = [act_shape, expo_shape, sender_base.shape, receiver_base.shape, share_shape, (1, width_all)]
     outs = (
-        struct(sender_base.shape, f32),
+        struct(act_shape, f32),
         struct(receiver_base.shape, f32),
         struct((n, width), f32),
     ) + (struct(packed_shape, bf16),) * quarter
-    new_sender_base, received, gain, *packed = pl.pallas_call(
+    new_rows, received, gain, *packed = pl.pallas_call(
         send_kernel,
         out_shape=outs,
         grid=(1,),
         in_specs=[SMEM, SMEM] + [once(x) for x in in_shapes],
-        out_specs=tuple(once(x.shape) for x in outs),
+        out_specs=(VMEM,) * len(outs),
         scratch_shapes=[pltpu.VMEM((n, rows, LANES), f32)],
         compiler_params=params(8),
     )(
@@ -364,8 +370,7 @@
         micros=STAGE,
     )
     blocks = [blocks[0]] + [swap(blocks[e], e) for e in range(1, 4)]
-    cot_row = swap(cot_line, 2)
-    cots = [cot_line, cot_row, swap(cot_line, 1), swap(cot_row, 1)]
+    cots = [cot_line]
 
     ANY = pl.BlockSpec(memory_space=pl.ANY)
     share_f32 = struct(share_shape, f32)
@@ -393,27 +398,47 @@
 
     together = lax.optimization_barrier
     grads = [grad_active_part(0)]
+    cot_line, grads[0] = together((cot_line, grads[0]))
+    cots.append(swap(cot_line, 2))
     blocks, grads[0] = together((blocks, grads[0]))
 
-    new_receiver_base, share = call(
-        rebuild_kernel,
-        (struct(receiver_base.shape, f32), struct(share_shape, bf16)),
-        [SMEM] + [VMEM] * 5,
-        [me_in, *blocks, received],
-        [pltpu.VMEM((n * rows, LANES), f32), pltpu.VMEM((2 * width // LANES, 2 * n, LANES), f32)],
-        micros=STAGE,
-    )
+    def rebuild(out, micros):
+        return call(
+            rebuild_kernel,
+            out,
+            [SMEM] + [VMEM] * 5,
+            [me_in, *blocks, received],
+            [
+                pltpu.VMEM((n * rows, LANES), f32),
+                pltpu.VMEM((2 * width // LANES, 2 * n, LANES), f32),
+            ],
+            micros=micros,
+        )
+
+    share = rebuild(struct(share_shape, bf16), STAGE)
     lines = [shift(share, r) for r in range(quarter)]
     grads.append(grad_active_part(1))
+    cot_line, cot_row, grads[1] = together((cot_line, cots[1], grads[1]))
+    cots += [swap(cot_line, 1), swap(cot_row, 1)]
     lines, grads[1] = together((lines, grads[1]))
     rest_line = jnp.stack(lines)
     rest_row = swap(rest_line, 2)
-    rests = [rest_line, rest_row, swap(rest_line, 1)]
+    rests = [rest_line]
+    products = [up_product_part(0)]
+    rest_line, products[0] = together((rest_line, products[0]))
+    rest_line_other = swap(rest_line, 1)
     grads.append(grad_active_part(2))
-    products = [up_product_part(0)]
-    rest_row, grads[2], products[0] = together((rest_row, grads[2], products[0]))
-    rests[1] = rest_row
-    rests.append(swap(rest_row, 1))
+    new_receiver_base = rebuild(struct(receiver_base.shape, f32), 0.7)
+    new_sender_base = call(
+        sender_base_kernel,
+        struct(sender_base.shape, f32),
+        [SMEM] + [VMEM] * 2,
+        [offset, new_rows, sender_base],
+    )
+    rest_row, grads[2], new_sender_base, new_receiver_base = together(
+        (rest_row, grads[2], new_sender_base, new_receiver_base)
+    )
+    rests += [rest_row, rest_line_other, swap(rest_row, 1)]
     grads.append(grad_active_part(3))
     products += [up_product_part(1), up_product_part(2)]
     gas, own_cots = zip(*grads)

time: 66.5 us -> 64.7 us (0.973)
  starting transfers between devices: 28 us -> 25.5 us
  local copies, waits for them, and re-layouts: 0.53 us -> 3.02 us
  waiting for transfers between devices: 17.2 us -> 15.4 us
    ppermute x13, starting transfers between devices: 9.15 us -> 6.51 us  [swap(): return lax.ppermute(x, 'dp', [(d, d ^ bits) for d in range(n)])]
    unnamed x18 -> x20, local copies, waits for them, and re-layouts: 0.53 us -> 3.02 us
    ppermute x12, waiting for transfers between devices: 10.8 us -> 8.4 us  [shift(): return lax.ppermute(x, 'dp', [(d, d ^ 4 * r) for d in range(n)]) if r else x]
    pallas_call x1, Pallas kernels: 2.08 us -> 1.22 us  [on_device(): pl.pallas_call(send_kernel, out_shape=outs, grid=(1,), in_specs=[SMEM, SM...]
    pallas_call x16 -> x18, Pallas kernels: 17.1 us -> 17.9 us  [call(): pl.pallas_call(kernel, out_shape=outs, in_specs=ins, out_specs=jax.tree.m...]
  transfers between devices with their start and end apart: 25 -> 25, of which waited for: 9 -> 7; matrix products, arithmetic and copies ran while one was open for 0% -> 0% of each run, Pallas kernels for 16% -> 18%
where the time goes in v7:
time: 64.7 us; the launch traced here: 64.5 us
  starting transfers between devices  25.5 us (39%)
  Pallas kernels  19.1 us (30%)
  waiting for transfers between devices  15.4 us (24%)
  local copies, waits for them, and re-layouts  3.02 us (5%)
  between operations  1.49 us (2%)
    ppermute x12, starting transfers between devices, shift(): return lax.ppermute(x, 'dp', [(d, d ^ 4 * r) for d in range(n)]) if r else x  19 us
    pallas_call x18, Pallas kernels, call(): pl.pallas_call(kernel, out_shape=outs, in_specs=ins, out_specs=jax.tree.m...  17.9 us
    ppermute x12, waiting for transfers between devices, shift(): return lax.ppermute(x, 'dp', [(d, d ^ 4 * r) for d in range(n)]) if r else x  8.4 us
    ppermute x13, waiting for transfers between devices, swap(): return lax.ppermute(x, 'dp', [(d, d ^ bits) for d in range(n)])  6.95 us
    ppermute x13, starting transfers between devices, swap(): return lax.ppermute(x, 'dp', [(d, d ^ bits) for d in range(n)])  6.51 us
    unnamed x20, local copies, waits for them, and re-layouts  3.02 us
  transfers between devices with their start and end apart: 25, of which 7 were waited for; matrix products, arithmetic and copies ran while one was open for 0% of the time, Pallas kernels for 18%

profile of v7, /device:TPU:0, one launch (start us, length us, event | category | flops | bytes accessed | tf_op | source)
XLA Modules:
  0.0 64.5 jit_solution(12591061935916198251)
XLA Ops:
  1.3 1.2 %shard_map.129 = (f32[2,8192]{1,0:T(2,128)S(1)}, f32[2,32,512]{2,1,0:T(8,128)S(1)}, f32[16,512]{1,0:T(8,128)S(1)}, bf16[32,768]{1,0:T(8,128)(2,1)S(1)}, bf16[32,...) custom-call(s32[1]{0:T(128)} %bitcast.me_ref, s32[1]{0:T(128)S(6)} %sub.7.offset_ref, ...), custom_call_target="tpu_custom_call" | custom-call | tf_op jit(solution)/shard_map/pallas_call | solution.py:346
  2.5 3.1 %collective-permute-start = (bf16[32,768]{1,0:T(8,128)(2,1)S(1)}, bf16[32,768]{1,0:T(8,128)(2,1)S(1)}, u32[]{:S(2)}, u32[]{:S(2)}) collective-permute-start(bf16[32,768]{1,0:T(8,128)(2,1)S(1)} %get-tuple-element.80), channel_id=1, source_target_pairs={{0,4},{1,5},{2,6},{3,7},{4,0},{5,1},{6,2},{7,3},{8,12},{9,13},{10,... | collective-permute-start | bytes 147464 | tf_op jit(solution)/shard_map/ppermute | solution.py:313
  5.6 2.6 %collective-permute-start.1 = (bf16[32,768]{1,0:T(8,128)(2,1)S(1)}, bf16[32,768]{1,0:T(8,128)(2,1)S(1)}, u32[]{:S(2)}, u32[]{:S(2)}) collective-permute-start(bf16[32,768]{1,0:T(8,128)(2,1)S(1)} %get-tuple-element.81), channel_id=1, source_target_pairs={{0,8},{1,9},{2,10},{3,11},{4,12},{5,13},{6,14},{7,15},{8,0},{9,1},... | collective-permute-start | bytes 147464 | tf_op jit(solution)/shard_map/ppermute | solution.py:313
  9.8 1.7 %collective-permute-done.1.refs_2_ = bf16[32,768]{1,0:T(8,128)(2,1)S(1)} collective-permute-done((bf16[32,768]{1,0:T(8,128)(2,1)S(1)}, bf16[32,768]{1,0:T(8,128)(2,1)S(1)}, u32[]{:S(2)}, u32[]{:S(2)}) %collective-permute-start.1) | collective-permute-done | bytes 49184 | tf_op jit(solution)/shard_map/ppermute | solution.py:313
  11.5 2.6 %collective-permute-done.2.refs_3_ = bf16[32,768]{1,0:T(8,128)(2,1)S(1)} collective-permute-done((bf16[32,768]{1,0:T(8,128)(2,1)S(1)}, bf16[32,768]{1,0:T(8,128)(2,1)S(1)}, u32[]{:S(2)}, u32[]{:S(2)}) %collective-permute-start.2) | collective-permute-done | bytes 49184 | tf_op jit(solution)/shard_map/ppermute | solution.py:313
  14.2 1.6 %collective-permute-start.4 = (bf16[4,16,128]{2,1,0:T(8,128)(2,1)S(1)}, bf16[4,16,128]{2,1,0:T(8,128)(2,1)S(1)}, u32[]{:S(2)}, u32[]{:S(2)}) collective-permute-start(bf16[4,16,128]{2,1,0:T(8,128)(2,1)S(1)} %get-tuple-element.85), channel_id=1, source_target_pairs={{0,2},{1,3},{2,0},{3,1},{4,6},{5,7},{6,4},{7,5},{8,10},{9,11},{10,... | collective-permute-start | bytes 49160 | tf_op jit(solution)/shard_map/ppermute | solution.py:316
  16.3 1.3 %slice-done.2 = s8[4194304]{0:T(1024)(128)(4,1)S(1)} async-done(((s8[14680064]{0:T(1024)(128)(4,1)}), s8[4194304]{0:T(1024)(128)(4,1)S(1)}, s32[]{:S(2)}) %slice-start.2) | async-done | bytes 4194328
  18.1 1.2 %shard_map.131 = (f32[896,32]{1,0:T(8,128)S(1)}, f32[32,512]{1,0:T(8,128)S(1)}) custom-call(s32[1]{0:T(128)} %bitcast.me_ref, bf16[4,32,512]{2,1,0:T(8,128)(2,1)S(1)} %get-tuple-element.106.cot_ref, bf16[896,8192]{1,0:T(8,128)(2,1)S(1)} %bitcast.14), custom_call_target="tpu_custom_call" | custom-call | flops 1840000000 | tf_op jit(solution)/shard_map/pallas_call | solution.py:323
  19.4 1.6 %collective-permute-start.9 = (bf16[4,32,512]{2,1,0:T(8,128)(2,1)S(1)}, bf16[4,32,512]{2,1,0:T(8,128)(2,1)S(1)}, u32[]{:S(2)}, u32[]{:S(2)}) collective-permute-start(bf16[4,32,512]{2,1,0:T(8,128)(2,1)S(1)} %get-tuple-element.106.cot_ref), channel_id=1, source_target_pairs={{0,2},{1,3},{2,0},{3,1},{4,6},{5,7},{6,4},{7,5},{8,10},{9,11},{10,... | collective-permute-start | bytes 393224 | tf_op jit(solution)/shard_map/ppermute | solution.py:316
  21.9 3.6 %collective-permute-start.6 = (bf16[32,512]{1,0:T(8,128)(2,1)S(1)}, bf16[32,512]{1,0:T(8,128)(2,1)S(1)}, u32[]{:S(2)}, u32[]{:S(2)}) collective-permute-start(bf16[32,512]{1,0:T(8,128)(2,1)S(1)} %shard_map.132.share_ref), channel_id=1, source_target_pairs={{0,4},{1,5},{2,6},{3,7},{4,0},{5,1},{6,2},{7,3},{8,12},{9,13},{10,... | collective-permute-start | bytes 98312 | tf_op jit(solution)/shard_map/ppermute | solution.py:313
  26.3 1.2 %shard_map.133 = (f32[896,32]{1,0:T(8,128)S(1)}, f32[32,512]{1,0:T(8,128)S(1)}) custom-call(s32[1]{0:T(128)} %bitcast.me_ref, bf16[4,32,512]{2,1,0:T(8,128)(2,1)S(1)} %collective-permute-done.9.cot_ref, bf16[896,8192]{1,0:T(8,128)(2,1)S(1)} %bitcast.14), custom_call_target="tpu_custom_call" | custom-call | flops 1840000000 | tf_op jit(solution)/shard_map/pallas_call | solution.py:323
  29.5 1.2 %shard_map.134 = (f32[896,32]{1,0:T(8,128)S(1)}, f32[32,512]{1,0:T(8,128)S(1)}) custom-call(s32[1]{0:T(128)} %bitcast.me_ref, bf16[4,32,512]{2,1,0:T(8,128)(2,1)S(1)} %collective-permute-done.11.cot_ref, bf16[896,8192]{1,0:T(8,128)(2,1)S(1)} %bitcast.14), custom_call_target="tpu_custom_call" | custom-call | flops 1840000000 | tf_op jit(solution)/shard_map/pallas_call | solution.py:323
  30.7 2.9 %collective-permute-done.10.rest_ref = bf16[4,32,512]{2,1,0:T(8,128)(2,1)S(1)} collective-permute-done((bf16[4,32,512]{2,1,0:T(8,128)(2,1)S(1)}, bf16[4,32,512]{2,1,0:T(8,128)(2,1)S(1)}, u32[]{:S(2)}, u32[]{:S(2)}) %collective-permute-start.10) | collective-permute-done | bytes 131104 | tf_op jit(solution)/shard_map/ppermute | solution.py:316
  33.6 1.2 %shard_map.140 = (f32[896,32]{1,0:T(8,128)S(1)}, f32[32,512]{1,0:T(8,128)S(1)}) custom-call(s32[1]{0:T(128)} %bitcast.me_ref, bf16[4,32,512]{2,1,0:T(8,128)(2,1)S(1)} %collective-permute-done.14.cot_ref, bf16[896,8192]{1,0:T(8,128)(2,1)S(1)} %bitcast.14), custom_call_target="tpu_custom_call" | custom-call | flops 1840000000 | tf_op jit(solution)/shard_map/pallas_call | solution.py:323
  36.3 5.4 %shard_map.141 = (bf16[32,896]{1,0:T(8,128)(2,1)S(1)}, f32[32,512]{1,0:T(8,128)S(1)}, bf16[8,32,512]{2,1,0:T(8,128)(2,1)S(1)}, bf16[8,32,512]{2,1,0:T(8,128)(2,1)S(1)}) custom-call(s32[1]{0:T(128)} %bitcast.me_ref, bf16[4,32,512]{2,1,0:T(8,128)(2,1)S(1)} %collective-permute-done.13.rest_ref, f32[16,512]{1,0:T(8,128)S(1)} %get-tuple-element.112.gain_ref, ...), custom_call_target="tpu_custom_call" | custom-call | flops 7474999808 | tf_op jit(solution)/shard_map/pallas_call | solution.py:323
  42.3 1.5 %shard_map.144 = bf16[8,32,512]{2,1,0:T(8,128)(2,1)S(1)} custom-call(s32[1]{0:T(128)} %bitcast.me_ref, bf16[32,896]{1,0:T(8,128)(2,1)S(1)} %get-tuple-element.137.active_ref, bf16[896,8192]{1,0:T(8,128)(2,1)S(1)} %bitcast.14, bf16[8,32,512]{2,1,0:T(8,128)(2,1)S(1)} %get-tuple-element.139.after_ref), custom_call_target="tpu_custom_call" | custom-call | flops 1724999936 | tf_op jit(solution)/shard_map/pallas_call | solution.py:323
  44.5 1.5 %shard_map.143.kept_ref = bf16[8,32,512]{2,1,0:T(8,128)(2,1)S(1)} custom-call(s32[1]{0:T(128)} %bitcast.me_ref, bf16[32,896]{1,0:T(8,128)(2,1)S(1)} %get-tuple-element.137.active_ref, bf16[896,8192]{1,0:T(8,128)(2,1)S(1)} %bitcast.14, bf16[4,32,512]{2,1,0:T(8,128)(2,1)S(1)} %get-tuple-element.140.after_ref), custom_call_target="tpu_custom_call" | custom-call | flops 1724999936 | tf_op jit(solution)/shard_map/pallas_call | solution.py:323
  46.0 3.9 %collective-permute-done.17.refs_1_ = bf16[4,32,512]{2,1,0:T(8,128)(2,1)S(1)} collective-permute-done((bf16[4,32,512]{2,1,0:T(8,128)(2,1)S(1)}, bf16[4,32,512]{2,1,0:T(8,128)(2,1)S(1)}, u32[]{:S(2)}, u32[]{:S(2)}) %collective-permute-start.17) | collective-permute-done | bytes 131104 | tf_op jit(solution)/shard_map/ppermute | solution.py:316
  50.5 1.9 %collective-permute-start.18 = (bf16[32,512]{1,0:T(8,128)(2,1)S(1)}, bf16[32,512]{1,0:T(8,128)(2,1)S(1)}, u32[]{:S(2)}, u32[]{:S(2)}) collective-permute-start(bf16[32,512]{1,0:T(8,128)(2,1)S(1)} %get-tuple-element.143), channel_id=1, source_target_pairs={{0,4},{1,5},{2,6},{3,7},{4,0},{5,1},{6,2},{7,3},{8,12},{9,13},{10,... | collective-permute-start | bytes 98312 | tf_op jit(solution)/shard_map/ppermute | solution.py:313
  53.3 1.6 %collective-permute-start.20 = (bf16[32,512]{1,0:T(8,128)(2,1)S(1)}, bf16[32,512]{1,0:T(8,128)(2,1)S(1)}, u32[]{:S(2)}, u32[]{:S(2)}) collective-permute-start(bf16[32,512]{1,0:T(8,128)(2,1)S(1)} %get-tuple-element.145), channel_id=1, source_target_pairs={{0,12},{1,13},{2,14},{3,15},{4,8},{5,9},{6,10},{7,11},{8,4},{9,5},... | collective-permute-start | bytes 98312 | tf_op jit(solution)/shard_map/ppermute | solution.py:313
  55.1 1.9 %collective-permute-start.22 = (bf16[32,512]{1,0:T(8,128)(2,1)S(1)}, bf16[32,512]{1,0:T(8,128)(2,1)S(1)}, u32[]{:S(2)}, u32[]{:S(2)}) collective-permute-start(bf16[32,512]{1,0:T(8,128)(2,1)S(1)} %get-tuple-element.149), channel_id=1, source_target_pairs={{0,4},{1,5},{2,6},{3,7},{4,0},{5,1},{6,2},{7,3},{8,12},{9,13},{10,... | collective-permute-start | bytes 98312 | tf_op jit(solution)/shard_map/ppermute | solution.py:313
  58.0 1.6 %collective-permute-start.24 = (bf16[32,512]{1,0:T(8,128)(2,1)S(1)}, bf16[32,512]{1,0:T(8,128)(2,1)S(1)}, u32[]{:S(2)}, u32[]{:S(2)}) collective-permute-start(bf16[32,512]{1,0:T(8,128)(2,1)S(1)} %get-tuple-element.151), channel_id=1, source_target_pairs={{0,12},{1,13},{2,14},{3,15},{4,8},{5,9},{6,10},{7,11},{8,4},{9,5},... | collective-permute-start | bytes 98312 | tf_op jit(solution)/shard_map/ppermute | solution.py:313
  59.6 2.3 %collective-permute-done.23.refs_14_ = bf16[32,512]{1,0:T(8,128)(2,1)S(1)} collective-permute-done((bf16[32,512]{1,0:T(8,128)(2,1)S(1)}, bf16[32,512]{1,0:T(8,128)(2,1)S(1)}, u32[]{:S(2)}, u32[]{:S(2)}) %collective-permute-start.23) | collective-permute-done | bytes 32800 | tf_op jit(solution)/shard_map/ppermute | solution.py:313
  61.9 1.8 %collective-permute-done.24.refs_15_ = bf16[32,512]{1,0:T(8,128)(2,1)S(1)} collective-permute-done((bf16[32,512]{1,0:T(8,128)(2,1)S(1)}, bf16[32,512]{1,0:T(8,128)(2,1)S(1)}, u32[]{:S(2)}, u32[]{:S(2)}) %collective-permute-start.24) | collective-permute-done | bytes 32800 | tf_op jit(solution)/shard_map/ppermute | solution.py:313
  (68 shorter events, 12.7 us)
Async XLA Ops:
  2.5 7.3 %collective-permute-start = (bf16[32,768]{1,0:T(8,128)(2,1)S(1)}, bf16[32,768]{1,0:T(8,128)(2,1)S(1)}, u32[]{:S(2)}, u32[]{:S(2)}) collective-permute-start(bf16[32,768]{1,0:T(8,128)(2,1)S(1)} %get-tuple-element.80), channel_id=1, source_target_pairs={{0,4},{1,5},{2,6},{3,7},{4,0},{5,1},{6,2},{7,3},{8,12},{9,13},{10,... | collective-permute-start | bytes 147464 | tf_op jit(solution)/shard_map/ppermute | solution.py:313
  5.6 5.9 %collective-permute-start.1 = (bf16[32,768]{1,0:T(8,128)(2,1)S(1)}, bf16[32,768]{1,0:T(8,128)(2,1)S(1)}, u32[]{:S(2)}, u32[]{:S(2)}) collective-permute-start(bf16[32,768]{1,0:T(8,128)(2,1)S(1)} %get-tuple-element.81), channel_id=1, source_target_pairs={{0,8},{1,9},{2,10},{3,11},{4,12},{5,13},{6,14},{7,15},{8,0},{9,1},... | collective-permute-start | bytes 147464 | tf_op jit(solution)/shard_map/ppermute | solution.py:313
  8.2 5.9 %collective-permute-start.2 = (bf16[32,768]{1,0:T(8,128)(2,1)S(1)}, bf16[32,768]{1,0:T(8,128)(2,1)S(1)}, u32[]{:S(2)}, u32[]{:S(2)}) collective-permute-start(bf16[32,768]{1,0:T(8,128)(2,1)S(1)} %get-tuple-element.82), channel_id=1, source_target_pairs={{0,12},{1,13},{2,14},{3,15},{4,8},{5,9},{6,10},{7,11},{8,4},{9,5},... | collective-permute-start | bytes 147464 | tf_op jit(solution)/shard_map/ppermute | solution.py:313
  14.1 6.8 %collective-permute-start.3 = (bf16[4,16,128]{2,1,0:T(8,128)(2,1)S(1)}, bf16[4,16,128]{2,1,0:T(8,128)(2,1)S(1)}, u32[]{:S(2)}, u32[]{:S(2)}) collective-permute-start(bf16[4,16,128]{2,1,0:T(8,128)(2,1)S(1)} %get-tuple-element.84), channel_id=1, source_target_pairs={{0,1},{1,0},{2,3},{3,2},{4,5},{5,4},{6,7},{7,6},{8,9},{9,8},{10,11... | collective-permute-start | bytes 49160 | tf_op jit(solution)/shard_map/ppermute | solution.py:316
  14.2 6.8 %collective-permute-start.4 = (bf16[4,16,128]{2,1,0:T(8,128)(2,1)S(1)}, bf16[4,16,128]{2,1,0:T(8,128)(2,1)S(1)}, u32[]{:S(2)}, u32[]{:S(2)}) collective-permute-start(bf16[4,16,128]{2,1,0:T(8,128)(2,1)S(1)} %get-tuple-element.85), channel_id=1, source_target_pairs={{0,2},{1,3},{2,0},{3,1},{4,6},{5,7},{6,4},{7,5},{8,10},{9,11},{10,... | collective-permute-start | bytes 49160 | tf_op jit(solution)/shard_map/ppermute | solution.py:316
  15.8 5.2 %collective-permute-start.5 = (bf16[4,16,128]{2,1,0:T(8,128)(2,1)S(1)}, bf16[4,16,128]{2,1,0:T(8,128)(2,1)S(1)}, u32[]{:S(2)}, u32[]{:S(2)}) collective-permute-start(bf16[4,16,128]{2,1,0:T(8,128)(2,1)S(1)} %get-tuple-element.86), channel_id=1, source_target_pairs={{0,3},{1,2},{2,1},{3,0},{4,7},{5,6},{6,5},{7,4},{8,11},{9,10},{10,... | collective-permute-start | bytes 49160 | tf_op jit(solution)/shard_map/ppermute | solution.py:316
  19.4 6.9 %collective-permute-start.9 = (bf16[4,32,512]{2,1,0:T(8,128)(2,1)S(1)}, bf16[4,32,512]{2,1,0:T(8,128)(2,1)S(1)}, u32[]{:S(2)}, u32[]{:S(2)}) collective-permute-start(bf16[4,32,512]{2,1,0:T(8,128)(2,1)S(1)} %get-tuple-element.106.cot_ref), channel_id=1, source_target_pairs={{0,2},{1,3},{2,0},{3,1},{4,6},{5,7},{6,4},{7,5},{8,10},{9,11},{10,... | collective-permute-start | bytes 393224 | tf_op jit(solution)/shard_map/ppermute | solution.py:316
  21.1 6.4 %collective-permute-start.8 = (bf16[32,512]{1,0:T(8,128)(2,1)S(1)}, bf16[32,512]{1,0:T(8,128)(2,1)S(1)}, u32[]{:S(2)}, u32[]{:S(2)}) collective-permute-start(bf16[32,512]{1,0:T(8,128)(2,1)S(1)} %shard_map.132.share_ref), channel_id=1, source_target_pairs={{0,12},{1,13},{2,14},{3,15},{4,8},{5,9},{6,10},{7,11},{8,4},{9,5},... | collective-permute-start | bytes 98312 | tf_op jit(solution)/shard_map/ppermute | solution.py:313
  21.9 5.6 %collective-permute-start.7 = (bf16[32,512]{1,0:T(8,128)(2,1)S(1)}, bf16[32,512]{1,0:T(8,128)(2,1)S(1)}, u32[]{:S(2)}, u32[]{:S(2)}) collective-permute-start(bf16[32,512]{1,0:T(8,128)(2,1)S(1)} %shard_map.132.share_ref), channel_id=1, source_target_pairs={{0,8},{1,9},{2,10},{3,11},{4,12},{5,13},{6,14},{7,15},{8,0},{9,1},... | collective-permute-start | bytes 98312 | tf_op jit(solution)/shard_map/ppermute | solution.py:313
  21.9 5.6 %collective-permute-start.6 = (bf16[32,512]{1,0:T(8,128)(2,1)S(1)}, bf16[32,512]{1,0:T(8,128)(2,1)S(1)}, u32[]{:S(2)}, u32[]{:S(2)}) collective-permute-start(bf16[32,512]{1,0:T(8,128)(2,1)S(1)} %shard_map.132.share_ref), channel_id=1, source_target_pairs={{0,4},{1,5},{2,6},{3,7},{4,0},{5,1},{6,2},{7,3},{8,12},{9,13},{10,... | collective-permute-start | bytes 98312 | tf_op jit(solution)/shard_map/ppermute | solution.py:313
  27.6 6.0 %collective-permute-start.10 = (bf16[4,32,512]{2,1,0:T(8,128)(2,1)S(1)}, bf16[4,32,512]{2,1,0:T(8,128)(2,1)S(1)}, u32[]{:S(2)}, u32[]{:S(2)}) collective-permute-start(bf16[4,32,512]{2,1,0:T(8,128)(2,1)S(1)} %pad_maximum_fusion.rest_ref), channel_id=1, source_target_pairs={{0,2},{1,3},{2,0},{3,1},{4,6},{5,7},{6,4},{7,5},{8,10},{9,11},{10,... | collective-permute-start | bytes 393224 | tf_op jit(solution)/shard_map/ppermute | solution.py:316
  28.2 5.4 %collective-permute-start.14 = (bf16[4,32,512]{2,1,0:T(8,128)(2,1)S(1)}, bf16[4,32,512]{2,1,0:T(8,128)(2,1)S(1)}, u32[]{:S(2)}, u32[]{:S(2)}) collective-permute-start(bf16[4,32,512]{2,1,0:T(8,128)(2,1)S(1)} %collective-permute-done.9.cot_ref), channel_id=1, source_target_pairs={{0,1},{1,0},{2,3},{3,2},{4,5},{5,4},{6,7},{7,6},{8,9},{9,8},{10,11... | collective-permute-start | bytes 393224 | tf_op jit(solution)/shard_map/ppermute | solution.py:316
  29.1 6.4 %collective-permute-start.12 = (bf16[4,32,512]{2,1,0:T(8,128)(2,1)S(1)}, bf16[4,32,512]{2,1,0:T(8,128)(2,1)S(1)}, u32[]{:S(2)}, u32[]{:S(2)}) collective-permute-start(bf16[4,32,512]{2,1,0:T(8,128)(2,1)S(1)} %pad_maximum_fusion.rest_ref), channel_id=1, source_target_pairs={{0,1},{1,0},{2,3},{3,2},{4,5},{5,4},{6,7},{7,6},{8,9},{9,8},{10,11... | collective-permute-start | bytes 393224 | tf_op jit(solution)/shard_map/ppermute | solution.py:316
  33.6 2.7 %collective-permute-start.13 = (bf16[4,32,512]{2,1,0:T(8,128)(2,1)S(1)}, bf16[4,32,512]{2,1,0:T(8,128)(2,1)S(1)}, u32[]{:S(2)}, u32[]{:S(2)}) collective-permute-start(bf16[4,32,512]{2,1,0:T(8,128)(2,1)S(1)} %collective-permute-done.10.rest_ref), channel_id=1, source_target_pairs={{0,1},{1,0},{2,3},{3,2},{4,5},{5,4},{6,7},{7,6},{8,9},{9,8},{10,11... | collective-permute-start | bytes 393224 | tf_op jit(solution)/shard_map/ppermute | solution.py:316
  41.7 2.1 %collective-permute-start.15 = (bf16[8,32,512]{2,1,0:T(8,128)(2,1)S(1)}, bf16[8,32,512]{2,1,0:T(8,128)(2,1)S(1)}, u32[]{:S(2)}, u32[]{:S(2)}) collective-permute-start(bf16[8,32,512]{2,1,0:T(8,128)(2,1)S(1)} %get-tuple-element.139.after_ref), channel_id=1, source_target_pairs={{0,1},{1,0},{2,3},{3,2},{4,5},{5,4},{6,7},{7,6},{8,9},{9,8},{10,11... | collective-permute-start | bytes 786440 | tf_op jit(solution)/shard_map/ppermute | solution.py:316
  43.8 2.2 %collective-permute-start.16 = (bf16[8,32,512]{2,1,0:T(8,128)(2,1)S(1)}, bf16[8,32,512]{2,1,0:T(8,128)(2,1)S(1)}, u32[]{:S(2)}, u32[]{:S(2)}) collective-permute-start(bf16[8,32,512]{2,1,0:T(8,128)(2,1)S(1)} %shard_map.144), channel_id=1, source_target_pairs={{0,1},{1,0},{2,3},{3,2},{4,5},{5,4},{6,7},{7,6},{8,9},{9,8},{10,11... | collective-permute-start | bytes 786440 | tf_op jit(solution)/shard_map/ppermute | solution.py:316
  43.9 5.9 %collective-permute-start.17 = (bf16[4,32,512]{2,1,0:T(8,128)(2,1)S(1)}, bf16[4,32,512]{2,1,0:T(8,128)(2,1)S(1)}, u32[]{:S(2)}, u32[]{:S(2)}) collective-permute-start(bf16[4,32,512]{2,1,0:T(8,128)(2,1)S(1)} %get-tuple-element.140.after_ref), channel_id=1, source_target_pairs={{0,2},{1,3},{2,0},{3,1},{4,6},{5,7},{6,4},{7,5},{8,10},{9,11},{10,... | collective-permute-start | bytes 393224 | tf_op jit(solution)/shard_map/ppermute | solution.py:316
  49.9 5.2 %collective-permute-start.21 = (bf16[4,32,512]{2,1,0:T(8,128)(2,1)S(1)}, bf16[4,32,512]{2,1,0:T(8,128)(2,1)S(1)}, u32[]{:S(2)}, u32[]{:S(2)}) collective-permute-start(bf16[4,32,512]{2,1,0:T(8,128)(2,1)S(1)} %get-tuple-element.147), channel_id=1, source_target_pairs={{0,2},{1,3},{2,0},{3,1},{4,6},{5,7},{6,4},{7,5},{8,10},{9,11},{10,... | collective-permute-start | bytes 393224 | tf_op jit(solution)/shard_map/ppermute | solution.py:316
  50.5 7.5 %collective-permute-start.18 = (bf16[32,512]{1,0:T(8,128)(2,1)S(1)}, bf16[32,512]{1,0:T(8,128)(2,1)S(1)}, u32[]{:S(2)}, u32[]{:S(2)}) collective-permute-start(bf16[32,512]{1,0:T(8,128)(2,1)S(1)} %get-tuple-element.143), channel_id=1, source_target_pairs={{0,4},{1,5},{2,6},{3,7},{4,0},{5,1},{6,2},{7,3},{8,12},{9,13},{10,... | collective-permute-start | bytes 98312 | tf_op jit(solution)/shard_map/ppermute | solution.py:313
  52.4 7.2 %collective-permute-start.19 = (bf16[32,512]{1,0:T(8,128)(2,1)S(1)}, bf16[32,512]{1,0:T(8,128)(2,1)S(1)}, u32[]{:S(2)}, u32[]{:S(2)}) collective-permute-start(bf16[32,512]{1,0:T(8,128)(2,1)S(1)} %get-tuple-element.144), channel_id=1, source_target_pairs={{0,8},{1,9},{2,10},{3,11},{4,12},{5,13},{6,14},{7,15},{8,0},{9,1},... | collective-permute-start | bytes 98312 | tf_op jit(solution)/shard_map/ppermute | solution.py:313
  53.3 6.3 %collective-permute-start.20 = (bf16[32,512]{1,0:T(8,128)(2,1)S(1)}, bf16[32,512]{1,0:T(8,128)(2,1)S(1)}, u32[]{:S(2)}, u32[]{:S(2)}) collective-permute-start(bf16[32,512]{1,0:T(8,128)(2,1)S(1)} %get-tuple-element.145), channel_id=1, source_target_pairs={{0,12},{1,13},{2,14},{3,15},{4,8},{5,9},{6,10},{7,11},{8,4},{9,5},... | collective-permute-start | bytes 98312 | tf_op jit(solution)/shard_map/ppermute | solution.py:313
  55.1 4.5 %collective-permute-start.22 = (bf16[32,512]{1,0:T(8,128)(2,1)S(1)}, bf16[32,512]{1,0:T(8,128)(2,1)S(1)}, u32[]{:S(2)}, u32[]{:S(2)}) collective-permute-start(bf16[32,512]{1,0:T(8,128)(2,1)S(1)} %get-tuple-element.149), channel_id=1, source_target_pairs={{0,4},{1,5},{2,6},{3,7},{4,0},{5,1},{6,2},{7,3},{8,12},{9,13},{10,... | collective-permute-start | bytes 98312 | tf_op jit(solution)/shard_map/ppermute | solution.py:313
  57.0 4.8 %collective-permute-start.23 = (bf16[32,512]{1,0:T(8,128)(2,1)S(1)}, bf16[32,512]{1,0:T(8,128)(2,1)S(1)}, u32[]{:S(2)}, u32[]{:S(2)}) collective-permute-start(bf16[32,512]{1,0:T(8,128)(2,1)S(1)} %get-tuple-element.150), channel_id=1, source_target_pairs={{0,8},{1,9},{2,10},{3,11},{4,12},{5,13},{6,14},{7,15},{8,0},{9,1},... | collective-permute-start | bytes 98312 | tf_op jit(solution)/shard_map/ppermute | solution.py:313
  58.0 5.7 %collective-permute-start.24 = (bf16[32,512]{1,0:T(8,128)(2,1)S(1)}, bf16[32,512]{1,0:T(8,128)(2,1)S(1)}, u32[]{:S(2)}, u32[]{:S(2)}) collective-permute-start(bf16[32,512]{1,0:T(8,128)(2,1)S(1)} %get-tuple-element.151), channel_id=1, source_target_pairs={{0,12},{1,13},{2,14},{3,15},{4,8},{5,9},{6,10},{7,11},{8,4},{9,5},... | collective-permute-start | bytes 98312 | tf_op jit(solution)/shard_map/ppermute | solution.py:313
  (11 other events, 65.4 us)

commit v8 on v7

--- a/solution.py
+++ b/solution.py
@@ -10,7 +10,7 @@
 clip_top = 448.0
 eps = 1e-05
 LANES = 128
-STAGE = 7
+STAGE = 4
 FLOPS_PER_MICRO = 1.15e9
 f32 = jnp.float32
 bf16 = jnp.bfloat16
@@ -190,23 +190,31 @@
         acc_ref[...] = terms if k == 0 else acc_ref[...] + terms
 
 
-def middle_kernel(me_ref, rest_ref, gain_ref, weight_ref, *refs):
+def activation_kernel(me_ref, rest_ref, gain_ref, weight_ref, *refs):
     ins, refs = refs[:10], refs[10:]
-    active_ref, own_ref, send_ref, keep_ref, acc_ref, square_ref, piece_ref, rows_ref = refs
-    quarter, tokens, width = rest_ref.shape
-    half, n, chunks = 2 * quarter, 4 * quarter, width // LANES
-    width_all = weight_ref.shape[0]
-    me = me_ref[0]
+    active_ref, gh_ref, own_ref, acc_ref, square_ref, piece_ref = refs
     up_kernel(3, me_ref, rest_ref, gain_ref, weight_ref, acc_ref, square_ref, own_ref, piece_ref)
     product = acc_ref[...] + (ins[0][...] + ins[1][...] + ins[2][...])
     squares = square_ref[...] + (ins[3][...] + ins[4][...] + ins[5][...])
     total = jnp.sum(squares, axis=1, keepdims=True)
-    hidden = lax.rsqrt(total / width_all + eps) * product
+    hidden = lax.rsqrt(total / weight_ref.shape[0] + eps) * product
     sigma = jax.nn.sigmoid(hidden)
     active_ref[...] = (hidden * sigma).astype(bf16)
     grad_active = (ins[6][...] + ins[7][...] + (ins[8][...] + ins[9][...])).T
-    gh = (grad_active * sigma * (1.0 + hidden * (1.0 - sigma))).astype(bf16)
-    for share in range(n):
+    gh_ref[...] = (grad_active * sigma * (1.0 + hidden * (1.0 - sigma))).astype(bf16)
+
+
+def grad_norm_kernel(first, last, me_ref, gh_ref, weight_ref, *refs):
+    if first:
+        rows_in_ref, send_ref, keep_ref, rows_ref = refs
+        rows_ref[...] = rows_in_ref[...]
+    else:
+        (rows_ref,) = refs
+    chunks = rows_ref.shape[0]
+    tokens, width = gh_ref.shape[0], chunks * LANES
+    half, n = tokens // 4, tokens // 2
+    gh = gh_ref[...]
+    for share in range(first, last):
         block = weight_ref[share * width : (share + 1) * width, :]
         terms = dot_by_halves(block, gh).T
         for p in range(2):
@@ -214,7 +222,9 @@
                 rows_ref[c, pl.ds(p * n + share, n, stride=tokens), :] = terms[
                     p * n : (p + 1) * n, c * LANES : (c + 1) * LANES
                 ]
-    core = lax.rem(me, 2)
+    if last < n:
+        return
+    core = lax.rem(me_ref[0], 2)
     for k in range(half):
         keep_at = pl.multiple_of((2 * k + core) * tokens, tokens)
         send_at = pl.multiple_of((2 * k + 1 - core) * tokens, tokens)
@@ -224,7 +234,7 @@
             send_ref[k, :, cols] = rows_ref[c, pl.ds(send_at, tokens), :].astype(bf16)
 
 
-def down_kernel(other, me_ref, active_ref, weight_ref, after_ref, out_ref):
+def down_kernel(other, me_ref, active_ref, weight_ref, out_ref):
     half, _, width = out_ref.shape
     core = lax.rem(me_ref[0] + other, 2)
 
@@ -236,15 +246,11 @@
     pl.loop(0, half, unroll=4)(share)
 
 
-def pair_kernel(me_ref, kept_ref, arrived_ref, *refs):
-    ins, (send_ref, keep_ref), shares = (refs[:2], refs[2:4], refs[4:]) if len(refs) > 2 else ((), refs, ())
-    quarter = send_ref.shape[0]
+def pair_kernel(me_ref, kept_ref, arrived_ref, send_ref, keep_ref):
     _, row, _ = place(me_ref[0])
-    for k in range(quarter):
+    for k in range(send_ref.shape[0]):
         for out_ref, at in ((send_ref, 2 * k + 1 - row), (keep_ref, 2 * k + row)):
             out_ref[k] = (kept_ref[at].astype(f32) + arrived_ref[at].astype(f32)).astype(bf16)
-    if shares:
-        line_kernel(me_ref, *ins, *shares)
 
 
 def line_kernel(me_ref, kept_ref, arrived_ref, *refs):
@@ -397,11 +403,6 @@
         )
 
     together = lax.optimization_barrier
-    grads = [grad_active_part(0)]
-    cot_line, grads[0] = together((cot_line, grads[0]))
-    cots.append(swap(cot_line, 2))
-    blocks, grads[0] = together((blocks, grads[0]))
-
     def rebuild(out, micros):
         return call(
             rebuild_kernel,
@@ -417,75 +418,102 @@
 
     share = rebuild(struct(share_shape, bf16), STAGE)
     lines = [shift(share, r) for r in range(quarter)]
-    grads.append(grad_active_part(1))
-    cot_line, cot_row, grads[1] = together((cot_line, cots[1], grads[1]))
-    cots += [swap(cot_line, 1), swap(cot_row, 1)]
-    lines, grads[1] = together((lines, grads[1]))
+    cots[0], share_after = together((cot_line, share))
+    cot_row = swap(cots[0], 2)
+    grads = [grad_active_part(0)]
+    new_receiver_base = rebuild(struct(receiver_base.shape, f32), 0.7)
+    lines, grads[0], new_receiver_base = together((lines, grads[0], new_receiver_base))
     rest_line = jnp.stack(lines)
     rest_row = swap(rest_line, 2)
     rests = [rest_line]
     products = [up_product_part(0)]
-    rest_line, products[0] = together((rest_line, products[0]))
+    rest_line, cot_line, cot_row, products[0] = together((rest_line, cots[0], cot_row, products[0]))
     rest_line_other = swap(rest_line, 1)
-    grads.append(grad_active_part(2))
-    new_receiver_base = rebuild(struct(receiver_base.shape, f32), 0.7)
+    cots += [cot_row, swap(cot_line, 1)]
+    grads += [grad_active_part(1), grad_active_part(2)]
     new_sender_base = call(
         sender_base_kernel,
         struct(sender_base.shape, f32),
         [SMEM] + [VMEM] * 2,
         [offset, new_rows, sender_base],
     )
-    rest_row, grads[2], new_sender_base, new_receiver_base = together(
-        (rest_row, grads[2], new_sender_base, new_receiver_base)
+    rest_row, cot_row, grads[1], grads[2], new_sender_base = together(
+        (rest_row, cot_row, grads[1], grads[2], new_sender_base)
     )
     rests += [rest_row, rest_line_other, swap(rest_row, 1)]
+    cots.append(swap(cot_row, 1))
     grads.append(grad_active_part(3))
     products += [up_product_part(1), up_product_part(2)]
     gas, own_cots = zip(*grads)
     accs, squares, owns = map(list, zip(*products))
 
     half_out = struct((half, tokens, width), bf16)
-    active, own, grad_send, grad_keep = call(
-        middle_kernel,
-        (struct(hidden_shape, bf16), share_f32, half_out, half_out),
+    active, grad_hidden, own = call(
+        activation_kernel,
+        (struct(hidden_shape, bf16), struct(hidden_shape, bf16), share_f32),
         [SMEM] + [VMEM] * 13,
         [me_in, rests[3], gain, up_weight, *accs, *squares, *gas],
-        [pltpu.VMEM(x.shape, x.dtype) for x in sums]
-        + [
-            pltpu.VMEM(share_shape, f32),
-            pltpu.VMEM((width // LANES, n * tokens, LANES), f32),
-        ],
-        micros=6.5,
+        [pltpu.VMEM(x.shape, x.dtype) for x in sums] + [pltpu.VMEM(share_shape, f32)],
+        micros=1.5,
     )
     owns.append(own)
 
-    def down_terms(other, after):
+    def down_terms(other, active):
         return call(
             functools.partial(down_kernel, other),
             half_out,
-            [SMEM] + [VMEM] * 2 + [ANY],
-            [me_in, active, down_weight, after],
+            [SMEM] + [VMEM] * 2,
+            [me_in, active, down_weight],
             micros=1.5,
         )
 
-    pair_out = (struct(line_shape, bf16),) * 2
-    line_out = (struct(share_shape, bf16),) * quarter
+    def pair_sum(kept, arrived):
+        return call(
+            pair_kernel,
+            (struct(line_shape, bf16),) * 2,
+            [SMEM] + [VMEM] * 2,
+            [me_in, kept, arrived],
+        )
+
+    def line_sum(kept, arrived):
+        shares = call(
+            line_kernel,
+            (struct(share_shape, bf16),) * quarter,
+            [SMEM] + [VMEM] * 2,
+            [me_in, kept, arrived],
+        )
+        return [shift(x, r) for r, x in enumerate(shares)]
+
+    out_send = down_terms(1, active)
+    out_in = swap(out_send, 1)
+    active, out_send = together((active, out_send))
+    out_send, out_row = pair_sum(down_terms(0, active), out_in)
+    out_row_in = swap(out_send, 2)
+    grad_hidden, out_row = together((grad_hidden, out_row))
+    rows_out = struct((width // LANES, n * tokens, LANES), f32)
+    most = n - n // 8
+    grad_rows = call(
+        functools.partial(grad_norm_kernel, 0, most),
+        rows_out,
+        [SMEM] + [VMEM] * 2,
+        [me_in, grad_hidden, up_weight],
+        micros=4,
+    )
+    grad_rows, out_row_in = together((grad_rows, out_row_in))
+    grad_send, grad_keep = call(
+        functools.partial(grad_norm_kernel, most, n),
+        (half_out, half_out),
+        [SMEM] + [VMEM] * 3,
+        [me_in, grad_hidden, up_weight, grad_rows],
+        [pltpu.VMEM(rows_out.shape, f32)],
+        micros=0.7,
+    )
     grad_in = swap(grad_send, 1)
-    out_in = swap(down_terms(1, grad_send), 1)
-    grad_send, grad_row = call(
-        pair_kernel, pair_out, [SMEM] + [VMEM] * 2, [me_in, grad_keep, grad_in]
-    )
+    grad_send, grad_row = pair_sum(grad_keep, grad_in)
     grad_row_in = swap(grad_send, 2)
-    out_send, out_row, *grad_line = call(
-        pair_kernel,
-        pair_out + line_out,
-        [SMEM] + [VMEM] * 4,
-        [me_in, down_terms(0, grad_send), out_in, grad_row, grad_row_in],
-    )
-    out_row_in = swap(out_send, 2)
-    grad_line = [shift(x, r) for r, x in enumerate(grad_line)]
-    out_line = call(line_kernel, line_out, [SMEM] + [VMEM] * 2, [me_in, out_row, out_row_in])
-    out_line = [shift(x, r) for r, x in enumerate(out_line)]
+    out_row, grad_row = together((out_row, grad_row))
+    out_line = line_sum(out_row, out_row_in)
+    grad_line = line_sum(grad_row, grad_row_in)
     layer_out, returned = call(
         functools.partial(final_kernel, width_all),
         (struct(share_shape, bf16), struct((2, width_all // LANES, LANES), f32)),

time: 64.7 us -> 61.5 us (0.951)
  local copies, waits for them, and re-layouts: 3.02 us -> 0.04 us
    unnamed x20, local copies, waits for them, and re-layouts: 3.02 us -> 0.04 us
    pallas_call x18 -> x21, Pallas kernels: 17.9 us -> 18 us  [call(): pl.pallas_call(kernel, out_shape=outs, in_specs=ins, out_specs=jax.tree.m...]
  transfers between devices with their start and end apart: 25 -> 25, of which waited for: 7 -> 10; matrix products, arithmetic and copies ran while one was open for 0% -> 0% of each run, Pallas kernels for 18% -> 22%
where the time goes in v8:
time: 61.5 us; the launch traced here: 61.4 us
  starting transfers between devices  25.3 us (41%)
  Pallas kernels  19.2 us (31%)
  waiting for transfers between devices  15.2 us (25%)
  between operations  1.55 us (3%)
    ppermute x12, starting transfers between devices, shift(): return lax.ppermute(x, 'dp', [(d, d ^ 4 * r) for d in range(n)]) if r else x  19 us
    pallas_call x21, Pallas kernels, call(): pl.pallas_call(kernel, out_shape=outs, in_specs=ins, out_specs=jax.tree.m...  18 us
    ppermute x12, waiting for transfers between devices, shift(): return lax.ppermute(x, 'dp', [(d, d ^ 4 * r) for d in range(n)]) if r else x  8.48 us
    ppermute x13, waiting for transfers between devices, swap(): return lax.ppermute(x, 'dp', [(d, d ^ bits) for d in range(n)])  6.7 us
    ppermute x13, starting transfers between devices, swap(): return lax.ppermute(x, 'dp', [(d, d ^ bits) for d in range(n)])  6.31 us
  transfers between devices with their start and end apart: 25, of which 10 were waited for; matrix products, arithmetic and copies ran while one was open for 0% of the time, Pallas kernels for 22%

profile of v8, /device:TPU:0, one launch (start us, length us, event | category | flops | bytes accessed | tf_op | source)
XLA Modules:
  0.0 61.4 jit_solution(2601424030122649865)
XLA Ops:
  1.3 1.2 %shard_map.129 = (f32[2,8192]{1,0:T(2,128)S(1)}, f32[2,32,512]{2,1,0:T(8,128)S(1)}, f32[16,512]{1,0:T(8,128)S(1)}, bf16[32,768]{1,0:T(8,128)(2,1)S(1)}, bf16[32,...) custom-call(s32[1]{0:T(128)} %bitcast.me_ref, s32[1]{0:T(128)S(6)} %sub.7.offset_ref, ...), custom_call_target="tpu_custom_call" | custom-call | tf_op jit(solution)/shard_map/pallas_call | solution.py:352
  2.6 3.1 %collective-permute-start = (bf16[32,768]{1,0:T(8,128)(2,1)S(1)}, bf16[32,768]{1,0:T(8,128)(2,1)S(1)}, u32[]{:S(2)}, u32[]{:S(2)}) collective-permute-start(bf16[32,768]{1,0:T(8,128)(2,1)S(1)} %get-tuple-element.81), channel_id=1, source_target_pairs={{0,4},{1,5},{2,6},{3,7},{4,0},{5,1},{6,2},{7,3},{8,12},{9,13},{10,... | collective-permute-start | bytes 147464 | tf_op jit(solution)/shard_map/ppermute | solution.py:319
  5.6 2.6 %collective-permute-start.1 = (bf16[32,768]{1,0:T(8,128)(2,1)S(1)}, bf16[32,768]{1,0:T(8,128)(2,1)S(1)}, u32[]{:S(2)}, u32[]{:S(2)}) collective-permute-start(bf16[32,768]{1,0:T(8,128)(2,1)S(1)} %get-tuple-element.82), channel_id=1, source_target_pairs={{0,8},{1,9},{2,10},{3,11},{4,12},{5,13},{6,14},{7,15},{8,0},{9,1},... | collective-permute-start | bytes 147464 | tf_op jit(solution)/shard_map/ppermute | solution.py:319
  8.2 3.3 %collective-permute-done.1.refs_2_ = bf16[32,768]{1,0:T(8,128)(2,1)S(1)} collective-permute-done((bf16[32,768]{1,0:T(8,128)(2,1)S(1)}, bf16[32,768]{1,0:T(8,128)(2,1)S(1)}, u32[]{:S(2)}, u32[]{:S(2)}) %collective-permute-start.1) | collective-permute-done | bytes 49184 | tf_op jit(solution)/shard_map/ppermute | solution.py:319
  11.6 2.6 %collective-permute-done.2.refs_3_ = bf16[32,768]{1,0:T(8,128)(2,1)S(1)} collective-permute-done((bf16[32,768]{1,0:T(8,128)(2,1)S(1)}, bf16[32,768]{1,0:T(8,128)(2,1)S(1)}, u32[]{:S(2)}, u32[]{:S(2)}) %collective-permute-start.2) | collective-permute-done | bytes 49184 | tf_op jit(solution)/shard_map/ppermute | solution.py:319
  14.2 1.6 %collective-permute-start.4 = (bf16[4,16,128]{2,1,0:T(8,128)(2,1)S(1)}, bf16[4,16,128]{2,1,0:T(8,128)(2,1)S(1)}, u32[]{:S(2)}, u32[]{:S(2)}) collective-permute-start(bf16[4,16,128]{2,1,0:T(8,128)(2,1)S(1)} %get-tuple-element.86), channel_id=1, source_target_pairs={{0,2},{1,3},{2,0},{3,1},{4,6},{5,7},{6,4},{7,5},{8,10},{9,11},{10,... | collective-permute-start | bytes 49160 | tf_op jit(solution)/shard_map/ppermute | solution.py:322
  16.8 1.2 %collective-permute-done.4.b2 = bf16[4,16,128]{2,1,0:T(8,128)(2,1)S(1)} collective-permute-done((bf16[4,16,128]{2,1,0:T(8,128)(2,1)S(1)}, bf16[4,16,128]{2,1,0:T(8,128)(2,1)S(1)}, u32[]{:S(2)}, u32[]{:S(2)}) %collective-permute-start.4) | collective-permute-done | bytes 16416 | tf_op jit(solution)/shard_map/ppermute | solution.py:322
  18.0 0.9 %collective-permute-done.5.b3 = bf16[4,16,128]{2,1,0:T(8,128)(2,1)S(1)} collective-permute-done((bf16[4,16,128]{2,1,0:T(8,128)(2,1)S(1)}, bf16[4,16,128]{2,1,0:T(8,128)(2,1)S(1)}, u32[]{:S(2)}, u32[]{:S(2)}) %collective-permute-start.5) | collective-permute-done | bytes 16416 | tf_op jit(solution)/shard_map/ppermute | solution.py:322
  19.9 3.6 %collective-permute-start.6 = (bf16[32,512]{1,0:T(8,128)(2,1)S(1)}, bf16[32,512]{1,0:T(8,128)(2,1)S(1)}, u32[]{:S(2)}, u32[]{:S(2)}) collective-permute-start(bf16[32,512]{1,0:T(8,128)(2,1)S(1)} %shard_map.131.share_ref), channel_id=1, source_target_pairs={{0,4},{1,5},{2,6},{3,7},{4,0},{5,1},{6,2},{7,3},{8,12},{9,13},{10,... | collective-permute-start | bytes 98312 | tf_op jit(solution)/shard_map/ppermute | solution.py:319
  24.2 1.2 %shard_map.132 = (f32[896,32]{1,0:T(8,128)S(1)}, f32[32,512]{1,0:T(8,128)S(1)}) custom-call(s32[1]{0:T(128)} %bitcast.me_ref, bf16[4,32,512]{2,1,0:T(8,128)(2,1)S(1)} %get-tuple-element.104.cot_ref, bf16[896,8192]{1,0:T(8,128)(2,1)S(1)} %bitcast.14), custom_call_target="tpu_custom_call" | custom-call | flops 1840000000 | tf_op jit(solution)/shard_map/pallas_call | solution.py:329
  26.2 1.4 %collective-permute-start.9 = (bf16[4,32,512]{2,1,0:T(8,128)(2,1)S(1)}, bf16[4,32,512]{2,1,0:T(8,128)(2,1)S(1)}, u32[]{:S(2)}, u32[]{:S(2)}) collective-permute-start(bf16[4,32,512]{2,1,0:T(8,128)(2,1)S(1)} %pad_maximum_fusion.rest_ref), channel_id=1, source_target_pairs={{0,2},{1,3},{2,0},{3,1},{4,6},{5,7},{6,4},{7,5},{8,10},{9,11},{10,... | collective-permute-start | bytes 393224 | tf_op jit(solution)/shard_map/ppermute | solution.py:322
  29.6 1.2 %shard_map.135 = (f32[896,32]{1,0:T(8,128)S(1)}, f32[32,512]{1,0:T(8,128)S(1)}) custom-call(s32[1]{0:T(128)} %bitcast.me_ref, bf16[4,32,512]{2,1,0:T(8,128)(2,1)S(1)} %collective-permute-done.10.cot_ref, bf16[896,8192]{1,0:T(8,128)(2,1)S(1)} %bitcast.14), custom_call_target="tpu_custom_call" | custom-call | flops 1840000000 | tf_op jit(solution)/shard_map/pallas_call | solution.py:329
  30.8 1.2 %shard_map.136 = (f32[896,32]{1,0:T(8,128)S(1)}, f32[32,512]{1,0:T(8,128)S(1)}) custom-call(s32[1]{0:T(128)} %bitcast.me_ref, bf16[4,32,512]{2,1,0:T(8,128)(2,1)S(1)} %collective-permute-done.11.cot_ref, bf16[896,8192]{1,0:T(8,128)(2,1)S(1)} %bitcast.14), custom_call_target="tpu_custom_call" | custom-call | flops 1840000000 | tf_op jit(solution)/shard_map/pallas_call | solution.py:329
  34.1 1.2 %shard_map.140 = (f32[896,32]{1,0:T(8,128)S(1)}, f32[32,512]{1,0:T(8,128)S(1)}) custom-call(s32[1]{0:T(128)} %bitcast.me_ref, bf16[4,32,512]{2,1,0:T(8,128)(2,1)S(1)} %collective-permute-done.14.cot_ref, bf16[896,8192]{1,0:T(8,128)(2,1)S(1)} %bitcast.14), custom_call_target="tpu_custom_call" | custom-call | flops 1840000000 | tf_op jit(solution)/shard_map/pallas_call | solution.py:329
  36.1 1.7 %shard_map.142 = bf16[8,32,512]{2,1,0:T(8,128)(2,1)S(1)} custom-call(s32[1]{0:T(128)} %bitcast.me_ref, bf16[32,896]{1,0:T(8,128)(2,1)S(1)} %get-tuple-element.133.active_ref, bf16[896,8192]{1,0:T(8,128)(2,1)S(1)} %bitcast.14), custom_call_target="tpu_custom_call" | custom-call | flops 1724999936 | tf_op jit(solution)/shard_map/pallas_call | solution.py:329
  37.8 1.5 %shard_map.143.kept_ref = bf16[8,32,512]{2,1,0:T(8,128)(2,1)S(1)} custom-call(s32[1]{0:T(128)} %bitcast.me_ref, bf16[32,896]{1,0:T(8,128)(2,1)S(1)} %get-tuple-element.133.active_ref, bf16[896,8192]{1,0:T(8,128)(2,1)S(1)} %bitcast.14), custom_call_target="tpu_custom_call" | custom-call | flops 1724999936 | tf_op jit(solution)/shard_map/pallas_call | solution.py:329
  39.9 3.7 %shard_map.145.refs_0_ = f32[4,512,128]{2,1,0:T(8,128)S(1)} custom-call(s32[1]{0:T(128)} %bitcast.me_ref, bf16[32,896]{1,0:T(8,128)(2,1)S(1)} %get-tuple-element.136.gh_ref, bf16[8192,896]{1,0:T(8,128)(2,1)S(1)} %bitcast.16), custom_call_target="tpu_custom_call" | custom-call | flops 4600000000 | tf_op jit(solution)/shard_map/pallas_call | solution.py:329
  43.7 1.7 %collective-permute-done.16.arrived_ref = bf16[4,32,512]{2,1,0:T(8,128)(2,1)S(1)} collective-permute-done((bf16[4,32,512]{2,1,0:T(8,128)(2,1)S(1)}, bf16[4,32,512]{2,1,0:T(8,128)(2,1)S(1)}, u32[]{:S(2)}, u32[]{:S(2)}) %collective-permute-start.16) | collective-permute-done | bytes 131104 | tf_op jit(solution)/shard_map/ppermute | solution.py:322
  46.3 1.5 %collective-permute-done.17.arrived_ref = bf16[8,32,512]{2,1,0:T(8,128)(2,1)S(1)} collective-permute-done((bf16[8,32,512]{2,1,0:T(8,128)(2,1)S(1)}, bf16[8,32,512]{2,1,0:T(8,128)(2,1)S(1)}, u32[]{:S(2)}, u32[]{:S(2)}) %collective-permute-start.17) | collective-permute-done | bytes 262176 | tf_op jit(solution)/shard_map/ppermute | solution.py:322
  49.3 0.9 %collective-permute-start.23 = (bf16[32,512]{1,0:T(8,128)(2,1)S(1)}, bf16[32,512]{1,0:T(8,128)(2,1)S(1)}, u32[]{:S(2)}, u32[]{:S(2)}) collective-permute-start(bf16[32,512]{1,0:T(8,128)(2,1)S(1)} %get-tuple-element.152), channel_id=1, source_target_pairs={{0,8},{1,9},{2,10},{3,11},{4,12},{5,13},{6,14},{7,15},{8,0},{9,1},... | collective-permute-start | bytes 98312 | tf_op jit(solution)/shard_map/ppermute | solution.py:319
  50.2 2.7 %collective-permute-start.24 = (bf16[32,512]{1,0:T(8,128)(2,1)S(1)}, bf16[32,512]{1,0:T(8,128)(2,1)S(1)}, u32[]{:S(2)}, u32[]{:S(2)}) collective-permute-start(bf16[32,512]{1,0:T(8,128)(2,1)S(1)} %get-tuple-element.153), channel_id=1, source_target_pairs={{0,12},{1,13},{2,14},{3,15},{4,8},{5,9},{6,10},{7,11},{8,4},{9,5},... | collective-permute-start | bytes 98312 | tf_op jit(solution)/shard_map/ppermute | solution.py:319
  53.9 0.9 %collective-permute-start.20 = (bf16[32,512]{1,0:T(8,128)(2,1)S(1)}, bf16[32,512]{1,0:T(8,128)(2,1)S(1)}, u32[]{:S(2)}, u32[]{:S(2)}) collective-permute-start(bf16[32,512]{1,0:T(8,128)(2,1)S(1)} %get-tuple-element.146), channel_id=1, source_target_pairs={{0,8},{1,9},{2,10},{3,11},{4,12},{5,13},{6,14},{7,15},{8,0},{9,1},... | collective-permute-start | bytes 98312 | tf_op jit(solution)/shard_map/ppermute | solution.py:319
  54.9 3.1 %collective-permute-start.21 = (bf16[32,512]{1,0:T(8,128)(2,1)S(1)}, bf16[32,512]{1,0:T(8,128)(2,1)S(1)}, u32[]{:S(2)}, u32[]{:S(2)}) collective-permute-start(bf16[32,512]{1,0:T(8,128)(2,1)S(1)} %get-tuple-element.147), channel_id=1, source_target_pairs={{0,12},{1,13},{2,14},{3,15},{4,8},{5,9},{6,10},{7,11},{8,4},{9,5},... | collective-permute-start | bytes 98312 | tf_op jit(solution)/shard_map/ppermute | solution.py:319
  58.8 1.8 %collective-permute-done.21.refs_11_ = bf16[32,512]{1,0:T(8,128)(2,1)S(1)} collective-permute-done((bf16[32,512]{1,0:T(8,128)(2,1)S(1)}, bf16[32,512]{1,0:T(8,128)(2,1)S(1)}, u32[]{:S(2)}, u32[]{:S(2)}) %collective-permute-start.21) | collective-permute-done | bytes 32800 | tf_op jit(solution)/shard_map/ppermute | solution.py:319
  (71 shorter events, 13.9 us)
Async XLA Ops:
  2.6 5.7 %collective-permute-start = (bf16[32,768]{1,0:T(8,128)(2,1)S(1)}, bf16[32,768]{1,0:T(8,128)(2,1)S(1)}, u32[]{:S(2)}, u32[]{:S(2)}) collective-permute-start(bf16[32,768]{1,0:T(8,128)(2,1)S(1)} %get-tuple-element.81), channel_id=1, source_target_pairs={{0,4},{1,5},{2,6},{3,7},{4,0},{5,1},{6,2},{7,3},{8,12},{9,13},{10,... | collective-permute-start | bytes 147464 | tf_op jit(solution)/shard_map/ppermute | solution.py:319
  5.6 5.9 %collective-permute-start.1 = (bf16[32,768]{1,0:T(8,128)(2,1)S(1)}, bf16[32,768]{1,0:T(8,128)(2,1)S(1)}, u32[]{:S(2)}, u32[]{:S(2)}) collective-permute-start(bf16[32,768]{1,0:T(8,128)(2,1)S(1)} %get-tuple-element.82), channel_id=1, source_target_pairs={{0,8},{1,9},{2,10},{3,11},{4,12},{5,13},{6,14},{7,15},{8,0},{9,1},... | collective-permute-start | bytes 147464 | tf_op jit(solution)/shard_map/ppermute | solution.py:319
  8.2 5.9 %collective-permute-start.2 = (bf16[32,768]{1,0:T(8,128)(2,1)S(1)}, bf16[32,768]{1,0:T(8,128)(2,1)S(1)}, u32[]{:S(2)}, u32[]{:S(2)}) collective-permute-start(bf16[32,768]{1,0:T(8,128)(2,1)S(1)} %get-tuple-element.83), channel_id=1, source_target_pairs={{0,12},{1,13},{2,14},{3,15},{4,8},{5,9},{6,10},{7,11},{8,4},{9,5},... | collective-permute-start | bytes 147464 | tf_op jit(solution)/shard_map/ppermute | solution.py:319
  14.2 2.6 %collective-permute-start.3 = (bf16[4,16,128]{2,1,0:T(8,128)(2,1)S(1)}, bf16[4,16,128]{2,1,0:T(8,128)(2,1)S(1)}, u32[]{:S(2)}, u32[]{:S(2)}) collective-permute-start(bf16[4,16,128]{2,1,0:T(8,128)(2,1)S(1)} %get-tuple-element.85), channel_id=1, source_target_pairs={{0,1},{1,0},{2,3},{3,2},{4,5},{5,4},{6,7},{7,6},{8,9},{9,8},{10,11... | collective-permute-start | bytes 49160 | tf_op jit(solution)/shard_map/ppermute | solution.py:322
  14.2 3.8 %collective-permute-start.4 = (bf16[4,16,128]{2,1,0:T(8,128)(2,1)S(1)}, bf16[4,16,128]{2,1,0:T(8,128)(2,1)S(1)}, u32[]{:S(2)}, u32[]{:S(2)}) collective-permute-start(bf16[4,16,128]{2,1,0:T(8,128)(2,1)S(1)} %get-tuple-element.86), channel_id=1, source_target_pairs={{0,2},{1,3},{2,0},{3,1},{4,6},{5,7},{6,4},{7,5},{8,10},{9,11},{10,... | collective-permute-start | bytes 49160 | tf_op jit(solution)/shard_map/ppermute | solution.py:322
  15.8 3.2 %collective-permute-start.5 = (bf16[4,16,128]{2,1,0:T(8,128)(2,1)S(1)}, bf16[4,16,128]{2,1,0:T(8,128)(2,1)S(1)}, u32[]{:S(2)}, u32[]{:S(2)}) collective-permute-start(bf16[4,16,128]{2,1,0:T(8,128)(2,1)S(1)} %get-tuple-element.87), channel_id=1, source_target_pairs={{0,3},{1,2},{2,1},{3,0},{4,7},{5,6},{6,5},{7,4},{8,11},{9,10},{10,... | collective-permute-start | bytes 49160 | tf_op jit(solution)/shard_map/ppermute | solution.py:322
  19.1 7.1 %collective-permute-start.8 = (bf16[32,512]{1,0:T(8,128)(2,1)S(1)}, bf16[32,512]{1,0:T(8,128)(2,1)S(1)}, u32[]{:S(2)}, u32[]{:S(2)}) collective-permute-start(bf16[32,512]{1,0:T(8,128)(2,1)S(1)} %shard_map.131.share_ref), channel_id=1, source_target_pairs={{0,12},{1,13},{2,14},{3,15},{4,8},{5,9},{6,10},{7,11},{8,4},{9,5},... | collective-permute-start | bytes 98312 | tf_op jit(solution)/shard_map/ppermute | solution.py:319
  19.9 6.3 %collective-permute-start.7 = (bf16[32,512]{1,0:T(8,128)(2,1)S(1)}, bf16[32,512]{1,0:T(8,128)(2,1)S(1)}, u32[]{:S(2)}, u32[]{:S(2)}) collective-permute-start(bf16[32,512]{1,0:T(8,128)(2,1)S(1)} %shard_map.131.share_ref), channel_id=1, source_target_pairs={{0,8},{1,9},{2,10},{3,11},{4,12},{5,13},{6,14},{7,15},{8,0},{9,1},... | collective-permute-start | bytes 98312 | tf_op jit(solution)/shard_map/ppermute | solution.py:319
  19.9 6.3 %collective-permute-start.6 = (bf16[32,512]{1,0:T(8,128)(2,1)S(1)}, bf16[32,512]{1,0:T(8,128)(2,1)S(1)}, u32[]{:S(2)}, u32[]{:S(2)}) collective-permute-start(bf16[32,512]{1,0:T(8,128)(2,1)S(1)} %shard_map.131.share_ref), channel_id=1, source_target_pairs={{0,4},{1,5},{2,6},{3,7},{4,0},{5,1},{6,2},{7,3},{8,12},{9,13},{10,... | collective-permute-start | bytes 98312 | tf_op jit(solution)/shard_map/ppermute | solution.py:319
  23.5 5.6 %collective-permute-start.10 = (bf16[4,32,512]{2,1,0:T(8,128)(2,1)S(1)}, bf16[4,32,512]{2,1,0:T(8,128)(2,1)S(1)}, u32[]{:S(2)}, u32[]{:S(2)}) collective-permute-start(bf16[4,32,512]{2,1,0:T(8,128)(2,1)S(1)} %get-tuple-element.104.cot_ref), channel_id=1, source_target_pairs={{0,2},{1,3},{2,0},{3,1},{4,6},{5,7},{6,4},{7,5},{8,10},{9,11},{10,... | collective-permute-start | bytes 393224 | tf_op jit(solution)/shard_map/ppermute | solution.py:322
  26.2 5.8 %collective-permute-start.9 = (bf16[4,32,512]{2,1,0:T(8,128)(2,1)S(1)}, bf16[4,32,512]{2,1,0:T(8,128)(2,1)S(1)}, u32[]{:S(2)}, u32[]{:S(2)}) collective-permute-start(bf16[4,32,512]{2,1,0:T(8,128)(2,1)S(1)} %pad_maximum_fusion.rest_ref), channel_id=1, source_target_pairs={{0,2},{1,3},{2,0},{3,1},{4,6},{5,7},{6,4},{7,5},{8,10},{9,11},{10,... | collective-permute-start | bytes 393224 | tf_op jit(solution)/shard_map/ppermute | solution.py:322
  29.1 1.7 %collective-permute-start.11 = (bf16[4,32,512]{2,1,0:T(8,128)(2,1)S(1)}, bf16[4,32,512]{2,1,0:T(8,128)(2,1)S(1)}, u32[]{:S(2)}, u32[]{:S(2)}) collective-permute-start(bf16[4,32,512]{2,1,0:T(8,128)(2,1)S(1)} %get-tuple-element.104.cot_ref), channel_id=1, source_target_pairs={{0,1},{1,0},{2,3},{3,2},{4,5},{5,4},{6,7},{7,6},{8,9},{9,8},{10,11... | collective-permute-start | bytes 393224 | tf_op jit(solution)/shard_map/ppermute | solution.py:322
  29.1 4.2 %collective-permute-start.12 = (bf16[4,32,512]{2,1,0:T(8,128)(2,1)S(1)}, bf16[4,32,512]{2,1,0:T(8,128)(2,1)S(1)}, u32[]{:S(2)}, u32[]{:S(2)}) collective-permute-start(bf16[4,32,512]{2,1,0:T(8,128)(2,1)S(1)} %pad_maximum_fusion.rest_ref), channel_id=1, source_target_pairs={{0,1},{1,0},{2,3},{3,2},{4,5},{5,4},{6,7},{7,6},{8,9},{9,8},{10,11... | collective-permute-start | bytes 393224 | tf_op jit(solution)/shard_map/ppermute | solution.py:322
  32.1 2.0 %collective-permute-start.14 = (bf16[4,32,512]{2,1,0:T(8,128)(2,1)S(1)}, bf16[4,32,512]{2,1,0:T(8,128)(2,1)S(1)}, u32[]{:S(2)}, u32[]{:S(2)}) collective-permute-start(bf16[4,32,512]{2,1,0:T(8,128)(2,1)S(1)} %collective-permute-done.10.cot_ref), channel_id=1, source_target_pairs={{0,1},{1,0},{2,3},{3,2},{4,5},{5,4},{6,7},{7,6},{8,9},{9,8},{10,11... | collective-permute-start | bytes 393224 | tf_op jit(solution)/shard_map/ppermute | solution.py:322
  32.1 3.2 %collective-permute-start.13 = (bf16[4,32,512]{2,1,0:T(8,128)(2,1)S(1)}, bf16[4,32,512]{2,1,0:T(8,128)(2,1)S(1)}, u32[]{:S(2)}, u32[]{:S(2)}) collective-permute-start(bf16[4,32,512]{2,1,0:T(8,128)(2,1)S(1)} %collective-permute-done.9.rest_ref), channel_id=1, source_target_pairs={{0,1},{1,0},{2,3},{3,2},{4,5},{5,4},{6,7},{7,6},{8,9},{9,8},{10,11... | collective-permute-start | bytes 393224 | tf_op jit(solution)/shard_map/ppermute | solution.py:322
  39.4 5.9 %collective-permute-start.16 = (bf16[4,32,512]{2,1,0:T(8,128)(2,1)S(1)}, bf16[4,32,512]{2,1,0:T(8,128)(2,1)S(1)}, u32[]{:S(2)}, u32[]{:S(2)}) collective-permute-start(bf16[4,32,512]{2,1,0:T(8,128)(2,1)S(1)} %get-tuple-element.137), channel_id=1, source_target_pairs={{0,2},{1,3},{2,0},{3,1},{4,6},{5,7},{6,4},{7,5},{8,10},{9,11},{10,... | collective-permute-start | bytes 393224 | tf_op jit(solution)/shard_map/ppermute | solution.py:322
  46.2 1.6 %collective-permute-start.17 = (bf16[8,32,512]{2,1,0:T(8,128)(2,1)S(1)}, bf16[8,32,512]{2,1,0:T(8,128)(2,1)S(1)}, u32[]{:S(2)}, u32[]{:S(2)}) collective-permute-start(bf16[8,32,512]{2,1,0:T(8,128)(2,1)S(1)} %get-tuple-element.140), channel_id=1, source_target_pairs={{0,1},{1,0},{2,3},{3,2},{4,5},{5,4},{6,7},{7,6},{8,9},{9,8},{10,11... | collective-permute-start | bytes 786440 | tf_op jit(solution)/shard_map/ppermute | solution.py:322
  47.9 5.6 %collective-permute-start.18 = (bf16[4,32,512]{2,1,0:T(8,128)(2,1)S(1)}, bf16[4,32,512]{2,1,0:T(8,128)(2,1)S(1)}, u32[]{:S(2)}, u32[]{:S(2)}) collective-permute-start(bf16[4,32,512]{2,1,0:T(8,128)(2,1)S(1)} %get-tuple-element.143), channel_id=1, source_target_pairs={{0,2},{1,3},{2,0},{3,1},{4,6},{5,7},{6,4},{7,5},{8,10},{9,11},{10,... | collective-permute-start | bytes 393224 | tf_op jit(solution)/shard_map/ppermute | solution.py:322
  48.5 6.4 %collective-permute-start.22 = (bf16[32,512]{1,0:T(8,128)(2,1)S(1)}, bf16[32,512]{1,0:T(8,128)(2,1)S(1)}, u32[]{:S(2)}, u32[]{:S(2)}) collective-permute-start(bf16[32,512]{1,0:T(8,128)(2,1)S(1)} %get-tuple-element.151), channel_id=1, source_target_pairs={{0,4},{1,5},{2,6},{3,7},{4,0},{5,1},{6,2},{7,3},{8,12},{9,13},{10,... | collective-permute-start | bytes 98312 | tf_op jit(solution)/shard_map/ppermute | solution.py:319
  49.3 8.7 %collective-permute-start.23 = (bf16[32,512]{1,0:T(8,128)(2,1)S(1)}, bf16[32,512]{1,0:T(8,128)(2,1)S(1)}, u32[]{:S(2)}, u32[]{:S(2)}) collective-permute-start(bf16[32,512]{1,0:T(8,128)(2,1)S(1)} %get-tuple-element.152), channel_id=1, source_target_pairs={{0,8},{1,9},{2,10},{3,11},{4,12},{5,13},{6,14},{7,15},{8,0},{9,1},... | collective-permute-start | bytes 98312 | tf_op jit(solution)/shard_map/ppermute | solution.py:319
  50.2 7.8 %collective-permute-start.24 = (bf16[32,512]{1,0:T(8,128)(2,1)S(1)}, bf16[32,512]{1,0:T(8,128)(2,1)S(1)}, u32[]{:S(2)}, u32[]{:S(2)}) collective-permute-start(bf16[32,512]{1,0:T(8,128)(2,1)S(1)} %get-tuple-element.153), channel_id=1, source_target_pairs={{0,12},{1,13},{2,14},{3,15},{4,8},{5,9},{6,10},{7,11},{8,4},{9,5},... | collective-permute-start | bytes 98312 | tf_op jit(solution)/shard_map/ppermute | solution.py:319
  53.5 4.5 %collective-permute-start.19 = (bf16[32,512]{1,0:T(8,128)(2,1)S(1)}, bf16[32,512]{1,0:T(8,128)(2,1)S(1)}, u32[]{:S(2)}, u32[]{:S(2)}) collective-permute-start(bf16[32,512]{1,0:T(8,128)(2,1)S(1)} %get-tuple-element.145), channel_id=1, source_target_pairs={{0,4},{1,5},{2,6},{3,7},{4,0},{5,1},{6,2},{7,3},{8,12},{9,13},{10,... | collective-permute-start | bytes 98312 | tf_op jit(solution)/shard_map/ppermute | solution.py:319
  53.9 4.8 %collective-permute-start.20 = (bf16[32,512]{1,0:T(8,128)(2,1)S(1)}, bf16[32,512]{1,0:T(8,128)(2,1)S(1)}, u32[]{:S(2)}, u32[]{:S(2)}) collective-permute-start(bf16[32,512]{1,0:T(8,128)(2,1)S(1)} %get-tuple-element.146), channel_id=1, source_target_pairs={{0,8},{1,9},{2,10},{3,11},{4,12},{5,13},{6,14},{7,15},{8,0},{9,1},... | collective-permute-start | bytes 98312 | tf_op jit(solution)/shard_map/ppermute | solution.py:319
  54.9 5.7 %collective-permute-start.21 = (bf16[32,512]{1,0:T(8,128)(2,1)S(1)}, bf16[32,512]{1,0:T(8,128)(2,1)S(1)}, u32[]{:S(2)}, u32[]{:S(2)}) collective-permute-start(bf16[32,512]{1,0:T(8,128)(2,1)S(1)} %get-tuple-element.147), channel_id=1, source_target_pairs={{0,12},{1,13},{2,14},{3,15},{4,8},{5,9},{6,10},{7,11},{8,4},{9,5},... | collective-permute-start | bytes 98312 | tf_op jit(solution)/shard_map/ppermute | solution.py:319
  (11 other events, 93.1 us)

commit v9 on v8

--- a/solution.py
+++ b/solution.py
@@ -47,20 +47,14 @@
     return 4 * at + 2 * flip(row, part % 2) + flip(core, part // 2)
 
 
-def block_spot(q, tokens, rows, width):
-    per_column = tokens // rows
-    r, c = rows * (q % per_column), width + LANES * (q // per_column)
-    return slice(r, r + rows), slice(c, c + LANES)
-
-
 def send_kernel(
-    me_ref, offset_ref, act_ref, expo_ref, base_ref, received_ref, cot_ref, gain_ref,
+    me_ref, offset_ref, act_ref, expo_ref, base_ref, received_ref, gain_ref,
     new_rows_ref, received_out_ref, gain_out_ref, *refs,
 ):
     *packed_refs, rows_ref = refs
     n, rows, _ = rows_ref.shape
-    tokens, share = cot_ref.shape
     width = act_ref.shape[1]
+    share = width // n
     per_dev = width // LANES // n
     received_out_ref[...] = received_ref[...]
     for j in range(n):
@@ -81,12 +75,10 @@
     for d in range(n):
         rows_ref[d, 2 * per_dev :, :] = fill
     along, _, _ = place(me_ref[0])
-    cot = cot_ref[...]
     for r, packed_ref in enumerate(packed_refs):
         to = jnp.bitwise_xor(along, r)
-        packed_ref[:, :share] = cot
         for q in range(4):
-            packed_ref[block_spot(q, tokens, rows, share)] = rows_ref[4 * to + q].astype(bf16)
+            packed_ref[q] = rows_ref[4 * to + q].astype(bf16)
     new_rows_ref[...] = chosen + jnp.concatenate(pieces, axis=1)
 
 
@@ -99,18 +91,16 @@
 
 
 def sort_kernel(me_ref, *refs):
-    *packed_refs, line_ref, b0, b1, b2, b3 = refs
-    quarter, tokens, share = line_ref.shape
-    rows = b0.shape[1]
+    *packed_refs, b0, b1, b2, b3 = refs
     _, row, core = place(me_ref[0])
     for r, packed_ref in enumerate(packed_refs):
-        line_ref[r] = packed_ref[:, :share]
-        block = [packed_ref[block_spot(q, tokens, rows, share)] for q in range(4)]
         for e, out_ref in enumerate((b0, b1, b2, b3)):
-            to_row, to_core = flip(row, e // 2), flip(core, e % 2)
-            low = jnp.where(to_core == 0, block[0], block[1])
-            high = jnp.where(to_core == 0, block[2], block[3])
-            out_ref[r] = jnp.where(to_row == 0, low, high)
+            out_ref[r] = packed_ref[2 * flip(row, e // 2) + flip(core, e % 2)]
+
+
+def interleave_kernel(a_ref, b_ref, out_ref):
+    for k in range(a_ref.shape[0]):
+        out_ref[2 * k], out_ref[2 * k + 1] = a_ref[k], b_ref[k]
 
 
 def rebuild_kernel(me_ref, b0, b1, b2, b3, base_ref, out_ref, rows_ref, slots_ref):
@@ -216,7 +206,8 @@
     gh = gh_ref[...]
     for share in range(first, last):
         block = weight_ref[share * width : (share + 1) * width, :]
-        terms = dot_by_halves(block, gh).T
+        middle = width // 2
+        terms = jnp.concatenate([dot_nt(block[:middle], gh), dot_nt(block[middle:], gh)], axis=0).T
         for p in range(2):
             for c in range(chunks):
                 rows_ref[c, pl.ds(p * n + share, n, stride=tokens), :] = terms[
@@ -253,11 +244,18 @@
             out_ref[k] = (kept_ref[at].astype(f32) + arrived_ref[at].astype(f32)).astype(bf16)
 
 
-def line_kernel(me_ref, kept_ref, arrived_ref, *refs):
+def line_kernel(me_ref, kept_ref, arrived_ref, send_ref, keep_ref):
     along, _, _ = place(me_ref[0])
-    for r, ref in enumerate(refs):
-        at = jnp.bitwise_xor(along, r)
-        ref[...] = (kept_ref[at].astype(f32) + arrived_ref[at].astype(f32)).astype(bf16)
+    for k in range(send_ref.shape[0]):
+        for ref, r in ((keep_ref, 2 * k), (send_ref, 2 * k + 1)):
+            at = jnp.bitwise_xor(along, r)
+            ref[k] = (kept_ref[at].astype(f32) + arrived_ref[at].astype(f32)).astype(bf16)
+
+
+def halve_kernel(kept_ref, arrived_ref, send_ref, keep_ref):
+    for k in range(send_ref.shape[0]):
+        for ref, at in ((keep_ref, 2 * k), (send_ref, 2 * k + 1)):
+            ref[k] = (kept_ref[at].astype(f32) + arrived_ref[at].astype(f32)).astype(bf16)
 
 
 def added(refs):
@@ -266,9 +264,8 @@
 
 def final_kernel(width_all, share_ref, gain_ref, expo_ref, *refs):
     *refs, layer_ref, grad_ref = refs
-    quarter = (len(refs) - 8) // 2
     own_all, cot_all = added(refs[:4]), added(refs[4:8])
-    grad, layer = added(refs[8 : 8 + quarter]), added(refs[8 + quarter :])
+    grad, layer = added(refs[8:10])[0], added(refs[10:12])[0]
     layer_ref[...] = (share_ref[...].astype(f32) + layer).astype(bf16)
     n, width = gain_ref.shape
     down, up = powers(expo_ref[...], -1), powers(expo_ref[...], 1)
@@ -340,10 +337,10 @@
 
     offset = sample_ids - sender_base.shape[1] * me
     rows = -(-(2 * width // LANES + 1) // 16) * 16
-    packed_shape = (tokens, width + LANES * -(-4 * rows // tokens))
+    packed_shape = (4, rows, LANES)
     act_shape, expo_shape = (2, width_all), (2, width_all // LANES)
     once = lambda shape: pl.BlockSpec(shape, lambda i: (0,) * len(shape))
-    in_shapes = [act_shape, expo_shape, sender_base.shape, receiver_base.shape, share_shape, (1, width_all)]
+    in_shapes = [act_shape, expo_shape, sender_base.shape, receiver_base.shape, (1, width_all)]
     outs = (
         struct(act_shape, f32),
         struct(receiver_base.shape, f32),
@@ -364,19 +361,30 @@
         hbm(forward_exponent.reshape(expo_shape)),
         hbm(sender_base),
         hbm(receiver_base),
-        hbm(cotangent.reshape(share_shape)),
         hbm(norm_gain.reshape(1, width_all)),
     )
     packed = [shift(x, r) for r, x in enumerate(packed)]
-    cot_line, *blocks = call(
+    blocks = call(
         sort_kernel,
-        (struct(line_shape, bf16),) + (struct((quarter, rows, LANES), bf16),) * 4,
+        (struct((quarter, rows, LANES), bf16),) * 4,
         [SMEM] + [VMEM] * quarter,
         [me_in, *packed],
         micros=STAGE,
     )
     blocks = [blocks[0]] + [swap(blocks[e], e) for e in range(1, 4)]
-    cots = [cot_line]
+
+    cot_line, blocks[0] = lax.optimization_barrier(
+        (cotangent.reshape(1, tokens, width), blocks[0])
+    )
+    bit = quarter // 2
+    while bit:
+        cot_line = call(
+            interleave_kernel,
+            struct((2 * cot_line.shape[0], tokens, width), bf16),
+            [VMEM] * 2,
+            [cot_line, shift(cot_line, bit)],
+        )
+        bit //= 2
 
     ANY = pl.BlockSpec(memory_space=pl.ANY)
     share_f32 = struct(share_shape, f32)
@@ -418,11 +426,10 @@
 
     share = rebuild(struct(share_shape, bf16), STAGE)
     lines = [shift(share, r) for r in range(quarter)]
-    cots[0], share_after = together((cot_line, share))
-    cot_row = swap(cots[0], 2)
+    cots = [cot_line]
+    cot_row = swap(cot_line, 2)
     grads = [grad_active_part(0)]
-    new_receiver_base = rebuild(struct(receiver_base.shape, f32), 0.7)
-    lines, grads[0], new_receiver_base = together((lines, grads[0], new_receiver_base))
+    lines, grads[0] = together((lines, grads[0]))
     rest_line = jnp.stack(lines)
     rest_row = swap(rest_line, 2)
     rests = [rest_line]
@@ -476,13 +483,17 @@
         )
 
     def line_sum(kept, arrived):
-        shares = call(
-            line_kernel,
-            (struct(share_shape, bf16),) * quarter,
-            [SMEM] + [VMEM] * 2,
-            [me_in, kept, arrived],
-        )
-        return [shift(x, r) for r, x in enumerate(shares)]
+        half_line = lambda parts: (struct((parts, tokens, width), bf16),) * 2
+        parts, bit = quarter // 2, 1
+        send, keep = call(
+            line_kernel, half_line(parts), [SMEM] + [VMEM] * 2, [me_in, kept, arrived]
+        )
+        arrived = shift(send, bit)
+        while parts > 1:
+            parts, bit = parts // 2, 2 * bit
+            send, keep = call(halve_kernel, half_line(parts), [VMEM] * 2, [keep, arrived])
+            arrived = shift(send, bit)
+        return [keep, arrived]
 
     out_send = down_terms(1, active)
     out_in = swap(out_send, 1)
@@ -509,6 +520,9 @@
         micros=0.7,
     )
     grad_in = swap(grad_send, 1)
+    received, blocks, grad_send = together((received, blocks, grad_send))
+    new_receiver_base = rebuild(struct(receiver_base.shape, f32), 0.7)
+    grad_in, new_receiver_base = together((grad_in, new_receiver_base))
     grad_send, grad_row = pair_sum(grad_keep, grad_in)
     grad_row_in = swap(grad_send, 2)
     out_row, grad_row = together((out_row, grad_row))
@@ -517,7 +531,7 @@
     layer_out, returned = call(
         functools.partial(final_kernel, width_all),
         (struct(share_shape, bf16), struct((2, width_all // LANES, LANES), f32)),
-        [VMEM] * (11 + 2 * quarter),
+        [VMEM] * 15,
         [
             share,
             gain,

time: 61.5 us -> 63.9 us (1.039)
  starting transfers between devices: 25.3 us -> 26.5 us
  waiting for transfers between devices: 15.2 us -> 16.2 us
    ppermute x12, waiting for transfers between devices: 8.48 us -> 11.7 us  [shift(): return lax.ppermute(x, 'dp', [(d, d ^ 4 * r) for d in range(n)]) if r else x]
    ppermute x13, starting transfers between devices: 6.31 us -> 8.68 us  [swap(): return lax.ppermute(x, 'dp', [(d, d ^ bits) for d in range(n)])]
    ppermute x13, waiting for transfers between devices: 6.7 us -> 4.49 us  [swap(): return lax.ppermute(x, 'dp', [(d, d ^ bits) for d in range(n)])]
    ppermute x12, starting transfers between devices: 19 us -> 17.9 us  [shift(): return lax.ppermute(x, 'dp', [(d, d ^ 4 * r) for d in range(n)]) if r else x]
    pallas_call x21 -> x25, Pallas kernels: 18 us -> 18.1 us  [call(): pl.pallas_call(kernel, out_shape=outs, in_specs=ins, out_specs=jax.tree.m...]
  transfers between devices with their start and end apart: 25 -> 25, of which waited for: 10 -> 12; matrix products, arithmetic and copies ran while one was open for 0% -> 0% of each run, Pallas kernels for 22% -> 22%
where the time goes in v9:
time: 63.9 us; the launch traced here: 63.8 us
  starting transfers between devices  26.5 us (41%)
  Pallas kernels  19.3 us (30%)
  waiting for transfers between devices  16.2 us (25%)
  between operations  1.63 us (3%)
    pallas_call x25, Pallas kernels, call(): pl.pallas_call(kernel, out_shape=outs, in_specs=ins, out_specs=jax.tree.m...  18.1 us
    ppermute x12, starting transfers between devices, shift(): return lax.ppermute(x, 'dp', [(d, d ^ 4 * r) for d in range(n)]) if r else x  17.9 us
    ppermute x12, waiting for transfers between devices, shift(): return lax.ppermute(x, 'dp', [(d, d ^ 4 * r) for d in range(n)]) if r else x  11.7 us
    ppermute x13, starting transfers between devices, swap(): return lax.ppermute(x, 'dp', [(d, d ^ bits) for d in range(n)])  8.68 us
    ppermute x13, waiting for transfers between devices, swap(): return lax.ppermute(x, 'dp', [(d, d ^ bits) for d in range(n)])  4.49 us
  transfers between devices with their start and end apart: 25, of which 12 were waited for; matrix products, arithmetic and copies ran while one was open for 0% of the time, Pallas kernels for 22%

profile of v9, /device:TPU:0, one launch (start us, length us, event | category | flops | bytes accessed | tf_op | source)
XLA Modules:
  0.0 63.8 jit_solution(919754068413804106)
XLA Ops:
  1.3 1.2 %shard_map.129 = (f32[2,8192]{1,0:T(2,128)S(1)}, f32[2,32,512]{2,1,0:T(8,128)S(1)}, f32[16,512]{1,0:T(8,128)S(1)}, bf16[4,16,128]{2,1,0:T(8,128)(2,1)S(1)}, bf16...) custom-call(s32[1]{0:T(128)} %bitcast.me_ref, s32[1]{0:T(128)S(6)} %sub.7.offset_ref, ...), custom_call_target="tpu_custom_call" | custom-call | tf_op jit(solution)/shard_map/pallas_call | solution.py:349
  2.6 3.1 %collective-permute-start = (bf16[4,16,128]{2,1,0:T(8,128)(2,1)S(1)}, bf16[4,16,128]{2,1,0:T(8,128)(2,1)S(1)}, u32[]{:S(2)}, u32[]{:S(2)}) collective-permute-start(bf16[4,16,128]{2,1,0:T(8,128)(2,1)S(1)} %get-tuple-element.87), channel_id=1, source_target_pairs={{0,4},{1,5},{2,6},{3,7},{4,0},{5,1},{6,2},{7,3},{8,12},{9,13},{10,... | collective-permute-start | bytes 49160 | tf_op jit(solution)/shard_map/ppermute | solution.py:316
  5.7 2.6 %collective-permute-start.1 = (bf16[4,16,128]{2,1,0:T(8,128)(2,1)S(1)}, bf16[4,16,128]{2,1,0:T(8,128)(2,1)S(1)}, u32[]{:S(2)}, u32[]{:S(2)}) collective-permute-start(bf16[4,16,128]{2,1,0:T(8,128)(2,1)S(1)} %get-tuple-element.88), channel_id=1, source_target_pairs={{0,8},{1,9},{2,10},{3,11},{4,12},{5,13},{6,14},{7,15},{8,0},{9,1},... | collective-permute-start | bytes 49160 | tf_op jit(solution)/shard_map/ppermute | solution.py:316
  8.3 2.1 %collective-permute-done.1.refs_2_ = bf16[4,16,128]{2,1,0:T(8,128)(2,1)S(1)} collective-permute-done((bf16[4,16,128]{2,1,0:T(8,128)(2,1)S(1)}, bf16[4,16,128]{2,1,0:T(8,128)(2,1)S(1)}, u32[]{:S(2)}, u32[]{:S(2)}) %collective-permute-start.1) | collective-permute-done | bytes 16416 | tf_op jit(solution)/shard_map/ppermute | solution.py:316
  10.4 3.5 %collective-permute-done.2.refs_3_ = bf16[4,16,128]{2,1,0:T(8,128)(2,1)S(1)} collective-permute-done((bf16[4,16,128]{2,1,0:T(8,128)(2,1)S(1)}, bf16[4,16,128]{2,1,0:T(8,128)(2,1)S(1)}, u32[]{:S(2)}, u32[]{:S(2)}) %collective-permute-start.2) | collective-permute-done | bytes 16416 | tf_op jit(solution)/shard_map/ppermute | solution.py:316
  14.7 1.5 %collective-permute-start.4 = (bf16[4,16,128]{2,1,0:T(8,128)(2,1)S(1)}, bf16[4,16,128]{2,1,0:T(8,128)(2,1)S(1)}, u32[]{:S(2)}, u32[]{:S(2)}) collective-permute-start(bf16[4,16,128]{2,1,0:T(8,128)(2,1)S(1)} %get-tuple-element.93), channel_id=1, source_target_pairs={{0,2},{1,3},{2,0},{3,1},{4,6},{5,7},{6,4},{7,5},{8,10},{9,11},{10,... | collective-permute-start | bytes 49160 | tf_op jit(solution)/shard_map/ppermute | solution.py:319
  16.5 2.2 %collective-permute-done.9.b_ref = bf16[1,32,512]{2,1,0:T(8,128)(2,1)S(1)} collective-permute-done((bf16[1,32,512]{2,1,0:T(8,128)(2,1)S(1)}, bf16[1,32,512]{2,1,0:T(8,128)(2,1)S(1)}, u32[]{:S(2)}, u32[]{:S(2)}) %collective-permute-start.9) | collective-permute-done | bytes 32800 | tf_op jit(solution)/shard_map/ppermute | solution.py:316
  19.4 1.8 %collective-permute-start.8 = (bf16[32,512]{1,0:T(8,128)(2,1)S(1)}, bf16[32,512]{1,0:T(8,128)(2,1)S(1)}, u32[]{:S(2)}, u32[]{:S(2)}) collective-permute-start(bf16[32,512]{1,0:T(8,128)(2,1)S(1)} %shard_map.131.share_ref), channel_id=1, source_target_pairs={{0,12},{1,13},{2,14},{3,15},{4,8},{5,9},{6,10},{7,11},{8,4},{9,5},... | collective-permute-start | bytes 98312 | tf_op jit(solution)/shard_map/ppermute | solution.py:316
  21.2 1.3 %collective-permute-start.7 = (bf16[32,512]{1,0:T(8,128)(2,1)S(1)}, bf16[32,512]{1,0:T(8,128)(2,1)S(1)}, u32[]{:S(2)}, u32[]{:S(2)}) collective-permute-start(bf16[32,512]{1,0:T(8,128)(2,1)S(1)} %shard_map.131.share_ref), channel_id=1, source_target_pairs={{0,8},{1,9},{2,10},{3,11},{4,12},{5,13},{6,14},{7,15},{8,0},{9,1},... | collective-permute-start | bytes 98312 | tf_op jit(solution)/shard_map/ppermute | solution.py:316
  22.5 1.4 %collective-permute-start.6 = (bf16[32,512]{1,0:T(8,128)(2,1)S(1)}, bf16[32,512]{1,0:T(8,128)(2,1)S(1)}, u32[]{:S(2)}, u32[]{:S(2)}) collective-permute-start(bf16[32,512]{1,0:T(8,128)(2,1)S(1)} %shard_map.131.share_ref), channel_id=1, source_target_pairs={{0,4},{1,5},{2,6},{3,7},{4,0},{5,1},{6,2},{7,3},{8,12},{9,13},{10,... | collective-permute-start | bytes 98312 | tf_op jit(solution)/shard_map/ppermute | solution.py:316
  25.0 1.2 %shard_map.134 = (f32[896,32]{1,0:T(8,128)S(1)}, f32[32,512]{1,0:T(8,128)S(1)}) custom-call(s32[1]{0:T(128)} %bitcast.me_ref, bf16[4,32,512]{2,1,0:T(8,128)(2,1)S(1)} %shard_map.133.cot_ref, bf16[896,8192]{1,0:T(8,128)(2,1)S(1)} %bitcast.14), custom_call_target="tpu_custom_call" | custom-call | flops 1840000000 | tf_op jit(solution)/shard_map/pallas_call | solution.py:326
  26.5 1.4 %collective-permute-start.11 = (bf16[4,32,512]{2,1,0:T(8,128)(2,1)S(1)}, bf16[4,32,512]{2,1,0:T(8,128)(2,1)S(1)}, u32[]{:S(2)}, u32[]{:S(2)}) collective-permute-start(bf16[4,32,512]{2,1,0:T(8,128)(2,1)S(1)} %pad_maximum_fusion.rest_ref), channel_id=1, source_target_pairs={{0,2},{1,3},{2,0},{3,1},{4,6},{5,7},{6,4},{7,5},{8,10},{9,11},{10,... | collective-permute-start | bytes 393224 | tf_op jit(solution)/shard_map/ppermute | solution.py:319
  36.0 1.7 %shard_map.143 = bf16[8,32,512]{2,1,0:T(8,128)(2,1)S(1)} custom-call(s32[1]{0:T(128)} %bitcast.me_ref, bf16[32,896]{1,0:T(8,128)(2,1)S(1)} %get-tuple-element.130.active_ref, bf16[896,8192]{1,0:T(8,128)(2,1)S(1)} %bitcast.14), custom_call_target="tpu_custom_call" | custom-call | flops 1724999936 | tf_op jit(solution)/shard_map/pallas_call | solution.py:326
  37.7 1.5 %shard_map.144.kept_ref = bf16[8,32,512]{2,1,0:T(8,128)(2,1)S(1)} custom-call(s32[1]{0:T(128)} %bitcast.me_ref, bf16[32,896]{1,0:T(8,128)(2,1)S(1)} %get-tuple-element.130.active_ref, bf16[896,8192]{1,0:T(8,128)(2,1)S(1)} %bitcast.14), custom_call_target="tpu_custom_call" | custom-call | flops 1724999936 | tf_op jit(solution)/shard_map/pallas_call | solution.py:326
  39.3 1.5 %collective-permute-start.18 = (bf16[4,32,512]{2,1,0:T(8,128)(2,1)S(1)}, bf16[4,32,512]{2,1,0:T(8,128)(2,1)S(1)}, u32[]{:S(2)}, u32[]{:S(2)}) collective-permute-start(bf16[4,32,512]{2,1,0:T(8,128)(2,1)S(1)} %get-tuple-element.133), channel_id=1, source_target_pairs={{0,2},{1,3},{2,0},{3,1},{4,6},{5,7},{6,4},{7,5},{8,10},{9,11},{10,... | collective-permute-start | bytes 393224 | tf_op jit(solution)/shard_map/ppermute | solution.py:319
  40.8 3.8 %shard_map.146.refs_0_ = f32[4,512,128]{2,1,0:T(8,128)S(1)} custom-call(s32[1]{0:T(128)} %bitcast.me_ref, bf16[32,896]{1,0:T(8,128)(2,1)S(1)} %get-tuple-element.132.gh_ref, bf16[8192,896]{1,0:T(8,128)(2,1)S(1)} %bitcast.16), custom_call_target="tpu_custom_call" | custom-call | flops 4600000000 | tf_op jit(solution)/shard_map/pallas_call | solution.py:326
  47.7 1.5 %collective-permute-start.20 = (bf16[4,32,512]{2,1,0:T(8,128)(2,1)S(1)}, bf16[4,32,512]{2,1,0:T(8,128)(2,1)S(1)}, u32[]{:S(2)}, u32[]{:S(2)}) collective-permute-start(bf16[4,32,512]{2,1,0:T(8,128)(2,1)S(1)} %get-tuple-element.155), channel_id=1, source_target_pairs={{0,2},{1,3},{2,0},{3,1},{4,6},{5,7},{6,4},{7,5},{8,10},{9,11},{10,... | collective-permute-start | bytes 393224 | tf_op jit(solution)/shard_map/ppermute | solution.py:319
  49.3 1.7 %collective-permute-start.23 = (bf16[2,32,512]{2,1,0:T(8,128)(2,1)S(1)}, bf16[2,32,512]{2,1,0:T(8,128)(2,1)S(1)}, u32[]{:S(2)}, u32[]{:S(2)}) collective-permute-start(bf16[2,32,512]{2,1,0:T(8,128)(2,1)S(1)} %get-tuple-element.163), channel_id=1, source_target_pairs={{0,4},{1,5},{2,6},{3,7},{4,0},{5,1},{6,2},{7,3},{8,12},{9,13},{10,... | collective-permute-start | bytes 196616 | tf_op jit(solution)/shard_map/ppermute | solution.py:316
  51.0 2.3 %collective-permute-done.20.arrived_ref = bf16[4,32,512]{2,1,0:T(8,128)(2,1)S(1)} collective-permute-done((bf16[4,32,512]{2,1,0:T(8,128)(2,1)S(1)}, bf16[4,32,512]{2,1,0:T(8,128)(2,1)S(1)}, u32[]{:S(2)}, u32[]{:S(2)}) %collective-permute-start.20) | collective-permute-done | bytes 131104 | tf_op jit(solution)/shard_map/ppermute | solution.py:319
  53.4 1.4 %collective-permute-start.21 = (bf16[2,32,512]{2,1,0:T(8,128)(2,1)S(1)}, bf16[2,32,512]{2,1,0:T(8,128)(2,1)S(1)}, u32[]{:S(2)}, u32[]{:S(2)}) collective-permute-start(bf16[2,32,512]{2,1,0:T(8,128)(2,1)S(1)} %get-tuple-element.157), channel_id=1, source_target_pairs={{0,4},{1,5},{2,6},{3,7},{4,0},{5,1},{6,2},{7,3},{8,12},{9,13},{10,... | collective-permute-start | bytes 196616 | tf_op jit(solution)/shard_map/ppermute | solution.py:316
  54.8 1.8 %collective-permute-start.24 = (bf16[1,32,512]{2,1,0:T(8,128)(2,1)S(1)}, bf16[1,32,512]{2,1,0:T(8,128)(2,1)S(1)}, u32[]{:S(2)}, u32[]{:S(2)}) collective-permute-start(bf16[1,32,512]{2,1,0:T(8,128)(2,1)S(1)} %get-tuple-element.165), channel_id=1, source_target_pairs={{0,8},{1,9},{2,10},{3,11},{4,12},{5,13},{6,14},{7,15},{8,0},{9,1},... | collective-permute-start | bytes 98312 | tf_op jit(solution)/shard_map/ppermute | solution.py:316
  56.6 1.5 %collective-permute-done.21.arrived_ref = bf16[2,32,512]{2,1,0:T(8,128)(2,1)S(1)} collective-permute-done((bf16[2,32,512]{2,1,0:T(8,128)(2,1)S(1)}, bf16[2,32,512]{2,1,0:T(8,128)(2,1)S(1)}, u32[]{:S(2)}, u32[]{:S(2)}) %collective-permute-start.21) | collective-permute-done | bytes 65568 | tf_op jit(solution)/shard_map/ppermute | solution.py:316
  58.1 2.8 %collective-permute-start.22 = (bf16[1,32,512]{2,1,0:T(8,128)(2,1)S(1)}, bf16[1,32,512]{2,1,0:T(8,128)(2,1)S(1)}, u32[]{:S(2)}, u32[]{:S(2)}) collective-permute-start(bf16[1,32,512]{2,1,0:T(8,128)(2,1)S(1)} %get-tuple-element.159), channel_id=1, source_target_pairs={{0,8},{1,9},{2,10},{3,11},{4,12},{5,13},{6,14},{7,15},{8,0},{9,1},... | collective-permute-start | bytes 98312 | tf_op jit(solution)/shard_map/ppermute | solution.py:316
  60.8 2.1 %collective-permute-done.22.refs_9_ = bf16[1,32,512]{2,1,0:T(8,128)(2,1)S(1)} collective-permute-done((bf16[1,32,512]{2,1,0:T(8,128)(2,1)S(1)}, bf16[1,32,512]{2,1,0:T(8,128)(2,1)S(1)}, u32[]{:S(2)}, u32[]{:S(2)}) %collective-permute-start.22) | collective-permute-done | bytes 32800 | tf_op jit(solution)/shard_map/ppermute | solution.py:316
  (77 shorter events, 15.3 us)
Async XLA Ops:
  2.6 5.7 %collective-permute-start = (bf16[4,16,128]{2,1,0:T(8,128)(2,1)S(1)}, bf16[4,16,128]{2,1,0:T(8,128)(2,1)S(1)}, u32[]{:S(2)}, u32[]{:S(2)}) collective-permute-start(bf16[4,16,128]{2,1,0:T(8,128)(2,1)S(1)} %get-tuple-element.87), channel_id=1, source_target_pairs={{0,4},{1,5},{2,6},{3,7},{4,0},{5,1},{6,2},{7,3},{8,12},{9,13},{10,... | collective-permute-start | bytes 49160 | tf_op jit(solution)/shard_map/ppermute | solution.py:316
  5.7 4.7 %collective-permute-start.1 = (bf16[4,16,128]{2,1,0:T(8,128)(2,1)S(1)}, bf16[4,16,128]{2,1,0:T(8,128)(2,1)S(1)}, u32[]{:S(2)}, u32[]{:S(2)}) collective-permute-start(bf16[4,16,128]{2,1,0:T(8,128)(2,1)S(1)} %get-tuple-element.88), channel_id=1, source_target_pairs={{0,8},{1,9},{2,10},{3,11},{4,12},{5,13},{6,14},{7,15},{8,0},{9,1},... | collective-permute-start | bytes 49160 | tf_op jit(solution)/shard_map/ppermute | solution.py:316
  8.2 5.6 %collective-permute-start.2 = (bf16[4,16,128]{2,1,0:T(8,128)(2,1)S(1)}, bf16[4,16,128]{2,1,0:T(8,128)(2,1)S(1)}, u32[]{:S(2)}, u32[]{:S(2)}) collective-permute-start(bf16[4,16,128]{2,1,0:T(8,128)(2,1)S(1)} %get-tuple-element.89), channel_id=1, source_target_pairs={{0,12},{1,13},{2,14},{3,15},{4,8},{5,9},{6,10},{7,11},{8,4},{9,5},... | collective-permute-start | bytes 49160 | tf_op jit(solution)/shard_map/ppermute | solution.py:316
  13.9 4.9 %collective-permute-start.9 = (bf16[1,32,512]{2,1,0:T(8,128)(2,1)S(1)}, bf16[1,32,512]{2,1,0:T(8,128)(2,1)S(1)}, u32[]{:S(2)}, u32[]{:S(2)}) collective-permute-start(bf16[1,32,512]{2,1,0:T(8,128)(2,1)S(1)} %bitcast.18), channel_id=1, source_target_pairs={{0,8},{1,9},{2,10},{3,11},{4,12},{5,13},{6,14},{7,15},{8,0},{9,1},... | collective-permute-start | bytes 98312 | tf_op jit(solution)/shard_map/ppermute | solution.py:316
  14.7 4.1 %collective-permute-start.3 = (bf16[4,16,128]{2,1,0:T(8,128)(2,1)S(1)}, bf16[4,16,128]{2,1,0:T(8,128)(2,1)S(1)}, u32[]{:S(2)}, u32[]{:S(2)}) collective-permute-start(bf16[4,16,128]{2,1,0:T(8,128)(2,1)S(1)} %get-tuple-element.92), channel_id=1, source_target_pairs={{0,1},{1,0},{2,3},{3,2},{4,5},{5,4},{6,7},{7,6},{8,9},{9,8},{10,11... | collective-permute-start | bytes 49160 | tf_op jit(solution)/shard_map/ppermute | solution.py:319
  14.7 4.1 %collective-permute-start.4 = (bf16[4,16,128]{2,1,0:T(8,128)(2,1)S(1)}, bf16[4,16,128]{2,1,0:T(8,128)(2,1)S(1)}, u32[]{:S(2)}, u32[]{:S(2)}) collective-permute-start(bf16[4,16,128]{2,1,0:T(8,128)(2,1)S(1)} %get-tuple-element.93), channel_id=1, source_target_pairs={{0,2},{1,3},{2,0},{3,1},{4,6},{5,7},{6,4},{7,5},{8,10},{9,11},{10,... | collective-permute-start | bytes 49160 | tf_op jit(solution)/shard_map/ppermute | solution.py:319
  16.1 3.2 %collective-permute-start.5 = (bf16[4,16,128]{2,1,0:T(8,128)(2,1)S(1)}, bf16[4,16,128]{2,1,0:T(8,128)(2,1)S(1)}, u32[]{:S(2)}, u32[]{:S(2)}) collective-permute-start(bf16[4,16,128]{2,1,0:T(8,128)(2,1)S(1)} %get-tuple-element.94), channel_id=1, source_target_pairs={{0,3},{1,2},{2,1},{3,0},{4,7},{5,6},{6,5},{7,4},{8,11},{9,10},{10,... | collective-permute-start | bytes 49160 | tf_op jit(solution)/shard_map/ppermute | solution.py:319
  18.8 5.1 %collective-permute-start.10 = (bf16[2,32,512]{2,1,0:T(8,128)(2,1)S(1)}, bf16[2,32,512]{2,1,0:T(8,128)(2,1)S(1)}, u32[]{:S(2)}, u32[]{:S(2)}) collective-permute-start(bf16[2,32,512]{2,1,0:T(8,128)(2,1)S(1)} %shard_map.132.a_ref), channel_id=1, source_target_pairs={{0,4},{1,5},{2,6},{3,7},{4,0},{5,1},{6,2},{7,3},{8,12},{9,13},{10,... | collective-permute-start | bytes 196616 | tf_op jit(solution)/shard_map/ppermute | solution.py:316
  19.4 6.8 %collective-permute-start.8 = (bf16[32,512]{1,0:T(8,128)(2,1)S(1)}, bf16[32,512]{1,0:T(8,128)(2,1)S(1)}, u32[]{:S(2)}, u32[]{:S(2)}) collective-permute-start(bf16[32,512]{1,0:T(8,128)(2,1)S(1)} %shard_map.131.share_ref), channel_id=1, source_target_pairs={{0,12},{1,13},{2,14},{3,15},{4,8},{5,9},{6,10},{7,11},{8,4},{9,5},... | collective-permute-start | bytes 98312 | tf_op jit(solution)/shard_map/ppermute | solution.py:316
  21.2 5.2 %collective-permute-start.7 = (bf16[32,512]{1,0:T(8,128)(2,1)S(1)}, bf16[32,512]{1,0:T(8,128)(2,1)S(1)}, u32[]{:S(2)}, u32[]{:S(2)}) collective-permute-start(bf16[32,512]{1,0:T(8,128)(2,1)S(1)} %shard_map.131.share_ref), channel_id=1, source_target_pairs={{0,8},{1,9},{2,10},{3,11},{4,12},{5,13},{6,14},{7,15},{8,0},{9,1},... | collective-permute-start | bytes 98312 | tf_op jit(solution)/shard_map/ppermute | solution.py:316
  22.5 4.0 %collective-permute-start.6 = (bf16[32,512]{1,0:T(8,128)(2,1)S(1)}, bf16[32,512]{1,0:T(8,128)(2,1)S(1)}, u32[]{:S(2)}, u32[]{:S(2)}) collective-permute-start(bf16[32,512]{1,0:T(8,128)(2,1)S(1)} %shard_map.131.share_ref), channel_id=1, source_target_pairs={{0,4},{1,5},{2,6},{3,7},{4,0},{5,1},{6,2},{7,3},{8,12},{9,13},{10,... | collective-permute-start | bytes 98312 | tf_op jit(solution)/shard_map/ppermute | solution.py:316
  23.9 5.1 %collective-permute-start.12 = (bf16[4,32,512]{2,1,0:T(8,128)(2,1)S(1)}, bf16[4,32,512]{2,1,0:T(8,128)(2,1)S(1)}, u32[]{:S(2)}, u32[]{:S(2)}) collective-permute-start(bf16[4,32,512]{2,1,0:T(8,128)(2,1)S(1)} %shard_map.133.cot_ref), channel_id=1, source_target_pairs={{0,2},{1,3},{2,0},{3,1},{4,6},{5,7},{6,4},{7,5},{8,10},{9,11},{10,... | collective-permute-start | bytes 393224 | tf_op jit(solution)/shard_map/ppermute | solution.py:319
  26.5 5.4 %collective-permute-start.11 = (bf16[4,32,512]{2,1,0:T(8,128)(2,1)S(1)}, bf16[4,32,512]{2,1,0:T(8,128)(2,1)S(1)}, u32[]{:S(2)}, u32[]{:S(2)}) collective-permute-start(bf16[4,32,512]{2,1,0:T(8,128)(2,1)S(1)} %pad_maximum_fusion.rest_ref), channel_id=1, source_target_pairs={{0,2},{1,3},{2,0},{3,1},{4,6},{5,7},{6,4},{7,5},{8,10},{9,11},{10,... | collective-permute-start | bytes 393224 | tf_op jit(solution)/shard_map/ppermute | solution.py:319
  29.0 1.7 %collective-permute-start.13 = (bf16[4,32,512]{2,1,0:T(8,128)(2,1)S(1)}, bf16[4,32,512]{2,1,0:T(8,128)(2,1)S(1)}, u32[]{:S(2)}, u32[]{:S(2)}) collective-permute-start(bf16[4,32,512]{2,1,0:T(8,128)(2,1)S(1)} %shard_map.133.cot_ref), channel_id=1, source_target_pairs={{0,1},{1,0},{2,3},{3,2},{4,5},{5,4},{6,7},{7,6},{8,9},{9,8},{10,11... | collective-permute-start | bytes 393224 | tf_op jit(solution)/shard_map/ppermute | solution.py:319
  29.0 4.2 %collective-permute-start.15 = (bf16[4,32,512]{2,1,0:T(8,128)(2,1)S(1)}, bf16[4,32,512]{2,1,0:T(8,128)(2,1)S(1)}, u32[]{:S(2)}, u32[]{:S(2)}) collective-permute-start(bf16[4,32,512]{2,1,0:T(8,128)(2,1)S(1)} %pad_maximum_fusion.rest_ref), channel_id=1, source_target_pairs={{0,1},{1,0},{2,3},{3,2},{4,5},{5,4},{6,7},{7,6},{8,9},{9,8},{10,11... | collective-permute-start | bytes 393224 | tf_op jit(solution)/shard_map/ppermute | solution.py:319
  31.9 2.0 %collective-permute-start.16 = (bf16[4,32,512]{2,1,0:T(8,128)(2,1)S(1)}, bf16[4,32,512]{2,1,0:T(8,128)(2,1)S(1)}, u32[]{:S(2)}, u32[]{:S(2)}) collective-permute-start(bf16[4,32,512]{2,1,0:T(8,128)(2,1)S(1)} %collective-permute-done.12.cot_ref), channel_id=1, source_target_pairs={{0,1},{1,0},{2,3},{3,2},{4,5},{5,4},{6,7},{7,6},{8,9},{9,8},{10,11... | collective-permute-start | bytes 393224 | tf_op jit(solution)/shard_map/ppermute | solution.py:319
  32.0 3.2 %collective-permute-start.14 = (bf16[4,32,512]{2,1,0:T(8,128)(2,1)S(1)}, bf16[4,32,512]{2,1,0:T(8,128)(2,1)S(1)}, u32[]{:S(2)}, u32[]{:S(2)}) collective-permute-start(bf16[4,32,512]{2,1,0:T(8,128)(2,1)S(1)} %collective-permute-done.11.rest_ref), channel_id=1, source_target_pairs={{0,1},{1,0},{2,3},{3,2},{4,5},{5,4},{6,7},{7,6},{8,9},{9,8},{10,11... | collective-permute-start | bytes 393224 | tf_op jit(solution)/shard_map/ppermute | solution.py:319
  39.3 5.9 %collective-permute-start.18 = (bf16[4,32,512]{2,1,0:T(8,128)(2,1)S(1)}, bf16[4,32,512]{2,1,0:T(8,128)(2,1)S(1)}, u32[]{:S(2)}, u32[]{:S(2)}) collective-permute-start(bf16[4,32,512]{2,1,0:T(8,128)(2,1)S(1)} %get-tuple-element.133), channel_id=1, source_target_pairs={{0,2},{1,3},{2,0},{3,1},{4,6},{5,7},{6,4},{7,5},{8,10},{9,11},{10,... | collective-permute-start | bytes 393224 | tf_op jit(solution)/shard_map/ppermute | solution.py:319
  46.1 1.6 %collective-permute-start.19 = (bf16[8,32,512]{2,1,0:T(8,128)(2,1)S(1)}, bf16[8,32,512]{2,1,0:T(8,128)(2,1)S(1)}, u32[]{:S(2)}, u32[]{:S(2)}) collective-permute-start(bf16[8,32,512]{2,1,0:T(8,128)(2,1)S(1)} %get-tuple-element.135), channel_id=1, source_target_pairs={{0,1},{1,0},{2,3},{3,2},{4,5},{5,4},{6,7},{7,6},{8,9},{9,8},{10,11... | collective-permute-start | bytes 786440 | tf_op jit(solution)/shard_map/ppermute | solution.py:319
  47.7 5.6 %collective-permute-start.20 = (bf16[4,32,512]{2,1,0:T(8,128)(2,1)S(1)}, bf16[4,32,512]{2,1,0:T(8,128)(2,1)S(1)}, u32[]{:S(2)}, u32[]{:S(2)}) collective-permute-start(bf16[4,32,512]{2,1,0:T(8,128)(2,1)S(1)} %get-tuple-element.155), channel_id=1, source_target_pairs={{0,2},{1,3},{2,0},{3,1},{4,6},{5,7},{6,4},{7,5},{8,10},{9,11},{10,... | collective-permute-start | bytes 393224 | tf_op jit(solution)/shard_map/ppermute | solution.py:319
  49.3 5.5 %collective-permute-start.23 = (bf16[2,32,512]{2,1,0:T(8,128)(2,1)S(1)}, bf16[2,32,512]{2,1,0:T(8,128)(2,1)S(1)}, u32[]{:S(2)}, u32[]{:S(2)}) collective-permute-start(bf16[2,32,512]{2,1,0:T(8,128)(2,1)S(1)} %get-tuple-element.163), channel_id=1, source_target_pairs={{0,4},{1,5},{2,6},{3,7},{4,0},{5,1},{6,2},{7,3},{8,12},{9,13},{10,... | collective-permute-start | bytes 196616 | tf_op jit(solution)/shard_map/ppermute | solution.py:316
  53.4 4.7 %collective-permute-start.21 = (bf16[2,32,512]{2,1,0:T(8,128)(2,1)S(1)}, bf16[2,32,512]{2,1,0:T(8,128)(2,1)S(1)}, u32[]{:S(2)}, u32[]{:S(2)}) collective-permute-start(bf16[2,32,512]{2,1,0:T(8,128)(2,1)S(1)} %get-tuple-element.157), channel_id=1, source_target_pairs={{0,4},{1,5},{2,6},{3,7},{4,0},{5,1},{6,2},{7,3},{8,12},{9,13},{10,... | collective-permute-start | bytes 196616 | tf_op jit(solution)/shard_map/ppermute | solution.py:316
  54.8 6.0 %collective-permute-start.24 = (bf16[1,32,512]{2,1,0:T(8,128)(2,1)S(1)}, bf16[1,32,512]{2,1,0:T(8,128)(2,1)S(1)}, u32[]{:S(2)}, u32[]{:S(2)}) collective-permute-start(bf16[1,32,512]{2,1,0:T(8,128)(2,1)S(1)} %get-tuple-element.165), channel_id=1, source_target_pairs={{0,8},{1,9},{2,10},{3,11},{4,12},{5,13},{6,14},{7,15},{8,0},{9,1},... | collective-permute-start | bytes 98312 | tf_op jit(solution)/shard_map/ppermute | solution.py:316
  58.1 4.9 %collective-permute-start.22 = (bf16[1,32,512]{2,1,0:T(8,128)(2,1)S(1)}, bf16[1,32,512]{2,1,0:T(8,128)(2,1)S(1)}, u32[]{:S(2)}, u32[]{:S(2)}) collective-permute-start(bf16[1,32,512]{2,1,0:T(8,128)(2,1)S(1)} %get-tuple-element.159), channel_id=1, source_target_pairs={{0,8},{1,9},{2,10},{3,11},{4,12},{5,13},{6,14},{7,15},{8,0},{9,1},... | collective-permute-start | bytes 98312 | tf_op jit(solution)/shard_map/ppermute | solution.py:316
  (12 other events, 113.0 us)

commit v10 on v8

--- a/solution.py
+++ b/solution.py
@@ -54,7 +54,7 @@
 
 
 def send_kernel(
-    me_ref, offset_ref, act_ref, expo_ref, base_ref, received_ref, cot_ref, gain_ref,
+    me_ref, ids_ref, act_ref, expo_ref, base_ref, received_ref, cot_ref, gain_ref,
     new_rows_ref, received_out_ref, gain_out_ref, *refs,
 ):
     *packed_refs, rows_ref = refs
@@ -65,12 +65,13 @@
     received_out_ref[...] = received_ref[...]
     for j in range(n):
         gain_out_ref[j : j + 1, :] = gain_ref[:, j * share : (j + 1) * share]
-    first = offset_ref[0] == 0
+    offset = ids_ref[0] - base_ref.shape[1] * me_ref[0]
+    first = offset == 0
     down, up = powers(expo_ref[...], -1), powers(expo_ref[...], 1)
     old = [base_ref[p] for p in range(2)]
     chosen = jnp.concatenate([jnp.where(first, o[0:1], o[1:2]) for o in old], axis=0)
     delta = act_ref[...].astype(f32) - chosen
-    fill = jnp.full((rows - 2 * per_dev, LANES), offset_ref[0].astype(f32))
+    fill = jnp.full((rows - 2 * per_dev, LANES), offset.astype(f32))
     pieces = []
     for b in range(width // LANES):
         scaled = delta[:, b * LANES : (b + 1) * LANES] * down[:, b : b + 1]
@@ -90,8 +91,8 @@
     new_rows_ref[...] = chosen + jnp.concatenate(pieces, axis=1)
 
 
-def sender_base_kernel(offset_ref, rows_ref, base_ref, new_ref):
-    first = offset_ref[0] == 0
+def sender_base_kernel(me_ref, ids_ref, rows_ref, base_ref, new_ref):
+    first = ids_ref[0] == base_ref.shape[1] * me_ref[0]
     for p in range(2):
         row, old = rows_ref[p : p + 1, :], base_ref[p]
         new_ref[p, 0:1, :] = jnp.where(first, row, old[0:1])
@@ -204,17 +205,12 @@
     gh_ref[...] = (grad_active * sigma * (1.0 + hidden * (1.0 - sigma))).astype(bf16)
 
 
-def grad_norm_kernel(first, last, me_ref, gh_ref, weight_ref, *refs):
-    if first:
-        rows_in_ref, send_ref, keep_ref, rows_ref = refs
-        rows_ref[...] = rows_in_ref[...]
-    else:
-        (rows_ref,) = refs
+def grad_norm_kernel(me_ref, gh_ref, weight_ref, rows_ref):
     chunks = rows_ref.shape[0]
     tokens, width = gh_ref.shape[0], chunks * LANES
-    half, n = tokens // 4, tokens // 2
+    n = tokens // 2
     gh = gh_ref[...]
-    for share in range(first, last):
+    for share in range(n):
         block = weight_ref[share * width : (share + 1) * width, :]
         terms = dot_by_halves(block, gh).T
         for p in range(2):
@@ -222,13 +218,15 @@
                 rows_ref[c, pl.ds(p * n + share, n, stride=tokens), :] = terms[
                     p * n : (p + 1) * n, c * LANES : (c + 1) * LANES
                 ]
-    if last < n:
-        return
+
+
+def split_kernel(me_ref, rows_ref, send_ref, keep_ref):
+    half, tokens, _ = send_ref.shape
     core = lax.rem(me_ref[0], 2)
     for k in range(half):
         keep_at = pl.multiple_of((2 * k + core) * tokens, tokens)
         send_at = pl.multiple_of((2 * k + 1 - core) * tokens, tokens)
-        for c in range(chunks):
+        for c in range(rows_ref.shape[0]):
             cols = slice(c * LANES, (c + 1) * LANES)
             keep_ref[k, :, cols] = rows_ref[c, pl.ds(keep_at, tokens), :].astype(bf16)
             send_ref[k, :, cols] = rows_ref[c, pl.ds(send_at, tokens), :].astype(bf16)
@@ -338,7 +336,6 @@
             ),
         )(*args)
 
-    offset = sample_ids - sender_base.shape[1] * me
     rows = -(-(2 * width // LANES + 1) // 16) * 16
     packed_shape = (tokens, width + LANES * -(-4 * rows // tokens))
     act_shape, expo_shape = (2, width_all), (2, width_all // LANES)
@@ -359,7 +356,7 @@
         compiler_params=params(8),
     )(
         me_in,
-        offset,
+        sample_ids,
         hbm(activations.reshape(act_shape)),
         hbm(forward_exponent.reshape(expo_shape)),
         hbm(sender_base),
@@ -421,8 +418,7 @@
     cots[0], share_after = together((cot_line, share))
     cot_row = swap(cots[0], 2)
     grads = [grad_active_part(0)]
-    new_receiver_base = rebuild(struct(receiver_base.shape, f32), 0.7)
-    lines, grads[0], new_receiver_base = together((lines, grads[0], new_receiver_base))
+    lines, grads[0] = together((lines, grads[0]))
     rest_line = jnp.stack(lines)
     rest_row = swap(rest_line, 2)
     rests = [rest_line]
@@ -434,8 +430,8 @@
     new_sender_base = call(
         sender_base_kernel,
         struct(sender_base.shape, f32),
-        [SMEM] + [VMEM] * 2,
-        [offset, new_rows, sender_base],
+        [SMEM, SMEM] + [VMEM] * 2,
+        [me_in, sample_ids, new_rows, sender_base],
     )
     rest_row, cot_row, grads[1], grads[2], new_sender_base = together(
         (rest_row, cot_row, grads[1], grads[2], new_sender_base)
@@ -482,7 +478,8 @@
             [SMEM] + [VMEM] * 2,
             [me_in, kept, arrived],
         )
-        return [shift(x, r) for r, x in enumerate(shares)]
+        far_first = [shift(shares[r], r) for r in reversed(range(quarter))]
+        return far_first
 
     out_send = down_terms(1, active)
     out_in = swap(out_send, 1)
@@ -491,24 +488,21 @@
     out_row_in = swap(out_send, 2)
     grad_hidden, out_row = together((grad_hidden, out_row))
     rows_out = struct((width // LANES, n * tokens, LANES), f32)
-    most = n - n // 8
     grad_rows = call(
-        functools.partial(grad_norm_kernel, 0, most),
+        grad_norm_kernel,
         rows_out,
         [SMEM] + [VMEM] * 2,
         [me_in, grad_hidden, up_weight],
-        micros=4,
+        micros=4.5,
     )
     grad_rows, out_row_in = together((grad_rows, out_row_in))
     grad_send, grad_keep = call(
-        functools.partial(grad_norm_kernel, most, n),
-        (half_out, half_out),
-        [SMEM] + [VMEM] * 3,
-        [me_in, grad_hidden, up_weight, grad_rows],
-        [pltpu.VMEM(rows_out.shape, f32)],
-        micros=0.7,
+        split_kernel, (half_out, half_out), [SMEM, VMEM], [me_in, grad_rows], micros=0.4
     )
     grad_in = swap(grad_send, 1)
+    received, blocks, grad_send = together((received, blocks, grad_send))
+    new_receiver_base = rebuild(struct(receiver_base.shape, f32), 0.7)
+    grad_in, new_receiver_base = together((grad_in, new_receiver_base))
     grad_send, grad_row = pair_sum(grad_keep, grad_in)
     grad_row_in = swap(grad_send, 2)
     out_row, grad_row = together((out_row, grad_row))

time: 61.5 us -> 60.7 us (0.987)
    ppermute x12, waiting for transfers between devices: 8.48 us -> 7.79 us  [shift(): return lax.ppermute(x, 'dp', [(d, d ^ 4 * r) for d in range(n)]) if r else x]
  transfers between devices with their start and end apart: 25 -> 25, of which waited for: 10 -> 10; matrix products, arithmetic and copies ran while one was open for 0% -> 0% of each run, Pallas kernels for 22% -> 23%
where the time goes in v10:
time: 60.7 us; the launch traced here: 60.6 us
  starting transfers between devices  24.9 us (41%)
  Pallas kernels  18.9 us (31%)
  waiting for transfers between devices  15.1 us (25%)
  between operations  1.57 us (3%)
    ppermute x12, starting transfers between devices, shift(): return lax.ppermute(x, 'dp', [(d, d ^ 4 * r) for d in range(n)]) if r else x  19 us
    pallas_call x21, Pallas kernels, call(): pl.pallas_call(kernel, out_shape=outs, in_specs=ins, out_specs=jax.tree.m...  17.7 us
    ppermute x12, waiting for transfers between devices, shift(): return lax.ppermute(x, 'dp', [(d, d ^ 4 * r) for d in range(n)]) if r else x  7.79 us
    ppermute x13, waiting for transfers between devices, swap(): return lax.ppermute(x, 'dp', [(d, d ^ bits) for d in range(n)])  7.29 us
    ppermute x13, starting transfers between devices, swap(): return lax.ppermute(x, 'dp', [(d, d ^ bits) for d in range(n)])  5.89 us
    pallas_call x1, Pallas kernels, on_device(): pl.pallas_call(send_kernel, out_shape=outs, grid=(1,), in_specs=[SMEM, SM...  1.22 us
  transfers between devices with their start and end apart: 25, of which 10 were waited for; matrix products, arithmetic and copies ran while one was open for 0% of the time, Pallas kernels for 23%

profile of v10, /device:TPU:0, one launch (start us, length us, event | category | flops | bytes accessed | tf_op | source)
XLA Modules:
  0.0 60.6 jit_solution(9850171399699594357)
XLA Ops:
  1.3 1.2 %shard_map.129 = (f32[2,8192]{1,0:T(2,128)S(1)}, f32[2,32,512]{2,1,0:T(8,128)S(1)}, f32[16,512]{1,0:T(8,128)S(1)}, bf16[32,768]{1,0:T(8,128)(2,1)S(1)}, bf16[32,...) custom-call(s32[1]{0:T(128)} %bitcast.me_ref, s32[1]{0:T(128)S(6)} %copy.15.ids_ref, ...), custom_call_target="tpu_custom_call" | custom-call | tf_op jit(solution)/shard_map/pallas_call | solution.py:349
  2.6 3.1 %collective-permute-start = (bf16[32,768]{1,0:T(8,128)(2,1)S(1)}, bf16[32,768]{1,0:T(8,128)(2,1)S(1)}, u32[]{:S(2)}, u32[]{:S(2)}) collective-permute-start(bf16[32,768]{1,0:T(8,128)(2,1)S(1)} %get-tuple-element.87), channel_id=1, source_target_pairs={{0,4},{1,5},{2,6},{3,7},{4,0},{5,1},{6,2},{7,3},{8,12},{9,13},{10,... | collective-permute-start | bytes 147464 | tf_op jit(solution)/shard_map/ppermute | solution.py:317
  5.6 2.6 %collective-permute-start.1 = (bf16[32,768]{1,0:T(8,128)(2,1)S(1)}, bf16[32,768]{1,0:T(8,128)(2,1)S(1)}, u32[]{:S(2)}, u32[]{:S(2)}) collective-permute-start(bf16[32,768]{1,0:T(8,128)(2,1)S(1)} %get-tuple-element.88), channel_id=1, source_target_pairs={{0,8},{1,9},{2,10},{3,11},{4,12},{5,13},{6,14},{7,15},{8,0},{9,1},... | collective-permute-start | bytes 147464 | tf_op jit(solution)/shard_map/ppermute | solution.py:317
  8.2 3.3 %collective-permute-done.1.refs_2_ = bf16[32,768]{1,0:T(8,128)(2,1)S(1)} collective-permute-done((bf16[32,768]{1,0:T(8,128)(2,1)S(1)}, bf16[32,768]{1,0:T(8,128)(2,1)S(1)}, u32[]{:S(2)}, u32[]{:S(2)}) %collective-permute-start.1) | collective-permute-done | bytes 49184 | tf_op jit(solution)/shard_map/ppermute | solution.py:317
  11.6 2.6 %collective-permute-done.2.refs_3_ = bf16[32,768]{1,0:T(8,128)(2,1)S(1)} collective-permute-done((bf16[32,768]{1,0:T(8,128)(2,1)S(1)}, bf16[32,768]{1,0:T(8,128)(2,1)S(1)}, u32[]{:S(2)}, u32[]{:S(2)}) %collective-permute-start.2) | collective-permute-done | bytes 49184 | tf_op jit(solution)/shard_map/ppermute | solution.py:317
  14.2 1.6 %collective-permute-start.4 = (bf16[4,16,128]{2,1,0:T(8,128)(2,1)S(1)}, bf16[4,16,128]{2,1,0:T(8,128)(2,1)S(1)}, u32[]{:S(2)}, u32[]{:S(2)}) collective-permute-start(bf16[4,16,128]{2,1,0:T(8,128)(2,1)S(1)} %get-tuple-element.92), channel_id=1, source_target_pairs={{0,2},{1,3},{2,0},{3,1},{4,6},{5,7},{6,4},{7,5},{8,10},{9,11},{10,... | collective-permute-start | bytes 49160 | tf_op jit(solution)/shard_map/ppermute | solution.py:320
  16.8 1.2 %collective-permute-done.4.b2 = bf16[4,16,128]{2,1,0:T(8,128)(2,1)S(1)} collective-permute-done((bf16[4,16,128]{2,1,0:T(8,128)(2,1)S(1)}, bf16[4,16,128]{2,1,0:T(8,128)(2,1)S(1)}, u32[]{:S(2)}, u32[]{:S(2)}) %collective-permute-start.4) | collective-permute-done | bytes 16416 | tf_op jit(solution)/shard_map/ppermute | solution.py:320
  18.0 0.9 %collective-permute-done.5.b3 = bf16[4,16,128]{2,1,0:T(8,128)(2,1)S(1)} collective-permute-done((bf16[4,16,128]{2,1,0:T(8,128)(2,1)S(1)}, bf16[4,16,128]{2,1,0:T(8,128)(2,1)S(1)}, u32[]{:S(2)}, u32[]{:S(2)}) %collective-permute-start.5) | collective-permute-done | bytes 16416 | tf_op jit(solution)/shard_map/ppermute | solution.py:320
  19.9 3.6 %collective-permute-start.6 = (bf16[32,512]{1,0:T(8,128)(2,1)S(1)}, bf16[32,512]{1,0:T(8,128)(2,1)S(1)}, u32[]{:S(2)}, u32[]{:S(2)}) collective-permute-start(bf16[32,512]{1,0:T(8,128)(2,1)S(1)} %shard_map.131.share_ref), channel_id=1, source_target_pairs={{0,4},{1,5},{2,6},{3,7},{4,0},{5,1},{6,2},{7,3},{8,12},{9,13},{10,... | collective-permute-start | bytes 98312 | tf_op jit(solution)/shard_map/ppermute | solution.py:317
  24.2 1.2 %shard_map.132 = (f32[896,32]{1,0:T(8,128)S(1)}, f32[32,512]{1,0:T(8,128)S(1)}) custom-call(s32[1]{0:T(128)} %bitcast.me_ref, bf16[4,32,512]{2,1,0:T(8,128)(2,1)S(1)} %get-tuple-element.110.cot_ref, bf16[896,8192]{1,0:T(8,128)(2,1)S(1)} %bitcast.13), custom_call_target="tpu_custom_call" | custom-call | flops 1840000000 | tf_op jit(solution)/shard_map/pallas_call | solution.py:327
  25.5 1.4 %collective-permute-start.9 = (bf16[4,32,512]{2,1,0:T(8,128)(2,1)S(1)}, bf16[4,32,512]{2,1,0:T(8,128)(2,1)S(1)}, u32[]{:S(2)}, u32[]{:S(2)}) collective-permute-start(bf16[4,32,512]{2,1,0:T(8,128)(2,1)S(1)} %pad_maximum_fusion.rest_ref), channel_id=1, source_target_pairs={{0,2},{1,3},{2,0},{3,1},{4,6},{5,7},{6,4},{7,5},{8,10},{9,11},{10,... | collective-permute-start | bytes 393224 | tf_op jit(solution)/shard_map/ppermute | solution.py:320
  27.7 2.1 %collective-permute-done.10.cot_ref = bf16[4,32,512]{2,1,0:T(8,128)(2,1)S(1)} collective-permute-done((bf16[4,32,512]{2,1,0:T(8,128)(2,1)S(1)}, bf16[4,32,512]{2,1,0:T(8,128)(2,1)S(1)}, u32[]{:S(2)}, u32[]{:S(2)}) %collective-permute-start.10) | collective-permute-done | bytes 131104 | tf_op jit(solution)/shard_map/ppermute | solution.py:320
  30.3 1.2 %shard_map.134 = (f32[896,32]{1,0:T(8,128)S(1)}, f32[32,512]{1,0:T(8,128)S(1)}) custom-call(s32[1]{0:T(128)} %bitcast.me_ref, bf16[4,32,512]{2,1,0:T(8,128)(2,1)S(1)} %collective-permute-done.10.cot_ref, bf16[896,8192]{1,0:T(8,128)(2,1)S(1)} %bitcast.13), custom_call_target="tpu_custom_call" | custom-call | flops 1840000000 | tf_op jit(solution)/shard_map/pallas_call | solution.py:327
  31.5 1.2 %shard_map.135 = (f32[896,32]{1,0:T(8,128)S(1)}, f32[32,512]{1,0:T(8,128)S(1)}) custom-call(s32[1]{0:T(128)} %bitcast.me_ref, bf16[4,32,512]{2,1,0:T(8,128)(2,1)S(1)} %collective-permute-done.11.cot_ref, bf16[896,8192]{1,0:T(8,128)(2,1)S(1)} %bitcast.13), custom_call_target="tpu_custom_call" | custom-call | flops 1840000000 | tf_op jit(solution)/shard_map/pallas_call | solution.py:327
  34.8 1.2 %shard_map.139 = (f32[896,32]{1,0:T(8,128)S(1)}, f32[32,512]{1,0:T(8,128)S(1)}) custom-call(s32[1]{0:T(128)} %bitcast.me_ref, bf16[4,32,512]{2,1,0:T(8,128)(2,1)S(1)} %collective-permute-done.14.cot_ref, bf16[896,8192]{1,0:T(8,128)(2,1)S(1)} %bitcast.13), custom_call_target="tpu_custom_call" | custom-call | flops 1840000000 | tf_op jit(solution)/shard_map/pallas_call | solution.py:327
  36.8 1.7 %shard_map.141 = bf16[8,32,512]{2,1,0:T(8,128)(2,1)S(1)} custom-call(s32[1]{0:T(128)} %bitcast.me_ref, bf16[32,896]{1,0:T(8,128)(2,1)S(1)} %get-tuple-element.130.active_ref, bf16[896,8192]{1,0:T(8,128)(2,1)S(1)} %bitcast.13), custom_call_target="tpu_custom_call" | custom-call | flops 1724999936 | tf_op jit(solution)/shard_map/pallas_call | solution.py:327
  38.5 1.5 %shard_map.142.kept_ref = bf16[8,32,512]{2,1,0:T(8,128)(2,1)S(1)} custom-call(s32[1]{0:T(128)} %bitcast.me_ref, bf16[32,896]{1,0:T(8,128)(2,1)S(1)} %get-tuple-element.130.active_ref, bf16[896,8192]{1,0:T(8,128)(2,1)S(1)} %bitcast.13), custom_call_target="tpu_custom_call" | custom-call | flops 1724999936 | tf_op jit(solution)/shard_map/pallas_call | solution.py:327
  40.2 4.2 %shard_map.144.rows_ref = f32[4,512,128]{2,1,0:T(8,128)S(1)} custom-call(s32[1]{0:T(128)} %bitcast.me_ref, bf16[32,896]{1,0:T(8,128)(2,1)S(1)} %get-tuple-element.132.gh_ref, bf16[8192,896]{1,0:T(8,128)(2,1)S(1)} %bitcast.15), custom_call_target="tpu_custom_call" | custom-call | flops 5175000064 | tf_op jit(solution)/shard_map/pallas_call | solution.py:327
  44.5 1.5 %collective-permute-done.16.arrived_ref = bf16[4,32,512]{2,1,0:T(8,128)(2,1)S(1)} collective-permute-done((bf16[4,32,512]{2,1,0:T(8,128)(2,1)S(1)}, bf16[4,32,512]{2,1,0:T(8,128)(2,1)S(1)}, u32[]{:S(2)}, u32[]{:S(2)}) %collective-permute-start.16) | collective-permute-done | bytes 131104 | tf_op jit(solution)/shard_map/ppermute | solution.py:320
  48.9 1.1 %collective-permute-start.23 = (bf16[32,512]{1,0:T(8,128)(2,1)S(1)}, bf16[32,512]{1,0:T(8,128)(2,1)S(1)}, u32[]{:S(2)}, u32[]{:S(2)}) collective-permute-start(bf16[32,512]{1,0:T(8,128)(2,1)S(1)} %get-tuple-element.163), channel_id=1, source_target_pairs={{0,8},{1,9},{2,10},{3,11},{4,12},{5,13},{6,14},{7,15},{8,0},{9,1},... | collective-permute-start | bytes 98312 | tf_op jit(solution)/shard_map/ppermute | solution.py:317
  50.0 2.8 %collective-permute-start.24 = (bf16[32,512]{1,0:T(8,128)(2,1)S(1)}, bf16[32,512]{1,0:T(8,128)(2,1)S(1)}, u32[]{:S(2)}, u32[]{:S(2)}) collective-permute-start(bf16[32,512]{1,0:T(8,128)(2,1)S(1)} %get-tuple-element.164), channel_id=1, source_target_pairs={{0,4},{1,5},{2,6},{3,7},{4,0},{5,1},{6,2},{7,3},{8,12},{9,13},{10,... | collective-permute-start | bytes 98312 | tf_op jit(solution)/shard_map/ppermute | solution.py:317
  53.5 1.1 %collective-permute-start.20 = (bf16[32,512]{1,0:T(8,128)(2,1)S(1)}, bf16[32,512]{1,0:T(8,128)(2,1)S(1)}, u32[]{:S(2)}, u32[]{:S(2)}) collective-permute-start(bf16[32,512]{1,0:T(8,128)(2,1)S(1)} %get-tuple-element.157), channel_id=1, source_target_pairs={{0,8},{1,9},{2,10},{3,11},{4,12},{5,13},{6,14},{7,15},{8,0},{9,1},... | collective-permute-start | bytes 98312 | tf_op jit(solution)/shard_map/ppermute | solution.py:317
  54.6 3.2 %collective-permute-start.21 = (bf16[32,512]{1,0:T(8,128)(2,1)S(1)}, bf16[32,512]{1,0:T(8,128)(2,1)S(1)}, u32[]{:S(2)}, u32[]{:S(2)}) collective-permute-start(bf16[32,512]{1,0:T(8,128)(2,1)S(1)} %get-tuple-element.158), channel_id=1, source_target_pairs={{0,4},{1,5},{2,6},{3,7},{4,0},{5,1},{6,2},{7,3},{8,12},{9,13},{10,... | collective-permute-start | bytes 98312 | tf_op jit(solution)/shard_map/ppermute | solution.py:317
  57.9 1.3 %collective-permute-done.19.refs_8_ = bf16[32,512]{1,0:T(8,128)(2,1)S(1)} collective-permute-done((bf16[32,512]{1,0:T(8,128)(2,1)S(1)}, bf16[32,512]{1,0:T(8,128)(2,1)S(1)}, u32[]{:S(2)}, u32[]{:S(2)}) %collective-permute-start.19) | collective-permute-done | bytes 32800 | tf_op jit(solution)/shard_map/ppermute | solution.py:317
  (71 shorter events, 12.0 us)
Async XLA Ops:
  2.6 5.7 %collective-permute-start = (bf16[32,768]{1,0:T(8,128)(2,1)S(1)}, bf16[32,768]{1,0:T(8,128)(2,1)S(1)}, u32[]{:S(2)}, u32[]{:S(2)}) collective-permute-start(bf16[32,768]{1,0:T(8,128)(2,1)S(1)} %get-tuple-element.87), channel_id=1, source_target_pairs={{0,4},{1,5},{2,6},{3,7},{4,0},{5,1},{6,2},{7,3},{8,12},{9,13},{10,... | collective-permute-start | bytes 147464 | tf_op jit(solution)/shard_map/ppermute | solution.py:317
  5.6 5.9 %collective-permute-start.1 = (bf16[32,768]{1,0:T(8,128)(2,1)S(1)}, bf16[32,768]{1,0:T(8,128)(2,1)S(1)}, u32[]{:S(2)}, u32[]{:S(2)}) collective-permute-start(bf16[32,768]{1,0:T(8,128)(2,1)S(1)} %get-tuple-element.88), channel_id=1, source_target_pairs={{0,8},{1,9},{2,10},{3,11},{4,12},{5,13},{6,14},{7,15},{8,0},{9,1},... | collective-permute-start | bytes 147464 | tf_op jit(solution)/shard_map/ppermute | solution.py:317
  8.2 5.9 %collective-permute-start.2 = (bf16[32,768]{1,0:T(8,128)(2,1)S(1)}, bf16[32,768]{1,0:T(8,128)(2,1)S(1)}, u32[]{:S(2)}, u32[]{:S(2)}) collective-permute-start(bf16[32,768]{1,0:T(8,128)(2,1)S(1)} %get-tuple-element.89), channel_id=1, source_target_pairs={{0,12},{1,13},{2,14},{3,15},{4,8},{5,9},{6,10},{7,11},{8,4},{9,5},... | collective-permute-start | bytes 147464 | tf_op jit(solution)/shard_map/ppermute | solution.py:317
  14.2 2.6 %collective-permute-start.3 = (bf16[4,16,128]{2,1,0:T(8,128)(2,1)S(1)}, bf16[4,16,128]{2,1,0:T(8,128)(2,1)S(1)}, u32[]{:S(2)}, u32[]{:S(2)}) collective-permute-start(bf16[4,16,128]{2,1,0:T(8,128)(2,1)S(1)} %get-tuple-element.91), channel_id=1, source_target_pairs={{0,1},{1,0},{2,3},{3,2},{4,5},{5,4},{6,7},{7,6},{8,9},{9,8},{10,11... | collective-permute-start | bytes 49160 | tf_op jit(solution)/shard_map/ppermute | solution.py:320
  14.2 3.8 %collective-permute-start.4 = (bf16[4,16,128]{2,1,0:T(8,128)(2,1)S(1)}, bf16[4,16,128]{2,1,0:T(8,128)(2,1)S(1)}, u32[]{:S(2)}, u32[]{:S(2)}) collective-permute-start(bf16[4,16,128]{2,1,0:T(8,128)(2,1)S(1)} %get-tuple-element.92), channel_id=1, source_target_pairs={{0,2},{1,3},{2,0},{3,1},{4,6},{5,7},{6,4},{7,5},{8,10},{9,11},{10,... | collective-permute-start | bytes 49160 | tf_op jit(solution)/shard_map/ppermute | solution.py:320
  15.8 3.2 %collective-permute-start.5 = (bf16[4,16,128]{2,1,0:T(8,128)(2,1)S(1)}, bf16[4,16,128]{2,1,0:T(8,128)(2,1)S(1)}, u32[]{:S(2)}, u32[]{:S(2)}) collective-permute-start(bf16[4,16,128]{2,1,0:T(8,128)(2,1)S(1)} %get-tuple-element.93), channel_id=1, source_target_pairs={{0,3},{1,2},{2,1},{3,0},{4,7},{5,6},{6,5},{7,4},{8,11},{9,10},{10,... | collective-permute-start | bytes 49160 | tf_op jit(solution)/shard_map/ppermute | solution.py:320
  19.1 6.4 %collective-permute-start.8 = (bf16[32,512]{1,0:T(8,128)(2,1)S(1)}, bf16[32,512]{1,0:T(8,128)(2,1)S(1)}, u32[]{:S(2)}, u32[]{:S(2)}) collective-permute-start(bf16[32,512]{1,0:T(8,128)(2,1)S(1)} %shard_map.131.share_ref), channel_id=1, source_target_pairs={{0,12},{1,13},{2,14},{3,15},{4,8},{5,9},{6,10},{7,11},{8,4},{9,5},... | collective-permute-start | bytes 98312 | tf_op jit(solution)/shard_map/ppermute | solution.py:317
  19.9 5.6 %collective-permute-start.7 = (bf16[32,512]{1,0:T(8,128)(2,1)S(1)}, bf16[32,512]{1,0:T(8,128)(2,1)S(1)}, u32[]{:S(2)}, u32[]{:S(2)}) collective-permute-start(bf16[32,512]{1,0:T(8,128)(2,1)S(1)} %shard_map.131.share_ref), channel_id=1, source_target_pairs={{0,8},{1,9},{2,10},{3,11},{4,12},{5,13},{6,14},{7,15},{8,0},{9,1},... | collective-permute-start | bytes 98312 | tf_op jit(solution)/shard_map/ppermute | solution.py:317
  19.9 5.6 %collective-permute-start.6 = (bf16[32,512]{1,0:T(8,128)(2,1)S(1)}, bf16[32,512]{1,0:T(8,128)(2,1)S(1)}, u32[]{:S(2)}, u32[]{:S(2)}) collective-permute-start(bf16[32,512]{1,0:T(8,128)(2,1)S(1)} %shard_map.131.share_ref), channel_id=1, source_target_pairs={{0,4},{1,5},{2,6},{3,7},{4,0},{5,1},{6,2},{7,3},{8,12},{9,13},{10,... | collective-permute-start | bytes 98312 | tf_op jit(solution)/shard_map/ppermute | solution.py:317
  23.5 6.3 %collective-permute-start.10 = (bf16[4,32,512]{2,1,0:T(8,128)(2,1)S(1)}, bf16[4,32,512]{2,1,0:T(8,128)(2,1)S(1)}, u32[]{:S(2)}, u32[]{:S(2)}) collective-permute-start(bf16[4,32,512]{2,1,0:T(8,128)(2,1)S(1)} %get-tuple-element.110.cot_ref), channel_id=1, source_target_pairs={{0,2},{1,3},{2,0},{3,1},{4,6},{5,7},{6,4},{7,5},{8,10},{9,11},{10,... | collective-permute-start | bytes 393224 | tf_op jit(solution)/shard_map/ppermute | solution.py:320
  25.5 7.2 %collective-permute-start.9 = (bf16[4,32,512]{2,1,0:T(8,128)(2,1)S(1)}, bf16[4,32,512]{2,1,0:T(8,128)(2,1)S(1)}, u32[]{:S(2)}, u32[]{:S(2)}) collective-permute-start(bf16[4,32,512]{2,1,0:T(8,128)(2,1)S(1)} %pad_maximum_fusion.rest_ref), channel_id=1, source_target_pairs={{0,2},{1,3},{2,0},{3,1},{4,6},{5,7},{6,4},{7,5},{8,10},{9,11},{10,... | collective-permute-start | bytes 393224 | tf_op jit(solution)/shard_map/ppermute | solution.py:320
  29.8 1.7 %collective-permute-start.11 = (bf16[4,32,512]{2,1,0:T(8,128)(2,1)S(1)}, bf16[4,32,512]{2,1,0:T(8,128)(2,1)S(1)}, u32[]{:S(2)}, u32[]{:S(2)}) collective-permute-start(bf16[4,32,512]{2,1,0:T(8,128)(2,1)S(1)} %get-tuple-element.110.cot_ref), channel_id=1, source_target_pairs={{0,1},{1,0},{2,3},{3,2},{4,5},{5,4},{6,7},{7,6},{8,9},{9,8},{10,11... | collective-permute-start | bytes 393224 | tf_op jit(solution)/shard_map/ppermute | solution.py:320
  29.8 4.2 %collective-permute-start.13 = (bf16[4,32,512]{2,1,0:T(8,128)(2,1)S(1)}, bf16[4,32,512]{2,1,0:T(8,128)(2,1)S(1)}, u32[]{:S(2)}, u32[]{:S(2)}) collective-permute-start(bf16[4,32,512]{2,1,0:T(8,128)(2,1)S(1)} %pad_maximum_fusion.rest_ref), channel_id=1, source_target_pairs={{0,1},{1,0},{2,3},{3,2},{4,5},{5,4},{6,7},{7,6},{8,9},{9,8},{10,11... | collective-permute-start | bytes 393224 | tf_op jit(solution)/shard_map/ppermute | solution.py:320
  32.7 2.0 %collective-permute-start.14 = (bf16[4,32,512]{2,1,0:T(8,128)(2,1)S(1)}, bf16[4,32,512]{2,1,0:T(8,128)(2,1)S(1)}, u32[]{:S(2)}, u32[]{:S(2)}) collective-permute-start(bf16[4,32,512]{2,1,0:T(8,128)(2,1)S(1)} %collective-permute-done.10.cot_ref), channel_id=1, source_target_pairs={{0,1},{1,0},{2,3},{3,2},{4,5},{5,4},{6,7},{7,6},{8,9},{9,8},{10,11... | collective-permute-start | bytes 393224 | tf_op jit(solution)/shard_map/ppermute | solution.py:320
  32.8 3.2 %collective-permute-start.12 = (bf16[4,32,512]{2,1,0:T(8,128)(2,1)S(1)}, bf16[4,32,512]{2,1,0:T(8,128)(2,1)S(1)}, u32[]{:S(2)}, u32[]{:S(2)}) collective-permute-start(bf16[4,32,512]{2,1,0:T(8,128)(2,1)S(1)} %collective-permute-done.9.rest_ref), channel_id=1, source_target_pairs={{0,1},{1,0},{2,3},{3,2},{4,5},{5,4},{6,7},{7,6},{8,9},{9,8},{10,11... | collective-permute-start | bytes 393224 | tf_op jit(solution)/shard_map/ppermute | solution.py:320
  40.1 5.9 %collective-permute-start.16 = (bf16[4,32,512]{2,1,0:T(8,128)(2,1)S(1)}, bf16[4,32,512]{2,1,0:T(8,128)(2,1)S(1)}, u32[]{:S(2)}, u32[]{:S(2)}) collective-permute-start(bf16[4,32,512]{2,1,0:T(8,128)(2,1)S(1)} %get-tuple-element.133), channel_id=1, source_target_pairs={{0,2},{1,3},{2,0},{3,1},{4,6},{5,7},{6,4},{7,5},{8,10},{9,11},{10,... | collective-permute-start | bytes 393224 | tf_op jit(solution)/shard_map/ppermute | solution.py:320
  46.1 1.6 %collective-permute-start.17 = (bf16[8,32,512]{2,1,0:T(8,128)(2,1)S(1)}, bf16[8,32,512]{2,1,0:T(8,128)(2,1)S(1)}, u32[]{:S(2)}, u32[]{:S(2)}) collective-permute-start(bf16[8,32,512]{2,1,0:T(8,128)(2,1)S(1)} %get-tuple-element.135), channel_id=1, source_target_pairs={{0,1},{1,0},{2,3},{3,2},{4,5},{5,4},{6,7},{7,6},{8,9},{9,8},{10,11... | collective-permute-start | bytes 786440 | tf_op jit(solution)/shard_map/ppermute | solution.py:320
  47.8 5.6 %collective-permute-start.18 = (bf16[4,32,512]{2,1,0:T(8,128)(2,1)S(1)}, bf16[4,32,512]{2,1,0:T(8,128)(2,1)S(1)}, u32[]{:S(2)}, u32[]{:S(2)}) collective-permute-start(bf16[4,32,512]{2,1,0:T(8,128)(2,1)S(1)} %get-tuple-element.155), channel_id=1, source_target_pairs={{0,2},{1,3},{2,0},{3,1},{4,6},{5,7},{6,4},{7,5},{8,10},{9,11},{10,... | collective-permute-start | bytes 393224 | tf_op jit(solution)/shard_map/ppermute | solution.py:320
  48.3 6.3 %collective-permute-start.22 = (bf16[32,512]{1,0:T(8,128)(2,1)S(1)}, bf16[32,512]{1,0:T(8,128)(2,1)S(1)}, u32[]{:S(2)}, u32[]{:S(2)}) collective-permute-start(bf16[32,512]{1,0:T(8,128)(2,1)S(1)} %get-tuple-element.162), channel_id=1, source_target_pairs={{0,12},{1,13},{2,14},{3,15},{4,8},{5,9},{6,10},{7,11},{8,4},{9,5},... | collective-permute-start | bytes 98312 | tf_op jit(solution)/shard_map/ppermute | solution.py:317
  48.9 9.0 %collective-permute-start.23 = (bf16[32,512]{1,0:T(8,128)(2,1)S(1)}, bf16[32,512]{1,0:T(8,128)(2,1)S(1)}, u32[]{:S(2)}, u32[]{:S(2)}) collective-permute-start(bf16[32,512]{1,0:T(8,128)(2,1)S(1)} %get-tuple-element.163), channel_id=1, source_target_pairs={{0,8},{1,9},{2,10},{3,11},{4,12},{5,13},{6,14},{7,15},{8,0},{9,1},... | collective-permute-start | bytes 98312 | tf_op jit(solution)/shard_map/ppermute | solution.py:317
  50.0 7.9 %collective-permute-start.24 = (bf16[32,512]{1,0:T(8,128)(2,1)S(1)}, bf16[32,512]{1,0:T(8,128)(2,1)S(1)}, u32[]{:S(2)}, u32[]{:S(2)}) collective-permute-start(bf16[32,512]{1,0:T(8,128)(2,1)S(1)} %get-tuple-element.164), channel_id=1, source_target_pairs={{0,4},{1,5},{2,6},{3,7},{4,0},{5,1},{6,2},{7,3},{8,12},{9,13},{10,... | collective-permute-start | bytes 98312 | tf_op jit(solution)/shard_map/ppermute | solution.py:317
  53.4 5.8 %collective-permute-start.19 = (bf16[32,512]{1,0:T(8,128)(2,1)S(1)}, bf16[32,512]{1,0:T(8,128)(2,1)S(1)}, u32[]{:S(2)}, u32[]{:S(2)}) collective-permute-start(bf16[32,512]{1,0:T(8,128)(2,1)S(1)} %get-tuple-element.156), channel_id=1, source_target_pairs={{0,12},{1,13},{2,14},{3,15},{4,8},{5,9},{6,10},{7,11},{8,4},{9,5},... | collective-permute-start | bytes 98312 | tf_op jit(solution)/shard_map/ppermute | solution.py:317
  53.5 5.7 %collective-permute-start.20 = (bf16[32,512]{1,0:T(8,128)(2,1)S(1)}, bf16[32,512]{1,0:T(8,128)(2,1)S(1)}, u32[]{:S(2)}, u32[]{:S(2)}) collective-permute-start(bf16[32,512]{1,0:T(8,128)(2,1)S(1)} %get-tuple-element.157), channel_id=1, source_target_pairs={{0,8},{1,9},{2,10},{3,11},{4,12},{5,13},{6,14},{7,15},{8,0},{9,1},... | collective-permute-start | bytes 98312 | tf_op jit(solution)/shard_map/ppermute | solution.py:317
  54.6 5.1 %collective-permute-start.21 = (bf16[32,512]{1,0:T(8,128)(2,1)S(1)}, bf16[32,512]{1,0:T(8,128)(2,1)S(1)}, u32[]{:S(2)}, u32[]{:S(2)}) collective-permute-start(bf16[32,512]{1,0:T(8,128)(2,1)S(1)} %get-tuple-element.158), channel_id=1, source_target_pairs={{0,4},{1,5},{2,6},{3,7},{4,0},{5,1},{6,2},{7,3},{8,12},{9,13},{10,... | collective-permute-start | bytes 98312 | tf_op jit(solution)/shard_map/ppermute | solution.py:317
  (11 other events, 97.5 us)

commit v11 on v10

--- a/solution.py
+++ b/solution.py
@@ -415,8 +415,9 @@
 
     share = rebuild(struct(share_shape, bf16), STAGE)
     lines = [shift(share, r) for r in range(quarter)]
-    cots[0], share_after = together((cot_line, share))
-    cot_row = swap(cots[0], 2)
+    cot_row = swap(cot_line, 2)
+    cot_line, cot_row, share_after = together((cot_line, cot_row, share))
+    cots = [cot_line]
     grads = [grad_active_part(0)]
     lines, grads[0] = together((lines, grads[0]))
     rest_line = jnp.stack(lines)
@@ -425,7 +426,7 @@
     products = [up_product_part(0)]
     rest_line, cot_line, cot_row, products[0] = together((rest_line, cots[0], cot_row, products[0]))
     rest_line_other = swap(rest_line, 1)
-    cots += [cot_row, swap(cot_line, 1)]
+    cots += [cot_row, swap(cot_line, 1), swap(cot_row, 1)]
     grads += [grad_active_part(1), grad_active_part(2)]
     new_sender_base = call(
         sender_base_kernel,
@@ -433,11 +434,10 @@
         [SMEM, SMEM] + [VMEM] * 2,
         [me_in, sample_ids, new_rows, sender_base],
     )
-    rest_row, cot_row, grads[1], grads[2], new_sender_base = together(
-        (rest_row, cot_row, grads[1], grads[2], new_sender_base)
+    rest_row, grads[1], grads[2], new_sender_base = together(
+        (rest_row, grads[1], grads[2], new_sender_base)
     )
     rests += [rest_row, rest_line_other, swap(rest_row, 1)]
-    cots.append(swap(cot_row, 1))
     grads.append(grad_active_part(3))
     products += [up_product_part(1), up_product_part(2)]
     gas, own_cots = zip(*grads)

time: 60.7 us -> 59.4 us (0.979)
  waiting for transfers between devices: 15.1 us -> 11.8 us
  starting transfers between devices: 24.9 us -> 26.9 us
    ppermute x13, waiting for transfers between devices: 7.29 us -> 2.21 us  [swap(): return lax.ppermute(x, 'dp', [(d, d ^ bits) for d in range(n)])]
    ppermute x13, starting transfers between devices: 5.89 us -> 7.86 us  [swap(): return lax.ppermute(x, 'dp', [(d, d ^ bits) for d in range(n)])]
    ppermute x12, waiting for transfers between devices: 7.79 us -> 9.6 us  [shift(): return lax.ppermute(x, 'dp', [(d, d ^ 4 * r) for d in range(n)]) if r else x]
  transfers between devices with their start and end apart: 25 -> 25, of which waited for: 10 -> 11; matrix products, arithmetic and copies ran while one was open for 0% -> 0% of each run, Pallas kernels for 23% -> 24%
where the time goes in v11:
time: 59.4 us; the launch traced here: 59.3 us
  starting transfers between devices  26.9 us (45%)
  Pallas kernels  18.9 us (32%)
  waiting for transfers between devices  11.8 us (20%)
  between operations  1.55 us (3%)
    ppermute x12, starting transfers between devices, shift(): return lax.ppermute(x, 'dp', [(d, d ^ 4 * r) for d in range(n)]) if r else x  19 us
    pallas_call x21, Pallas kernels, call(): pl.pallas_call(kernel, out_shape=outs, in_specs=ins, out_specs=jax.tree.m...  17.7 us
    ppermute x12, waiting for transfers between devices, shift(): return lax.ppermute(x, 'dp', [(d, d ^ 4 * r) for d in range(n)]) if r else x  9.6 us
    ppermute x13, starting transfers between devices, swap(): return lax.ppermute(x, 'dp', [(d, d ^ bits) for d in range(n)])  7.86 us
    ppermute x13, waiting for transfers between devices, swap(): return lax.ppermute(x, 'dp', [(d, d ^ bits) for d in range(n)])  2.21 us
    pallas_call x1, Pallas kernels, on_device(): pl.pallas_call(send_kernel, out_shape=outs, grid=(1,), in_specs=[SMEM, SM...  1.22 us
  transfers between devices with their start and end apart: 25, of which 11 were waited for; matrix products, arithmetic and copies ran while one was open for 0% of the time, Pallas kernels for 24%

profile of v11, /device:TPU:0, one launch (start us, length us, event | category | flops | bytes accessed | tf_op | source)
XLA Modules:
  0.0 59.3 jit_solution(4554810595979786278)
XLA Ops:
  1.3 1.2 %shard_map.129 = (f32[2,8192]{1,0:T(2,128)S(1)}, f32[2,32,512]{2,1,0:T(8,128)S(1)}, f32[16,512]{1,0:T(8,128)S(1)}, bf16[32,768]{1,0:T(8,128)(2,1)S(1)}, bf16[32,...) custom-call(s32[1]{0:T(128)} %bitcast.me_ref, s32[1]{0:T(128)S(6)} %copy.15.ids_ref, ...), custom_call_target="tpu_custom_call" | custom-call | tf_op jit(solution)/shard_map/pallas_call | solution.py:349
  2.6 3.1 %collective-permute-start = (bf16[32,768]{1,0:T(8,128)(2,1)S(1)}, bf16[32,768]{1,0:T(8,128)(2,1)S(1)}, u32[]{:S(2)}, u32[]{:S(2)}) collective-permute-start(bf16[32,768]{1,0:T(8,128)(2,1)S(1)} %get-tuple-element.87), channel_id=1, source_target_pairs={{0,4},{1,5},{2,6},{3,7},{4,0},{5,1},{6,2},{7,3},{8,12},{9,13},{10,... | collective-permute-start | bytes 147464 | tf_op jit(solution)/shard_map/ppermute | solution.py:317
  5.6 2.6 %collective-permute-start.1 = (bf16[32,768]{1,0:T(8,128)(2,1)S(1)}, bf16[32,768]{1,0:T(8,128)(2,1)S(1)}, u32[]{:S(2)}, u32[]{:S(2)}) collective-permute-start(bf16[32,768]{1,0:T(8,128)(2,1)S(1)} %get-tuple-element.88), channel_id=1, source_target_pairs={{0,8},{1,9},{2,10},{3,11},{4,12},{5,13},{6,14},{7,15},{8,0},{9,1},... | collective-permute-start | bytes 147464 | tf_op jit(solution)/shard_map/ppermute | solution.py:317
  8.2 3.3 %collective-permute-done.1.refs_2_ = bf16[32,768]{1,0:T(8,128)(2,1)S(1)} collective-permute-done((bf16[32,768]{1,0:T(8,128)(2,1)S(1)}, bf16[32,768]{1,0:T(8,128)(2,1)S(1)}, u32[]{:S(2)}, u32[]{:S(2)}) %collective-permute-start.1) | collective-permute-done | bytes 49184 | tf_op jit(solution)/shard_map/ppermute | solution.py:317
  11.6 2.6 %collective-permute-done.2.refs_3_ = bf16[32,768]{1,0:T(8,128)(2,1)S(1)} collective-permute-done((bf16[32,768]{1,0:T(8,128)(2,1)S(1)}, bf16[32,768]{1,0:T(8,128)(2,1)S(1)}, u32[]{:S(2)}, u32[]{:S(2)}) %collective-permute-start.2) | collective-permute-done | bytes 49184 | tf_op jit(solution)/shard_map/ppermute | solution.py:317
  14.2 1.6 %collective-permute-start.4 = (bf16[4,16,128]{2,1,0:T(8,128)(2,1)S(1)}, bf16[4,16,128]{2,1,0:T(8,128)(2,1)S(1)}, u32[]{:S(2)}, u32[]{:S(2)}) collective-permute-start(bf16[4,16,128]{2,1,0:T(8,128)(2,1)S(1)} %get-tuple-element.92), channel_id=1, source_target_pairs={{0,2},{1,3},{2,0},{3,1},{4,6},{5,7},{6,4},{7,5},{8,10},{9,11},{10,... | collective-permute-start | bytes 49160 | tf_op jit(solution)/shard_map/ppermute | solution.py:320
  16.8 1.5 %collective-permute-start.9 = (bf16[4,32,512]{2,1,0:T(8,128)(2,1)S(1)}, bf16[4,32,512]{2,1,0:T(8,128)(2,1)S(1)}, u32[]{:S(2)}, u32[]{:S(2)}) collective-permute-start(bf16[4,32,512]{2,1,0:T(8,128)(2,1)S(1)} %get-tuple-element.111.cot_ref), channel_id=1, source_target_pairs={{0,2},{1,3},{2,0},{3,1},{4,6},{5,7},{6,4},{7,5},{8,10},{9,11},{10,... | collective-permute-start | bytes 393224 | tf_op jit(solution)/shard_map/ppermute | solution.py:320
  19.9 3.6 %collective-permute-start.6 = (bf16[32,512]{1,0:T(8,128)(2,1)S(1)}, bf16[32,512]{1,0:T(8,128)(2,1)S(1)}, u32[]{:S(2)}, u32[]{:S(2)}) collective-permute-start(bf16[32,512]{1,0:T(8,128)(2,1)S(1)} %shard_map.131.share_ref), channel_id=1, source_target_pairs={{0,4},{1,5},{2,6},{3,7},{4,0},{5,1},{6,2},{7,3},{8,12},{9,13},{10,... | collective-permute-start | bytes 98312 | tf_op jit(solution)/shard_map/ppermute | solution.py:317
  23.6 1.2 %shard_map.132 = (f32[896,32]{1,0:T(8,128)S(1)}, f32[32,512]{1,0:T(8,128)S(1)}) custom-call(s32[1]{0:T(128)} %bitcast.me_ref, bf16[4,32,512]{2,1,0:T(8,128)(2,1)S(1)} %get-tuple-element.111.cot_ref, bf16[896,8192]{1,0:T(8,128)(2,1)S(1)} %bitcast.13), custom_call_target="tpu_custom_call" | custom-call | flops 1840000000 | tf_op jit(solution)/shard_map/pallas_call | solution.py:327
  27.6 1.2 %shard_map.134 = (f32[896,32]{1,0:T(8,128)S(1)}, f32[32,512]{1,0:T(8,128)S(1)}) custom-call(s32[1]{0:T(128)} %bitcast.me_ref, bf16[4,32,512]{2,1,0:T(8,128)(2,1)S(1)} %collective-permute-done.9.cot_ref, bf16[896,8192]{1,0:T(8,128)(2,1)S(1)} %bitcast.13), custom_call_target="tpu_custom_call" | custom-call | flops 1840000000 | tf_op jit(solution)/shard_map/pallas_call | solution.py:327
  28.8 1.2 %shard_map.135 = (f32[896,32]{1,0:T(8,128)S(1)}, f32[32,512]{1,0:T(8,128)S(1)}) custom-call(s32[1]{0:T(128)} %bitcast.me_ref, bf16[4,32,512]{2,1,0:T(8,128)(2,1)S(1)} %collective-permute-done.11.cot_ref, bf16[896,8192]{1,0:T(8,128)(2,1)S(1)} %bitcast.13), custom_call_target="tpu_custom_call" | custom-call | flops 1840000000 | tf_op jit(solution)/shard_map/pallas_call | solution.py:327
  30.6 1.2 %shard_map.139 = (f32[896,32]{1,0:T(8,128)S(1)}, f32[32,512]{1,0:T(8,128)S(1)}) custom-call(s32[1]{0:T(128)} %bitcast.me_ref, bf16[4,32,512]{2,1,0:T(8,128)(2,1)S(1)} %collective-permute-done.14.cot_ref, bf16[896,8192]{1,0:T(8,128)(2,1)S(1)} %bitcast.13), custom_call_target="tpu_custom_call" | custom-call | flops 1840000000 | tf_op jit(solution)/shard_map/pallas_call | solution.py:327
  34.0 1.7 %shard_map.141 = bf16[8,32,512]{2,1,0:T(8,128)(2,1)S(1)} custom-call(s32[1]{0:T(128)} %bitcast.me_ref, bf16[32,896]{1,0:T(8,128)(2,1)S(1)} %get-tuple-element.130.active_ref, bf16[896,8192]{1,0:T(8,128)(2,1)S(1)} %bitcast.13), custom_call_target="tpu_custom_call" | custom-call | flops 1724999936 | tf_op jit(solution)/shard_map/pallas_call | solution.py:327
  36.2 1.5 %shard_map.142.kept_ref = bf16[8,32,512]{2,1,0:T(8,128)(2,1)S(1)} custom-call(s32[1]{0:T(128)} %bitcast.me_ref, bf16[32,896]{1,0:T(8,128)(2,1)S(1)} %get-tuple-element.130.active_ref, bf16[896,8192]{1,0:T(8,128)(2,1)S(1)} %bitcast.13), custom_call_target="tpu_custom_call" | custom-call | flops 1724999936 | tf_op jit(solution)/shard_map/pallas_call | solution.py:327
  37.8 1.0 %collective-permute-start.16 = (bf16[4,32,512]{2,1,0:T(8,128)(2,1)S(1)}, bf16[4,32,512]{2,1,0:T(8,128)(2,1)S(1)}, u32[]{:S(2)}, u32[]{:S(2)}) collective-permute-start(bf16[4,32,512]{2,1,0:T(8,128)(2,1)S(1)} %get-tuple-element.133), channel_id=1, source_target_pairs={{0,2},{1,3},{2,0},{3,1},{4,6},{5,7},{6,4},{7,5},{8,10},{9,11},{10,... | collective-permute-start | bytes 393224 | tf_op jit(solution)/shard_map/ppermute | solution.py:320
  38.8 4.2 %shard_map.144.rows_ref = f32[4,512,128]{2,1,0:T(8,128)S(1)} custom-call(s32[1]{0:T(128)} %bitcast.me_ref, bf16[32,896]{1,0:T(8,128)(2,1)S(1)} %get-tuple-element.132.gh_ref, bf16[8192,896]{1,0:T(8,128)(2,1)S(1)} %bitcast.15), custom_call_target="tpu_custom_call" | custom-call | flops 5175000064 | tf_op jit(solution)/shard_map/pallas_call | solution.py:327
  45.0 1.4 %collective-permute-start.18 = (bf16[4,32,512]{2,1,0:T(8,128)(2,1)S(1)}, bf16[4,32,512]{2,1,0:T(8,128)(2,1)S(1)}, u32[]{:S(2)}, u32[]{:S(2)}) collective-permute-start(bf16[4,32,512]{2,1,0:T(8,128)(2,1)S(1)} %get-tuple-element.155), channel_id=1, source_target_pairs={{0,2},{1,3},{2,0},{3,1},{4,6},{5,7},{6,4},{7,5},{8,10},{9,11},{10,... | collective-permute-start | bytes 393224 | tf_op jit(solution)/shard_map/ppermute | solution.py:320
  46.5 2.4 %collective-permute-start.22 = (bf16[32,512]{1,0:T(8,128)(2,1)S(1)}, bf16[32,512]{1,0:T(8,128)(2,1)S(1)}, u32[]{:S(2)}, u32[]{:S(2)}) collective-permute-start(bf16[32,512]{1,0:T(8,128)(2,1)S(1)} %get-tuple-element.162), channel_id=1, source_target_pairs={{0,12},{1,13},{2,14},{3,15},{4,8},{5,9},{6,10},{7,11},{8,4},{9,5},... | collective-permute-start | bytes 98312 | tf_op jit(solution)/shard_map/ppermute | solution.py:317
  48.9 1.1 %collective-permute-start.23 = (bf16[32,512]{1,0:T(8,128)(2,1)S(1)}, bf16[32,512]{1,0:T(8,128)(2,1)S(1)}, u32[]{:S(2)}, u32[]{:S(2)}) collective-permute-start(bf16[32,512]{1,0:T(8,128)(2,1)S(1)} %get-tuple-element.163), channel_id=1, source_target_pairs={{0,8},{1,9},{2,10},{3,11},{4,12},{5,13},{6,14},{7,15},{8,0},{9,1},... | collective-permute-start | bytes 98312 | tf_op jit(solution)/shard_map/ppermute | solution.py:317
  50.0 1.0 %collective-permute-start.24 = (bf16[32,512]{1,0:T(8,128)(2,1)S(1)}, bf16[32,512]{1,0:T(8,128)(2,1)S(1)}, u32[]{:S(2)}, u32[]{:S(2)}) collective-permute-start(bf16[32,512]{1,0:T(8,128)(2,1)S(1)} %get-tuple-element.164), channel_id=1, source_target_pairs={{0,4},{1,5},{2,6},{3,7},{4,0},{5,1},{6,2},{7,3},{8,12},{9,13},{10,... | collective-permute-start | bytes 98312 | tf_op jit(solution)/shard_map/ppermute | solution.py:317
  51.0 2.4 %collective-permute-start.19 = (bf16[32,512]{1,0:T(8,128)(2,1)S(1)}, bf16[32,512]{1,0:T(8,128)(2,1)S(1)}, u32[]{:S(2)}, u32[]{:S(2)}) collective-permute-start(bf16[32,512]{1,0:T(8,128)(2,1)S(1)} %get-tuple-element.156), channel_id=1, source_target_pairs={{0,12},{1,13},{2,14},{3,15},{4,8},{5,9},{6,10},{7,11},{8,4},{9,5},... | collective-permute-start | bytes 98312 | tf_op jit(solution)/shard_map/ppermute | solution.py:317
  54.2 1.3 %collective-permute-start.21 = (bf16[32,512]{1,0:T(8,128)(2,1)S(1)}, bf16[32,512]{1,0:T(8,128)(2,1)S(1)}, u32[]{:S(2)}, u32[]{:S(2)}) collective-permute-start(bf16[32,512]{1,0:T(8,128)(2,1)S(1)} %get-tuple-element.158), channel_id=1, source_target_pairs={{0,4},{1,5},{2,6},{3,7},{4,0},{5,1},{6,2},{7,3},{8,12},{9,13},{10,... | collective-permute-start | bytes 98312 | tf_op jit(solution)/shard_map/ppermute | solution.py:317
  55.5 1.3 %collective-permute-done.19.refs_8_ = bf16[32,512]{1,0:T(8,128)(2,1)S(1)} collective-permute-done((bf16[32,512]{1,0:T(8,128)(2,1)S(1)}, bf16[32,512]{1,0:T(8,128)(2,1)S(1)}, u32[]{:S(2)}, u32[]{:S(2)}) %collective-permute-start.19) | collective-permute-done | bytes 32800 | tf_op jit(solution)/shard_map/ppermute | solution.py:317
  56.8 1.5 %collective-permute-done.20.refs_9_ = bf16[32,512]{1,0:T(8,128)(2,1)S(1)} collective-permute-done((bf16[32,512]{1,0:T(8,128)(2,1)S(1)}, bf16[32,512]{1,0:T(8,128)(2,1)S(1)}, u32[]{:S(2)}, u32[]{:S(2)}) %collective-permute-start.20) | collective-permute-done | bytes 32800 | tf_op jit(solution)/shard_map/ppermute | solution.py:317
  (71 shorter events, 12.7 us)
Async XLA Ops:
  2.6 5.7 %collective-permute-start = (bf16[32,768]{1,0:T(8,128)(2,1)S(1)}, bf16[32,768]{1,0:T(8,128)(2,1)S(1)}, u32[]{:S(2)}, u32[]{:S(2)}) collective-permute-start(bf16[32,768]{1,0:T(8,128)(2,1)S(1)} %get-tuple-element.87), channel_id=1, source_target_pairs={{0,4},{1,5},{2,6},{3,7},{4,0},{5,1},{6,2},{7,3},{8,12},{9,13},{10,... | collective-permute-start | bytes 147464 | tf_op jit(solution)/shard_map/ppermute | solution.py:317
  5.6 5.9 %collective-permute-start.1 = (bf16[32,768]{1,0:T(8,128)(2,1)S(1)}, bf16[32,768]{1,0:T(8,128)(2,1)S(1)}, u32[]{:S(2)}, u32[]{:S(2)}) collective-permute-start(bf16[32,768]{1,0:T(8,128)(2,1)S(1)} %get-tuple-element.88), channel_id=1, source_target_pairs={{0,8},{1,9},{2,10},{3,11},{4,12},{5,13},{6,14},{7,15},{8,0},{9,1},... | collective-permute-start | bytes 147464 | tf_op jit(solution)/shard_map/ppermute | solution.py:317
  8.2 5.9 %collective-permute-start.2 = (bf16[32,768]{1,0:T(8,128)(2,1)S(1)}, bf16[32,768]{1,0:T(8,128)(2,1)S(1)}, u32[]{:S(2)}, u32[]{:S(2)}) collective-permute-start(bf16[32,768]{1,0:T(8,128)(2,1)S(1)} %get-tuple-element.89), channel_id=1, source_target_pairs={{0,12},{1,13},{2,14},{3,15},{4,8},{5,9},{6,10},{7,11},{8,4},{9,5},... | collective-permute-start | bytes 147464 | tf_op jit(solution)/shard_map/ppermute | solution.py:317
  14.2 4.2 %collective-permute-start.3 = (bf16[4,16,128]{2,1,0:T(8,128)(2,1)S(1)}, bf16[4,16,128]{2,1,0:T(8,128)(2,1)S(1)}, u32[]{:S(2)}, u32[]{:S(2)}) collective-permute-start(bf16[4,16,128]{2,1,0:T(8,128)(2,1)S(1)} %get-tuple-element.91), channel_id=1, source_target_pairs={{0,1},{1,0},{2,3},{3,2},{4,5},{5,4},{6,7},{7,6},{8,9},{9,8},{10,11... | collective-permute-start | bytes 49160 | tf_op jit(solution)/shard_map/ppermute | solution.py:320
  14.2 4.1 %collective-permute-start.4 = (bf16[4,16,128]{2,1,0:T(8,128)(2,1)S(1)}, bf16[4,16,128]{2,1,0:T(8,128)(2,1)S(1)}, u32[]{:S(2)}, u32[]{:S(2)}) collective-permute-start(bf16[4,16,128]{2,1,0:T(8,128)(2,1)S(1)} %get-tuple-element.92), channel_id=1, source_target_pairs={{0,2},{1,3},{2,0},{3,1},{4,6},{5,7},{6,4},{7,5},{8,10},{9,11},{10,... | collective-permute-start | bytes 49160 | tf_op jit(solution)/shard_map/ppermute | solution.py:320
  15.8 3.2 %collective-permute-start.5 = (bf16[4,16,128]{2,1,0:T(8,128)(2,1)S(1)}, bf16[4,16,128]{2,1,0:T(8,128)(2,1)S(1)}, u32[]{:S(2)}, u32[]{:S(2)}) collective-permute-start(bf16[4,16,128]{2,1,0:T(8,128)(2,1)S(1)} %get-tuple-element.93), channel_id=1, source_target_pairs={{0,3},{1,2},{2,1},{3,0},{4,7},{5,6},{6,5},{7,4},{8,11},{9,10},{10,... | collective-permute-start | bytes 49160 | tf_op jit(solution)/shard_map/ppermute | solution.py:320
  16.8 6.8 %collective-permute-start.9 = (bf16[4,32,512]{2,1,0:T(8,128)(2,1)S(1)}, bf16[4,32,512]{2,1,0:T(8,128)(2,1)S(1)}, u32[]{:S(2)}, u32[]{:S(2)}) collective-permute-start(bf16[4,32,512]{2,1,0:T(8,128)(2,1)S(1)} %get-tuple-element.111.cot_ref), channel_id=1, source_target_pairs={{0,2},{1,3},{2,0},{3,1},{4,6},{5,7},{6,4},{7,5},{8,10},{9,11},{10,... | collective-permute-start | bytes 393224 | tf_op jit(solution)/shard_map/ppermute | solution.py:320
  19.1 6.1 %collective-permute-start.8 = (bf16[32,512]{1,0:T(8,128)(2,1)S(1)}, bf16[32,512]{1,0:T(8,128)(2,1)S(1)}, u32[]{:S(2)}, u32[]{:S(2)}) collective-permute-start(bf16[32,512]{1,0:T(8,128)(2,1)S(1)} %shard_map.131.share_ref), channel_id=1, source_target_pairs={{0,12},{1,13},{2,14},{3,15},{4,8},{5,9},{6,10},{7,11},{8,4},{9,5},... | collective-permute-start | bytes 98312 | tf_op jit(solution)/shard_map/ppermute | solution.py:317
  19.9 5.3 %collective-permute-start.7 = (bf16[32,512]{1,0:T(8,128)(2,1)S(1)}, bf16[32,512]{1,0:T(8,128)(2,1)S(1)}, u32[]{:S(2)}, u32[]{:S(2)}) collective-permute-start(bf16[32,512]{1,0:T(8,128)(2,1)S(1)} %shard_map.131.share_ref), channel_id=1, source_target_pairs={{0,8},{1,9},{2,10},{3,11},{4,12},{5,13},{6,14},{7,15},{8,0},{9,1},... | collective-permute-start | bytes 98312 | tf_op jit(solution)/shard_map/ppermute | solution.py:317
  19.9 5.6 %collective-permute-start.6 = (bf16[32,512]{1,0:T(8,128)(2,1)S(1)}, bf16[32,512]{1,0:T(8,128)(2,1)S(1)}, u32[]{:S(2)}, u32[]{:S(2)}) collective-permute-start(bf16[32,512]{1,0:T(8,128)(2,1)S(1)} %shard_map.131.share_ref), channel_id=1, source_target_pairs={{0,4},{1,5},{2,6},{3,7},{4,0},{5,1},{6,2},{7,3},{8,12},{9,13},{10,... | collective-permute-start | bytes 98312 | tf_op jit(solution)/shard_map/ppermute | solution.py:317
  25.5 5.0 %collective-permute-start.10 = (bf16[4,32,512]{2,1,0:T(8,128)(2,1)S(1)}, bf16[4,32,512]{2,1,0:T(8,128)(2,1)S(1)}, u32[]{:S(2)}, u32[]{:S(2)}) collective-permute-start(bf16[4,32,512]{2,1,0:T(8,128)(2,1)S(1)} %pad_maximum_fusion.rest_ref), channel_id=1, source_target_pairs={{0,2},{1,3},{2,0},{3,1},{4,6},{5,7},{6,4},{7,5},{8,10},{9,11},{10,... | collective-permute-start | bytes 393224 | tf_op jit(solution)/shard_map/ppermute | solution.py:320
  27.0 1.9 %collective-permute-start.11 = (bf16[4,32,512]{2,1,0:T(8,128)(2,1)S(1)}, bf16[4,32,512]{2,1,0:T(8,128)(2,1)S(1)}, u32[]{:S(2)}, u32[]{:S(2)}) collective-permute-start(bf16[4,32,512]{2,1,0:T(8,128)(2,1)S(1)} %get-tuple-element.111.cot_ref), channel_id=1, source_target_pairs={{0,1},{1,0},{2,3},{3,2},{4,5},{5,4},{6,7},{7,6},{8,9},{9,8},{10,11... | collective-permute-start | bytes 393224 | tf_op jit(solution)/shard_map/ppermute | solution.py:320
  27.0 5.5 %collective-permute-start.13 = (bf16[4,32,512]{2,1,0:T(8,128)(2,1)S(1)}, bf16[4,32,512]{2,1,0:T(8,128)(2,1)S(1)}, u32[]{:S(2)}, u32[]{:S(2)}) collective-permute-start(bf16[4,32,512]{2,1,0:T(8,128)(2,1)S(1)} %pad_maximum_fusion.rest_ref), channel_id=1, source_target_pairs={{0,1},{1,0},{2,3},{3,2},{4,5},{5,4},{6,7},{7,6},{8,9},{9,8},{10,11... | collective-permute-start | bytes 393224 | tf_op jit(solution)/shard_map/ppermute | solution.py:320
  27.5 3.0 %collective-permute-start.14 = (bf16[4,32,512]{2,1,0:T(8,128)(2,1)S(1)}, bf16[4,32,512]{2,1,0:T(8,128)(2,1)S(1)}, u32[]{:S(2)}, u32[]{:S(2)}) collective-permute-start(bf16[4,32,512]{2,1,0:T(8,128)(2,1)S(1)} %collective-permute-done.9.cot_ref), channel_id=1, source_target_pairs={{0,1},{1,0},{2,3},{3,2},{4,5},{5,4},{6,7},{7,6},{8,9},{9,8},{10,11... | collective-permute-start | bytes 393224 | tf_op jit(solution)/shard_map/ppermute | solution.py:320
  30.6 2.7 %collective-permute-start.12 = (bf16[4,32,512]{2,1,0:T(8,128)(2,1)S(1)}, bf16[4,32,512]{2,1,0:T(8,128)(2,1)S(1)}, u32[]{:S(2)}, u32[]{:S(2)}) collective-permute-start(bf16[4,32,512]{2,1,0:T(8,128)(2,1)S(1)} %collective-permute-done.10.rest_ref), channel_id=1, source_target_pairs={{0,1},{1,0},{2,3},{3,2},{4,5},{5,4},{6,7},{7,6},{8,9},{9,8},{10,11... | collective-permute-start | bytes 393224 | tf_op jit(solution)/shard_map/ppermute | solution.py:320
  35.7 2.0 %collective-permute-start.15 = (bf16[8,32,512]{2,1,0:T(8,128)(2,1)S(1)}, bf16[8,32,512]{2,1,0:T(8,128)(2,1)S(1)}, u32[]{:S(2)}, u32[]{:S(2)}) collective-permute-start(bf16[8,32,512]{2,1,0:T(8,128)(2,1)S(1)} %shard_map.141), channel_id=1, source_target_pairs={{0,1},{1,0},{2,3},{3,2},{4,5},{5,4},{6,7},{7,6},{8,9},{9,8},{10,11... | collective-permute-start | bytes 786440 | tf_op jit(solution)/shard_map/ppermute | solution.py:320
  37.8 5.5 %collective-permute-start.16 = (bf16[4,32,512]{2,1,0:T(8,128)(2,1)S(1)}, bf16[4,32,512]{2,1,0:T(8,128)(2,1)S(1)}, u32[]{:S(2)}, u32[]{:S(2)}) collective-permute-start(bf16[4,32,512]{2,1,0:T(8,128)(2,1)S(1)} %get-tuple-element.133), channel_id=1, source_target_pairs={{0,2},{1,3},{2,0},{3,1},{4,6},{5,7},{6,4},{7,5},{8,10},{9,11},{10,... | collective-permute-start | bytes 393224 | tf_op jit(solution)/shard_map/ppermute | solution.py:320
  45.0 5.9 %collective-permute-start.18 = (bf16[4,32,512]{2,1,0:T(8,128)(2,1)S(1)}, bf16[4,32,512]{2,1,0:T(8,128)(2,1)S(1)}, u32[]{:S(2)}, u32[]{:S(2)}) collective-permute-start(bf16[4,32,512]{2,1,0:T(8,128)(2,1)S(1)} %get-tuple-element.155), channel_id=1, source_target_pairs={{0,2},{1,3},{2,0},{3,1},{4,6},{5,7},{6,4},{7,5},{8,10},{9,11},{10,... | collective-permute-start | bytes 393224 | tf_op jit(solution)/shard_map/ppermute | solution.py:320
  46.5 7.7 %collective-permute-start.22 = (bf16[32,512]{1,0:T(8,128)(2,1)S(1)}, bf16[32,512]{1,0:T(8,128)(2,1)S(1)}, u32[]{:S(2)}, u32[]{:S(2)}) collective-permute-start(bf16[32,512]{1,0:T(8,128)(2,1)S(1)} %get-tuple-element.162), channel_id=1, source_target_pairs={{0,12},{1,13},{2,14},{3,15},{4,8},{5,9},{6,10},{7,11},{8,4},{9,5},... | collective-permute-start | bytes 98312 | tf_op jit(solution)/shard_map/ppermute | solution.py:317
  48.9 6.6 %collective-permute-start.23 = (bf16[32,512]{1,0:T(8,128)(2,1)S(1)}, bf16[32,512]{1,0:T(8,128)(2,1)S(1)}, u32[]{:S(2)}, u32[]{:S(2)}) collective-permute-start(bf16[32,512]{1,0:T(8,128)(2,1)S(1)} %get-tuple-element.163), channel_id=1, source_target_pairs={{0,8},{1,9},{2,10},{3,11},{4,12},{5,13},{6,14},{7,15},{8,0},{9,1},... | collective-permute-start | bytes 98312 | tf_op jit(solution)/shard_map/ppermute | solution.py:317
  50.0 5.5 %collective-permute-start.24 = (bf16[32,512]{1,0:T(8,128)(2,1)S(1)}, bf16[32,512]{1,0:T(8,128)(2,1)S(1)}, u32[]{:S(2)}, u32[]{:S(2)}) collective-permute-start(bf16[32,512]{1,0:T(8,128)(2,1)S(1)} %get-tuple-element.164), channel_id=1, source_target_pairs={{0,4},{1,5},{2,6},{3,7},{4,0},{5,1},{6,2},{7,3},{8,12},{9,13},{10,... | collective-permute-start | bytes 98312 | tf_op jit(solution)/shard_map/ppermute | solution.py:317
  51.0 5.8 %collective-permute-start.19 = (bf16[32,512]{1,0:T(8,128)(2,1)S(1)}, bf16[32,512]{1,0:T(8,128)(2,1)S(1)}, u32[]{:S(2)}, u32[]{:S(2)}) collective-permute-start(bf16[32,512]{1,0:T(8,128)(2,1)S(1)} %get-tuple-element.156), channel_id=1, source_target_pairs={{0,12},{1,13},{2,14},{3,15},{4,8},{5,9},{6,10},{7,11},{8,4},{9,5},... | collective-permute-start | bytes 98312 | tf_op jit(solution)/shard_map/ppermute | solution.py:317
  53.3 4.9 %collective-permute-start.20 = (bf16[32,512]{1,0:T(8,128)(2,1)S(1)}, bf16[32,512]{1,0:T(8,128)(2,1)S(1)}, u32[]{:S(2)}, u32[]{:S(2)}) collective-permute-start(bf16[32,512]{1,0:T(8,128)(2,1)S(1)} %get-tuple-element.157), channel_id=1, source_target_pairs={{0,8},{1,9},{2,10},{3,11},{4,12},{5,13},{6,14},{7,15},{8,0},{9,1},... | collective-permute-start | bytes 98312 | tf_op jit(solution)/shard_map/ppermute | solution.py:317
  54.2 4.3 %collective-permute-start.21 = (bf16[32,512]{1,0:T(8,128)(2,1)S(1)}, bf16[32,512]{1,0:T(8,128)(2,1)S(1)}, u32[]{:S(2)}, u32[]{:S(2)}) collective-permute-start(bf16[32,512]{1,0:T(8,128)(2,1)S(1)} %get-tuple-element.158), channel_id=1, source_target_pairs={{0,4},{1,5},{2,6},{3,7},{4,0},{5,1},{6,2},{7,3},{8,12},{9,13},{10,... | collective-permute-start | bytes 98312 | tf_op jit(solution)/shard_map/ppermute | solution.py:317
  (11 other events, 97.5 us)

commit v12 on v11

--- a/solution.py
+++ b/solution.py
@@ -166,9 +166,12 @@
         owner = owner_of(me, 4 * quarter, part, k)
         piece_ref[...] = cot_ref[k].astype(f32)
         own_rows(piece_ref, own_ref, me, owner)
+    total = 0.0
+    for k in range(quarter):
+        owner = owner_of(me, 4 * quarter, part, k)
         columns = pl.ds(pl.multiple_of(owner * width, width), width)
-        terms = dot_by_halves(weight_ref[:, columns], cot_ref[k])
-        acc_ref[...] = terms if k == 0 else acc_ref[...] + terms
+        total = total + dot_by_halves(weight_ref[:, columns], cot_ref[k])
+    acc_ref[...] = total
 
 
 def up_kernel(
@@ -177,6 +180,7 @@
     quarter, _, width = rest_ref.shape
     me = me_ref[0]
     own_ref[...] = jnp.zeros_like(own_ref)
+    products = 0.0
     for k in range(quarter):
         owner = owner_of(me, 4 * quarter, part, k)
         piece = rest_ref[k].astype(f32)
@@ -187,8 +191,8 @@
         square_ref[...] = total if k == 0 else square_ref[...] + total
         scaled = (piece * gain_ref[pl.ds(owner, 1), :]).astype(bf16)
         rows = pl.ds(pl.multiple_of(owner * width, width), width)
-        terms = jnp.dot(scaled, weight_ref[rows, :], preferred_element_type=f32)
-        acc_ref[...] = terms if k == 0 else acc_ref[...] + terms
+        products = products + jnp.dot(scaled, weight_ref[rows, :], preferred_element_type=f32)
+    acc_ref[...] = products
 
 
 def activation_kernel(me_ref, rest_ref, gain_ref, weight_ref, *refs):
@@ -210,13 +214,15 @@
     tokens, width = gh_ref.shape[0], chunks * LANES
     n = tokens // 2
     gh = gh_ref[...]
-    for share in range(n):
-        block = weight_ref[share * width : (share + 1) * width, :]
+    step = n // 4
+    for first in range(0, n, step):
+        block = weight_ref[first * width : (first + step) * width, :]
         terms = dot_by_halves(block, gh).T
         for p in range(2):
-            for c in range(chunks):
+            for at in range(step * chunks):
+                share, c = first + at // chunks, at % chunks
                 rows_ref[c, pl.ds(p * n + share, n, stride=tokens), :] = terms[
-                    p * n : (p + 1) * n, c * LANES : (c + 1) * LANES
+                    p * n : (p + 1) * n, at * LANES : (at + 1) * LANES
                 ]
 
 
@@ -241,7 +247,7 @@
         terms = jnp.dot(active_ref[...], weight_ref[:, columns], preferred_element_type=f32)
         out_ref[k] = terms.astype(bf16)
 
-    pl.loop(0, half, unroll=4)(share)
+    pl.loop(0, half, unroll=8)(share)
 
 
 def pair_kernel(me_ref, kept_ref, arrived_ref, send_ref, keep_ref):

time: 59.4 us -> 58.8 us (0.990)
  Pallas kernels: 18.9 us -> 18.3 us
    pallas_call x21, Pallas kernels: 17.7 us -> 17.1 us  [call(): pl.pallas_call(kernel, out_shape=outs, in_specs=ins, out_specs=jax.tree.m...]
where the time goes in v12:
time: 58.8 us; the launch traced here: 58.6 us
  starting transfers between devices  26.5 us (45%)
  Pallas kernels  18.3 us (31%)
  waiting for transfers between devices  12.2 us (21%)
  between operations  1.54 us (3%)
    ppermute x12, starting transfers between devices, shift(): return lax.ppermute(x, 'dp', [(d, d ^ 4 * r) for d in range(n)]) if r else x  19 us
    pallas_call x21, Pallas kernels, call(): pl.pallas_call(kernel, out_shape=outs, in_specs=ins, out_specs=jax.tree.m...  17.1 us
    ppermute x12, waiting for transfers between devices, shift(): return lax.ppermute(x, 'dp', [(d, d ^ 4 * r) for d in range(n)]) if r else x  9.75 us
    ppermute x13, starting transfers between devices, swap(): return lax.ppermute(x, 'dp', [(d, d ^ bits) for d in range(n)])  7.45 us
    ppermute x13, waiting for transfers between devices, swap(): return lax.ppermute(x, 'dp', [(d, d ^ bits) for d in range(n)])  2.42 us
    pallas_call x1, Pallas kernels, on_device(): pl.pallas_call(send_kernel, out_shape=outs, grid=(1,), in_specs=[SMEM, SM...  1.22 us
  transfers between devices with their start and end apart: 25, of which 11 were waited for; matrix products, arithmetic and copies ran while one was open for 0% of the time, Pallas kernels for 24%

profile of v12, /device:TPU:0, one launch (start us, length us, event | category | flops | bytes accessed | tf_op | source)
XLA Modules:
  0.0 58.6 jit_solution(12548317198938271456)
XLA Ops:
  1.3 1.2 %shard_map.129 = (f32[2,8192]{1,0:T(2,128)S(1)}, f32[2,32,512]{2,1,0:T(8,128)S(1)}, f32[16,512]{1,0:T(8,128)S(1)}, bf16[32,768]{1,0:T(8,128)(2,1)S(1)}, bf16[32,...) custom-call(s32[1]{0:T(128)} %bitcast.me_ref, s32[1]{0:T(128)S(6)} %copy.15.ids_ref, ...), custom_call_target="tpu_custom_call" | custom-call | tf_op jit(solution)/shard_map/pallas_call | solution.py:355
  2.6 3.1 %collective-permute-start = (bf16[32,768]{1,0:T(8,128)(2,1)S(1)}, bf16[32,768]{1,0:T(8,128)(2,1)S(1)}, u32[]{:S(2)}, u32[]{:S(2)}) collective-permute-start(bf16[32,768]{1,0:T(8,128)(2,1)S(1)} %get-tuple-element.87), channel_id=1, source_target_pairs={{0,4},{1,5},{2,6},{3,7},{4,0},{5,1},{6,2},{7,3},{8,12},{9,13},{10,... | collective-permute-start | bytes 147464 | tf_op jit(solution)/shard_map/ppermute | solution.py:323
  5.6 2.6 %collective-permute-start.1 = (bf16[32,768]{1,0:T(8,128)(2,1)S(1)}, bf16[32,768]{1,0:T(8,128)(2,1)S(1)}, u32[]{:S(2)}, u32[]{:S(2)}) collective-permute-start(bf16[32,768]{1,0:T(8,128)(2,1)S(1)} %get-tuple-element.88), channel_id=1, source_target_pairs={{0,8},{1,9},{2,10},{3,11},{4,12},{5,13},{6,14},{7,15},{8,0},{9,1},... | collective-permute-start | bytes 147464 | tf_op jit(solution)/shard_map/ppermute | solution.py:323
  8.2 3.3 %collective-permute-done.1.refs_2_ = bf16[32,768]{1,0:T(8,128)(2,1)S(1)} collective-permute-done((bf16[32,768]{1,0:T(8,128)(2,1)S(1)}, bf16[32,768]{1,0:T(8,128)(2,1)S(1)}, u32[]{:S(2)}, u32[]{:S(2)}) %collective-permute-start.1) | collective-permute-done | bytes 49184 | tf_op jit(solution)/shard_map/ppermute | solution.py:323
  11.6 2.6 %collective-permute-done.2.refs_3_ = bf16[32,768]{1,0:T(8,128)(2,1)S(1)} collective-permute-done((bf16[32,768]{1,0:T(8,128)(2,1)S(1)}, bf16[32,768]{1,0:T(8,128)(2,1)S(1)}, u32[]{:S(2)}, u32[]{:S(2)}) %collective-permute-start.2) | collective-permute-done | bytes 49184 | tf_op jit(solution)/shard_map/ppermute | solution.py:323
  14.2 1.6 %collective-permute-start.4 = (bf16[4,16,128]{2,1,0:T(8,128)(2,1)S(1)}, bf16[4,16,128]{2,1,0:T(8,128)(2,1)S(1)}, u32[]{:S(2)}, u32[]{:S(2)}) collective-permute-start(bf16[4,16,128]{2,1,0:T(8,128)(2,1)S(1)} %get-tuple-element.92), channel_id=1, source_target_pairs={{0,2},{1,3},{2,0},{3,1},{4,6},{5,7},{6,4},{7,5},{8,10},{9,11},{10,... | collective-permute-start | bytes 49160 | tf_op jit(solution)/shard_map/ppermute | solution.py:326
  16.8 1.5 %collective-permute-start.9 = (bf16[4,32,512]{2,1,0:T(8,128)(2,1)S(1)}, bf16[4,32,512]{2,1,0:T(8,128)(2,1)S(1)}, u32[]{:S(2)}, u32[]{:S(2)}) collective-permute-start(bf16[4,32,512]{2,1,0:T(8,128)(2,1)S(1)} %get-tuple-element.111.cot_ref), channel_id=1, source_target_pairs={{0,2},{1,3},{2,0},{3,1},{4,6},{5,7},{6,4},{7,5},{8,10},{9,11},{10,... | collective-permute-start | bytes 393224 | tf_op jit(solution)/shard_map/ppermute | solution.py:326
  19.9 3.6 %collective-permute-start.6 = (bf16[32,512]{1,0:T(8,128)(2,1)S(1)}, bf16[32,512]{1,0:T(8,128)(2,1)S(1)}, u32[]{:S(2)}, u32[]{:S(2)}) collective-permute-start(bf16[32,512]{1,0:T(8,128)(2,1)S(1)} %shard_map.131.share_ref), channel_id=1, source_target_pairs={{0,4},{1,5},{2,6},{3,7},{4,0},{5,1},{6,2},{7,3},{8,12},{9,13},{10,... | collective-permute-start | bytes 98312 | tf_op jit(solution)/shard_map/ppermute | solution.py:323
  23.6 1.1 %shard_map.132 = (f32[896,32]{1,0:T(8,128)S(1)}, f32[32,512]{1,0:T(8,128)S(1)}) custom-call(s32[1]{0:T(128)} %bitcast.me_ref, bf16[4,32,512]{2,1,0:T(8,128)(2,1)S(1)} %get-tuple-element.111.cot_ref, bf16[896,8192]{1,0:T(8,128)(2,1)S(1)} %bitcast.13), custom_call_target="tpu_custom_call" | custom-call | flops 1840000000 | tf_op jit(solution)/shard_map/pallas_call | solution.py:333
  27.6 1.1 %shard_map.134 = (f32[896,32]{1,0:T(8,128)S(1)}, f32[32,512]{1,0:T(8,128)S(1)}) custom-call(s32[1]{0:T(128)} %bitcast.me_ref, bf16[4,32,512]{2,1,0:T(8,128)(2,1)S(1)} %collective-permute-done.9.cot_ref, bf16[896,8192]{1,0:T(8,128)(2,1)S(1)} %bitcast.13), custom_call_target="tpu_custom_call" | custom-call | flops 1840000000 | tf_op jit(solution)/shard_map/pallas_call | solution.py:333
  28.7 1.1 %shard_map.135 = (f32[896,32]{1,0:T(8,128)S(1)}, f32[32,512]{1,0:T(8,128)S(1)}) custom-call(s32[1]{0:T(128)} %bitcast.me_ref, bf16[4,32,512]{2,1,0:T(8,128)(2,1)S(1)} %collective-permute-done.11.cot_ref, bf16[896,8192]{1,0:T(8,128)(2,1)S(1)} %bitcast.13), custom_call_target="tpu_custom_call" | custom-call | flops 1840000000 | tf_op jit(solution)/shard_map/pallas_call | solution.py:333
  30.6 1.1 %shard_map.139 = (f32[896,32]{1,0:T(8,128)S(1)}, f32[32,512]{1,0:T(8,128)S(1)}) custom-call(s32[1]{0:T(128)} %bitcast.me_ref, bf16[4,32,512]{2,1,0:T(8,128)(2,1)S(1)} %collective-permute-done.14.cot_ref, bf16[896,8192]{1,0:T(8,128)(2,1)S(1)} %bitcast.13), custom_call_target="tpu_custom_call" | custom-call | flops 1840000000 | tf_op jit(solution)/shard_map/pallas_call | solution.py:333
  33.9 1.4 %shard_map.141 = bf16[8,32,512]{2,1,0:T(8,128)(2,1)S(1)} custom-call(s32[1]{0:T(128)} %bitcast.me_ref, bf16[32,896]{1,0:T(8,128)(2,1)S(1)} %get-tuple-element.130.active_ref, bf16[896,8192]{1,0:T(8,128)(2,1)S(1)} %bitcast.13), custom_call_target="tpu_custom_call" | custom-call | flops 1724999936 | tf_op jit(solution)/shard_map/pallas_call | solution.py:333
  35.8 1.4 %shard_map.142.kept_ref = bf16[8,32,512]{2,1,0:T(8,128)(2,1)S(1)} custom-call(s32[1]{0:T(128)} %bitcast.me_ref, bf16[32,896]{1,0:T(8,128)(2,1)S(1)} %get-tuple-element.130.active_ref, bf16[896,8192]{1,0:T(8,128)(2,1)S(1)} %bitcast.13), custom_call_target="tpu_custom_call" | custom-call | flops 1724999936 | tf_op jit(solution)/shard_map/pallas_call | solution.py:333
  38.2 4.4 %shard_map.144.rows_ref = f32[4,512,128]{2,1,0:T(8,128)S(1)} custom-call(s32[1]{0:T(128)} %bitcast.me_ref, bf16[32,896]{1,0:T(8,128)(2,1)S(1)} %get-tuple-element.132.gh_ref, bf16[8192,896]{1,0:T(8,128)(2,1)S(1)} %bitcast.15), custom_call_target="tpu_custom_call" | custom-call | flops 5175000064 | tf_op jit(solution)/shard_map/pallas_call | solution.py:333
  44.6 1.1 %collective-permute-start.18 = (bf16[4,32,512]{2,1,0:T(8,128)(2,1)S(1)}, bf16[4,32,512]{2,1,0:T(8,128)(2,1)S(1)}, u32[]{:S(2)}, u32[]{:S(2)}) collective-permute-start(bf16[4,32,512]{2,1,0:T(8,128)(2,1)S(1)} %get-tuple-element.155), channel_id=1, source_target_pairs={{0,2},{1,3},{2,0},{3,1},{4,6},{5,7},{6,4},{7,5},{8,10},{9,11},{10,... | collective-permute-start | bytes 393224 | tf_op jit(solution)/shard_map/ppermute | solution.py:326
  45.8 2.4 %collective-permute-start.22 = (bf16[32,512]{1,0:T(8,128)(2,1)S(1)}, bf16[32,512]{1,0:T(8,128)(2,1)S(1)}, u32[]{:S(2)}, u32[]{:S(2)}) collective-permute-start(bf16[32,512]{1,0:T(8,128)(2,1)S(1)} %get-tuple-element.162), channel_id=1, source_target_pairs={{0,12},{1,13},{2,14},{3,15},{4,8},{5,9},{6,10},{7,11},{8,4},{9,5},... | collective-permute-start | bytes 98312 | tf_op jit(solution)/shard_map/ppermute | solution.py:323
  48.1 1.1 %collective-permute-start.23 = (bf16[32,512]{1,0:T(8,128)(2,1)S(1)}, bf16[32,512]{1,0:T(8,128)(2,1)S(1)}, u32[]{:S(2)}, u32[]{:S(2)}) collective-permute-start(bf16[32,512]{1,0:T(8,128)(2,1)S(1)} %get-tuple-element.163), channel_id=1, source_target_pairs={{0,8},{1,9},{2,10},{3,11},{4,12},{5,13},{6,14},{7,15},{8,0},{9,1},... | collective-permute-start | bytes 98312 | tf_op jit(solution)/shard_map/ppermute | solution.py:323
  49.3 1.0 %collective-permute-start.24 = (bf16[32,512]{1,0:T(8,128)(2,1)S(1)}, bf16[32,512]{1,0:T(8,128)(2,1)S(1)}, u32[]{:S(2)}, u32[]{:S(2)}) collective-permute-start(bf16[32,512]{1,0:T(8,128)(2,1)S(1)} %get-tuple-element.164), channel_id=1, source_target_pairs={{0,4},{1,5},{2,6},{3,7},{4,0},{5,1},{6,2},{7,3},{8,12},{9,13},{10,... | collective-permute-start | bytes 98312 | tf_op jit(solution)/shard_map/ppermute | solution.py:323
  50.3 2.4 %collective-permute-start.19 = (bf16[32,512]{1,0:T(8,128)(2,1)S(1)}, bf16[32,512]{1,0:T(8,128)(2,1)S(1)}, u32[]{:S(2)}, u32[]{:S(2)}) collective-permute-start(bf16[32,512]{1,0:T(8,128)(2,1)S(1)} %get-tuple-element.156), channel_id=1, source_target_pairs={{0,12},{1,13},{2,14},{3,15},{4,8},{5,9},{6,10},{7,11},{8,4},{9,5},... | collective-permute-start | bytes 98312 | tf_op jit(solution)/shard_map/ppermute | solution.py:323
  52.6 1.1 %collective-permute-start.20 = (bf16[32,512]{1,0:T(8,128)(2,1)S(1)}, bf16[32,512]{1,0:T(8,128)(2,1)S(1)}, u32[]{:S(2)}, u32[]{:S(2)}) collective-permute-start(bf16[32,512]{1,0:T(8,128)(2,1)S(1)} %get-tuple-element.157), channel_id=1, source_target_pairs={{0,8},{1,9},{2,10},{3,11},{4,12},{5,13},{6,14},{7,15},{8,0},{9,1},... | collective-permute-start | bytes 98312 | tf_op jit(solution)/shard_map/ppermute | solution.py:323
  53.7 1.0 %collective-permute-start.21 = (bf16[32,512]{1,0:T(8,128)(2,1)S(1)}, bf16[32,512]{1,0:T(8,128)(2,1)S(1)}, u32[]{:S(2)}, u32[]{:S(2)}) collective-permute-start(bf16[32,512]{1,0:T(8,128)(2,1)S(1)} %get-tuple-element.158), channel_id=1, source_target_pairs={{0,4},{1,5},{2,6},{3,7},{4,0},{5,1},{6,2},{7,3},{8,12},{9,13},{10,... | collective-permute-start | bytes 98312 | tf_op jit(solution)/shard_map/ppermute | solution.py:323
  54.7 1.4 %collective-permute-done.19.refs_8_ = bf16[32,512]{1,0:T(8,128)(2,1)S(1)} collective-permute-done((bf16[32,512]{1,0:T(8,128)(2,1)S(1)}, bf16[32,512]{1,0:T(8,128)(2,1)S(1)}, u32[]{:S(2)}, u32[]{:S(2)}) %collective-permute-start.19) | collective-permute-done | bytes 32800 | tf_op jit(solution)/shard_map/ppermute | solution.py:323
  56.2 1.3 %collective-permute-done.20.refs_9_ = bf16[32,512]{1,0:T(8,128)(2,1)S(1)} collective-permute-done((bf16[32,512]{1,0:T(8,128)(2,1)S(1)}, bf16[32,512]{1,0:T(8,128)(2,1)S(1)}, u32[]{:S(2)}, u32[]{:S(2)}) %collective-permute-start.20) | collective-permute-done | bytes 32800 | tf_op jit(solution)/shard_map/ppermute | solution.py:323
  (71 shorter events, 13.2 us)
Async XLA Ops:
  2.6 5.7 %collective-permute-start = (bf16[32,768]{1,0:T(8,128)(2,1)S(1)}, bf16[32,768]{1,0:T(8,128)(2,1)S(1)}, u32[]{:S(2)}, u32[]{:S(2)}) collective-permute-start(bf16[32,768]{1,0:T(8,128)(2,1)S(1)} %get-tuple-element.87), channel_id=1, source_target_pairs={{0,4},{1,5},{2,6},{3,7},{4,0},{5,1},{6,2},{7,3},{8,12},{9,13},{10,... | collective-permute-start | bytes 147464 | tf_op jit(solution)/shard_map/ppermute | solution.py:323
  5.6 5.9 %collective-permute-start.1 = (bf16[32,768]{1,0:T(8,128)(2,1)S(1)}, bf16[32,768]{1,0:T(8,128)(2,1)S(1)}, u32[]{:S(2)}, u32[]{:S(2)}) collective-permute-start(bf16[32,768]{1,0:T(8,128)(2,1)S(1)} %get-tuple-element.88), channel_id=1, source_target_pairs={{0,8},{1,9},{2,10},{3,11},{4,12},{5,13},{6,14},{7,15},{8,0},{9,1},... | collective-permute-start | bytes 147464 | tf_op jit(solution)/shard_map/ppermute | solution.py:323
  8.2 5.9 %collective-permute-start.2 = (bf16[32,768]{1,0:T(8,128)(2,1)S(1)}, bf16[32,768]{1,0:T(8,128)(2,1)S(1)}, u32[]{:S(2)}, u32[]{:S(2)}) collective-permute-start(bf16[32,768]{1,0:T(8,128)(2,1)S(1)} %get-tuple-element.89), channel_id=1, source_target_pairs={{0,12},{1,13},{2,14},{3,15},{4,8},{5,9},{6,10},{7,11},{8,4},{9,5},... | collective-permute-start | bytes 147464 | tf_op jit(solution)/shard_map/ppermute | solution.py:323
  14.2 4.2 %collective-permute-start.3 = (bf16[4,16,128]{2,1,0:T(8,128)(2,1)S(1)}, bf16[4,16,128]{2,1,0:T(8,128)(2,1)S(1)}, u32[]{:S(2)}, u32[]{:S(2)}) collective-permute-start(bf16[4,16,128]{2,1,0:T(8,128)(2,1)S(1)} %get-tuple-element.91), channel_id=1, source_target_pairs={{0,1},{1,0},{2,3},{3,2},{4,5},{5,4},{6,7},{7,6},{8,9},{9,8},{10,11... | collective-permute-start | bytes 49160 | tf_op jit(solution)/shard_map/ppermute | solution.py:326
  14.2 4.1 %collective-permute-start.4 = (bf16[4,16,128]{2,1,0:T(8,128)(2,1)S(1)}, bf16[4,16,128]{2,1,0:T(8,128)(2,1)S(1)}, u32[]{:S(2)}, u32[]{:S(2)}) collective-permute-start(bf16[4,16,128]{2,1,0:T(8,128)(2,1)S(1)} %get-tuple-element.92), channel_id=1, source_target_pairs={{0,2},{1,3},{2,0},{3,1},{4,6},{5,7},{6,4},{7,5},{8,10},{9,11},{10,... | collective-permute-start | bytes 49160 | tf_op jit(solution)/shard_map/ppermute | solution.py:326
  15.8 3.2 %collective-permute-start.5 = (bf16[4,16,128]{2,1,0:T(8,128)(2,1)S(1)}, bf16[4,16,128]{2,1,0:T(8,128)(2,1)S(1)}, u32[]{:S(2)}, u32[]{:S(2)}) collective-permute-start(bf16[4,16,128]{2,1,0:T(8,128)(2,1)S(1)} %get-tuple-element.93), channel_id=1, source_target_pairs={{0,3},{1,2},{2,1},{3,0},{4,7},{5,6},{6,5},{7,4},{8,11},{9,10},{10,... | collective-permute-start | bytes 49160 | tf_op jit(solution)/shard_map/ppermute | solution.py:326
  16.8 6.8 %collective-permute-start.9 = (bf16[4,32,512]{2,1,0:T(8,128)(2,1)S(1)}, bf16[4,32,512]{2,1,0:T(8,128)(2,1)S(1)}, u32[]{:S(2)}, u32[]{:S(2)}) collective-permute-start(bf16[4,32,512]{2,1,0:T(8,128)(2,1)S(1)} %get-tuple-element.111.cot_ref), channel_id=1, source_target_pairs={{0,2},{1,3},{2,0},{3,1},{4,6},{5,7},{6,4},{7,5},{8,10},{9,11},{10,... | collective-permute-start | bytes 393224 | tf_op jit(solution)/shard_map/ppermute | solution.py:326
  19.1 6.1 %collective-permute-start.8 = (bf16[32,512]{1,0:T(8,128)(2,1)S(1)}, bf16[32,512]{1,0:T(8,128)(2,1)S(1)}, u32[]{:S(2)}, u32[]{:S(2)}) collective-permute-start(bf16[32,512]{1,0:T(8,128)(2,1)S(1)} %shard_map.131.share_ref), channel_id=1, source_target_pairs={{0,12},{1,13},{2,14},{3,15},{4,8},{5,9},{6,10},{7,11},{8,4},{9,5},... | collective-permute-start | bytes 98312 | tf_op jit(solution)/shard_map/ppermute | solution.py:323
  19.9 5.3 %collective-permute-start.7 = (bf16[32,512]{1,0:T(8,128)(2,1)S(1)}, bf16[32,512]{1,0:T(8,128)(2,1)S(1)}, u32[]{:S(2)}, u32[]{:S(2)}) collective-permute-start(bf16[32,512]{1,0:T(8,128)(2,1)S(1)} %shard_map.131.share_ref), channel_id=1, source_target_pairs={{0,8},{1,9},{2,10},{3,11},{4,12},{5,13},{6,14},{7,15},{8,0},{9,1},... | collective-permute-start | bytes 98312 | tf_op jit(solution)/shard_map/ppermute | solution.py:323
  19.9 5.6 %collective-permute-start.6 = (bf16[32,512]{1,0:T(8,128)(2,1)S(1)}, bf16[32,512]{1,0:T(8,128)(2,1)S(1)}, u32[]{:S(2)}, u32[]{:S(2)}) collective-permute-start(bf16[32,512]{1,0:T(8,128)(2,1)S(1)} %shard_map.131.share_ref), channel_id=1, source_target_pairs={{0,4},{1,5},{2,6},{3,7},{4,0},{5,1},{6,2},{7,3},{8,12},{9,13},{10,... | collective-permute-start | bytes 98312 | tf_op jit(solution)/shard_map/ppermute | solution.py:323
  25.5 5.0 %collective-permute-start.10 = (bf16[4,32,512]{2,1,0:T(8,128)(2,1)S(1)}, bf16[4,32,512]{2,1,0:T(8,128)(2,1)S(1)}, u32[]{:S(2)}, u32[]{:S(2)}) collective-permute-start(bf16[4,32,512]{2,1,0:T(8,128)(2,1)S(1)} %pad_maximum_fusion.rest_ref), channel_id=1, source_target_pairs={{0,2},{1,3},{2,0},{3,1},{4,6},{5,7},{6,4},{7,5},{8,10},{9,11},{10,... | collective-permute-start | bytes 393224 | tf_op jit(solution)/shard_map/ppermute | solution.py:326
  27.0 1.8 %collective-permute-start.11 = (bf16[4,32,512]{2,1,0:T(8,128)(2,1)S(1)}, bf16[4,32,512]{2,1,0:T(8,128)(2,1)S(1)}, u32[]{:S(2)}, u32[]{:S(2)}) collective-permute-start(bf16[4,32,512]{2,1,0:T(8,128)(2,1)S(1)} %get-tuple-element.111.cot_ref), channel_id=1, source_target_pairs={{0,1},{1,0},{2,3},{3,2},{4,5},{5,4},{6,7},{7,6},{8,9},{9,8},{10,11... | collective-permute-start | bytes 393224 | tf_op jit(solution)/shard_map/ppermute | solution.py:326
  27.1 5.3 %collective-permute-start.13 = (bf16[4,32,512]{2,1,0:T(8,128)(2,1)S(1)}, bf16[4,32,512]{2,1,0:T(8,128)(2,1)S(1)}, u32[]{:S(2)}, u32[]{:S(2)}) collective-permute-start(bf16[4,32,512]{2,1,0:T(8,128)(2,1)S(1)} %pad_maximum_fusion.rest_ref), channel_id=1, source_target_pairs={{0,1},{1,0},{2,3},{3,2},{4,5},{5,4},{6,7},{7,6},{8,9},{9,8},{10,11... | collective-permute-start | bytes 393224 | tf_op jit(solution)/shard_map/ppermute | solution.py:326
  27.5 3.0 %collective-permute-start.14 = (bf16[4,32,512]{2,1,0:T(8,128)(2,1)S(1)}, bf16[4,32,512]{2,1,0:T(8,128)(2,1)S(1)}, u32[]{:S(2)}, u32[]{:S(2)}) collective-permute-start(bf16[4,32,512]{2,1,0:T(8,128)(2,1)S(1)} %collective-permute-done.9.cot_ref), channel_id=1, source_target_pairs={{0,1},{1,0},{2,3},{3,2},{4,5},{5,4},{6,7},{7,6},{8,9},{9,8},{10,11... | collective-permute-start | bytes 393224 | tf_op jit(solution)/shard_map/ppermute | solution.py:326
  30.6 2.6 %collective-permute-start.12 = (bf16[4,32,512]{2,1,0:T(8,128)(2,1)S(1)}, bf16[4,32,512]{2,1,0:T(8,128)(2,1)S(1)}, u32[]{:S(2)}, u32[]{:S(2)}) collective-permute-start(bf16[4,32,512]{2,1,0:T(8,128)(2,1)S(1)} %collective-permute-done.10.rest_ref), channel_id=1, source_target_pairs={{0,1},{1,0},{2,3},{3,2},{4,5},{5,4},{6,7},{7,6},{8,9},{9,8},{10,11... | collective-permute-start | bytes 393224 | tf_op jit(solution)/shard_map/ppermute | solution.py:326
  35.3 1.9 %collective-permute-start.15 = (bf16[8,32,512]{2,1,0:T(8,128)(2,1)S(1)}, bf16[8,32,512]{2,1,0:T(8,128)(2,1)S(1)}, u32[]{:S(2)}, u32[]{:S(2)}) collective-permute-start(bf16[8,32,512]{2,1,0:T(8,128)(2,1)S(1)} %shard_map.141), channel_id=1, source_target_pairs={{0,1},{1,0},{2,3},{3,2},{4,5},{5,4},{6,7},{7,6},{8,9},{9,8},{10,11... | collective-permute-start | bytes 786440 | tf_op jit(solution)/shard_map/ppermute | solution.py:326
  37.3 5.6 %collective-permute-start.16 = (bf16[4,32,512]{2,1,0:T(8,128)(2,1)S(1)}, bf16[4,32,512]{2,1,0:T(8,128)(2,1)S(1)}, u32[]{:S(2)}, u32[]{:S(2)}) collective-permute-start(bf16[4,32,512]{2,1,0:T(8,128)(2,1)S(1)} %get-tuple-element.133), channel_id=1, source_target_pairs={{0,2},{1,3},{2,0},{3,1},{4,6},{5,7},{6,4},{7,5},{8,10},{9,11},{10,... | collective-permute-start | bytes 393224 | tf_op jit(solution)/shard_map/ppermute | solution.py:326
  44.6 5.6 %collective-permute-start.18 = (bf16[4,32,512]{2,1,0:T(8,128)(2,1)S(1)}, bf16[4,32,512]{2,1,0:T(8,128)(2,1)S(1)}, u32[]{:S(2)}, u32[]{:S(2)}) collective-permute-start(bf16[4,32,512]{2,1,0:T(8,128)(2,1)S(1)} %get-tuple-element.155), channel_id=1, source_target_pairs={{0,2},{1,3},{2,0},{3,1},{4,6},{5,7},{6,4},{7,5},{8,10},{9,11},{10,... | collective-permute-start | bytes 393224 | tf_op jit(solution)/shard_map/ppermute | solution.py:326
  45.8 8.0 %collective-permute-start.22 = (bf16[32,512]{1,0:T(8,128)(2,1)S(1)}, bf16[32,512]{1,0:T(8,128)(2,1)S(1)}, u32[]{:S(2)}, u32[]{:S(2)}) collective-permute-start(bf16[32,512]{1,0:T(8,128)(2,1)S(1)} %get-tuple-element.162), channel_id=1, source_target_pairs={{0,12},{1,13},{2,14},{3,15},{4,8},{5,9},{6,10},{7,11},{8,4},{9,5},... | collective-permute-start | bytes 98312 | tf_op jit(solution)/shard_map/ppermute | solution.py:323
  48.1 6.6 %collective-permute-start.23 = (bf16[32,512]{1,0:T(8,128)(2,1)S(1)}, bf16[32,512]{1,0:T(8,128)(2,1)S(1)}, u32[]{:S(2)}, u32[]{:S(2)}) collective-permute-start(bf16[32,512]{1,0:T(8,128)(2,1)S(1)} %get-tuple-element.163), channel_id=1, source_target_pairs={{0,8},{1,9},{2,10},{3,11},{4,12},{5,13},{6,14},{7,15},{8,0},{9,1},... | collective-permute-start | bytes 98312 | tf_op jit(solution)/shard_map/ppermute | solution.py:323
  49.3 5.5 %collective-permute-start.24 = (bf16[32,512]{1,0:T(8,128)(2,1)S(1)}, bf16[32,512]{1,0:T(8,128)(2,1)S(1)}, u32[]{:S(2)}, u32[]{:S(2)}) collective-permute-start(bf16[32,512]{1,0:T(8,128)(2,1)S(1)} %get-tuple-element.164), channel_id=1, source_target_pairs={{0,4},{1,5},{2,6},{3,7},{4,0},{5,1},{6,2},{7,3},{8,12},{9,13},{10,... | collective-permute-start | bytes 98312 | tf_op jit(solution)/shard_map/ppermute | solution.py:323
  50.3 5.9 %collective-permute-start.19 = (bf16[32,512]{1,0:T(8,128)(2,1)S(1)}, bf16[32,512]{1,0:T(8,128)(2,1)S(1)}, u32[]{:S(2)}, u32[]{:S(2)}) collective-permute-start(bf16[32,512]{1,0:T(8,128)(2,1)S(1)} %get-tuple-element.156), channel_id=1, source_target_pairs={{0,12},{1,13},{2,14},{3,15},{4,8},{5,9},{6,10},{7,11},{8,4},{9,5},... | collective-permute-start | bytes 98312 | tf_op jit(solution)/shard_map/ppermute | solution.py:323
  52.6 4.8 %collective-permute-start.20 = (bf16[32,512]{1,0:T(8,128)(2,1)S(1)}, bf16[32,512]{1,0:T(8,128)(2,1)S(1)}, u32[]{:S(2)}, u32[]{:S(2)}) collective-permute-start(bf16[32,512]{1,0:T(8,128)(2,1)S(1)} %get-tuple-element.157), channel_id=1, source_target_pairs={{0,8},{1,9},{2,10},{3,11},{4,12},{5,13},{6,14},{7,15},{8,0},{9,1},... | collective-permute-start | bytes 98312 | tf_op jit(solution)/shard_map/ppermute | solution.py:323
  53.7 4.1 %collective-permute-start.21 = (bf16[32,512]{1,0:T(8,128)(2,1)S(1)}, bf16[32,512]{1,0:T(8,128)(2,1)S(1)}, u32[]{:S(2)}, u32[]{:S(2)}) collective-permute-start(bf16[32,512]{1,0:T(8,128)(2,1)S(1)} %get-tuple-element.158), channel_id=1, source_target_pairs={{0,4},{1,5},{2,6},{3,7},{4,0},{5,1},{6,2},{7,3},{8,12},{9,13},{10,... | collective-permute-start | bytes 98312 | tf_op jit(solution)/shard_map/ppermute | solution.py:323
  (11 other events, 97.4 us)

commit v13 on v12

--- a/solution.py
+++ b/solution.py
@@ -214,7 +214,7 @@
     tokens, width = gh_ref.shape[0], chunks * LANES
     n = tokens // 2
     gh = gh_ref[...]
-    step = n // 4
+    step = 1
     for first in range(0, n, step):
         block = weight_ref[first * width : (first + step) * width, :]
         terms = dot_by_halves(block, gh).T
@@ -268,12 +268,15 @@
     return functools.reduce(lambda a, b: a + b, [ref[...].astype(f32) for ref in refs])
 
 
-def final_kernel(width_all, share_ref, gain_ref, expo_ref, *refs):
-    *refs, layer_ref, grad_ref = refs
-    quarter = (len(refs) - 8) // 2
-    own_all, cot_all = added(refs[:4]), added(refs[4:8])
-    grad, layer = added(refs[8 : 8 + quarter]), added(refs[8 + quarter :])
-    layer_ref[...] = (share_ref[...].astype(f32) + layer).astype(bf16)
+def layer_kernel(share_ref, *refs):
+    *refs, layer_ref, own_ref, cot_ref = refs
+    own_ref[...], cot_ref[...] = added(refs[:4]), added(refs[4:8])
+    layer_ref[...] = (share_ref[...].astype(f32) + added(refs[8:])).astype(bf16)
+
+
+def final_kernel(width_all, own_ref, cot_ref, gain_ref, expo_ref, *refs):
+    *refs, grad_ref = refs
+    own_all, cot_all, grad = own_ref[...], cot_ref[...], added(refs)
     n, width = gain_ref.shape
     down, up = powers(expo_ref[...], -1), powers(expo_ref[...], 1)
     gain = gain_ref[...]
@@ -433,18 +436,15 @@
     rest_line, cot_line, cot_row, products[0] = together((rest_line, cots[0], cot_row, products[0]))
     rest_line_other = swap(rest_line, 1)
     cots += [cot_row, swap(cot_line, 1), swap(cot_row, 1)]
-    grads += [grad_active_part(1), grad_active_part(2)]
+    grads += [grad_active_part(part) for part in (1, 2, 3)]
     new_sender_base = call(
         sender_base_kernel,
         struct(sender_base.shape, f32),
         [SMEM, SMEM] + [VMEM] * 2,
         [me_in, sample_ids, new_rows, sender_base],
     )
-    rest_row, grads[1], grads[2], new_sender_base = together(
-        (rest_row, grads[1], grads[2], new_sender_base)
-    )
+    rest_row, grads, new_sender_base = together((rest_row, grads, new_sender_base))
     rests += [rest_row, rest_line_other, swap(rest_row, 1)]
-    grads.append(grad_active_part(3))
     products += [up_product_part(1), up_product_part(2)]
     gas, own_cots = zip(*grads)
     accs, squares, owns = map(list, zip(*products))
@@ -514,19 +514,18 @@
     out_row, grad_row = together((out_row, grad_row))
     out_line = line_sum(out_row, out_row_in)
     grad_line = line_sum(grad_row, grad_row_in)
-    layer_out, returned = call(
+    layer_out, own, own_cot = call(
+        layer_kernel,
+        (struct(share_shape, bf16), share_f32, share_f32),
+        [VMEM] * (9 + quarter),
+        [share, *owns, *own_cots, *out_line],
+    )
+    grad_line, layer_out, own, own_cot = together((grad_line, layer_out, own, own_cot))
+    returned = call(
         functools.partial(final_kernel, width_all),
-        (struct(share_shape, bf16), struct((2, width_all // LANES, LANES), f32)),
-        [VMEM] * (11 + 2 * quarter),
-        [
-            share,
-            gain,
-            backward_exponent.reshape(expo_shape),
-            *owns,
-            *own_cots,
-            *grad_line,
-            *out_line,
-        ],
+        struct((2, width_all // LANES, LANES), f32),
+        [VMEM] * (4 + quarter),
+        [own, own_cot, gain, backward_exponent.reshape(expo_shape), *grad_line],
     )
     return (
         new_sender_base,

time: 58.8 us -> 58.7 us (level)
  waiting for transfers between devices: 12.2 us -> 10.7 us
  starting transfers between devices: 26.5 us -> 27.4 us
    ppermute x13, starting transfers between devices: 7.45 us -> 8.39 us  [swap(): return lax.ppermute(x, 'dp', [(d, d ^ bits) for d in range(n)])]
    ppermute x13, waiting for transfers between devices: 2.42 us -> 1.69 us  [swap(): return lax.ppermute(x, 'dp', [(d, d ^ bits) for d in range(n)])]
    ppermute x12, waiting for transfers between devices: 9.75 us -> 9.05 us  [shift(): return lax.ppermute(x, 'dp', [(d, d ^ 4 * r) for d in range(n)]) if r else x]
    pallas_call x21 -> x22, Pallas kernels: 17.1 us -> 17.5 us  [call(): pl.pallas_call(kernel, out_shape=outs, in_specs=ins, out_specs=jax.tree.m...]
  transfers between devices with their start and end apart: 25 -> 25, of which waited for: 11 -> 11; matrix products, arithmetic and copies ran while one was open for 0% -> 0% of each run, Pallas kernels for 24% -> 25%
where the time goes in v13:
time: 58.7 us; the launch traced here: 58.5 us
  starting transfers between devices  27.4 us (47%)
  Pallas kernels  18.8 us (32%)
  waiting for transfers between devices  10.7 us (18%)
  between operations  1.55 us (3%)
    ppermute x12, starting transfers between devices, shift(): return lax.ppermute(x, 'dp', [(d, d ^ 4 * r) for d in range(n)]) if r else x  19 us
    pallas_call x22, Pallas kernels, call(): pl.pallas_call(kernel, out_shape=outs, in_specs=ins, out_specs=jax.tree.m...  17.5 us
    ppermute x12, waiting for transfers between devices, shift(): return lax.ppermute(x, 'dp', [(d, d ^ 4 * r) for d in range(n)]) if r else x  9.05 us
    ppermute x13, starting transfers between devices, swap(): return lax.ppermute(x, 'dp', [(d, d ^ bits) for d in range(n)])  8.39 us
    ppermute x13, waiting for transfers between devices, swap(): return lax.ppermute(x, 'dp', [(d, d ^ bits) for d in range(n)])  1.69 us
    pallas_call x1, Pallas kernels, on_device(): pl.pallas_call(send_kernel, out_shape=outs, grid=(1,), in_specs=[SMEM, SM...  1.22 us
  transfers between devices with their start and end apart: 25, of which 11 were waited for; matrix products, arithmetic and copies ran while one was open for 0% of the time, Pallas kernels for 25%

profile of v13, /device:TPU:0, one launch (start us, length us, event | category | flops | bytes accessed | tf_op | source)
XLA Modules:
  0.0 58.5 jit_solution(11069251432029317678)
XLA Ops:
  1.3 1.2 %shard_map.129 = (f32[2,8192]{1,0:T(2,128)S(1)}, f32[2,32,512]{2,1,0:T(8,128)S(1)}, f32[16,512]{1,0:T(8,128)S(1)}, bf16[32,768]{1,0:T(8,128)(2,1)S(1)}, bf16[32,...) custom-call(s32[1]{0:T(128)} %bitcast.me_ref, s32[1]{0:T(128)S(6)} %copy.15.ids_ref, ...), custom_call_target="tpu_custom_call" | custom-call | tf_op jit(solution)/shard_map/pallas_call | solution.py:358
  2.6 3.1 %collective-permute-start = (bf16[32,768]{1,0:T(8,128)(2,1)S(1)}, bf16[32,768]{1,0:T(8,128)(2,1)S(1)}, u32[]{:S(2)}, u32[]{:S(2)}) collective-permute-start(bf16[32,768]{1,0:T(8,128)(2,1)S(1)} %get-tuple-element.99), channel_id=1, source_target_pairs={{0,4},{1,5},{2,6},{3,7},{4,0},{5,1},{6,2},{7,3},{8,12},{9,13},{10,... | collective-permute-start | bytes 147464 | tf_op jit(solution)/shard_map/ppermute | solution.py:326
  5.6 2.6 %collective-permute-start.1 = (bf16[32,768]{1,0:T(8,128)(2,1)S(1)}, bf16[32,768]{1,0:T(8,128)(2,1)S(1)}, u32[]{:S(2)}, u32[]{:S(2)}) collective-permute-start(bf16[32,768]{1,0:T(8,128)(2,1)S(1)} %get-tuple-element.100), channel_id=1, source_target_pairs={{0,8},{1,9},{2,10},{3,11},{4,12},{5,13},{6,14},{7,15},{8,0},{9,1},... | collective-permute-start | bytes 147464 | tf_op jit(solution)/shard_map/ppermute | solution.py:326
  8.2 3.3 %collective-permute-done.1.refs_2_ = bf16[32,768]{1,0:T(8,128)(2,1)S(1)} collective-permute-done((bf16[32,768]{1,0:T(8,128)(2,1)S(1)}, bf16[32,768]{1,0:T(8,128)(2,1)S(1)}, u32[]{:S(2)}, u32[]{:S(2)}) %collective-permute-start.1) | collective-permute-done | bytes 49184 | tf_op jit(solution)/shard_map/ppermute | solution.py:326
  11.6 2.6 %collective-permute-done.2.refs_3_ = bf16[32,768]{1,0:T(8,128)(2,1)S(1)} collective-permute-done((bf16[32,768]{1,0:T(8,128)(2,1)S(1)}, bf16[32,768]{1,0:T(8,128)(2,1)S(1)}, u32[]{:S(2)}, u32[]{:S(2)}) %collective-permute-start.2) | collective-permute-done | bytes 49184 | tf_op jit(solution)/shard_map/ppermute | solution.py:326
  14.2 1.6 %collective-permute-start.4 = (bf16[4,16,128]{2,1,0:T(8,128)(2,1)S(1)}, bf16[4,16,128]{2,1,0:T(8,128)(2,1)S(1)}, u32[]{:S(2)}, u32[]{:S(2)}) collective-permute-start(bf16[4,16,128]{2,1,0:T(8,128)(2,1)S(1)} %get-tuple-element.104), channel_id=1, source_target_pairs={{0,2},{1,3},{2,0},{3,1},{4,6},{5,7},{6,4},{7,5},{8,10},{9,11},{10,... | collective-permute-start | bytes 49160 | tf_op jit(solution)/shard_map/ppermute | solution.py:329
  16.8 1.5 %collective-permute-start.9 = (bf16[4,32,512]{2,1,0:T(8,128)(2,1)S(1)}, bf16[4,32,512]{2,1,0:T(8,128)(2,1)S(1)}, u32[]{:S(2)}, u32[]{:S(2)}) collective-permute-start(bf16[4,32,512]{2,1,0:T(8,128)(2,1)S(1)} %get-tuple-element.125.cot_ref), channel_id=1, source_target_pairs={{0,2},{1,3},{2,0},{3,1},{4,6},{5,7},{6,4},{7,5},{8,10},{9,11},{10,... | collective-permute-start | bytes 393224 | tf_op jit(solution)/shard_map/ppermute | solution.py:329
  19.9 3.6 %collective-permute-start.6 = (bf16[32,512]{1,0:T(8,128)(2,1)S(1)}, bf16[32,512]{1,0:T(8,128)(2,1)S(1)}, u32[]{:S(2)}, u32[]{:S(2)}) collective-permute-start(bf16[32,512]{1,0:T(8,128)(2,1)S(1)} %shard_map.131.share_ref), channel_id=1, source_target_pairs={{0,4},{1,5},{2,6},{3,7},{4,0},{5,1},{6,2},{7,3},{8,12},{9,13},{10,... | collective-permute-start | bytes 98312 | tf_op jit(solution)/shard_map/ppermute | solution.py:326
  23.6 1.1 %shard_map.132 = (f32[896,32]{1,0:T(8,128)S(1)}, f32[32,512]{1,0:T(8,128)S(1)}) custom-call(s32[1]{0:T(128)} %bitcast.me_ref, bf16[4,32,512]{2,1,0:T(8,128)(2,1)S(1)} %get-tuple-element.125.cot_ref, bf16[896,8192]{1,0:T(8,128)(2,1)S(1)} %bitcast.13), custom_call_target="tpu_custom_call" | custom-call | flops 1840000000 | tf_op jit(solution)/shard_map/pallas_call | solution.py:336
  27.6 1.1 %shard_map.134 = (f32[896,32]{1,0:T(8,128)S(1)}, f32[32,512]{1,0:T(8,128)S(1)}) custom-call(s32[1]{0:T(128)} %bitcast.me_ref, bf16[4,32,512]{2,1,0:T(8,128)(2,1)S(1)} %collective-permute-done.9.cot_ref, bf16[896,8192]{1,0:T(8,128)(2,1)S(1)} %bitcast.13), custom_call_target="tpu_custom_call" | custom-call | flops 1840000000 | tf_op jit(solution)/shard_map/pallas_call | solution.py:336
  28.9 1.1 %shard_map.136 = (f32[896,32]{1,0:T(8,128)S(1)}, f32[32,512]{1,0:T(8,128)S(1)}) custom-call(s32[1]{0:T(128)} %bitcast.me_ref, bf16[4,32,512]{2,1,0:T(8,128)(2,1)S(1)} %collective-permute-done.12.cot_ref, bf16[896,8192]{1,0:T(8,128)(2,1)S(1)} %bitcast.13), custom_call_target="tpu_custom_call" | custom-call | flops 1840000000 | tf_op jit(solution)/shard_map/pallas_call | solution.py:336
  30.0 1.1 %shard_map.135 = (f32[896,32]{1,0:T(8,128)S(1)}, f32[32,512]{1,0:T(8,128)S(1)}) custom-call(s32[1]{0:T(128)} %bitcast.me_ref, bf16[4,32,512]{2,1,0:T(8,128)(2,1)S(1)} %collective-permute-done.11.cot_ref, bf16[896,8192]{1,0:T(8,128)(2,1)S(1)} %bitcast.13), custom_call_target="tpu_custom_call" | custom-call | flops 1840000000 | tf_op jit(solution)/shard_map/pallas_call | solution.py:336
  33.7 1.4 %shard_map.141 = bf16[8,32,512]{2,1,0:T(8,128)(2,1)S(1)} custom-call(s32[1]{0:T(128)} %bitcast.me_ref, bf16[32,896]{1,0:T(8,128)(2,1)S(1)} %get-tuple-element.146.active_ref, bf16[896,8192]{1,0:T(8,128)(2,1)S(1)} %bitcast.13), custom_call_target="tpu_custom_call" | custom-call | flops 1724999936 | tf_op jit(solution)/shard_map/pallas_call | solution.py:336
  35.3 1.4 %shard_map.142.kept_ref = bf16[8,32,512]{2,1,0:T(8,128)(2,1)S(1)} custom-call(s32[1]{0:T(128)} %bitcast.me_ref, bf16[32,896]{1,0:T(8,128)(2,1)S(1)} %get-tuple-element.146.active_ref, bf16[896,8192]{1,0:T(8,128)(2,1)S(1)} %bitcast.13), custom_call_target="tpu_custom_call" | custom-call | flops 1724999936 | tf_op jit(solution)/shard_map/pallas_call | solution.py:336
  36.8 1.5 %collective-permute-start.16 = (bf16[4,32,512]{2,1,0:T(8,128)(2,1)S(1)}, bf16[4,32,512]{2,1,0:T(8,128)(2,1)S(1)}, u32[]{:S(2)}, u32[]{:S(2)}) collective-permute-start(bf16[4,32,512]{2,1,0:T(8,128)(2,1)S(1)} %get-tuple-element.149), channel_id=1, source_target_pairs={{0,2},{1,3},{2,0},{3,1},{4,6},{5,7},{6,4},{7,5},{8,10},{9,11},{10,... | collective-permute-start | bytes 393224 | tf_op jit(solution)/shard_map/ppermute | solution.py:329
  38.2 4.2 %shard_map.144.rows_ref = f32[4,512,128]{2,1,0:T(8,128)S(1)} custom-call(s32[1]{0:T(128)} %bitcast.me_ref, bf16[32,896]{1,0:T(8,128)(2,1)S(1)} %get-tuple-element.148.gh_ref, bf16[8192,896]{1,0:T(8,128)(2,1)S(1)} %bitcast.15), custom_call_target="tpu_custom_call" | custom-call | flops 5175000064 | tf_op jit(solution)/shard_map/pallas_call | solution.py:336
  44.3 1.5 %collective-permute-start.18 = (bf16[4,32,512]{2,1,0:T(8,128)(2,1)S(1)}, bf16[4,32,512]{2,1,0:T(8,128)(2,1)S(1)}, u32[]{:S(2)}, u32[]{:S(2)}) collective-permute-start(bf16[4,32,512]{2,1,0:T(8,128)(2,1)S(1)} %get-tuple-element.163), channel_id=1, source_target_pairs={{0,2},{1,3},{2,0},{3,1},{4,6},{5,7},{6,4},{7,5},{8,10},{9,11},{10,... | collective-permute-start | bytes 393224 | tf_op jit(solution)/shard_map/ppermute | solution.py:329
  45.8 2.4 %collective-permute-start.22 = (bf16[32,512]{1,0:T(8,128)(2,1)S(1)}, bf16[32,512]{1,0:T(8,128)(2,1)S(1)}, u32[]{:S(2)}, u32[]{:S(2)}) collective-permute-start(bf16[32,512]{1,0:T(8,128)(2,1)S(1)} %get-tuple-element.178), channel_id=1, source_target_pairs={{0,12},{1,13},{2,14},{3,15},{4,8},{5,9},{6,10},{7,11},{8,4},{9,5},... | collective-permute-start | bytes 98312 | tf_op jit(solution)/shard_map/ppermute | solution.py:326
  48.1 1.1 %collective-permute-start.23 = (bf16[32,512]{1,0:T(8,128)(2,1)S(1)}, bf16[32,512]{1,0:T(8,128)(2,1)S(1)}, u32[]{:S(2)}, u32[]{:S(2)}) collective-permute-start(bf16[32,512]{1,0:T(8,128)(2,1)S(1)} %get-tuple-element.179), channel_id=1, source_target_pairs={{0,8},{1,9},{2,10},{3,11},{4,12},{5,13},{6,14},{7,15},{8,0},{9,1},... | collective-permute-start | bytes 98312 | tf_op jit(solution)/shard_map/ppermute | solution.py:326
  49.2 1.0 %collective-permute-start.24 = (bf16[32,512]{1,0:T(8,128)(2,1)S(1)}, bf16[32,512]{1,0:T(8,128)(2,1)S(1)}, u32[]{:S(2)}, u32[]{:S(2)}) collective-permute-start(bf16[32,512]{1,0:T(8,128)(2,1)S(1)} %get-tuple-element.180), channel_id=1, source_target_pairs={{0,4},{1,5},{2,6},{3,7},{4,0},{5,1},{6,2},{7,3},{8,12},{9,13},{10,... | collective-permute-start | bytes 98312 | tf_op jit(solution)/shard_map/ppermute | solution.py:326
  50.3 2.4 %collective-permute-start.19 = (bf16[32,512]{1,0:T(8,128)(2,1)S(1)}, bf16[32,512]{1,0:T(8,128)(2,1)S(1)}, u32[]{:S(2)}, u32[]{:S(2)}) collective-permute-start(bf16[32,512]{1,0:T(8,128)(2,1)S(1)} %get-tuple-element.164), channel_id=1, source_target_pairs={{0,12},{1,13},{2,14},{3,15},{4,8},{5,9},{6,10},{7,11},{8,4},{9,5},... | collective-permute-start | bytes 98312 | tf_op jit(solution)/shard_map/ppermute | solution.py:326
  52.6 0.8 %collective-permute-start.20 = (bf16[32,512]{1,0:T(8,128)(2,1)S(1)}, bf16[32,512]{1,0:T(8,128)(2,1)S(1)}, u32[]{:S(2)}, u32[]{:S(2)}) collective-permute-start(bf16[32,512]{1,0:T(8,128)(2,1)S(1)} %get-tuple-element.165), channel_id=1, source_target_pairs={{0,8},{1,9},{2,10},{3,11},{4,12},{5,13},{6,14},{7,15},{8,0},{9,1},... | collective-permute-start | bytes 98312 | tf_op jit(solution)/shard_map/ppermute | solution.py:326
  53.5 1.3 %collective-permute-start.21 = (bf16[32,512]{1,0:T(8,128)(2,1)S(1)}, bf16[32,512]{1,0:T(8,128)(2,1)S(1)}, u32[]{:S(2)}, u32[]{:S(2)}) collective-permute-start(bf16[32,512]{1,0:T(8,128)(2,1)S(1)} %get-tuple-element.166), channel_id=1, source_target_pairs={{0,4},{1,5},{2,6},{3,7},{4,0},{5,1},{6,2},{7,3},{8,12},{9,13},{10,... | collective-permute-start | bytes 98312 | tf_op jit(solution)/shard_map/ppermute | solution.py:326
  56.0 1.5 %collective-permute-done.20.refs_1_ = bf16[32,512]{1,0:T(8,128)(2,1)S(1)} collective-permute-done((bf16[32,512]{1,0:T(8,128)(2,1)S(1)}, bf16[32,512]{1,0:T(8,128)(2,1)S(1)}, u32[]{:S(2)}, u32[]{:S(2)}) %collective-permute-start.20) | collective-permute-done | bytes 32800 | tf_op jit(solution)/shard_map/ppermute | solution.py:326
  (72 shorter events, 12.7 us)
Async XLA Ops:
  2.6 5.7 %collective-permute-start = (bf16[32,768]{1,0:T(8,128)(2,1)S(1)}, bf16[32,768]{1,0:T(8,128)(2,1)S(1)}, u32[]{:S(2)}, u32[]{:S(2)}) collective-permute-start(bf16[32,768]{1,0:T(8,128)(2,1)S(1)} %get-tuple-element.99), channel_id=1, source_target_pairs={{0,4},{1,5},{2,6},{3,7},{4,0},{5,1},{6,2},{7,3},{8,12},{9,13},{10,... | collective-permute-start | bytes 147464 | tf_op jit(solution)/shard_map/ppermute | solution.py:326
  5.6 5.9 %collective-permute-start.1 = (bf16[32,768]{1,0:T(8,128)(2,1)S(1)}, bf16[32,768]{1,0:T(8,128)(2,1)S(1)}, u32[]{:S(2)}, u32[]{:S(2)}) collective-permute-start(bf16[32,768]{1,0:T(8,128)(2,1)S(1)} %get-tuple-element.100), channel_id=1, source_target_pairs={{0,8},{1,9},{2,10},{3,11},{4,12},{5,13},{6,14},{7,15},{8,0},{9,1},... | collective-permute-start | bytes 147464 | tf_op jit(solution)/shard_map/ppermute | solution.py:326
  8.2 5.9 %collective-permute-start.2 = (bf16[32,768]{1,0:T(8,128)(2,1)S(1)}, bf16[32,768]{1,0:T(8,128)(2,1)S(1)}, u32[]{:S(2)}, u32[]{:S(2)}) collective-permute-start(bf16[32,768]{1,0:T(8,128)(2,1)S(1)} %get-tuple-element.101), channel_id=1, source_target_pairs={{0,12},{1,13},{2,14},{3,15},{4,8},{5,9},{6,10},{7,11},{8,4},{9,5},... | collective-permute-start | bytes 147464 | tf_op jit(solution)/shard_map/ppermute | solution.py:326
  14.2 4.2 %collective-permute-start.3 = (bf16[4,16,128]{2,1,0:T(8,128)(2,1)S(1)}, bf16[4,16,128]{2,1,0:T(8,128)(2,1)S(1)}, u32[]{:S(2)}, u32[]{:S(2)}) collective-permute-start(bf16[4,16,128]{2,1,0:T(8,128)(2,1)S(1)} %get-tuple-element.103), channel_id=1, source_target_pairs={{0,1},{1,0},{2,3},{3,2},{4,5},{5,4},{6,7},{7,6},{8,9},{9,8},{10,11... | collective-permute-start | bytes 49160 | tf_op jit(solution)/shard_map/ppermute | solution.py:329
  14.2 4.1 %collective-permute-start.4 = (bf16[4,16,128]{2,1,0:T(8,128)(2,1)S(1)}, bf16[4,16,128]{2,1,0:T(8,128)(2,1)S(1)}, u32[]{:S(2)}, u32[]{:S(2)}) collective-permute-start(bf16[4,16,128]{2,1,0:T(8,128)(2,1)S(1)} %get-tuple-element.104), channel_id=1, source_target_pairs={{0,2},{1,3},{2,0},{3,1},{4,6},{5,7},{6,4},{7,5},{8,10},{9,11},{10,... | collective-permute-start | bytes 49160 | tf_op jit(solution)/shard_map/ppermute | solution.py:329
  15.8 3.2 %collective-permute-start.5 = (bf16[4,16,128]{2,1,0:T(8,128)(2,1)S(1)}, bf16[4,16,128]{2,1,0:T(8,128)(2,1)S(1)}, u32[]{:S(2)}, u32[]{:S(2)}) collective-permute-start(bf16[4,16,128]{2,1,0:T(8,128)(2,1)S(1)} %get-tuple-element.105), channel_id=1, source_target_pairs={{0,3},{1,2},{2,1},{3,0},{4,7},{5,6},{6,5},{7,4},{8,11},{9,10},{10,... | collective-permute-start | bytes 49160 | tf_op jit(solution)/shard_map/ppermute | solution.py:329
  16.8 6.8 %collective-permute-start.9 = (bf16[4,32,512]{2,1,0:T(8,128)(2,1)S(1)}, bf16[4,32,512]{2,1,0:T(8,128)(2,1)S(1)}, u32[]{:S(2)}, u32[]{:S(2)}) collective-permute-start(bf16[4,32,512]{2,1,0:T(8,128)(2,1)S(1)} %get-tuple-element.125.cot_ref), channel_id=1, source_target_pairs={{0,2},{1,3},{2,0},{3,1},{4,6},{5,7},{6,4},{7,5},{8,10},{9,11},{10,... | collective-permute-start | bytes 393224 | tf_op jit(solution)/shard_map/ppermute | solution.py:329
  19.1 6.1 %collective-permute-start.8 = (bf16[32,512]{1,0:T(8,128)(2,1)S(1)}, bf16[32,512]{1,0:T(8,128)(2,1)S(1)}, u32[]{:S(2)}, u32[]{:S(2)}) collective-permute-start(bf16[32,512]{1,0:T(8,128)(2,1)S(1)} %shard_map.131.share_ref), channel_id=1, source_target_pairs={{0,12},{1,13},{2,14},{3,15},{4,8},{5,9},{6,10},{7,11},{8,4},{9,5},... | collective-permute-start | bytes 98312 | tf_op jit(solution)/shard_map/ppermute | solution.py:326
  19.9 5.3 %collective-permute-start.7 = (bf16[32,512]{1,0:T(8,128)(2,1)S(1)}, bf16[32,512]{1,0:T(8,128)(2,1)S(1)}, u32[]{:S(2)}, u32[]{:S(2)}) collective-permute-start(bf16[32,512]{1,0:T(8,128)(2,1)S(1)} %shard_map.131.share_ref), channel_id=1, source_target_pairs={{0,8},{1,9},{2,10},{3,11},{4,12},{5,13},{6,14},{7,15},{8,0},{9,1},... | collective-permute-start | bytes 98312 | tf_op jit(solution)/shard_map/ppermute | solution.py:326
  19.9 5.6 %collective-permute-start.6 = (bf16[32,512]{1,0:T(8,128)(2,1)S(1)}, bf16[32,512]{1,0:T(8,128)(2,1)S(1)}, u32[]{:S(2)}, u32[]{:S(2)}) collective-permute-start(bf16[32,512]{1,0:T(8,128)(2,1)S(1)} %shard_map.131.share_ref), channel_id=1, source_target_pairs={{0,4},{1,5},{2,6},{3,7},{4,0},{5,1},{6,2},{7,3},{8,12},{9,13},{10,... | collective-permute-start | bytes 98312 | tf_op jit(solution)/shard_map/ppermute | solution.py:326
  25.5 5.6 %collective-permute-start.10 = (bf16[4,32,512]{2,1,0:T(8,128)(2,1)S(1)}, bf16[4,32,512]{2,1,0:T(8,128)(2,1)S(1)}, u32[]{:S(2)}, u32[]{:S(2)}) collective-permute-start(bf16[4,32,512]{2,1,0:T(8,128)(2,1)S(1)} %pad_maximum_fusion.rest_ref), channel_id=1, source_target_pairs={{0,2},{1,3},{2,0},{3,1},{4,6},{5,7},{6,4},{7,5},{8,10},{9,11},{10,... | collective-permute-start | bytes 393224 | tf_op jit(solution)/shard_map/ppermute | solution.py:329
  27.0 3.0 %collective-permute-start.11 = (bf16[4,32,512]{2,1,0:T(8,128)(2,1)S(1)}, bf16[4,32,512]{2,1,0:T(8,128)(2,1)S(1)}, u32[]{:S(2)}, u32[]{:S(2)}) collective-permute-start(bf16[4,32,512]{2,1,0:T(8,128)(2,1)S(1)} %get-tuple-element.125.cot_ref), channel_id=1, source_target_pairs={{0,1},{1,0},{2,3},{3,2},{4,5},{5,4},{6,7},{7,6},{8,9},{9,8},{10,11... | collective-permute-start | bytes 393224 | tf_op jit(solution)/shard_map/ppermute | solution.py:329
  27.1 5.1 %collective-permute-start.14 = (bf16[4,32,512]{2,1,0:T(8,128)(2,1)S(1)}, bf16[4,32,512]{2,1,0:T(8,128)(2,1)S(1)}, u32[]{:S(2)}, u32[]{:S(2)}) collective-permute-start(bf16[4,32,512]{2,1,0:T(8,128)(2,1)S(1)} %pad_maximum_fusion.rest_ref), channel_id=1, source_target_pairs={{0,1},{1,0},{2,3},{3,2},{4,5},{5,4},{6,7},{7,6},{8,9},{9,8},{10,11... | collective-permute-start | bytes 393224 | tf_op jit(solution)/shard_map/ppermute | solution.py:329
  31.1 1.8 %collective-permute-start.13 = (bf16[4,32,512]{2,1,0:T(8,128)(2,1)S(1)}, bf16[4,32,512]{2,1,0:T(8,128)(2,1)S(1)}, u32[]{:S(2)}, u32[]{:S(2)}) collective-permute-start(bf16[4,32,512]{2,1,0:T(8,128)(2,1)S(1)} %collective-permute-done.10.rest_ref), channel_id=1, source_target_pairs={{0,1},{1,0},{2,3},{3,2},{4,5},{5,4},{6,7},{7,6},{8,9},{9,8},{10,11... | collective-permute-start | bytes 393224 | tf_op jit(solution)/shard_map/ppermute | solution.py:329
  35.1 1.6 %collective-permute-start.15 = (bf16[8,32,512]{2,1,0:T(8,128)(2,1)S(1)}, bf16[8,32,512]{2,1,0:T(8,128)(2,1)S(1)}, u32[]{:S(2)}, u32[]{:S(2)}) collective-permute-start(bf16[8,32,512]{2,1,0:T(8,128)(2,1)S(1)} %shard_map.141), channel_id=1, source_target_pairs={{0,1},{1,0},{2,3},{3,2},{4,5},{5,4},{6,7},{7,6},{8,9},{9,8},{10,11... | collective-permute-start | bytes 786440 | tf_op jit(solution)/shard_map/ppermute | solution.py:329
  36.8 5.8 %collective-permute-start.16 = (bf16[4,32,512]{2,1,0:T(8,128)(2,1)S(1)}, bf16[4,32,512]{2,1,0:T(8,128)(2,1)S(1)}, u32[]{:S(2)}, u32[]{:S(2)}) collective-permute-start(bf16[4,32,512]{2,1,0:T(8,128)(2,1)S(1)} %get-tuple-element.149), channel_id=1, source_target_pairs={{0,2},{1,3},{2,0},{3,1},{4,6},{5,7},{6,4},{7,5},{8,10},{9,11},{10,... | collective-permute-start | bytes 393224 | tf_op jit(solution)/shard_map/ppermute | solution.py:329
  42.6 1.6 %collective-permute-start.17 = (bf16[8,32,512]{2,1,0:T(8,128)(2,1)S(1)}, bf16[8,32,512]{2,1,0:T(8,128)(2,1)S(1)}, u32[]{:S(2)}, u32[]{:S(2)}) collective-permute-start(bf16[8,32,512]{2,1,0:T(8,128)(2,1)S(1)} %get-tuple-element.151), channel_id=1, source_target_pairs={{0,1},{1,0},{2,3},{3,2},{4,5},{5,4},{6,7},{7,6},{8,9},{9,8},{10,11... | collective-permute-start | bytes 786440 | tf_op jit(solution)/shard_map/ppermute | solution.py:329
  44.3 6.0 %collective-permute-start.18 = (bf16[4,32,512]{2,1,0:T(8,128)(2,1)S(1)}, bf16[4,32,512]{2,1,0:T(8,128)(2,1)S(1)}, u32[]{:S(2)}, u32[]{:S(2)}) collective-permute-start(bf16[4,32,512]{2,1,0:T(8,128)(2,1)S(1)} %get-tuple-element.163), channel_id=1, source_target_pairs={{0,2},{1,3},{2,0},{3,1},{4,6},{5,7},{6,4},{7,5},{8,10},{9,11},{10,... | collective-permute-start | bytes 393224 | tf_op jit(solution)/shard_map/ppermute | solution.py:329
  45.8 7.7 %collective-permute-start.22 = (bf16[32,512]{1,0:T(8,128)(2,1)S(1)}, bf16[32,512]{1,0:T(8,128)(2,1)S(1)}, u32[]{:S(2)}, u32[]{:S(2)}) collective-permute-start(bf16[32,512]{1,0:T(8,128)(2,1)S(1)} %get-tuple-element.178), channel_id=1, source_target_pairs={{0,12},{1,13},{2,14},{3,15},{4,8},{5,9},{6,10},{7,11},{8,4},{9,5},... | collective-permute-start | bytes 98312 | tf_op jit(solution)/shard_map/ppermute | solution.py:326
  48.1 6.6 %collective-permute-start.23 = (bf16[32,512]{1,0:T(8,128)(2,1)S(1)}, bf16[32,512]{1,0:T(8,128)(2,1)S(1)}, u32[]{:S(2)}, u32[]{:S(2)}) collective-permute-start(bf16[32,512]{1,0:T(8,128)(2,1)S(1)} %get-tuple-element.179), channel_id=1, source_target_pairs={{0,8},{1,9},{2,10},{3,11},{4,12},{5,13},{6,14},{7,15},{8,0},{9,1},... | collective-permute-start | bytes 98312 | tf_op jit(solution)/shard_map/ppermute | solution.py:326
  49.2 5.5 %collective-permute-start.24 = (bf16[32,512]{1,0:T(8,128)(2,1)S(1)}, bf16[32,512]{1,0:T(8,128)(2,1)S(1)}, u32[]{:S(2)}, u32[]{:S(2)}) collective-permute-start(bf16[32,512]{1,0:T(8,128)(2,1)S(1)} %get-tuple-element.180), channel_id=1, source_target_pairs={{0,4},{1,5},{2,6},{3,7},{4,0},{5,1},{6,2},{7,3},{8,12},{9,13},{10,... | collective-permute-start | bytes 98312 | tf_op jit(solution)/shard_map/ppermute | solution.py:326
  50.3 5.8 %collective-permute-start.19 = (bf16[32,512]{1,0:T(8,128)(2,1)S(1)}, bf16[32,512]{1,0:T(8,128)(2,1)S(1)}, u32[]{:S(2)}, u32[]{:S(2)}) collective-permute-start(bf16[32,512]{1,0:T(8,128)(2,1)S(1)} %get-tuple-element.164), channel_id=1, source_target_pairs={{0,12},{1,13},{2,14},{3,15},{4,8},{5,9},{6,10},{7,11},{8,4},{9,5},... | collective-permute-start | bytes 98312 | tf_op jit(solution)/shard_map/ppermute | solution.py:326
  52.6 4.9 %collective-permute-start.20 = (bf16[32,512]{1,0:T(8,128)(2,1)S(1)}, bf16[32,512]{1,0:T(8,128)(2,1)S(1)}, u32[]{:S(2)}, u32[]{:S(2)}) collective-permute-start(bf16[32,512]{1,0:T(8,128)(2,1)S(1)} %get-tuple-element.165), channel_id=1, source_target_pairs={{0,8},{1,9},{2,10},{3,11},{4,12},{5,13},{6,14},{7,15},{8,0},{9,1},... | collective-permute-start | bytes 98312 | tf_op jit(solution)/shard_map/ppermute | solution.py:326
  53.5 4.3 %collective-permute-start.21 = (bf16[32,512]{1,0:T(8,128)(2,1)S(1)}, bf16[32,512]{1,0:T(8,128)(2,1)S(1)}, u32[]{:S(2)}, u32[]{:S(2)}) collective-permute-start(bf16[32,512]{1,0:T(8,128)(2,1)S(1)} %get-tuple-element.166), channel_id=1, source_target_pairs={{0,4},{1,5},{2,6},{3,7},{4,0},{5,1},{6,2},{7,3},{8,12},{9,13},{10,... | collective-permute-start | bytes 98312 | tf_op jit(solution)/shard_map/ppermute | solution.py:326
  (11 other events, 97.5 us)
